TPU v7x, 32 devices: a whole 2x2x4 slice. The times are simulated.
32 devices in a mesh: col: 16 (over z, x, core), row: 2 (over y).
Axes of the slice: x: 2, y: 2, z: 4, core: 2. Of those that a mesh axis runs over, the one named last changes fastest.
Arguments:
- inputs: bfloat16 [512, 8192], P('col', 'row'), may hold values from -6 to 6
- weight: bfloat16 [8192, 28672], P('row', 'col'), may hold values from -0.0625 to 0.0625
- adapter_down_factors: bfloat16 [16, 16, 8192], P(None, None, 'row'), may hold values from -0.06629126 to 0.06629126
- adapter_up_factors: bfloat16 [16, 16, 28672], P(None, None, 'col'), may hold values from -1.5 to 1.5
- magnitude: float32 [16, 28672], P(None, 'col'), may hold values from 0.5 to 2
- cotangent: bfloat16 [512, 28672], P('row', 'col'), may hold values from -6 to 6
- tenant: int32 [512], replicated, may hold values from 0 to 15, as said below
Outputs:
- output: bfloat16 [512, 28672], P('row', 'col')
- grad_inputs: bfloat16 [512, 8192], P('col', 'row')
- grad_b: float32 [16, 16, 28672], P(None, None, 'col')
- grad_m: float32 [16, 28672], P(None, 'col')
Inputs may be any that keep to these rules, and one draw needn't show every extreme that they name: `tenant`: constant on each aligned block of 128 tokens; both 0 and 15 occur in every draw.
All inputs are finite; a program needn't handle non-finite values.
Results may differ from a plain program's by a relative error of at most 0.0051.
Values may be sent and summed in bfloat16 or wider, within the bound.
No kernel may reach another device: no remote copies, remote signals or barrier semaphores. Data moves between devices by JAX's collectives and lax.ppermute only.
A program may use at most 192 MiB of HBM per device.

v0:
```python
import jax
import jax.numpy as jnp
from jax import lax
from jax.sharding import PartitionSpec as P

BLOCK = 128


HIGH = lax.Precision.HIGHEST
EPS = 1e-06


def direct_norm_terms(weight, adapter_down_factors, adapter_up_factors):
    wf = weight.astype(jnp.float32)

    def single_tenant(pair):
        a_one, b_one = pair
        tile = wf + jnp.einsum(
            "rd,rj->dj", a_one.astype(jnp.float32), b_one.astype(jnp.float32), precision=HIGH
        )
        return jnp.sum(tile * tile, axis=0)

    return lax.map(single_tenant, (adapter_down_factors, adapter_up_factors))


def shards(inputs, weight, adapter_down_factors, adapter_up_factors, magnitude, cotangent, tenant):
    row_count = lax.axis_size("row")
    tenant_number, rank_dimension, width_dimension = adapter_down_factors.shape
    cols = weight.shape[1]
    gathered = lax.all_gather(inputs, "col", axis=0, tiled=True)
    tokens_all = gathered.shape[0]
    nblocks = tokens_all // BLOCK
    block_tenant_index = tenant.reshape(nblocks, BLOCK)[:, 0]
    tenants = jnp.arange(tenant_number, dtype=jnp.int32)
    onehot_tok = (tenant[:, None] == tenants[None, :]).astype(jnp.float32)
    onehot_blk = (tenants[:, None] == block_tenant_index[None, :]).astype(jnp.float32)
    down_factor_blocks = adapter_down_factors[block_tenant_index]
    low_part = jnp.einsum(
        "esc,etc->est",
        down_factor_blocks,
        gathered.reshape(nblocks, BLOCK, width_dimension),
        preferred_element_type=jnp.float32,
    )
    partial_column_norm = direct_norm_terms(weight, adapter_down_factors, adapter_up_factors)
    low_sum, norm_squared_total = lax.psum((low_part, partial_column_norm), "row")
    low_blocks = low_sum.astype(jnp.bfloat16)
    scale = magnitude / jnp.sqrt(norm_squared_total + EPS)
    rows_row = tokens_all // row_count
    row_scale = jnp.dot(onehot_tok, scale, precision=HIGH)
    partial_value = lax.psum_scatter(
        jnp.dot(gathered, weight, preferred_element_type=jnp.float32) * row_scale,
        "row",
        scatter_dimension=0,
        tiled=True,
    )
    blocks_mine = rows_row // BLOCK
    block_start = lax.axis_index("row") * blocks_mine
    local_low_rank = lax.dynamic_slice_in_dim(low_blocks, block_start, blocks_mine, 0)
    local_tenant_index = lax.dynamic_slice_in_dim(block_tenant_index, block_start, blocks_mine, 0)
    onehot_mine = lax.dynamic_slice_in_dim(onehot_blk, block_start, blocks_mine, 1)
    scale_mine = jnp.dot(onehot_mine.T, scale, precision=HIGH)
    adapter = jnp.einsum(
        "dyn,dyz->dnz",
        local_low_rank,
        adapter_up_factors[local_tenant_index],
        preferred_element_type=jnp.float32,
    )
    partial_value = partial_value.reshape(blocks_mine, BLOCK, cols)
    result = partial_value + scale_mine[:, None, :] * adapter
    output = result.reshape(rows_row, cols).astype(jnp.bfloat16)
    grad_all, out_all = (
        lax.all_gather(cotangent, "row", axis=0, tiled=True),
        lax.all_gather(output, "row", axis=0, tiled=True),
    )
    scale_blocks = jnp.dot(onehot_blk.T, scale, precision=HIGH)
    grad_three = grad_all.reshape(nblocks, BLOCK, cols).astype(jnp.float32)
    gradient_scaled = (grad_three * scale_blocks[:, None, :]).astype(jnp.bfloat16)
    per_block = jnp.einsum(
        "brk,bkj->brj", low_blocks, gradient_scaled, preferred_element_type=jnp.float32
    )
    grad_b = jnp.einsum("tb,brj->trj", onehot_blk, per_block, precision=HIGH)
    product = jnp.sum(
        grad_three * out_all.reshape(nblocks, BLOCK, cols).astype(jnp.float32), axis=1
    )
    grad_m = jnp.dot(onehot_blk, product, precision=HIGH) / magnitude
    back_part = jnp.einsum(
        "hty,hxy->htx",
        gradient_scaled,
        adapter_up_factors[block_tenant_index],
        preferred_element_type=jnp.float32,
    )
    back_part = back_part.reshape(tokens_all, rank_dimension)
    grad_flat = gradient_scaled.reshape(tokens_all, cols)
    down_factor_rows = adapter_down_factors[tenant].astype(jnp.float32)
    main = lax.dot_general(
        grad_flat, weight, (((1,), (1,)), ((), ())), preferred_element_type=jnp.float32
    )
    grad_inputs = lax.psum_scatter(
        main + jnp.sum(back_part[:, :, None] * down_factor_rows, axis=1),
        "col",
        scatter_dimension=0,
        tiled=True,
    ).astype(jnp.bfloat16)
    return (output, grad_inputs, grad_b, grad_m)


def solution(mesh):
    return jax.shard_map(
        shards,
        mesh=mesh,
        in_specs=(
            P("col", "row"),
            P("row", "col"),
            P(None, None, "row"),
            P(None, None, "col"),
            P(None, "col"),
            P("row", "col"),
            P(),
        ),
        out_specs=(P("row", "col"), P("col", "row"), P(None, None, "col"), P(None, "col")),
        check_vma=False,
    )
```

profile of v0, /device:TPU:8, one launch (start us, length us, event | category | flops | bytes accessed | tf_op | source)
XLA Modules:
  0.0 595.7 jit_solution(13272359915400535546)
XLA Ops:
  8.1 16.7 %convert_element_type.43 = f32[4096,1792]{1,0:T(8,128)} convert(bf16[4096,1792]{1,0:T(8,128)(2,1)} %param.10) | non-fusion elementwise | flops 7340032 | bytes 44040192 | tf_op jit(solution)/shard_map/convert_element_type | solution.py:14
  24.8 208.2 %while.10 = (s32[]{:T(128)}, f32[16,1792]{1,0:T(8,128)}, bf16[16,16,4096]{2,1,0:T(8,128)(2,1)S(1)}, bf16[16,16,1792]{2,1,0:T(8,128)(2,1)}, f32[4096,1792]{1,0:T(8,128)}, /*index=5*/s32[]{:T(128)}, s32[]{:T(128)}) while((s32[]{:T(128)}, f32[16,1792]{1,0:T(8,128)}, bf16[16,16,4096]{2,1,0:T(8,128)(2,1)S(1)}, bf16[16,16,1792]{2,1,0:T(8,128)(2,1)}, ...), condition=%wide.region_2.3_spmd, body=%wide.region_0.2_spmd.sunk | while | flops 256899328 | bytes 29585496 | solution.py:23
  24.8 11.6 %multiply_reduce_fusion.3 = f32[1792]{0:T(1024)S(1)} fusion(f32[4096,1792]{1,0:T(8,128)} %get-tuple-element.108, bf16[16,16,4096]{2,1,0:T(8,128)(2,1)S(1)} %get-tuple-element.106, s32[]{:T(128)S(6)} %copy.26, bf16[16,16,1792]{2,1,0:T(8,128)(2,1)} %get-tuple-element.107), kind=kOutput, calls=%fused_computation.4.clone.1 | convolution fusion | flops 256899328 | bytes 29556736 | tf_op jit(solution)/shard_map/while/body/eval_jaxpr/rd,rj->dj/dot_general | solution.py:18
  37.8 11.5 %multiply_reduce_fusion.3 = f32[1792]{0:T(1024)S(1)} fusion(f32[4096,1792]{1,0:T(8,128)} %get-tuple-element.108, bf16[16,16,4096]{2,1,0:T(8,128)(2,1)S(1)} %get-tuple-element.106, s32[]{:T(128)S(6)} %copy.26, bf16[16,16,1792]{2,1,0:T(8,128)(2,1)} %get-tuple-element.107), kind=kOutput, calls=%fused_computation.4.clone.1 | convolution fusion | flops 256899328 | bytes 29556736 | tf_op jit(solution)/shard_map/while/body/eval_jaxpr/rd,rj->dj/dot_general | solution.py:18
  50.9 11.5 %multiply_reduce_fusion.3 = f32[1792]{0:T(1024)S(1)} fusion(f32[4096,1792]{1,0:T(8,128)} %get-tuple-element.108, bf16[16,16,4096]{2,1,0:T(8,128)(2,1)S(1)} %get-tuple-element.106, s32[]{:T(128)S(6)} %copy.26, bf16[16,16,1792]{2,1,0:T(8,128)(2,1)} %get-tuple-element.107), kind=kOutput, calls=%fused_computation.4.clone.1 | convolution fusion | flops 256899328 | bytes 29556736 | tf_op jit(solution)/shard_map/while/body/eval_jaxpr/rd,rj->dj/dot_general | solution.py:18
  63.9 11.5 %multiply_reduce_fusion.3 = f32[1792]{0:T(1024)S(1)} fusion(f32[4096,1792]{1,0:T(8,128)} %get-tuple-element.108, bf16[16,16,4096]{2,1,0:T(8,128)(2,1)S(1)} %get-tuple-element.106, s32[]{:T(128)S(6)} %copy.26, bf16[16,16,1792]{2,1,0:T(8,128)(2,1)} %get-tuple-element.107), kind=kOutput, calls=%fused_computation.4.clone.1 | convolution fusion | flops 256899328 | bytes 29556736 | tf_op jit(solution)/shard_map/while/body/eval_jaxpr/rd,rj->dj/dot_general | solution.py:18
  76.9 11.5 %multiply_reduce_fusion.3 = f32[1792]{0:T(1024)S(1)} fusion(f32[4096,1792]{1,0:T(8,128)} %get-tuple-element.108, bf16[16,16,4096]{2,1,0:T(8,128)(2,1)S(1)} %get-tuple-element.106, s32[]{:T(128)S(6)} %copy.26, bf16[16,16,1792]{2,1,0:T(8,128)(2,1)} %get-tuple-element.107), kind=kOutput, calls=%fused_computation.4.clone.1 | convolution fusion | flops 256899328 | bytes 29556736 | tf_op jit(solution)/shard_map/while/body/eval_jaxpr/rd,rj->dj/dot_general | solution.py:18
  89.9 11.5 %multiply_reduce_fusion.3 = f32[1792]{0:T(1024)S(1)} fusion(f32[4096,1792]{1,0:T(8,128)} %get-tuple-element.108, bf16[16,16,4096]{2,1,0:T(8,128)(2,1)S(1)} %get-tuple-element.106, s32[]{:T(128)S(6)} %copy.26, bf16[16,16,1792]{2,1,0:T(8,128)(2,1)} %get-tuple-element.107), kind=kOutput, calls=%fused_computation.4.clone.1 | convolution fusion | flops 256899328 | bytes 29556736 | tf_op jit(solution)/shard_map/while/body/eval_jaxpr/rd,rj->dj/dot_general | solution.py:18
  101.4 1.5 dynamic_update_slice.5
  102.9 11.5 %multiply_reduce_fusion.3 = f32[1792]{0:T(1024)S(1)} fusion(f32[4096,1792]{1,0:T(8,128)} %get-tuple-element.108, bf16[16,16,4096]{2,1,0:T(8,128)(2,1)S(1)} %get-tuple-element.106, s32[]{:T(128)S(6)} %copy.26, bf16[16,16,1792]{2,1,0:T(8,128)(2,1)} %get-tuple-element.107), kind=kOutput, calls=%fused_computation.4.clone.1 | convolution fusion | flops 256899328 | bytes 29556736 | tf_op jit(solution)/shard_map/while/body/eval_jaxpr/rd,rj->dj/dot_general | solution.py:18
  114.4 1.5 dynamic_update_slice.5
  115.9 11.5 %multiply_reduce_fusion.3 = f32[1792]{0:T(1024)S(1)} fusion(f32[4096,1792]{1,0:T(8,128)} %get-tuple-element.108, bf16[16,16,4096]{2,1,0:T(8,128)(2,1)S(1)} %get-tuple-element.106, s32[]{:T(128)S(6)} %copy.26, bf16[16,16,1792]{2,1,0:T(8,128)(2,1)} %get-tuple-element.107), kind=kOutput, calls=%fused_computation.4.clone.1 | convolution fusion | flops 256899328 | bytes 29556736 | tf_op jit(solution)/shard_map/while/body/eval_jaxpr/rd,rj->dj/dot_general | solution.py:18
  128.9 11.5 %multiply_reduce_fusion.3 = f32[1792]{0:T(1024)S(1)} fusion(f32[4096,1792]{1,0:T(8,128)} %get-tuple-element.108, bf16[16,16,4096]{2,1,0:T(8,128)(2,1)S(1)} %get-tuple-element.106, s32[]{:T(128)S(6)} %copy.26, bf16[16,16,1792]{2,1,0:T(8,128)(2,1)} %get-tuple-element.107), kind=kOutput, calls=%fused_computation.4.clone.1 | convolution fusion | flops 256899328 | bytes 29556736 | tf_op jit(solution)/shard_map/while/body/eval_jaxpr/rd,rj->dj/dot_general | solution.py:18
  141.9 11.5 %multiply_reduce_fusion.3 = f32[1792]{0:T(1024)S(1)} fusion(f32[4096,1792]{1,0:T(8,128)} %get-tuple-element.108, bf16[16,16,4096]{2,1,0:T(8,128)(2,1)S(1)} %get-tuple-element.106, s32[]{:T(128)S(6)} %copy.26, bf16[16,16,1792]{2,1,0:T(8,128)(2,1)} %get-tuple-element.107), kind=kOutput, calls=%fused_computation.4.clone.1 | convolution fusion | flops 256899328 | bytes 29556736 | tf_op jit(solution)/shard_map/while/body/eval_jaxpr/rd,rj->dj/dot_general | solution.py:18
  153.4 1.5 dynamic_update_slice.5
  154.9 11.5 %multiply_reduce_fusion.3 = f32[1792]{0:T(1024)S(1)} fusion(f32[4096,1792]{1,0:T(8,128)} %get-tuple-element.108, bf16[16,16,4096]{2,1,0:T(8,128)(2,1)S(1)} %get-tuple-element.106, s32[]{:T(128)S(6)} %copy.26, bf16[16,16,1792]{2,1,0:T(8,128)(2,1)} %get-tuple-element.107), kind=kOutput, calls=%fused_computation.4.clone.1 | convolution fusion | flops 256899328 | bytes 29556736 | tf_op jit(solution)/shard_map/while/body/eval_jaxpr/rd,rj->dj/dot_general | solution.py:18
  166.4 1.5 dynamic_update_slice.5
  167.9 11.5 %multiply_reduce_fusion.3 = f32[1792]{0:T(1024)S(1)} fusion(f32[4096,1792]{1,0:T(8,128)} %get-tuple-element.108, bf16[16,16,4096]{2,1,0:T(8,128)(2,1)S(1)} %get-tuple-element.106, s32[]{:T(128)S(6)} %copy.26, bf16[16,16,1792]{2,1,0:T(8,128)(2,1)} %get-tuple-element.107), kind=kOutput, calls=%fused_computation.4.clone.1 | convolution fusion | flops 256899328 | bytes 29556736 | tf_op jit(solution)/shard_map/while/body/eval_jaxpr/rd,rj->dj/dot_general | solution.py:18
  179.4 1.5 dynamic_update_slice.5
  180.9 11.5 %multiply_reduce_fusion.3 = f32[1792]{0:T(1024)S(1)} fusion(f32[4096,1792]{1,0:T(8,128)} %get-tuple-element.108, bf16[16,16,4096]{2,1,0:T(8,128)(2,1)S(1)} %get-tuple-element.106, s32[]{:T(128)S(6)} %copy.26, bf16[16,16,1792]{2,1,0:T(8,128)(2,1)} %get-tuple-element.107), kind=kOutput, calls=%fused_computation.4.clone.1 | convolution fusion | flops 256899328 | bytes 29556736 | tf_op jit(solution)/shard_map/while/body/eval_jaxpr/rd,rj->dj/dot_general | solution.py:18
  192.4 1.5 dynamic_update_slice.5
  193.9 11.5 %multiply_reduce_fusion.3 = f32[1792]{0:T(1024)S(1)} fusion(f32[4096,1792]{1,0:T(8,128)} %get-tuple-element.108, bf16[16,16,4096]{2,1,0:T(8,128)(2,1)S(1)} %get-tuple-element.106, s32[]{:T(128)S(6)} %copy.26, bf16[16,16,1792]{2,1,0:T(8,128)(2,1)} %get-tuple-element.107), kind=kOutput, calls=%fused_computation.4.clone.1 | convolution fusion | flops 256899328 | bytes 29556736 | tf_op jit(solution)/shard_map/while/body/eval_jaxpr/rd,rj->dj/dot_general | solution.py:18
  206.9 11.5 %multiply_reduce_fusion.3 = f32[1792]{0:T(1024)S(1)} fusion(f32[4096,1792]{1,0:T(8,128)} %get-tuple-element.108, bf16[16,16,4096]{2,1,0:T(8,128)(2,1)S(1)} %get-tuple-element.106, s32[]{:T(128)S(6)} %copy.26, bf16[16,16,1792]{2,1,0:T(8,128)(2,1)} %get-tuple-element.107), kind=kOutput, calls=%fused_computation.4.clone.1 | convolution fusion | flops 256899328 | bytes 29556736 | tf_op jit(solution)/shard_map/while/body/eval_jaxpr/rd,rj->dj/dot_general | solution.py:18
  218.5 1.5 dynamic_update_slice.5
  219.9 11.5 %multiply_reduce_fusion.3 = f32[1792]{0:T(1024)S(1)} fusion(f32[4096,1792]{1,0:T(8,128)} %get-tuple-element.108, bf16[16,16,4096]{2,1,0:T(8,128)(2,1)S(1)} %get-tuple-element.106, s32[]{:T(128)S(6)} %copy.26, bf16[16,16,1792]{2,1,0:T(8,128)(2,1)} %get-tuple-element.107), kind=kOutput, calls=%fused_computation.4.clone.1 | convolution fusion | flops 256899328 | bytes 29556736 | tf_op jit(solution)/shard_map/while/body/eval_jaxpr/rd,rj->dj/dot_general | solution.py:18
  231.5 1.5 dynamic_update_slice.5
  233.6 22.0 %all-reduce.2.cloned.1.call-done = f32[16,1792]{1,0:T(8,128)} async-done(((f32[16,1792]{1,0:T(8,128)}), f32[16,1792]{1,0:T(8,128)}) %all-reduce.2.cloned.1.call-update) | async-done | bytes 114704 | tf_op jit(solution)/shard_map/psum | solution.py:45
  255.6 4.4 fusion.13
  259.9 27.5 %all-gather.4.cloned.1.call-done = bf16[512,4096]{1,0:T(8,128)(2,1)} async-done(((bf16[32,4096]{1,0:T(8,128)(2,1)}), bf16[512,4096]{1,0:T(8,128)(2,1)}) %all-gather.4.cloned.1.call-update) | async-done | bytes 4194320 | tf_op jit(solution)/shard_map/all_gather | solution.py:30
  287.4 15.5 %convolution_multiply_fusion = f32[512,1792]{1,0:T(8,128)} fusion(f32[512,1792]{1,0:T(8,128)} %fusion.13, bf16[512,4096]{1,0:T(8,128)(2,1)} %all-gather.4.cloned.1.call-done, bf16[4096,1792]{1,0:T(8,128)(2,1)} %param.10), kind=kOutput, calls=%fused_computation.17 | convolution fusion | flops 7517110272 | bytes 26214400 | tf_op jit(solution)/shard_map/dot_general | solution.py:51
  304.0 1.7 gather_fusion.1
  306.6 4.4 fusion.24
  311.0 9.0 %psum.15 = bf16[4,16,128]{2,1,0:T(8,128)(2,1)S(1)} all-reduce(f32[4,16,128]{2,1,0:T(8,128)S(1)} %fusion.24), channel_id=1, replica_groups=mesh['col'=16,'row'=2] {'row'}, use_global_device_ids=true, to_apply=%region_5.6 | all-reduce | flops 8192 | bytes 49152 | tf_op jit(solution)/shard_map/psum | solution.py:45
  320.0 31.4 %reduce-scatter.3.cloned.1.call-done = f32[256,1792]{1,0:T(8,128)} async-done(((f32[512,1792]{1,0:T(8,128)}), f32[256,1792]{1,0:T(8,128)}) %reduce-scatter.3.cloned.1.call-update) | async-done | bytes 1835024 | tf_op jit(solution)/shard_map/reduce_scatter | solution.py:50
  351.4 2.9 fusion.8
  354.6 1.7 gather_fusion.2
  356.3 24.0 %gather_fusion.3 = bf16[512,16,4096]{2,1,0:T(8,128)(2,1)} fusion(bf16[16,16,4096]{2,1,0:T(8,128)(2,1)S(1)} %get-tuple-element.117, s32[1024]{0:T(1024)S(1)} %pad_clamp_fusion), kind=kCustom, calls=%fused_computation.3 | custom fusion | bytes 134219776 | tf_op jit(solution)/shard_map/gather | solution.py:94
  380.5 2.8 all-gather.6.cloned.1.call-done
  383.4 3.2 fusion.6
  386.5 29.1 %all-gather.8.cloned.1.call-done = bf16[512,1792]{1,0:T(8,128)(2,1)} async-done(((bf16[256,1792]{1,0:T(8,128)(2,1)}), bf16[512,1792]{1,0:T(8,128)(2,1)}) %all-gather.8.cloned.1.call-update) | async-done | bytes 1835024 | tf_op jit(solution)/shard_map/all_gather | solution.py:73
  415.6 2.0 fusion.5
  417.6 1.8 copy-done.1
  420.1 36.7 %multiply_reduce_fusion.1 = f32[512,4096]{1,0:T(8,128)} fusion(bf16[512,16,4096]{2,1,0:T(8,128)(2,1)} %gather_fusion.3, f32[512,16]{1,0:T(8,128)S(1)} %bitcast.43), kind=kLoop, calls=%fused_computation.10 | loop fusion | flops 98566144 | bytes 75530240 | tf_op jit(solution)/shard_map/reduce_sum | solution.py:99
  456.8 26.4 %convolution_add_fusion = f32[512,4096]{1,0:T(8,128)} fusion(f32[512,4096]{1,0:T(8,128)} %multiply_reduce_fusion.1, bf16[512,1792]{1,0:T(8,128)(2,1)S(1)} %copy-done.3, bf16[4096,1792]{1,0:T(8,128)(2,1)} %param.10), kind=kOutput, calls=%fused_computation.11 | convolution fusion | flops 7518289920 | bytes 33292288 | tf_op jit(solution)/shard_map/dot_general | solution.py:95
  483.2 2.4 fusion.9
  486.8 2.3 copy.18
  490.1 96.7 %reduce-scatter.5.cloned.1.call-done = f32[32,4096]{1,0:T(8,128)} async-done(((f32[512,4096]{1,0:T(8,128)}), f32[32,4096]{1,0:T(8,128)}) %reduce-scatter.5.cloned.1.call-update) | async-done | bytes 524304 | tf_op jit(solution)/shard_map/reduce_scatter | solution.py:98
  586.8 1.8 convert_element_type.53
  (63 shorter events, 17.8 us)
Async XLA Ops:
  8.0 247.6 %all-reduce.2.cloned.1.call-start = ((), (), s32[]{:S(2)}) async-start(), calls=%async_computation.3 | async-start | bytes 229376 | tf_op jit(solution)/shard_map/psum | solution.py:45
  8.1 16.7 %copy-start = (bf16[16,16,4096]{2,1,0:T(8,128)(2,1)S(1)}, bf16[16,16,4096]{2,1,0:T(8,128)(2,1)}, u32[]{:S(2)}) copy-start(bf16[16,16,4096]{2,1,0:T(8,128)(2,1)} %param.11) | copy-start | bytes 6291460
  24.8 230.8 %copy-start.4 = (f32[16,1792]{1,0:T(8,128)S(1)}, f32[16,1792]{1,0:T(8,128)}, u32[]{:S(2)}) copy-start(f32[16,1792]{1,0:T(8,128)} %param.13) | copy-start | bytes 344068
  24.8 230.8 %copy-start.6 = (s32[512]{0:T(512)S(1)}, s32[512]{0:T(512)}, u32[]{:S(2)}) copy-start(s32[512]{0:T(512)} %param.15) | copy-start | bytes 6148
  233.0 54.4 %all-gather.4.cloned.1.call-start = ((), (), s32[]{:S(2)}) async-start(), calls=%async_computation.2 | async-start | bytes 4456448 | tf_op jit(solution)/shard_map/all_gather | solution.py:30
  233.5 117.9 %reduce-scatter.3.cloned.1.call-start = ((), (), s32[]{:S(2)}) async-start(), calls=%async_computation.4 | async-start | bytes 5505024 | tf_op jit(solution)/shard_map/reduce_scatter | solution.py:50
  302.9 3.5 copy-start.5
  303.0 80.4 %all-gather.6.cloned.1.call-start = ((), (), s32[]{:S(2)}) async-start(), calls=%async_computation.5 | async-start | bytes 2752512 | tf_op jit(solution)/shard_map/all_gather | solution.py:72
  303.7 111.9 %all-gather.8.cloned.1.call-start = ((), (), s32[]{:S(2)}) async-start(), calls=%async_computation.7 | async-start | bytes 2752512 | tf_op jit(solution)/shard_map/all_gather | solution.py:73
  354.3 232.5 %reduce-scatter.5.cloned.1.call-start = ((), (), s32[]{:S(2)}) async-start(), calls=%async_computation.6 | async-start | bytes 8912896 | tf_op jit(solution)/shard_map/reduce_scatter | solution.py:98
  383.3 32.3 %copy-start.2 = (bf16[512,1792]{1,0:T(8,128)(2,1)S(1)}, bf16[512,1792]{1,0:T(8,128)(2,1)}, u32[]{:S(2)}) copy-start(bf16[512,1792]{1,0:T(8,128)(2,1)} %all-gather.6.cloned.1.call-done) | copy-start | bytes 5505028
  417.6 1.8 copy-start.1
  420.1 36.7 %copy-start.3 = (bf16[512,1792]{1,0:T(8,128)(2,1)S(1)}, bf16[512,1792]{1,0:T(8,128)(2,1)}, u32[]{:S(2)}) copy-start(bf16[512,1792]{1,0:T(8,128)(2,1)} %fusion.6) | copy-start | bytes 5505028
Sparse Core Ops, SparseCore 0:
  233.1 22.4 all-reduce.1
  303.1 48.2 reduce-scatter.2
  353.1 30.2 all-gather.5
  385.4 30.1 all-gather.7
Sparse Core Ops, SparseCore 1:
  235.6 51.8 all-gather.3
  483.3 103.4 reduce-scatter.4
where the time goes:
time: 598 us; the launch traced here: 596 us
  matrix products  243 us (41%)
  waiting for transfers between devices  211 us (35%)
  other arithmetic  60.7 us (10%)
  local copies, waits for them, and re-layouts  55.9 us (9%)
  between operations  15.3 us (3%)
  blocking collectives  8.98 us (2%)
    dot_general x16, matrix products, single_tenant(): jnp.einsum('rd,rj->dj', a_one.astype(jnp.float32), b_one.astype(jnp.float...  184 us
    reduce_scatter x1, waiting for transfers between devices, shards(): lax.psum_scatter(main + jnp.sum(back_part[:, :, None] * down_factor_rows,...  96.7 us
    reduce_sum x1, other arithmetic, shards(): jnp.sum(back_part[:, :, None] * down_factor_rows, axis=1)  36.7 us
    reduce_scatter x1, waiting for transfers between devices, shards(): lax.psum_scatter(jnp.dot(gathered, weight, preferred_element_type=jnp.flo...  31.4 us
    all_gather x1, waiting for transfers between devices, shards(): lax.all_gather(output, 'row', axis=0, tiled=True)  29.1 us
    all_gather x1, waiting for transfers between devices, shards(): gathered = lax.all_gather(inputs, 'col', axis=0, tiled=True)  27.5 us
    dot_general x1, matrix products, shards(): lax.dot_general(grad_flat, weight, (((1,), (1,)), ((), ())), preferred_el...  26.4 us
    gather x1, local copies, waits for them, and re-layouts, shards(): down_factor_rows = adapter_down_factors[tenant].astype(jnp.float32)  24 us
  transfers between devices with their start and end apart: 6, of which 6 were waited for; matrix products, arithmetic and copies ran while one was open for 8% of the time, Pallas kernels for 0%

commit v1 on v0

v1 whole, which is shorter than its diff:
```python
import functools

import jax
import jax.numpy as jnp
from jax import lax
from jax.experimental import pallas as pl
from jax.experimental.pallas import tpu as pltpu
from jax.sharding import PartitionSpec as P

BLOCK = 128
EPS = 1e-06
HIGH = lax.Precision.HIGHEST
CHUNKS = 4
F32 = jnp.float32
BF16 = jnp.bfloat16
COST = pl.CostEstimate(flops=1000, bytes_accessed=1000, transcendentals=0)
LAST = (((1,), (1,)), ((), ()))
PARAMS = pltpu.CompilerParams(vmem_limit_bytes=40 * 1024 * 1024)


def cat_blocks(refs):
    return jnp.concatenate([ref[0] for ref in refs], axis=0)


def order_specs(deps):
    return [pl.BlockSpec(memory_space=pl.ANY)] * len(deps)


def column_block(cols):
    return 256 if cols % 256 == 0 else 128


def hi_lo(value, axis):
    hi = value.astype(BF16)
    lo = (value - hi.astype(F32)).astype(BF16)
    return jnp.concatenate([hi, lo], axis=axis)


def norm_body(nblk, rank, tenant_ref, w_ref, *refs):
    a_refs, up_refs = refs[:nblk], refs[nblk : 2 * nblk]
    nsq_ref, gram_ref = refs[2 * nblk :]
    depth, jb = w_ref.shape
    rows = nblk * rank

    @pl.when(pl.program_id(0) == 0)
    def _():
        a_all = cat_blocks(a_refs)
        gram = lax.dot_general(a_all, a_all, LAST, preferred_element_type=F32)
        row = lax.broadcasted_iota(jnp.int32, (rows, rows), 0) // rank
        col = lax.broadcasted_iota(jnp.int32, (rows, rows), 1) // rank
        gram_ref[...] = jnp.where(row == col, gram, 0.0)

    step = min(depth, 256)
    cross = jnp.zeros((rows, jb), F32)
    squares = jnp.zeros((8, jb), F32)
    for start in range(0, depth, step):
        w = w_ref[start : start + step, :]
        a_part = jnp.concatenate([ref[0, :, start : start + step] for ref in a_refs], axis=0)
        cross = cross + jnp.dot(a_part, w, preferred_element_type=F32)
        wf = w.astype(F32)
        squares = squares + jnp.sum((wf * wf).reshape(step // 8, 8, jb), axis=0)
    up = cat_blocks(up_refs).astype(F32)
    quad = jnp.dot(gram_ref[...], up, preferred_element_type=F32, precision=HIGH)
    mixed = jnp.sum((up * (2.0 * cross + quad)).reshape(nblk, rank, jb), axis=1)
    nsq_ref[...] = mixed + jnp.sum(squares, axis=0, keepdims=True)


def partial_norms(tenant, weight, down, up):
    depth, cols = weight.shape
    rank = down.shape[1]
    nblk = tenant.shape[0] // BLOCK
    jb = column_block(cols)

    def down_spec(b):
        return pl.BlockSpec((1, rank, depth), lambda j, t: (t[b * BLOCK], 0, 0))

    def up_spec(b):
        return pl.BlockSpec((1, rank, jb), lambda j, t: (t[b * BLOCK], 0, j))

    return pl.pallas_call(
        functools.partial(norm_body, nblk, rank),
        out_shape=jax.ShapeDtypeStruct((nblk, cols), F32),
        grid_spec=pltpu.PrefetchScalarGridSpec(
            num_scalar_prefetch=1,
            grid=(cols // jb,),
            in_specs=[pl.BlockSpec((depth, jb), lambda j, t: (0, j))]
            + [down_spec(b) for b in range(nblk)]
            + [up_spec(b) for b in range(nblk)],
            out_specs=pl.BlockSpec((nblk, jb), lambda j, t: (0, j)),
            scratch_shapes=[pltpu.VMEM((nblk * rank, nblk * rank), F32)],
        ),
        compiler_params=PARAMS,
        cost_estimate=COST,
        name="partial_norms",
    )(tenant, weight, *([down] * nblk), *([up] * nblk))


def scaled_body(nblk, rank, groups, tenant_ref, base_ref, *refs):
    cot_refs, refs = refs[:groups], refs[groups:]
    nsq_a, nsq_b, mag_ref = refs[:3]
    up_refs = refs[3 : 3 + nblk]
    scale_ref, sg_ref, back_ref = refs[-3:]
    for b in range(nblk):
        total = nsq_a[b : b + 1, :] + nsq_b[b : b + 1, :]
        mag = mag_ref[pl.ds(tenant_ref[b * BLOCK], 1), :]
        scale_ref[b : b + 1, :] = mag / jnp.sqrt(total + EPS)
    up_all = cat_blocks(up_refs)
    owner = lax.broadcasted_iota(jnp.int32, (BLOCK, nblk * rank), 1) // rank
    for g in range(groups):
        for i in range(cot_refs[g].shape[0] // BLOCK):
            b = base_ref[g] + i
            rows = pl.ds(pl.multiple_of(b * BLOCK, BLOCK), BLOCK)
            grad = cot_refs[g][i * BLOCK : (i + 1) * BLOCK, :].astype(F32)
            sg = (grad * scale_ref[pl.ds(b, 1), :]).astype(BF16)
            sg_ref[rows, :] = sg
            back = lax.dot_general(sg, up_all, LAST, preferred_element_type=F32)
            back_ref[rows, :] = hi_lo(jnp.where(owner == b, back, 0.0), 1)


def scaled_gradient(tenant, bases, cots, nsq_a, nsq_b, magnitude, up, deps):
    tokens = tenant.shape[0]
    nblk = tokens // BLOCK
    tenants, cols = magnitude.shape
    rank = up.shape[1]

    def whole(array):
        return pl.BlockSpec(array.shape, lambda i, t, s: (0,) * array.ndim)

    def up_spec(b):
        return pl.BlockSpec((1, rank, cols), lambda i, t, s: (t[b * BLOCK], 0, 0))

    shapes = (
        jax.ShapeDtypeStruct((nblk, cols), F32),
        jax.ShapeDtypeStruct((tokens, cols), BF16),
        jax.ShapeDtypeStruct((tokens, 2 * nblk * rank), BF16),
    )
    return pl.pallas_call(
        functools.partial(scaled_body, nblk, rank, len(cots)),
        out_shape=shapes,
        grid_spec=pltpu.PrefetchScalarGridSpec(
            num_scalar_prefetch=2,
            grid=(1,),
            in_specs=[whole(c) for c in cots]
            + [whole(nsq_a), whole(nsq_b), whole(magnitude)]
            + [up_spec(b) for b in range(nblk)]
            + order_specs(deps),
            out_specs=[whole(s) for s in shapes],
        ),
        compiler_params=PARAMS,
        cost_estimate=COST,
        name="scaled_gradient",
    )(tenant, bases, *cots, nsq_a, nsq_b, magnitude, *([up] * nblk), *deps)


def grad_body(nblk, rank, nz, tenant_ref, place_ref, sg_ref, back_ref, w_ref, *refs):
    a_refs = refs[:nblk]
    keep_ref, send_ref, sgp_ref, backp_ref = refs[-4:]
    tokens = sg_ref.shape[0]
    piece = tokens // (4 * nz)
    half = tokens // 2

    @pl.when(pl.program_id(0) == 0)
    def _():
        z, x, core = place_ref[0], place_ref[1], place_ref[2]
        for fc in range(2):
            for fx in range(2):
                for k in range(nz):
                    c = lax.rem(z + k, nz) * 4 + (x ^ fx) * 2 + (core ^ fc)
                    src = pl.ds(pl.multiple_of(c * piece, piece), piece)
                    at = ((fc * 2 + fx) * nz + k) * piece
                    sgp_ref[at : at + piece, :] = sg_ref[src, :]
                    backp_ref[at : at + piece, :] = back_ref[src, :]

    down = cat_blocks(a_refs)
    down = jnp.concatenate([down, down], axis=0)
    w = w_ref[...]
    for h, out in ((1, send_ref), (0, keep_ref)):
        rows = slice(h * half, (h + 1) * half)
        part = lax.dot_general(sgp_ref[rows, :], w, LAST, preferred_element_type=F32)
        part = part + jnp.dot(backp_ref[rows, :], down, preferred_element_type=F32)
        out[...] = part.astype(out.dtype)


def grad_chunk(tenant, place, sg, back, weight, down, nz, chunk, deps):
    depth, cols = weight.shape
    tokens = sg.shape[0]
    nblk = tokens // BLOCK
    rank = down.shape[1]
    size = depth // CHUNKS
    db = min(size, 512)
    steps = size // db

    def down_spec(b):
        return pl.BlockSpec((1, rank, db), lambda i, t, p: (t[b * BLOCK], 0, chunk * steps + i))

    return pl.pallas_call(
        functools.partial(grad_body, nblk, rank, nz),
        out_shape=(
            jax.ShapeDtypeStruct((tokens // 2, size), F32),
            jax.ShapeDtypeStruct((tokens // 2, size), BF16),
        ),
        grid_spec=pltpu.PrefetchScalarGridSpec(
            num_scalar_prefetch=2,
            grid=(steps,),
            in_specs=[
                pl.BlockSpec(sg.shape, lambda i, t, p: (0, 0)),
                pl.BlockSpec(back.shape, lambda i, t, p: (0, 0)),
                pl.BlockSpec((db, cols), lambda i, t, p: (chunk * steps + i, 0)),
            ]
            + [down_spec(b) for b in range(nblk)]
            + order_specs(deps),
            out_specs=[pl.BlockSpec((tokens // 2, db), lambda i, t, p: (0, i))] * 2,
            scratch_shapes=[pltpu.VMEM(sg.shape, BF16), pltpu.VMEM(back.shape, BF16)],
        ),
        compiler_params=PARAMS,
        cost_estimate=COST,
        name="grad_chunk",
    )(tenant, place, sg, back, weight, *([down] * nblk), *deps)


def add_core_body(keep_ref, recv_ref, *refs):
    mine_ref, send_ref = refs[-2:]
    half = mine_ref.shape[0]
    mine_ref[...] = keep_ref[:half, :] + recv_ref[:half, :].astype(F32)
    send_ref[...] = (keep_ref[half:, :] + recv_ref[half:, :].astype(F32)).astype(BF16)


def add_core(keep, recv, deps):
    rows, size = keep.shape
    return pl.pallas_call(
        add_core_body,
        out_shape=(
            jax.ShapeDtypeStruct((rows // 2, size), F32),
            jax.ShapeDtypeStruct((rows // 2, size), BF16),
        ),
        in_specs=[pl.BlockSpec(memory_space=pltpu.VMEM)] * 2 + order_specs(deps),
        compiler_params=PARAMS,
        cost_estimate=COST,
        name="add_core",
    )(keep, recv, *deps)


def add_x_body(keep_ref, recv_ref, *refs):
    nz = keep_ref.shape[0] // refs[-1].shape[0]
    outs = refs[-nz:]
    piece = outs[0].shape[0]
    for k in range(nz):
        rows = slice(k * piece, (k + 1) * piece)
        total = keep_ref[rows, :] + recv_ref[rows, :].astype(F32)
        outs[k][...] = total.astype(outs[k].dtype)


def add_x(keep, recv, nz, deps):
    rows, size = keep.shape
    return pl.pallas_call(
        add_x_body,
        out_shape=tuple(
            jax.ShapeDtypeStruct((rows // nz, size), BF16 if k else F32) for k in range(nz)
        ),
        in_specs=[pl.BlockSpec(memory_space=pltpu.VMEM)] * 2 + order_specs(deps),
        compiler_params=PARAMS,
        cost_estimate=COST,
        name="add_x",
    )(keep, recv, *deps)


def add_z_body(nz, *refs):
    out_ref = refs[-1]
    size = refs[0].shape[1]
    for chunk in range((len(refs) - 1) // nz):
        total = refs[chunk * nz][...]
        for k in range(1, nz):
            total = total + refs[chunk * nz + k][...].astype(F32)
        out_ref[:, chunk * size : (chunk + 1) * size] = total.astype(BF16)


def add_z(parts, nz):
    piece, size = parts[0].shape
    return pl.pallas_call(
        functools.partial(add_z_body, nz),
        out_shape=jax.ShapeDtypeStruct((piece, size * (len(parts) // nz)), BF16),
        in_specs=[pl.BlockSpec(memory_space=pltpu.VMEM)] * len(parts),
        compiler_params=PARAMS,
        cost_estimate=COST,
        name="add_z",
    )(*parts)


def forward_body(nb, rank, nz, tenant_ref, place_ref, w_ref, cot_ref, *refs):
    a_refs, up_refs = refs[:nb], refs[nb : 2 * nb]
    pieces = refs[2 * nb : 2 * nb + 4 * nz]
    part_ref, dot_ref, low_ref, x_ref, lowcat_ref, sem = refs[-6:]
    piece = pieces[0].shape[0]

    @pl.when(pl.program_id(0) == 0)
    def _():
        z, x, core, first = place_ref[0], place_ref[1], place_ref[2], place_ref[3]

        def each(act):
            for n in range(4 * nz):
                k, fx, fc = n // 4, (n // 2) % 2, n % 2
                b = lax.rem(z + (nz - k), nz) - first

                @pl.when(jnp.logical_and(b >= 0, b < nb))
                def _():
                    row = (b * 4 + (x ^ fx) * 2 + (core ^ fc)) * piece
                    rows = pl.ds(pl.multiple_of(row, piece), piece)
                    act(pltpu.make_async_copy(pieces[n], x_ref.at[rows, :], sem.at[n]))

        each(lambda copy: copy.start())
        each(lambda copy: copy.wait())
        low = lax.dot_general(cat_blocks(a_refs), x_ref[...], LAST, preferred_element_type=F32)
        owner = lax.broadcasted_iota(jnp.int32, low.shape, 0) // rank
        block = lax.broadcasted_iota(jnp.int32, low.shape, 1) // BLOCK
        low = jnp.where(owner == block, low, 0.0)
        low_ref[...] = jnp.sum(low.reshape(nb, rank, low.shape[1]), axis=0)
        hi = low.astype(BF16).astype(F32)
        lowcat_ref[...] = jnp.concatenate([hi, low - hi], axis=0).T.astype(BF16)

    up = cat_blocks(up_refs)
    up = jnp.concatenate([up, up], axis=0)
    part = jnp.dot(x_ref[...], w_ref[...], preferred_element_type=F32)
    part = part + jnp.dot(lowcat_ref[...], up, preferred_element_type=F32)
    part_ref[...] = part.astype(part_ref.dtype)
    product = part * cot_ref[...].astype(F32)
    dot_ref[...] = jnp.sum(product.reshape(nb, BLOCK, product.shape[1]), axis=1)


def forward_group(tenant, place, weight, cot, down, up, pieces, nz, out_dtype, deps):
    depth, cols = weight.shape
    rows = cot.shape[0]
    nb = rows // BLOCK
    rank = down.shape[1]
    jb = column_block(cols)

    def down_spec(b):
        return pl.BlockSpec((1, rank, depth), lambda j, t, p: (t[(p[3] + b) * BLOCK], 0, 0))

    def up_spec(b):
        return pl.BlockSpec((1, rank, jb), lambda j, t, p: (t[(p[3] + b) * BLOCK], 0, j))

    return pl.pallas_call(
        functools.partial(forward_body, nb, rank, nz),
        out_shape=(
            jax.ShapeDtypeStruct((rows, cols), out_dtype),
            jax.ShapeDtypeStruct((nb, cols), F32),
            jax.ShapeDtypeStruct((rank, rows), F32),
        ),
        grid_spec=pltpu.PrefetchScalarGridSpec(
            num_scalar_prefetch=2,
            grid=(cols // jb,),
            in_specs=[
                pl.BlockSpec((depth, jb), lambda j, t, p: (0, j)),
                pl.BlockSpec((rows, jb), lambda j, t, p: (0, j)),
            ]
            + [down_spec(b) for b in range(nb)]
            + [up_spec(b) for b in range(nb)]
            + [pl.BlockSpec(memory_space=pl.ANY)] * len(pieces)
            + order_specs(deps),
            out_specs=[
                pl.BlockSpec((rows, jb), lambda j, t, p: (0, j)),
                pl.BlockSpec((nb, jb), lambda j, t, p: (0, j)),
                pl.BlockSpec((rank, rows), lambda j, t, p: (0, 0)),
            ],
            scratch_shapes=[
                pltpu.VMEM((rows, depth), BF16),
                pltpu.VMEM((rows, 2 * nb * rank), BF16),
                pltpu.SemaphoreType.DMA((len(pieces),)),
            ],
        ),
        compiler_params=PARAMS,
        cost_estimate=COST,
        name="forward_group",
    )(tenant, place, weight, cot, *([down] * nb), *([up] * nb), *pieces, *deps)


def shards(inputs, weight, adapter_down_factors, adapter_up_factors, magnitude, cotangent, tenant):
    col_count, row_count = lax.axis_size("col"), lax.axis_size("row")
    nz = col_count // 4
    down, up = adapter_down_factors, adapter_up_factors
    tenant_number, rank, depth = down.shape
    cols = weight.shape[1]
    tokens = tenant.shape[0]
    nblk = tokens // BLOCK
    rows_row = tokens // row_count
    blocks_mine = rows_row // BLOCK
    col, row = lax.axis_index("col"), lax.axis_index("row")
    z, x, core = col >> 2, (col >> 1) & 1, col & 1

    def move(value, dz, fx, fc):
        perm = []
        for source in range(col_count):
            sz, sx, sc = source // 4, (source // 2) % 2, source % 2
            perm.append((source, ((sz + dz) % nz) * 4 + (sx ^ fx) * 2 + (sc ^ fc)))
        return lax.ppermute(value, "col", perm)

    def swap(value):
        return lax.ppermute(value, "row", [(0, 1), (1, 0)])

    pair = row_count == 2

    pieces = []
    for k in range(nz):
        base = inputs if k == 0 else move(inputs, k, 0, 0)
        flip = move(base, 0, 1, 0)
        pieces += [base, move(base, 0, 0, 1), flip, move(flip, 0, 0, 1)]

    if pair:
        cots = [cotangent, swap(cotangent)]
        bases = jnp.stack([row, 1 - row]).astype(jnp.int32) * blocks_mine
    else:
        cots = [lax.all_gather(cotangent, "row", axis=0, tiled=True)]
        bases = jnp.zeros((1,), jnp.int32)

    nsq = partial_norms(tenant, weight, down, up)
    if pair:
        nsq_a, nsq_b = nsq, swap(nsq)
    else:
        nsq_a = lax.psum(nsq, "row")
        nsq_b = jnp.zeros_like(nsq)
    scale, sg, back = scaled_gradient(tenant, bases, cots, nsq_a, nsq_b, magnitude, up, pieces[:3] + pieces[4::4])

    place = jnp.stack([z, x, core, 0 * z]).astype(jnp.int32)

    def grad(chunk, deps):
        return grad_chunk(tenant, place, sg, back, weight, down, nz, chunk, deps)

    def cross_core(made, deps):
        return add_core(made[0], move(made[1], 0, 0, 1), deps)

    def cross_x(made, deps):
        mine, *away = add_x(made[0], move(made[1], 0, 1, 0), nz, deps)
        return [mine] + [move(a, k + 1, 0, 0) for k, a in enumerate(away)], mine

    made, summed = [grad(0, pieces[5::4])], []
    for chunk in range(1, CHUNKS):
        last = [summed[-1][0]] if summed else [made[-1][0]] + pieces[6::4]
        made.append(grad(chunk, last))
        summed.append(cross_core(made[chunk - 1], [made[chunk][0]]))

    if pair:
        theirs, ours = [
            jnp.stack([z, x, core, first]).astype(jnp.int32)
            for first in ((1 - row) * blocks_mine, row * blocks_mine)
        ]
        away, dots_away, low_away = forward_group(
            tenant, theirs, weight, cots[1], down, up, pieces, nz, BF16, [summed[-1][0]]
        )
        arrived = swap(away)
        after = dots_away
    else:
        after = summed[-1][0]
    summed.append(cross_core(made[-1], [after]))
    finals, after = cross_x(summed[0], [summed[-1][0]])
    if pair:
        part, dots_here, low_here = forward_group(
            tenant, ours, weight, cots[0], down, up, pieces, nz, F32, [after]
        )
        pre = part + arrived.astype(F32)

        def ordered(here, there, axis):
            return jnp.where(
                row == 0,
                jnp.concatenate([here, there], axis=axis),
                jnp.concatenate([there, here], axis=axis),
            )

        dots = ordered(dots_here, dots_away, 0)
        low = ordered(low_here, low_away, 1)
        dots = dots + swap(dots)
        low = low + swap(low)
        after = dots_here
    else:
        part, dots, low = forward_group(
            tenant, place, weight, cots[0], down, up, pieces, nz, F32, [after]
        )
        pre = lax.psum_scatter(part, "row", scatter_dimension=0, tiled=True)
        dots, low = lax.psum((dots, low), "row")
        after = part
    for chunk in range(1, CHUNKS):
        more, after = cross_x(summed[chunk], [after])
        finals += more
    grad_inputs = add_z(finals, nz)

    scale_mine = lax.dynamic_slice_in_dim(scale, row * blocks_mine, blocks_mine, 0)
    output = (pre.reshape(blocks_mine, BLOCK, cols) * scale_mine[:, None, :]).astype(BF16)
    output = output.reshape(rows_row, cols)

    block_tenant = tenant.reshape(nblk, BLOCK)[:, 0]
    tenants = jnp.arange(tenant_number, dtype=jnp.int32)
    wide = jnp.where(
        (tenants[:, None] == tenant[None, :])[:, None, :], low.astype(BF16)[None], 0
    ).reshape(tenant_number * rank, tokens)
    grad_b = jnp.dot(wide, sg, preferred_element_type=F32)
    grad_b = grad_b.reshape(tenant_number, rank, cols)
    hit = (tenants[:, None] == block_tenant[None, :])[:, :, None]
    grad_m = jnp.sum(jnp.where(hit, (dots * scale)[None], 0.0), axis=1) / magnitude
    return (output, grad_inputs, grad_b, grad_m)


def solution(mesh):
    return jax.shard_map(
        shards,
        mesh=mesh,
        in_specs=(
            P("col", "row"),
            P("row", "col"),
            P(None, None, "row"),
            P(None, None, "col"),
            P(None, "col"),
            P("row", "col"),
            P(),
        ),
        out_specs=(P("row", "col"), P("col", "row"), P(None, None, "col"), P(None, "col")),
        check_vma=False,
    )
```

time: 598 us -> 173 us (0.29)
  matrix products: 243 us -> 1.87 us
  waiting for transfers between devices: 211 us -> 37.4 us
  Pallas kernels: 0 us -> 62.3 us
  other arithmetic: 60.7 us -> 2.88 us
  starting transfers between devices: 0.43 us -> 47.4 us
  local copies, waits for them, and re-layouts: 55.9 us -> 17.8 us
  between operations: 15.3 us -> 1.11 us
  blocking collectives: 8.98 us -> 0 us
    dot_general x26 -> x1, matrix products: 243 us -> 1.87 us  [shards(): grad_b = jnp.dot(wide, sg, preferred_element_type=F32)]
    reduce_scatter x2 -> x0, waiting for transfers between devices: 128 us -> none  [the longest x1 96.7 us: shards(): lax.psum_scatter(main + jnp.sum(back_part[:, :, None] * down_factor_rows,...]
    pallas_call x0 -> x17, Pallas kernels: none -> 62.3 us  [the longest x2 25.5 us: forward_group(): pl.pallas_call(functools.partial(forward_body, nb, rank, nz), out_shape=(...]
    all_gather x3 -> x0, waiting for transfers between devices: 59.4 us -> none  [the longest x1 29.1 us: shards(): lax.all_gather(output, 'row', axis=0, tiled=True)]
    ppermute x0 -> x40, starting transfers between devices: none -> 47.4 us  [the longest x35 41.6 us: move(): return lax.ppermute(value, 'col', perm)]
    reduce_sum x2 -> x1, other arithmetic: 38.7 us -> 0.1 us  [shards(): jnp.sum(jnp.where(hit, (dots * scale)[None], 0.0), axis=1) / magnitude]
    ppermute x0 -> x40, waiting for transfers between devices: none -> 37.4 us  [the longest x35 36.8 us: move(): return lax.ppermute(value, 'col', perm)]
    gather x4 -> x0, local copies, waits for them, and re-layouts: 28 us -> none  [the longest x1 24 us: shards(): down_factor_rows = adapter_down_factors[tenant].astype(jnp.float32)]
  transfers between devices with their start and end apart: 6 -> 40, of which waited for: 6 -> 12; matrix products, arithmetic and copies ran while one was open for 8% -> 3% of each run, Pallas kernels for 0% -> 34%
where the time goes in v1:
time: 173 us; the launch traced here: 171 us
  Pallas kernels  62.3 us (36%)
  starting transfers between devices  47.4 us (27%)
  waiting for transfers between devices  37.4 us (22%)
  local copies, waits for them, and re-layouts  17.8 us (10%)
  other arithmetic  2.88 us (2%)
  matrix products  1.87 us (1%)
    ppermute x35, starting transfers between devices, move(): return lax.ppermute(value, 'col', perm)  41.6 us
    ppermute x35, waiting for transfers between devices, move(): return lax.ppermute(value, 'col', perm)  36.8 us
    pallas_call x2, Pallas kernels, forward_group(): pl.pallas_call(functools.partial(forward_body, nb, rank, nz), out_shape=(...  25.5 us
    pallas_call x4, Pallas kernels, grad_chunk(): pl.pallas_call(functools.partial(grad_body, nblk, rank, nz), out_shape=(j...  20.2 us
    unnamed x78, local copies, waits for them, and re-layouts  17 us
    pallas_call x1, Pallas kernels, partial_norms(): pl.pallas_call(functools.partial(norm_body, nblk, rank), out_shape=jax.Sh...  9.73 us
    ppermute x5, starting transfers between devices, swap(): return lax.ppermute(value, 'row', [(0, 1), (1, 0)])  5.78 us
  transfers between devices with their start and end apart: 40, of which 12 were waited for; matrix products, arithmetic and copies ran while one was open for 3% of the time, Pallas kernels for 34%

profile of v1, /device:TPU:8, one launch (start us, length us, event | category | flops | bytes accessed | tf_op | source)
XLA Modules:
  0.0 170.7 jit_solution(16030980731604195005)
XLA Ops:
  0.6 1.6 collective-permute-start.15
  2.2 1.6 copy-done
  3.8 1.2 copy-done.2
  5.7 9.7 %partial_norms.1.refs_2_ = f32[4,1792]{1,0:T(4,128)S(1)} custom-call(s32[512]{0:T(512)S(1)} %copy-done.28, bf16[4096,1792]{1,0:T(8,128)(2,1)} %w_ref.13, bf16[16,16,4096]{2,1,0:T(8,128)(2,1)S(1)} %copy-done, bf16[16,16,4096]{2,1,0:T(8,128)(2,1)S(1)} %copy-done, bf16[16,16,4096]{2,1,0:T(8,128)(2,1)S(1)} %copy-done, bf16[16,16,4096]{2,1,0:T(8,128)(2,1)S(1)} %copy-done, ...), custom_call_target="tpu_custom_call" | custom-call | flops 1000 | bytes 1000 | tf_op jit(solution)/shard_map/partial_norms/pallas_call | solution.py:80
  16.6 2.0 %collective-permute-start.3 = (bf16[32,4096]{1,0:T(8,128)(2,1)S(1)}, bf16[32,4096]{1,0:T(8,128)(2,1)}, u32[]{:S(2)}, u32[]{:S(2)}) collective-permute-start(bf16[32,4096]{1,0:T(8,128)(2,1)S(1)} %copy-done.13), channel_id=1, source_target_pairs={{0,8},{2,10},{4,12},{6,14},{8,16},{10,18},{12,20},{14,22},{16,24},... | collective-permute-start | bytes 786440 | tf_op jit(solution)/shard_map/ppermute | solution.py:395
  18.6 4.4 %collective-permute-start.7 = (bf16[32,4096]{1,0:T(8,128)(2,1)S(1)}, bf16[32,4096]{1,0:T(8,128)(2,1)}, u32[]{:S(2)}, u32[]{:S(2)}) collective-permute-start(bf16[32,4096]{1,0:T(8,128)(2,1)S(1)} %copy-done.13), channel_id=1, source_target_pairs={{0,16},{2,18},{4,20},{6,22},{8,24},{10,26},{12,28},{14,30},{16,0},... | collective-permute-start | bytes 786440 | tf_op jit(solution)/shard_map/ppermute | solution.py:395
  24.2 1.5 collective-permute-start.1
  25.8 11.3 %collective-permute-done.11.refs_14_.refs_16_ = bf16[32,4096]{1,0:T(8,128)(2,1)S(1)} collective-permute-done((bf16[32,4096]{1,0:T(8,128)(2,1)S(1)}, bf16[32,4096]{1,0:T(8,128)(2,1)S(1)}, u32[]{:S(2)}, u32[]{:S(2)}) %collective-permute-start.11) | collective-permute-done | bytes 262176 | tf_op jit(solution)/shard_map/ppermute | solution.py:395
  37.6 2.6 %collective-permute-done.7.refs_13_.refs_12_ = bf16[32,4096]{1,0:T(8,128)(2,1)} collective-permute-done((bf16[32,4096]{1,0:T(8,128)(2,1)S(1)}, bf16[32,4096]{1,0:T(8,128)(2,1)}, u32[]{:S(2)}, u32[]{:S(2)}) %collective-permute-start.7) | collective-permute-done | bytes 262176 | tf_op jit(solution)/shard_map/ppermute | solution.py:395
  41.6 1.3 copy-done.11
  42.9 0.9 copy-done.15
  43.9 0.9 copy-done.26
  46.3 2.7 %scaled_gradient.1 = (f32[4,1792]{1,0:T(4,128)S(1)}, bf16[512,1792]{1,0:T(8,128)(2,1)S(1)}, bf16[512,128]{1,0:T(8,128)(2,1)S(1)}) custom-call(s32[512]{0:T(512)S(1)} %copy-done.29, s32[2]{0:T(128)S(1)} %add_multiply_fusion.1.base_ref, bf16[256,1792]{1,0:T(8,128)(2,1)S(1)} %copy-done.11, bf16[256,1792]{1,0:T(8,128)(2,1)} %collective-permute-done.15.refs_1_.cot_ref, ...), custom_call_target="tpu_custom_call" | custom-call | flops 1000 | bytes 1000 | tf_op jit(solution)/shard_map/scaled_gradient/pallas_call | solution.py:137
  49.0 4.9 %grad_chunk.4 = (f32[256,1024]{1,0:T(8,128)S(1)}, bf16[256,1024]{1,0:T(8,128)(2,1)S(1)}) custom-call(s32[512]{0:T(512)S(1)} %copy-done.29, s32[4]{0:T(128)S(1)} %get-tuple-element.88.place_ref, bf16[512,1792]{1,0:T(8,128)(2,1)S(1)} %get-tuple-element.45.sg_ref, bf16[512,128]{1,0:T(8,128)(2,1)S(1)} %get-tuple-element.46.back_ref, bf16[4096,1792]{1,0:T(8,128)(2,1)} %w_ref.13, ...), custom_call_target="tpu_custom_call" | custom-call | flops 1000 | bytes 1000 | tf_op jit(solution)/shard_map/grad_chunk/pallas_call | solution.py:196
  54.0 1.6 collective-permute-start.13
  56.1 1.5 collective-permute-start.9
  57.6 5.7 %collective-permute-done.13.refs_7_.refs_18_ = bf16[32,4096]{1,0:T(8,128)(2,1)} collective-permute-done((bf16[32,4096]{1,0:T(8,128)(2,1)S(1)}, bf16[32,4096]{1,0:T(8,128)(2,1)}, u32[]{:S(2)}, u32[]{:S(2)}) %collective-permute-start.13) | collective-permute-done | bytes 262176 | tf_op jit(solution)/shard_map/ppermute | solution.py:395
  63.3 5.6 %collective-permute-done.5.refs_5_.refs_10_ = bf16[32,4096]{1,0:T(8,128)(2,1)} collective-permute-done((bf16[32,4096]{1,0:T(8,128)(2,1)}, bf16[32,4096]{1,0:T(8,128)(2,1)}, u32[]{:S(2)}, u32[]{:S(2)}) %collective-permute-start.5) | collective-permute-done | bytes 262176 | tf_op jit(solution)/shard_map/ppermute | solution.py:395
  68.9 5.2 %collective-permute-done.9.refs_6_.refs_14_ = bf16[32,4096]{1,0:T(8,128)(2,1)} collective-permute-done((bf16[32,4096]{1,0:T(8,128)(2,1)}, bf16[32,4096]{1,0:T(8,128)(2,1)}, u32[]{:S(2)}, u32[]{:S(2)}) %collective-permute-start.9) | collective-permute-done | bytes 262176 | tf_op jit(solution)/shard_map/ppermute | solution.py:395
  74.1 4.9 %grad_chunk.5 = (f32[256,1024]{1,0:T(8,128)S(1)}, bf16[256,1024]{1,0:T(8,128)(2,1)S(1)}) custom-call(s32[512]{0:T(512)S(1)} %copy-done.29, s32[4]{0:T(128)S(1)} %get-tuple-element.88.place_ref, bf16[512,1792]{1,0:T(8,128)(2,1)S(1)} %get-tuple-element.45.sg_ref, bf16[512,128]{1,0:T(8,128)(2,1)S(1)} %get-tuple-element.46.back_ref, bf16[4096,1792]{1,0:T(8,128)(2,1)} %w_ref.13, ...), custom_call_target="tpu_custom_call" | custom-call | flops 1000 | bytes 1000 | tf_op jit(solution)/shard_map/grad_chunk/pallas_call | solution.py:196
  79.8 4.9 %grad_chunk.6 = (f32[256,1024]{1,0:T(8,128)S(1)}, bf16[256,1024]{1,0:T(8,128)(2,1)S(1)}) custom-call(s32[512]{0:T(512)S(1)} %copy-done.29, s32[4]{0:T(128)S(1)} %get-tuple-element.88.place_ref, bf16[512,1792]{1,0:T(8,128)(2,1)S(1)} %get-tuple-element.45.sg_ref, bf16[512,128]{1,0:T(8,128)(2,1)S(1)} %get-tuple-element.46.back_ref, bf16[4096,1792]{1,0:T(8,128)(2,1)} %w_ref.13, ...), custom_call_target="tpu_custom_call" | custom-call | flops 1000 | bytes 1000 | tf_op jit(solution)/shard_map/grad_chunk/pallas_call | solution.py:196
  86.1 5.6 %grad_chunk.7 = (f32[256,1024]{1,0:T(8,128)S(1)}, bf16[256,1024]{1,0:T(8,128)(2,1)}) custom-call(s32[512]{0:T(512)S(1)} %copy-done.29, s32[4]{0:T(128)S(1)} %get-tuple-element.88.place_ref, bf16[512,1792]{1,0:T(8,128)(2,1)S(1)} %get-tuple-element.45.sg_ref, bf16[512,128]{1,0:T(8,128)(2,1)S(1)} %get-tuple-element.46.back_ref, bf16[4096,1792]{1,0:T(8,128)(2,1)} %w_ref.13, ...), custom_call_target="tpu_custom_call" | custom-call | flops 1000 | bytes 1000 | tf_op jit(solution)/shard_map/grad_chunk/pallas_call | solution.py:196
  91.7 1.0 copy-done.6
  95.4 1.5 collective-permute-start.18
  97.7 1.2 copy-done.7
  98.9 1.2 copy-done.10
  100.1 1.0 copy-done.25
  101.3 0.8 copy-done.37
  102.7 12.8 %forward_group.2 = (bf16[256,1792]{1,0:T(8,128)(2,1)S(1)}, f32[2,1792]{1,0:T(2,128)S(1)}, f32[16,256]{1,0:T(8,128)S(1)}) custom-call(s32[512]{0:T(512)S(1)} %copy-done.29, s32[4]{0:T(128)S(1)} %get-tuple-element.86.place_ref, bf16[4096,1792]{1,0:T(8,128)(2,1)} %w_ref.13, bf16[256,1792]{1,0:T(8,128)(2,1)} %collective-permute-done.15.refs_1_.cot_ref, ...), custom_call_target="tpu_custom_call" | custom-call | flops 1000 | bytes 1000 | tf_op jit(solution)/shard_map/forward_group/pallas_call | solution.py:342
  115.6 1.3 add_core.7
  116.8 1.0 add_x.4
  117.9 12.6 %forward_group.3 = (f32[256,1792]{1,0:T(8,128)S(1)}, f32[2,1792]{1,0:T(2,128)S(1)}, f32[16,256]{1,0:T(8,128)S(1)}) custom-call(s32[512]{0:T(512)S(1)} %copy-done.29, s32[4]{0:T(128)S(1)} %get-tuple-element.89.place_ref, bf16[4096,1792]{1,0:T(8,128)(2,1)} %w_ref.13, bf16[256,1792]{1,0:T(8,128)(2,1)S(1)} %copy-done.12, bf16[16,16,4096]{2,1,0:T(8,128)(2,1)S(1)} %copy-done.1, ...), custom_call_target="tpu_custom_call" | custom-call | flops 1000 | bytes 1000 | tf_op jit(solution)/shard_map/forward_group/pallas_call | solution.py:342
  130.6 1.6 collective-permute-start.39
  132.7 1.5 collective-permute-start.30
  135.1 1.5 collective-permute-start.22
  136.7 4.4 %collective-permute-start.28 = (bf16[32,1024]{1,0:T(8,128)(2,1)S(1)}, bf16[32,1024]{1,0:T(8,128)(2,1)S(1)}, u32[]{:S(2)}, u32[]{:S(2)}) collective-permute-start(bf16[32,1024]{1,0:T(8,128)(2,1)S(1)} %get-tuple-element.72), channel_id=1, source_target_pairs={{0,16},{2,18},{4,20},{6,22},{8,24},{10,26},{12,28},{14,30},{16,0},... | collective-permute-start | bytes 196616 | tf_op jit(solution)/shard_map/ppermute | solution.py:395
  141.9 2.3 %collective-permute-start.29 = (bf16[32,1024]{1,0:T(8,128)(2,1)S(1)}, bf16[32,1024]{1,0:T(8,128)(2,1)S(1)}, u32[]{:S(2)}, u32[]{:S(2)}) collective-permute-start(bf16[32,1024]{1,0:T(8,128)(2,1)S(1)} %get-tuple-element.73), channel_id=1, source_target_pairs={{0,24},{2,26},{4,28},{6,30},{8,0},{10,2},{12,4},{14,6},{16,8},{18,... | collective-permute-start | bytes 196616 | tf_op jit(solution)/shard_map/ppermute | solution.py:395
  144.3 1.6 collective-permute-done.34.recv_ref
  147.1 4.4 %collective-permute-start.24 = (bf16[32,1024]{1,0:T(8,128)(2,1)S(1)}, bf16[32,1024]{1,0:T(8,128)(2,1)S(1)}, u32[]{:S(2)}, u32[]{:S(2)}) collective-permute-start(bf16[32,1024]{1,0:T(8,128)(2,1)S(1)} %get-tuple-element.66), channel_id=1, source_target_pairs={{0,16},{2,18},{4,20},{6,22},{8,24},{10,26},{12,28},{14,30},{16,0},... | collective-permute-start | bytes 196616 | tf_op jit(solution)/shard_map/ppermute | solution.py:395
  152.4 1.2 collective-permute-start.35
  153.6 1.9 %collective-permute-start.36 = (bf16[32,1024]{1,0:T(8,128)(2,1)S(1)}, bf16[32,1024]{1,0:T(8,128)(2,1)S(1)}, u32[]{:S(2)}, u32[]{:S(2)}) collective-permute-start(bf16[32,1024]{1,0:T(8,128)(2,1)S(1)} %get-tuple-element.82), channel_id=1, source_target_pairs={{0,16},{2,18},{4,20},{6,22},{8,24},{10,26},{12,28},{14,30},{16,0},... | collective-permute-start | bytes 196616 | tf_op jit(solution)/shard_map/ppermute | solution.py:395
  155.8 2.1 %collective-permute-start.37 = (bf16[32,1024]{1,0:T(8,128)(2,1)S(1)}, bf16[32,1024]{1,0:T(8,128)(2,1)S(1)}, u32[]{:S(2)}, u32[]{:S(2)}) collective-permute-start(bf16[32,1024]{1,0:T(8,128)(2,1)S(1)} %get-tuple-element.83), channel_id=1, source_target_pairs={{0,24},{2,26},{4,28},{6,30},{8,0},{10,2},{12,4},{14,6},{16,8},{18,... | collective-permute-start | bytes 196616 | tf_op jit(solution)/shard_map/ppermute | solution.py:395
  157.9 1.2 collective-permute-done.25.refs_3_
  159.2 5.3 %collective-permute-start.32 = (bf16[32,1024]{1,0:T(8,128)(2,1)S(1)}, bf16[32,1024]{1,0:T(8,128)(2,1)S(1)}, u32[]{:S(2)}, u32[]{:S(2)}) collective-permute-start(bf16[32,1024]{1,0:T(8,128)(2,1)S(1)} %get-tuple-element.77), channel_id=1, source_target_pairs={{0,16},{2,18},{4,20},{6,22},{8,24},{10,26},{12,28},{14,30},{16,0},... | collective-permute-start | bytes 196616 | tf_op jit(solution)/shard_map/ppermute | solution.py:395
  164.5 1.9 %fusion = f32[16,16,1792]{2,1,0:T(8,128)} fusion(bf16[512,1792]{1,0:T(8,128)(2,1)S(1)} %copy-done.5, pred[16,512]{1,0:T(8,128)(4,1)S(1)} %copy-done.38, bf16[16,512]{1,0:T(8,128)(2,1)S(1)} %add_convert_fusion), kind=kOutput, calls=%fused_computation | convolution fusion | flops 469893120 | bytes 3694592 | tf_op jit(solution)/shard_map/dot_general | solution.py:494
  166.4 1.0 collective-permute-done.32.refs_10_
  167.4 1.3 collective-permute-done.33.refs_11_
  169.6 1.1 fusion.2
  (142 shorter events, 19.1 us)
Async XLA Ops:
  0.6 41.0 %collective-permute-start.15 = (bf16[256,1792]{1,0:T(8,128)(2,1)}, bf16[256,1792]{1,0:T(8,128)(2,1)}, u32[]{:S(2)}, u32[]{:S(2)}) collective-permute-start(bf16[256,1792]{1,0:T(8,128)(2,1)} %cot_ref.1), channel_id=1, source_target_pairs={{0,1},{1,0},{2,3},{3,2},{4,5},{5,4},{6,7},{7,6},{8,9},{9,8},{10,11... | collective-permute-start | bytes 2752520 | tf_op jit(solution)/shard_map/ppermute | solution.py:398
  5.7 35.9 %copy-start.3 = (bf16[16,16,1792]{2,1,0:T(8,128)(2,1)S(1)}, bf16[16,16,1792]{2,1,0:T(8,128)(2,1)}, u32[]{:S(2)}) copy-start(bf16[16,16,1792]{2,1,0:T(8,128)(2,1)} %refs_3_.13) | copy-start | bytes 2752516
  5.7 35.9 %copy-start.29 = (s32[512]{0:T(512)S(1)}, s32[512]{0:T(512)}, u32[]{:S(2)}) copy-start(s32[512]{0:T(512)} %tenant_ref.15) | copy-start | bytes 6148
  15.4 8.2 %collective-permute-start.16 = (f32[4,1792]{1,0:T(4,128)S(1)}, f32[4,1792]{1,0:T(4,128)S(1)}, u32[]{:S(2)}, u32[]{:S(2)}) collective-permute-start(f32[4,1792]{1,0:T(4,128)S(1)} %partial_norms.1.refs_2_), channel_id=1, source_target_pairs={{0,1},{1,0},{2,3},{3,2},{4,5},{5,4},{6,7},{7,6},{8,9},{9,8},{10,11... | collective-permute-start | bytes 86024 | tf_op jit(solution)/shard_map/ppermute | solution.py:398
  16.6 20.5 %collective-permute-start.11 = (bf16[32,4096]{1,0:T(8,128)(2,1)S(1)}, bf16[32,4096]{1,0:T(8,128)(2,1)S(1)}, u32[]{:S(2)}, u32[]{:S(2)}) collective-permute-start(bf16[32,4096]{1,0:T(8,128)(2,1)S(1)} %copy-done.13), channel_id=1, source_target_pairs={{0,24},{2,26},{4,28},{6,30},{8,0},{10,2},{12,4},{14,6},{16,8},{18,... | collective-permute-start | bytes 786440 | tf_op jit(solution)/shard_map/ppermute | solution.py:395
  16.6 20.5 %collective-permute-start.3 = (bf16[32,4096]{1,0:T(8,128)(2,1)S(1)}, bf16[32,4096]{1,0:T(8,128)(2,1)}, u32[]{:S(2)}, u32[]{:S(2)}) collective-permute-start(bf16[32,4096]{1,0:T(8,128)(2,1)S(1)} %copy-done.13), channel_id=1, source_target_pairs={{0,8},{2,10},{4,12},{6,14},{8,16},{10,18},{12,20},{14,22},{16,24},... | collective-permute-start | bytes 786440 | tf_op jit(solution)/shard_map/ppermute | solution.py:395
  18.6 21.6 %collective-permute-start.7 = (bf16[32,4096]{1,0:T(8,128)(2,1)S(1)}, bf16[32,4096]{1,0:T(8,128)(2,1)}, u32[]{:S(2)}, u32[]{:S(2)}) collective-permute-start(bf16[32,4096]{1,0:T(8,128)(2,1)S(1)} %copy-done.13), channel_id=1, source_target_pairs={{0,16},{2,18},{4,20},{6,22},{8,24},{10,26},{12,28},{14,30},{16,0},... | collective-permute-start | bytes 786440 | tf_op jit(solution)/shard_map/ppermute | solution.py:395
  24.2 16.0 %collective-permute-start.1 = (bf16[32,4096]{1,0:T(8,128)(2,1)S(1)}, bf16[32,4096]{1,0:T(8,128)(2,1)S(1)}, u32[]{:S(2)}, u32[]{:S(2)}) collective-permute-start(bf16[32,4096]{1,0:T(8,128)(2,1)S(1)} %copy-done.13), channel_id=1, source_target_pairs={{0,4},{2,6},{4,0},{6,2},{8,12},{10,14},{12,8},{14,10},{16,20},{18,... | collective-permute-start | bytes 786440 | tf_op jit(solution)/shard_map/ppermute | solution.py:395
  37.1 4.5 %collective-permute-start = (bf16[32,4096]{1,0:T(8,128)(2,1)S(1)}, bf16[32,4096]{1,0:T(8,128)(2,1)}, u32[]{:S(2)}, u32[]{:S(2)}) collective-permute-start(bf16[32,4096]{1,0:T(8,128)(2,1)S(1)} %copy-done.13), channel_id=1, source_target_pairs={{0,2},{2,0},{4,6},{6,4},{8,10},{10,8},{12,14},{14,12},{16,18},{18,... | collective-permute-start | bytes 786440 | tf_op jit(solution)/shard_map/ppermute | solution.py:395
  37.1 11.9 %collective-permute-start.12 = (bf16[32,4096]{1,0:T(8,128)(2,1)S(1)}, bf16[32,4096]{1,0:T(8,128)(2,1)}, u32[]{:S(2)}, u32[]{:S(2)}) collective-permute-start(bf16[32,4096]{1,0:T(8,128)(2,1)S(1)} %collective-permute-done.11.refs_14_.refs_16_), channel_id=1, source_target_pairs={{0,2},{2,0},{4,6},{6,4},{8,10},{10,8},{12,14},{14,12},{16,18},{18,... | collective-permute-start | bytes 786440 | tf_op jit(solution)/shard_map/ppermute | solution.py:395
  40.2 8.8 %collective-permute-start.4 = (bf16[32,4096]{1,0:T(8,128)(2,1)}, bf16[32,4096]{1,0:T(8,128)(2,1)}, u32[]{:S(2)}, u32[]{:S(2)}) collective-permute-start(bf16[32,4096]{1,0:T(8,128)(2,1)} %collective-permute-done.3.refs_12_.refs_8_), channel_id=1, source_target_pairs={{0,2},{2,0},{4,6},{6,4},{8,10},{10,8},{12,14},{14,12},{16,18},{18,... | collective-permute-start | bytes 786440 | tf_op jit(solution)/shard_map/ppermute | solution.py:395
  40.9 8.1 %collective-permute-start.8 = (bf16[32,4096]{1,0:T(8,128)(2,1)}, bf16[32,4096]{1,0:T(8,128)(2,1)}, u32[]{:S(2)}, u32[]{:S(2)}) collective-permute-start(bf16[32,4096]{1,0:T(8,128)(2,1)} %collective-permute-done.7.refs_13_.refs_12_), channel_id=1, source_target_pairs={{0,2},{2,0},{4,6},{6,4},{8,10},{10,8},{12,14},{14,12},{16,18},{18,... | collective-permute-start | bytes 786440 | tf_op jit(solution)/shard_map/ppermute | solution.py:395
  49.0 37.1 %copy-start.4 = (bf16[512,1792]{1,0:T(8,128)(2,1)}, bf16[512,1792]{1,0:T(8,128)(2,1)S(1)}, u32[]{:S(2)}) copy-start(bf16[512,1792]{1,0:T(8,128)(2,1)S(1)} %get-tuple-element.45.sg_ref) | copy-start | bytes 5505028
  53.9 25.1 %collective-permute-start.17 = (bf16[256,1024]{1,0:T(8,128)(2,1)S(1)}, bf16[256,1024]{1,0:T(8,128)(2,1)S(1)}, u32[]{:S(2)}, u32[]{:S(2)}) collective-permute-start(bf16[256,1024]{1,0:T(8,128)(2,1)S(1)} %get-tuple-element.48), channel_id=1, source_target_pairs={{0,2},{2,0},{4,6},{6,4},{8,10},{10,8},{12,14},{14,12},{16,18},{18,... | collective-permute-start | bytes 1572872 | tf_op jit(solution)/shard_map/ppermute | solution.py:395
  54.0 9.3 %collective-permute-start.13 = (bf16[32,4096]{1,0:T(8,128)(2,1)S(1)}, bf16[32,4096]{1,0:T(8,128)(2,1)}, u32[]{:S(2)}, u32[]{:S(2)}) collective-permute-start(bf16[32,4096]{1,0:T(8,128)(2,1)S(1)} %collective-permute-done.11.refs_14_.refs_16_), channel_id=1, source_target_pairs={{0,4},{2,6},{4,0},{6,2},{8,12},{10,14},{12,8},{14,10},{16,20},{18,... | collective-permute-start | bytes 786440 | tf_op jit(solution)/shard_map/ppermute | solution.py:395
  55.6 13.3 %collective-permute-start.5 = (bf16[32,4096]{1,0:T(8,128)(2,1)}, bf16[32,4096]{1,0:T(8,128)(2,1)}, u32[]{:S(2)}, u32[]{:S(2)}) collective-permute-start(bf16[32,4096]{1,0:T(8,128)(2,1)} %collective-permute-done.3.refs_12_.refs_8_), channel_id=1, source_target_pairs={{0,4},{2,6},{4,0},{6,2},{8,12},{10,14},{12,8},{14,10},{16,20},{18,... | collective-permute-start | bytes 786440 | tf_op jit(solution)/shard_map/ppermute | solution.py:395
  56.1 18.0 %collective-permute-start.9 = (bf16[32,4096]{1,0:T(8,128)(2,1)}, bf16[32,4096]{1,0:T(8,128)(2,1)}, u32[]{:S(2)}, u32[]{:S(2)}) collective-permute-start(bf16[32,4096]{1,0:T(8,128)(2,1)} %collective-permute-done.7.refs_13_.refs_12_), channel_id=1, source_target_pairs={{0,4},{2,6},{4,0},{6,2},{8,12},{10,14},{12,8},{14,10},{16,20},{18,... | collective-permute-start | bytes 786440 | tf_op jit(solution)/shard_map/ppermute | solution.py:395
  78.9 7.0 %collective-permute-start.19 = (bf16[256,1024]{1,0:T(8,128)(2,1)S(1)}, bf16[256,1024]{1,0:T(8,128)(2,1)S(1)}, u32[]{:S(2)}, u32[]{:S(2)}) collective-permute-start(bf16[256,1024]{1,0:T(8,128)(2,1)S(1)} %get-tuple-element.52), channel_id=1, source_target_pairs={{0,2},{2,0},{4,6},{6,4},{8,10},{10,8},{12,14},{14,12},{16,18},{18,... | collective-permute-start | bytes 1572872 | tf_op jit(solution)/shard_map/ppermute | solution.py:395
  84.7 9.8 %collective-permute-start.21 = (bf16[256,1024]{1,0:T(8,128)(2,1)S(1)}, bf16[256,1024]{1,0:T(8,128)(2,1)S(1)}, u32[]{:S(2)}, u32[]{:S(2)}) collective-permute-start(bf16[256,1024]{1,0:T(8,128)(2,1)S(1)} %get-tuple-element.57), channel_id=1, source_target_pairs={{0,2},{2,0},{4,6},{6,4},{8,10},{10,8},{12,14},{14,12},{16,18},{18,... | collective-permute-start | bytes 1572872 | tf_op jit(solution)/shard_map/ppermute | solution.py:395
  85.3 8.5 %collective-permute-start.2 = (bf16[32,4096]{1,0:T(8,128)(2,1)S(1)}, bf16[32,4096]{1,0:T(8,128)(2,1)S(1)}, u32[]{:S(2)}, u32[]{:S(2)}) collective-permute-start(bf16[32,4096]{1,0:T(8,128)(2,1)S(1)} %copy-done.16), channel_id=1, source_target_pairs={{0,2},{2,0},{4,6},{6,4},{8,10},{10,8},{12,14},{14,12},{16,18},{18,... | collective-permute-start | bytes 786440 | tf_op jit(solution)/shard_map/ppermute | solution.py:395
  92.6 22.9 %collective-permute-start.20 = (bf16[256,1024]{1,0:T(8,128)(2,1)}, bf16[256,1024]{1,0:T(8,128)(2,1)}, u32[]{:S(2)}, u32[]{:S(2)}) collective-permute-start(bf16[256,1024]{1,0:T(8,128)(2,1)} %get-tuple-element.56), channel_id=1, source_target_pairs={{0,2},{2,0},{4,6},{6,4},{8,10},{10,8},{12,14},{14,12},{16,18},{18,... | collective-permute-start | bytes 1572872 | tf_op jit(solution)/shard_map/ppermute | solution.py:395
  93.2 8.1 %collective-permute-start.10 = (bf16[32,4096]{1,0:T(8,128)(2,1)}, bf16[32,4096]{1,0:T(8,128)(2,1)}, u32[]{:S(2)}, u32[]{:S(2)}) collective-permute-start(bf16[32,4096]{1,0:T(8,128)(2,1)} %collective-permute-done.9.refs_6_.refs_14_), channel_id=1, source_target_pairs={{0,2},{2,0},{4,6},{6,4},{8,10},{10,8},{12,14},{14,12},{16,18},{18,... | collective-permute-start | bytes 786440 | tf_op jit(solution)/shard_map/ppermute | solution.py:395
  93.3 9.4 %collective-permute-start.14 = (bf16[32,4096]{1,0:T(8,128)(2,1)}, bf16[32,4096]{1,0:T(8,128)(2,1)}, u32[]{:S(2)}, u32[]{:S(2)}) collective-permute-start(bf16[32,4096]{1,0:T(8,128)(2,1)} %collective-permute-done.13.refs_7_.refs_18_), channel_id=1, source_target_pairs={{0,2},{2,0},{4,6},{6,4},{8,10},{10,8},{12,14},{14,12},{16,18},{18,... | collective-permute-start | bytes 786440 | tf_op jit(solution)/shard_map/ppermute | solution.py:395
  94.5 8.2 %collective-permute-start.6 = (bf16[32,4096]{1,0:T(8,128)(2,1)}, bf16[32,4096]{1,0:T(8,128)(2,1)}, u32[]{:S(2)}, u32[]{:S(2)}) collective-permute-start(bf16[32,4096]{1,0:T(8,128)(2,1)} %collective-permute-done.5.refs_5_.refs_10_), channel_id=1, source_target_pairs={{0,2},{2,0},{4,6},{6,4},{8,10},{10,8},{12,14},{14,12},{16,18},{18,... | collective-permute-start | bytes 786440 | tf_op jit(solution)/shard_map/ppermute | solution.py:395
  95.4 21.5 %collective-permute-start.18 = (bf16[128,1024]{1,0:T(8,128)(2,1)}, bf16[128,1024]{1,0:T(8,128)(2,1)}, u32[]{:S(2)}, u32[]{:S(2)}) collective-permute-start(bf16[128,1024]{1,0:T(8,128)(2,1)} %get-tuple-element.51), channel_id=1, source_target_pairs={{0,4},{2,6},{4,0},{6,2},{8,12},{10,14},{12,8},{14,10},{16,20},{18,... | collective-permute-start | bytes 786440 | tf_op jit(solution)/shard_map/ppermute | solution.py:395
  102.1 32.6 %collective-permute-start.26 = (bf16[128,1024]{1,0:T(8,128)(2,1)S(1)}, bf16[128,1024]{1,0:T(8,128)(2,1)S(1)}, u32[]{:S(2)}, u32[]{:S(2)}) collective-permute-start(bf16[128,1024]{1,0:T(8,128)(2,1)S(1)} %copy-done.37), channel_id=1, source_target_pairs={{0,4},{2,6},{4,0},{6,2},{8,12},{10,14},{12,8},{14,10},{16,20},{18,... | collective-permute-start | bytes 786440 | tf_op jit(solution)/shard_map/ppermute | solution.py:395
  117.9 16.9 %copy-start.19 = (f32[128,1024]{1,0:T(8,128)S(1)}, f32[128,1024]{1,0:T(8,128)}, u32[]{:S(2)}) copy-start(f32[128,1024]{1,0:T(8,128)} %copy-done.18) | copy-start | bytes 1572868
  117.9 18.8 %copy-start.33 = (f32[4,1792]{1,0:T(4,128)S(1)}, f32[4,1792]{1,0:T(4,128)}, u32[]{:S(2)}) copy-start(f32[4,1792]{1,0:T(4,128)} %copy-done.32) | copy-start | bytes 86020
  117.9 28.4 %copy-start.27 = (f32[16,1792]{1,0:T(8,128)S(1)}, f32[16,1792]{1,0:T(8,128)}, u32[]{:S(2)}) copy-start(f32[16,1792]{1,0:T(8,128)} %refs_4_.5) | copy-start | bytes 344068
  130.5 33.9 %copy-start.5 = (bf16[512,1792]{1,0:T(8,128)(2,1)S(1)}, bf16[512,1792]{1,0:T(8,128)(2,1)}, u32[]{:S(2)}) copy-start(bf16[512,1792]{1,0:T(8,128)(2,1)} %copy-done.4) | copy-start | bytes 5505028
  130.6 33.9 %copy-start.38 = (pred[16,512]{1,0:T(8,128)(4,1)S(1)}, pred[16,512]{1,0:T(8,128)(4,1)}, u32[]{:S(2)}) copy-start(pred[16,512]{1,0:T(8,128)(4,1)} %iota_compare_fusion) | copy-start | bytes 24580
  130.6 4.5 %collective-permute-start.39 = (f32[4,1792]{1,0:T(4,128)S(1)}, f32[4,1792]{1,0:T(4,128)S(1)}, u32[]{:S(2)}, u32[]{:S(2)}) collective-permute-start(f32[4,1792]{1,0:T(4,128)S(1)} %maximum_select_fusion.1), channel_id=1, source_target_pairs={{0,1},{1,0},{2,3},{3,2},{4,5},{5,4},{6,7},{7,6},{8,9},{9,8},{10,11... | collective-permute-start | bytes 86024 | tf_op jit(solution)/shard_map/ppermute | solution.py:398
  132.2 4.5 %collective-permute-start.38 = (f32[16,512]{1,0:T(8,128)S(1)}, f32[16,512]{1,0:T(8,128)S(1)}, u32[]{:S(2)}, u32[]{:S(2)}) collective-permute-start(f32[16,512]{1,0:T(8,128)S(1)} %maximum_select_fusion), channel_id=1, source_target_pairs={{0,1},{1,0},{2,3},{3,2},{4,5},{5,4},{6,7},{7,6},{8,9},{9,8},{10,11... | collective-permute-start | bytes 98312 | tf_op jit(solution)/shard_map/ppermute | solution.py:398
  132.7 9.2 %collective-permute-start.30 = (bf16[128,1024]{1,0:T(8,128)(2,1)S(1)}, bf16[128,1024]{1,0:T(8,128)(2,1)S(1)}, u32[]{:S(2)}, u32[]{:S(2)}) collective-permute-start(bf16[128,1024]{1,0:T(8,128)(2,1)S(1)} %get-tuple-element.74), channel_id=1, source_target_pairs={{0,4},{2,6},{4,0},{6,2},{8,12},{10,14},{12,8},{14,10},{16,20},{18,... | collective-permute-start | bytes 786440 | tf_op jit(solution)/shard_map/ppermute | solution.py:395
  134.2 11.6 %collective-permute-start.34 = (bf16[128,1024]{1,0:T(8,128)(2,1)S(1)}, bf16[128,1024]{1,0:T(8,128)(2,1)S(1)}, u32[]{:S(2)}, u32[]{:S(2)}) collective-permute-start(bf16[128,1024]{1,0:T(8,128)(2,1)S(1)} %get-tuple-element.79), channel_id=1, source_target_pairs={{0,4},{2,6},{4,0},{6,2},{8,12},{10,14},{12,8},{14,10},{16,20},{18,... | collective-permute-start | bytes 786440 | tf_op jit(solution)/shard_map/ppermute | solution.py:395
  134.8 12.3 %collective-permute-start.27 = (bf16[32,1024]{1,0:T(8,128)(2,1)S(1)}, bf16[32,1024]{1,0:T(8,128)(2,1)S(1)}, u32[]{:S(2)}, u32[]{:S(2)}) collective-permute-start(bf16[32,1024]{1,0:T(8,128)(2,1)S(1)} %get-tuple-element.71), channel_id=1, source_target_pairs={{0,8},{2,10},{4,12},{6,14},{8,16},{10,18},{12,20},{14,22},{16,24},... | collective-permute-start | bytes 196616 | tf_op jit(solution)/shard_map/ppermute | solution.py:395
  135.1 34.4 %collective-permute-start.22 = (bf16[256,1792]{1,0:T(8,128)(2,1)S(1)}, bf16[256,1792]{1,0:T(8,128)(2,1)S(1)}, u32[]{:S(2)}, u32[]{:S(2)}) collective-permute-start(bf16[256,1792]{1,0:T(8,128)(2,1)S(1)} %get-tuple-element.63), channel_id=1, source_target_pairs={{0,1},{1,0},{2,3},{3,2},{4,5},{5,4},{6,7},{7,6},{8,9},{9,8},{10,11... | collective-permute-start | bytes 2752520 | tf_op jit(solution)/shard_map/ppermute | solution.py:398
  136.7 14.8 %collective-permute-start.28 = (bf16[32,1024]{1,0:T(8,128)(2,1)S(1)}, bf16[32,1024]{1,0:T(8,128)(2,1)S(1)}, u32[]{:S(2)}, u32[]{:S(2)}) collective-permute-start(bf16[32,1024]{1,0:T(8,128)(2,1)S(1)} %get-tuple-element.72), channel_id=1, source_target_pairs={{0,16},{2,18},{4,20},{6,22},{8,24},{10,26},{12,28},{14,30},{16,0},... | collective-permute-start | bytes 196616 | tf_op jit(solution)/shard_map/ppermute | solution.py:395
  141.9 10.4 %collective-permute-start.29 = (bf16[32,1024]{1,0:T(8,128)(2,1)S(1)}, bf16[32,1024]{1,0:T(8,128)(2,1)S(1)}, u32[]{:S(2)}, u32[]{:S(2)}) collective-permute-start(bf16[32,1024]{1,0:T(8,128)(2,1)S(1)} %get-tuple-element.73), channel_id=1, source_target_pairs={{0,24},{2,26},{4,28},{6,30},{8,0},{10,2},{12,4},{14,6},{16,8},{18,... | collective-permute-start | bytes 196616 | tf_op jit(solution)/shard_map/ppermute | solution.py:395
  145.8 7.7 %collective-permute-start.23 = (bf16[32,1024]{1,0:T(8,128)(2,1)S(1)}, bf16[32,1024]{1,0:T(8,128)(2,1)S(1)}, u32[]{:S(2)}, u32[]{:S(2)}) collective-permute-start(bf16[32,1024]{1,0:T(8,128)(2,1)S(1)} %get-tuple-element.65), channel_id=1, source_target_pairs={{0,8},{2,10},{4,12},{6,14},{8,16},{10,18},{12,20},{14,22},{16,24},... | collective-permute-start | bytes 196616 | tf_op jit(solution)/shard_map/ppermute | solution.py:395
  147.1 8.7 %collective-permute-start.24 = (bf16[32,1024]{1,0:T(8,128)(2,1)S(1)}, bf16[32,1024]{1,0:T(8,128)(2,1)S(1)}, u32[]{:S(2)}, u32[]{:S(2)}) collective-permute-start(bf16[32,1024]{1,0:T(8,128)(2,1)S(1)} %get-tuple-element.66), channel_id=1, source_target_pairs={{0,16},{2,18},{4,20},{6,22},{8,24},{10,26},{12,28},{14,30},{16,0},... | collective-permute-start | bytes 196616 | tf_op jit(solution)/shard_map/ppermute | solution.py:395
  151.5 7.7 %collective-permute-start.25 = (bf16[32,1024]{1,0:T(8,128)(2,1)S(1)}, bf16[32,1024]{1,0:T(8,128)(2,1)S(1)}, u32[]{:S(2)}, u32[]{:S(2)}) collective-permute-start(bf16[32,1024]{1,0:T(8,128)(2,1)S(1)} %get-tuple-element.67), channel_id=1, source_target_pairs={{0,24},{2,26},{4,28},{6,30},{8,0},{10,2},{12,4},{14,6},{16,8},{18,... | collective-permute-start | bytes 196616 | tf_op jit(solution)/shard_map/ppermute | solution.py:395
  152.4 6.8 %collective-permute-start.35 = (bf16[32,1024]{1,0:T(8,128)(2,1)S(1)}, bf16[32,1024]{1,0:T(8,128)(2,1)S(1)}, u32[]{:S(2)}, u32[]{:S(2)}) collective-permute-start(bf16[32,1024]{1,0:T(8,128)(2,1)S(1)} %get-tuple-element.81), channel_id=1, source_target_pairs={{0,8},{2,10},{4,12},{6,14},{8,16},{10,18},{12,20},{14,22},{16,24},... | collective-permute-start | bytes 196616 | tf_op jit(solution)/shard_map/ppermute | solution.py:395
  153.6 10.9 %collective-permute-start.36 = (bf16[32,1024]{1,0:T(8,128)(2,1)S(1)}, bf16[32,1024]{1,0:T(8,128)(2,1)S(1)}, u32[]{:S(2)}, u32[]{:S(2)}) collective-permute-start(bf16[32,1024]{1,0:T(8,128)(2,1)S(1)} %get-tuple-element.82), channel_id=1, source_target_pairs={{0,16},{2,18},{4,20},{6,22},{8,24},{10,26},{12,28},{14,30},{16,0},... | collective-permute-start | bytes 196616 | tf_op jit(solution)/shard_map/ppermute | solution.py:395
  155.8 10.6 %collective-permute-start.37 = (bf16[32,1024]{1,0:T(8,128)(2,1)S(1)}, bf16[32,1024]{1,0:T(8,128)(2,1)S(1)}, u32[]{:S(2)}, u32[]{:S(2)}) collective-permute-start(bf16[32,1024]{1,0:T(8,128)(2,1)S(1)} %get-tuple-element.83), channel_id=1, source_target_pairs={{0,24},{2,26},{4,28},{6,30},{8,0},{10,2},{12,4},{14,6},{16,8},{18,... | collective-permute-start | bytes 196616 | tf_op jit(solution)/shard_map/ppermute | solution.py:395
  159.2 7.2 %collective-permute-start.31 = (bf16[32,1024]{1,0:T(8,128)(2,1)S(1)}, bf16[32,1024]{1,0:T(8,128)(2,1)S(1)}, u32[]{:S(2)}, u32[]{:S(2)}) collective-permute-start(bf16[32,1024]{1,0:T(8,128)(2,1)S(1)} %get-tuple-element.76), channel_id=1, source_target_pairs={{0,8},{2,10},{4,12},{6,14},{8,16},{10,18},{12,20},{14,22},{16,24},... | collective-permute-start | bytes 196616 | tf_op jit(solution)/shard_map/ppermute | solution.py:395
  159.2 8.2 %collective-permute-start.32 = (bf16[32,1024]{1,0:T(8,128)(2,1)S(1)}, bf16[32,1024]{1,0:T(8,128)(2,1)S(1)}, u32[]{:S(2)}, u32[]{:S(2)}) collective-permute-start(bf16[32,1024]{1,0:T(8,128)(2,1)S(1)} %get-tuple-element.77), channel_id=1, source_target_pairs={{0,16},{2,18},{4,20},{6,22},{8,24},{10,26},{12,28},{14,30},{16,0},... | collective-permute-start | bytes 196616 | tf_op jit(solution)/shard_map/ppermute | solution.py:395
  164.5 4.3 %collective-permute-start.33 = (bf16[32,1024]{1,0:T(8,128)(2,1)S(1)}, bf16[32,1024]{1,0:T(8,128)(2,1)S(1)}, u32[]{:S(2)}, u32[]{:S(2)}) collective-permute-start(bf16[32,1024]{1,0:T(8,128)(2,1)S(1)} %get-tuple-element.78), channel_id=1, source_target_pairs={{0,24},{2,26},{4,28},{6,30},{8,0},{10,2},{12,4},{14,6},{16,8},{18,... | collective-permute-start | bytes 196616 | tf_op jit(solution)/shard_map/ppermute | solution.py:395
  (31 other events, 88.3 us)

commit v2 on v1

v2 whole, which is shorter than its diff:
```python
import functools

import jax
import jax.numpy as jnp
from jax import lax
from jax.experimental import pallas as pl
from jax.experimental.pallas import tpu as pltpu
from jax.sharding import PartitionSpec as P

BLOCK = 128
EPS = 1e-06
HIGH = lax.Precision.HIGHEST
CHUNKS = 2
STEPS = 8
F32 = jnp.float32
BF16 = jnp.bfloat16
COST = pl.CostEstimate(flops=1000, bytes_accessed=1000, transcendentals=0)
LAST = (((1,), (1,)), ((), ()))
PARAMS = pltpu.CompilerParams(vmem_limit_bytes=24 * 1024 * 1024)


def cat_blocks(refs):
    return jnp.concatenate([ref[0] for ref in refs], axis=0)


def order_specs(deps):
    return [pl.BlockSpec(memory_space=pl.ANY)] * len(deps)


def same_block(array):
    return pl.BlockSpec(array.shape, lambda *args: (0,) * array.ndim)


def hi_lo(value, axis):
    hi = value.astype(BF16)
    lo = (value - hi.astype(F32)).astype(BF16)
    return jnp.concatenate([hi, lo], axis=axis)


def norm_body(nblk, rank, tenant_ref, w_ref, *refs):
    a_refs, up_refs = refs[:nblk], refs[nblk : 2 * nblk]
    nsq_ref, gram_ref, cross_ref, square_ref = refs[2 * nblk :]
    depth, cols = w_ref.shape

    @pl.when(pl.program_id(0) == 0)
    def _():
        gram_ref[...] = jnp.zeros_like(gram_ref)
        cross_ref[...] = jnp.zeros_like(cross_ref)
        square_ref[...] = jnp.zeros_like(square_ref)

    a_all = cat_blocks(a_refs)
    gram_ref[...] += lax.dot_general(a_all, a_all, LAST, preferred_element_type=F32)
    step = min(depth, 256)
    for start in range(0, depth, step):
        w = w_ref[start : start + step, :]
        cross_ref[...] += jnp.dot(a_all[:, start : start + step], w, preferred_element_type=F32)
        wf = w.astype(F32)
        square_ref[...] += jnp.sum((wf * wf).reshape(step // 8, 8, cols), axis=0)

    @pl.when(pl.program_id(0) == pl.num_programs(0) - 1)
    def _():
        gram = gram_ref[...]
        row = lax.broadcasted_iota(jnp.int32, gram.shape, 0) // rank
        col = lax.broadcasted_iota(jnp.int32, gram.shape, 1) // rank
        gram = jnp.where(row == col, gram, 0.0)
        up = cat_blocks(up_refs).astype(F32)
        quad = jnp.dot(gram, up, preferred_element_type=F32, precision=HIGH)
        mixed = (up * (2.0 * cross_ref[...] + quad)).reshape(nblk, rank, cols)
        nsq_ref[...] = jnp.sum(mixed, axis=1) + jnp.sum(square_ref[...], axis=0, keepdims=True)


def partial_norms(tenant, weight, down, up):
    depth, cols = weight.shape
    rank = down.shape[1]
    nblk = tenant.shape[0] // BLOCK
    db = depth // STEPS

    def down_spec(b):
        return pl.BlockSpec((1, rank, db), lambda i, t: (t[b * BLOCK], 0, i))

    def up_spec(b):
        return pl.BlockSpec((1, rank, cols), lambda i, t: (t[b * BLOCK], 0, 0))

    return pl.pallas_call(
        functools.partial(norm_body, nblk, rank),
        out_shape=jax.ShapeDtypeStruct((nblk, cols), F32),
        grid_spec=pltpu.PrefetchScalarGridSpec(
            num_scalar_prefetch=1,
            grid=(STEPS,),
            in_specs=[pl.BlockSpec((db, cols), lambda i, t: (i, 0))]
            + [down_spec(b) for b in range(nblk)]
            + [up_spec(b) for b in range(nblk)],
            out_specs=pl.BlockSpec((nblk, cols), lambda i, t: (0, 0)),
            scratch_shapes=[
                pltpu.VMEM((nblk * rank, nblk * rank), F32),
                pltpu.VMEM((nblk * rank, cols), F32),
                pltpu.VMEM((8, cols), F32),
            ],
        ),
        compiler_params=PARAMS,
        cost_estimate=COST,
        name="partial_norms",
    )(tenant, weight, *([down] * nblk), *([up] * nblk))


def scaled_body(nb, rank, tenant_ref, place_ref, cot_ref, nsq_a, nsq_b, mag_ref, *refs):
    up_refs = refs[:nb]
    scale_ref, sg_ref, back_ref = refs[-3:]
    first = place_ref[3]
    up_all = cat_blocks(up_refs)
    owner = lax.broadcasted_iota(jnp.int32, (BLOCK, nb * rank), 1) // rank
    for i in range(nb):
        b = first + i
        total = nsq_a[pl.ds(b, 1), :] + nsq_b[pl.ds(b, 1), :]
        scale = mag_ref[pl.ds(tenant_ref[b * BLOCK], 1), :] / jnp.sqrt(total + EPS)
        scale_ref[i : i + 1, :] = scale
        rows = slice(i * BLOCK, (i + 1) * BLOCK)
        sg = (cot_ref[rows, :].astype(F32) * scale).astype(BF16)
        sg_ref[rows, :] = sg
        back = lax.dot_general(sg, up_all, LAST, preferred_element_type=F32)
        back_ref[rows, :] = hi_lo(jnp.where(owner == i, back, 0.0), 1)


def scaled_gradient(tenant, place, cot, nsq_a, nsq_b, magnitude, up, deps):
    rows, cols = cot.shape
    nb = rows // BLOCK
    rank = up.shape[1]

    def up_spec(b):
        return pl.BlockSpec((1, rank, cols), lambda i, t, p: (t[(p[3] + b) * BLOCK], 0, 0))

    shapes = (
        jax.ShapeDtypeStruct((nb, cols), F32),
        jax.ShapeDtypeStruct((rows, cols), BF16),
        jax.ShapeDtypeStruct((rows, 2 * nb * rank), BF16),
    )
    return pl.pallas_call(
        functools.partial(scaled_body, nb, rank),
        out_shape=shapes,
        grid_spec=pltpu.PrefetchScalarGridSpec(
            num_scalar_prefetch=2,
            grid=(1,),
            in_specs=[same_block(a) for a in (cot, nsq_a, nsq_b, magnitude)]
            + [up_spec(b) for b in range(nb)]
            + order_specs(deps),
            out_specs=[same_block(s) for s in shapes],
        ),
        compiler_params=PARAMS,
        cost_estimate=COST,
        name="scaled_gradient",
    )(tenant, place, cot, nsq_a, nsq_b, magnitude, *([up] * nb), *deps)


def grad_body(nb, rank, tenant_ref, place_ref, sg_ref, back_ref, w_ref, *refs):
    a_refs = refs[:nb]
    keep_ref, send_ref, sgp_ref, backp_ref = refs[-4:]
    rows = sg_ref.shape[0]
    piece = BLOCK // 4
    half = rows // 2

    @pl.when(pl.program_id(0) == 0)
    def _():
        x, core = place_ref[1], place_ref[2]
        for fc in range(2):
            for fx in range(2):
                for b in range(nb):
                    c = b * 4 + (x ^ fx) * 2 + (core ^ fc)
                    src = pl.ds(pl.multiple_of(c * piece, piece), piece)
                    at = ((fc * 2 + fx) * nb + b) * piece
                    sgp_ref[at : at + piece, :] = sg_ref[src, :]
                    backp_ref[at : at + piece, :] = back_ref[src, :]

    down = cat_blocks(a_refs)
    down = jnp.concatenate([down, down], axis=0)
    part = lax.dot_general(sgp_ref[...], w_ref[...], LAST, preferred_element_type=F32)
    part = part + jnp.dot(backp_ref[...], down, preferred_element_type=F32)
    keep_ref[...] = part[:half, :]
    send_ref[...] = part[half:, :].astype(BF16)


def grad_chunk(tenant, place, sg, back, weight, down, chunk, deps):
    depth, cols = weight.shape
    rows = sg.shape[0]
    nb = rows // BLOCK
    rank = down.shape[1]
    size = depth // CHUNKS
    db = depth // STEPS
    steps = size // db

    def down_spec(b):
        return pl.BlockSpec(
            (1, rank, db), lambda i, t, p: (t[(p[3] + b) * BLOCK], 0, chunk * steps + i)
        )

    return pl.pallas_call(
        functools.partial(grad_body, nb, rank),
        out_shape=(
            jax.ShapeDtypeStruct((rows // 2, size), F32),
            jax.ShapeDtypeStruct((rows // 2, size), BF16),
        ),
        grid_spec=pltpu.PrefetchScalarGridSpec(
            num_scalar_prefetch=2,
            grid=(steps,),
            in_specs=[
                same_block(sg),
                same_block(back),
                pl.BlockSpec((db, cols), lambda i, t, p: (chunk * steps + i, 0)),
            ]
            + [down_spec(b) for b in range(nb)]
            + order_specs(deps),
            out_specs=[pl.BlockSpec((rows // 2, db), lambda i, t, p: (0, i))] * 2,
            scratch_shapes=[pltpu.VMEM(sg.shape, BF16), pltpu.VMEM(back.shape, BF16)],
        ),
        compiler_params=PARAMS,
        cost_estimate=COST,
        name="grad_chunk",
    )(tenant, place, sg, back, weight, *([down] * nb), *deps)


def add_core_body(keep_ref, recv_ref, *refs):
    mine_ref, send_ref = refs[-2:]
    half = mine_ref.shape[0]
    mine_ref[...] = keep_ref[:half, :] + recv_ref[:half, :].astype(F32)
    send_ref[...] = (keep_ref[half:, :] + recv_ref[half:, :].astype(F32)).astype(BF16)


def add_core(keep, recv, deps):
    rows, size = keep.shape
    return pl.pallas_call(
        add_core_body,
        out_shape=(
            jax.ShapeDtypeStruct((rows // 2, size), F32),
            jax.ShapeDtypeStruct((rows // 2, size), BF16),
        ),
        in_specs=[pl.BlockSpec(memory_space=pltpu.VMEM)] * 2 + order_specs(deps),
        compiler_params=PARAMS,
        cost_estimate=COST,
        name="add_core",
    )(keep, recv, *deps)


def add_x_body(groups, nz, place_ref, *refs):
    outs, total_ref = refs[-nz - 1 : -1], refs[-1]
    piece = outs[0].shape[0]
    z = place_ref[0]
    for g in range(groups):
        keep_ref, recv_ref = refs[2 * g : 2 * g + 2]
        rows = keep_ref.shape[0]
        first = pl.multiple_of(place_ref[3 + g] * piece, piece)
        total_ref[pl.ds(first, rows), :] = keep_ref[...] + recv_ref[...].astype(F32)
    for k in range(nz):
        at = pl.multiple_of(lax.rem(z + k, nz) * piece, piece)
        outs[k][...] = total_ref[pl.ds(at, piece), :].astype(outs[k].dtype)


def add_x(place, pairs, nz, deps):
    size = pairs[0][0].shape[1]
    piece = BLOCK // 4
    operands = [array for pair in pairs for array in pair]
    shapes = tuple(jax.ShapeDtypeStruct((piece, size), BF16 if k else F32) for k in range(nz))
    return pl.pallas_call(
        functools.partial(add_x_body, len(pairs), nz),
        out_shape=shapes,
        grid_spec=pltpu.PrefetchScalarGridSpec(
            num_scalar_prefetch=1,
            grid=(1,),
            in_specs=[same_block(a) for a in operands] + order_specs(deps),
            out_specs=[same_block(s) for s in shapes],
            scratch_shapes=[pltpu.VMEM((nz * piece, size), F32)],
        ),
        compiler_params=PARAMS,
        cost_estimate=COST,
        name="add_x",
    )(place, *operands, *deps)


def add_z_body(nz, *refs):
    out_ref = refs[-1]
    size = refs[0].shape[1]
    for chunk in range((len(refs) - 1) // nz):
        total = refs[chunk * nz][...]
        for k in range(1, nz):
            total = total + refs[chunk * nz + k][...].astype(F32)
        out_ref[:, chunk * size : (chunk + 1) * size] = total.astype(BF16)


def add_z(parts, nz):
    piece, size = parts[0].shape
    return pl.pallas_call(
        functools.partial(add_z_body, nz),
        out_shape=jax.ShapeDtypeStruct((piece, size * (len(parts) // nz)), BF16),
        in_specs=[pl.BlockSpec(memory_space=pltpu.VMEM)] * len(parts),
        compiler_params=PARAMS,
        cost_estimate=COST,
        name="add_z",
    )(*parts)


def forward_body(nb, rank, nz, tenant_ref, place_ref, w_ref, cot_ref, *refs):
    a_refs, up_refs = refs[:nb], refs[nb : 2 * nb]
    pieces = refs[2 * nb : 2 * nb + 2 * nz + 2]
    part_ref, dot_ref, low_ref, x_ref, acc_ref, lowacc_ref, sem = refs[-7:]
    piece = BLOCK // 4
    db = w_ref.shape[0]
    step = pl.program_id(0)

    @pl.when(step == 0)
    def _():
        z, x, core, first = place_ref[0], place_ref[1], place_ref[2], place_ref[3]

        def each(act):
            for n in range(4 * nz):
                k, fx, fc = n // 4, (n // 2) % 2, n % 2
                src = pieces[2 * nz + fx].at[pl.ds(k * piece, piece), :] if fc else pieces[2 * k + fx]
                b = lax.rem(z + (nz - k), nz) - first

                @pl.when(jnp.logical_and(b >= 0, b < nb))
                def _():
                    row = (b * 4 + (x ^ fx) * 2 + (core ^ fc)) * piece
                    rows = pl.ds(pl.multiple_of(row, piece), piece)
                    act(pltpu.make_async_copy(src, x_ref.at[rows, :], sem.at[n]))

        each(lambda copy: copy.start())
        acc_ref[...] = jnp.zeros_like(acc_ref)
        lowacc_ref[...] = jnp.zeros_like(lowacc_ref)
        each(lambda copy: copy.wait())

    xs = x_ref[:, pl.ds(pl.multiple_of(step * db, db), db)]
    acc_ref[...] += jnp.dot(xs, w_ref[...], preferred_element_type=F32)
    lowacc_ref[...] += lax.dot_general(cat_blocks(a_refs), xs, LAST, preferred_element_type=F32)

    @pl.when(step == pl.num_programs(0) - 1)
    def _():
        low = lowacc_ref[...]
        owner = lax.broadcasted_iota(jnp.int32, low.shape, 0) // rank
        block = lax.broadcasted_iota(jnp.int32, low.shape, 1) // BLOCK
        low = jnp.where(owner == block, low, 0.0)
        low_ref[...] = jnp.sum(low.reshape(nb, rank, low.shape[1]), axis=0)
        hi = low.astype(BF16).astype(F32)
        lowcat = jnp.concatenate([hi, low - hi], axis=0).T.astype(BF16)
        up = cat_blocks(up_refs)
        up = jnp.concatenate([up, up], axis=0)
        for i in range(nb):
            rows = slice(i * BLOCK, (i + 1) * BLOCK)
            part = acc_ref[rows, :] + jnp.dot(lowcat[rows, :], up, preferred_element_type=F32)
            part_ref[rows, :] = part.astype(part_ref.dtype)
            product = part * cot_ref[rows, :].astype(F32)
            dot_ref[i : i + 1, :] = jnp.sum(product, axis=0, keepdims=True)


def forward_group(tenant, place, weight, cot, down, up, pieces, nz, out_dtype, deps):
    depth, cols = weight.shape
    rows = cot.shape[0]
    nb = rows // BLOCK
    rank = down.shape[1]
    db = depth // STEPS

    def down_spec(b):
        return pl.BlockSpec((1, rank, db), lambda i, t, p: (t[(p[3] + b) * BLOCK], 0, i))

    def up_spec(b):
        return pl.BlockSpec((1, rank, cols), lambda i, t, p: (t[(p[3] + b) * BLOCK], 0, 0))

    shapes = (
        jax.ShapeDtypeStruct((rows, cols), out_dtype),
        jax.ShapeDtypeStruct((nb, cols), F32),
        jax.ShapeDtypeStruct((rank, rows), F32),
    )
    return pl.pallas_call(
        functools.partial(forward_body, nb, rank, nz),
        out_shape=shapes,
        grid_spec=pltpu.PrefetchScalarGridSpec(
            num_scalar_prefetch=2,
            grid=(STEPS,),
            in_specs=[pl.BlockSpec((db, cols), lambda i, t, p: (i, 0)), same_block(cot)]
            + [down_spec(b) for b in range(nb)]
            + [up_spec(b) for b in range(nb)]
            + [pl.BlockSpec(memory_space=pl.ANY)] * len(pieces)
            + order_specs(deps),
            out_specs=[same_block(s) for s in shapes],
            scratch_shapes=[
                pltpu.VMEM((rows, depth), BF16),
                pltpu.VMEM((rows, cols), F32),
                pltpu.VMEM((nb * rank, rows), F32),
                pltpu.SemaphoreType.DMA((4 * nz,)),
            ],
        ),
        compiler_params=PARAMS,
        cost_estimate=COST,
        name="forward_group",
    )(tenant, place, weight, cot, *([down] * nb), *([up] * nb), *pieces, *deps)


def shards(inputs, weight, adapter_down_factors, adapter_up_factors, magnitude, cotangent, tenant):
    col_count, row_count = lax.axis_size("col"), lax.axis_size("row")
    nz = col_count // 4
    down, up = adapter_down_factors, adapter_up_factors
    tenant_number, rank, depth = down.shape
    cols = weight.shape[1]
    tokens = tenant.shape[0]
    nblk = tokens // BLOCK
    rows_row = tokens // row_count
    blocks_mine = rows_row // BLOCK
    col, row = lax.axis_index("col"), lax.axis_index("row")
    z, x, core = col >> 2, (col >> 1) & 1, col & 1

    def move(value, dz, fx, fc):
        perm = []
        for source in range(col_count):
            sz, sx, sc = source // 4, (source // 2) % 2, source % 2
            perm.append((source, ((sz + dz) % nz) * 4 + (sx ^ fx) * 2 + (sc ^ fc)))
        return lax.ppermute(value, "col", perm)

    def swap(value):
        return lax.ppermute(value, "row", [(0, 1), (1, 0)])

    def place(*firsts):
        return jnp.stack([z, x, core, *firsts]).astype(jnp.int32)

    pair = row_count == 2

    along_z = [inputs] + [move(inputs, k, 0, 0) for k in range(1, nz)]
    own, _ = lax.optimization_barrier((inputs, along_z[-1]))
    along_x = [move(piece, 0, 1, 0) for piece in [own] + along_z[1:]]
    pieces = [piece for both in zip(along_z, along_x) for piece in both]
    pieces += [move(jnp.concatenate(part, axis=0), 0, 0, 1) for part in (along_z, along_x)]

    nsq = partial_norms(tenant, weight, down, up)
    if pair:
        nsq_a, nsq_b = nsq, swap(nsq)
        firsts = [row * blocks_mine, (1 - row) * blocks_mine]
        cots = [cotangent, swap(cotangent)]
    else:
        nsq_a, nsq_b = lax.psum(nsq, "row"), jnp.zeros_like(nsq)
        firsts = [0 * row]
        cots = [lax.all_gather(cotangent, "row", axis=0, tiled=True)]
    places = [place(first) for first in firsts]

    def scaled(g, deps):
        return scaled_gradient(tenant, places[g], cots[g], nsq_a, nsq_b, magnitude, up, deps)

    def grad(g, part, chunk, deps):
        return grad_chunk(tenant, places[g], part[1], part[2], weight, down, chunk, deps)

    def cross_core(made, deps):
        return add_core(made[0], move(made[1], 0, 0, 1), deps)

    def cross_x(made, deps):
        pairs = [(mine, move(away, 0, 1, 0)) for mine, away in made]
        mine, *away = add_x(place(*firsts), pairs, nz, deps)
        return [mine] + [move(a, k + 1, 0, 0) for k, a in enumerate(away)], mine

    def forward(g, out_dtype, deps):
        return forward_group(
            tenant, places[g], weight, cots[g], down, up, pieces, nz, out_dtype, deps
        )

    if pair:
        ours = scaled(0, [])
        made = [grad(0, ours, 0, along_z[3:])]
        made += [grad(0, ours, 1, [made[0][0], cots[1]] + along_z[1:2])]
        theirs = scaled(1, [made[1][0]] + along_z[2:3])
        near = [cross_core(made[0], [theirs[0]])]
        far = [grad(1, theirs, 0, [near[0][0]] + along_x[1:2] + along_x[3:])]
        near += [cross_core(made[1], [far[0][0]])]
        far += [grad(1, theirs, 1, [near[1][0]] + along_x[2:3])]
        done = [cross_core(far[0], [far[1][0]])]
        away, dots_away, low_away = forward(1, BF16, [done[0][0]])
        arrived = swap(away)
        done += [cross_core(far[1], [dots_away])]
        finals, after = cross_x([near[0], done[0]], [done[1][0]])
        part, dots_here, low_here = forward(0, F32, [after])
        more, after = cross_x([near[1], done[1]], [dots_here])
        finals += more
        pre = part + arrived.astype(F32)
        dots = [dots_here, dots_away]
        low = [low_here, low_away]
        dots_new = swap(jnp.concatenate(dots[::-1], axis=0))
        low_new = swap(jnp.concatenate(low[::-1], axis=1))
        dots = jnp.concatenate(dots, axis=0) + dots_new
        low = jnp.concatenate(low, axis=1) + low_new
        parts = [ours, theirs]
    else:
        ours = scaled(0, [])
        near = [cross_core(grad(0, ours, chunk, []), []) for chunk in range(CHUNKS)]
        part, dots, low = forward(0, F32, [])
        finals = []
        for chunk in range(CHUNKS):
            finals += cross_x([near[chunk]], [])[0]
        pre = lax.psum_scatter(part, "row", scatter_dimension=0, tiled=True)
        dots, low = lax.psum((dots, low), "row")
        parts = [ours]

    grad_inputs = add_z(finals, nz)
    scales = jnp.concatenate([part[0] for part in parts], axis=0)
    if pair:
        scale_mine = parts[0][0]
    else:
        scale_mine = lax.dynamic_slice_in_dim(scales, row * blocks_mine, blocks_mine, 0)
    output = (pre.reshape(blocks_mine, BLOCK, cols) * scale_mine[:, None, :]).astype(BF16)
    output = output.reshape(rows_row, cols)

    tenants = jnp.arange(tenant_number, dtype=jnp.int32)
    block_tenant = tenant.reshape(nblk, BLOCK)[:, 0]
    size = nblk // len(parts)
    owners = jnp.concatenate(
        [lax.dynamic_slice_in_dim(block_tenant, first, size, 0) for first in firsts]
    )
    low = low.astype(BF16)
    grad_b = 0.0
    for g, made in enumerate(parts):
        owner = jnp.repeat(owners[g * size : (g + 1) * size], BLOCK)
        mine = low[:, g * size * BLOCK : (g + 1) * size * BLOCK]
        wide = jnp.where((tenants[:, None] == owner[None, :])[:, None, :], mine[None], 0)
        wide = wide.reshape(tenant_number * rank, size * BLOCK)
        grad_b = grad_b + jnp.dot(wide, made[1], preferred_element_type=F32)
    grad_b = grad_b.reshape(tenant_number, rank, cols)
    hit = (tenants[:, None] == owners[None, :])[:, :, None]
    terms = jnp.where(hit, (dots * scales)[None], 0.0)
    grad_m = 0.0
    for g in range(len(parts)):
        group = terms[:, g * size : (g + 1) * size]
        grad_m = grad_m + functools.reduce(jnp.add, [group[:, i] for i in range(size)])
    return (output, grad_inputs, grad_b, grad_m / magnitude)


def solution(mesh):
    return jax.shard_map(
        shards,
        mesh=mesh,
        in_specs=(
            P("col", "row"),
            P("row", "col"),
            P(None, None, "row"),
            P(None, None, "col"),
            P(None, "col"),
            P("row", "col"),
            P(),
        ),
        out_specs=(P("row", "col"), P("col", "row"), P(None, None, "col"), P(None, "col")),
        check_vma=False,
    )
```

time: 173 us -> 178 us (1.029)
  local copies, waits for them, and re-layouts: 17.8 us -> 50 us
  starting transfers between devices: 47.4 us -> 24.7 us
  Pallas kernels: 62.3 us -> 53.6 us
  other arithmetic: 2.88 us -> 7.23 us
    unnamed x78 -> x112, local copies, waits for them, and re-layouts: 17 us -> 49.1 us
    ppermute x35 -> x23, starting transfers between devices: 41.6 us -> 20 us  [move(): return lax.ppermute(value, 'col', perm)]
    pallas_call x11 -> x10, Pallas kernels: 49.5 us -> 41.6 us  [the longest x2 18.5 us: forward_group(): pl.pallas_call(functools.partial(forward_body, nb, rank, nz), out_shape=s...]
    ppermute x35 -> x23, waiting for transfers between devices: 36.8 us -> 30.3 us  [move(): return lax.ppermute(value, 'col', perm)]
    ppermute x5, waiting for transfers between devices: 0.61 us -> 6.46 us  [swap(): return lax.ppermute(value, 'row', [(0, 1), (1, 0)])]
    pallas_call x1, Pallas kernels: 9.73 us -> 5.95 us  [partial_norms(): pl.pallas_call(functools.partial(norm_body, nblk, rank), out_shape=jax.Sh...]
    concatenate x0 -> x5, other arithmetic: none -> 3.25 us  [the longest x2 3.16 us: shards(): jnp.concatenate(part, axis=0)]
    pallas_call x4, Pallas kernels: 2.22 us -> 5.22 us  [add_core(): pl.pallas_call(add_core_body, out_shape=(jax.ShapeDtypeStruct((rows // 2,...]
  transfers between devices with their start and end apart: 40 -> 28, of which waited for: 12 -> 12; matrix products, arithmetic and copies ran while one was open for 3% -> 5% of each run, Pallas kernels for 34% -> 31%
where the time goes in v2:
time: 178 us; the launch traced here: 175 us
  Pallas kernels  53.6 us (30%)
  local copies, waits for them, and re-layouts  50 us (28%)
  waiting for transfers between devices  36.8 us (21%)
  starting transfers between devices  24.7 us (14%)
  other arithmetic  7.23 us (4%)
  matrix products  2.05 us (1%)
    unnamed x112, local copies, waits for them, and re-layouts  49.1 us
    ppermute x23, waiting for transfers between devices, move(): return lax.ppermute(value, 'col', perm)  30.3 us
    ppermute x23, starting transfers between devices, move(): return lax.ppermute(value, 'col', perm)  20 us
    pallas_call x2, Pallas kernels, forward_group(): pl.pallas_call(functools.partial(forward_body, nb, rank, nz), out_shape=s...  18.5 us
    pallas_call x4, Pallas kernels, grad_chunk(): pl.pallas_call(functools.partial(grad_body, nb, rank), out_shape=(jax.Sha...  16.6 us
    ppermute x5, waiting for transfers between devices, swap(): return lax.ppermute(value, 'row', [(0, 1), (1, 0)])  6.46 us
    pallas_call x1, Pallas kernels, partial_norms(): pl.pallas_call(functools.partial(norm_body, nblk, rank), out_shape=jax.Sh...  5.95 us
    pallas_call x4, Pallas kernels, add_core(): pl.pallas_call(add_core_body, out_shape=(jax.ShapeDtypeStruct((rows // 2,...  5.22 us
  transfers between devices with their start and end apart: 28, of which 12 were waited for; matrix products, arithmetic and copies ran while one was open for 5% of the time, Pallas kernels for 31%

profile of v2, /device:TPU:8, one launch (start us, length us, event | category | flops | bytes accessed | tf_op | source)
XLA Modules:
  0.0 175.4 jit_solution(5546833276777505547)
XLA Ops:
  0.6 1.6 collective-permute-start.11
  2.7 1.6 collective-permute-start.2
  4.2 4.4 %collective-permute-start.4 = (bf16[32,4096]{1,0:T(8,128)(2,1)}, bf16[32,4096]{1,0:T(8,128)(2,1)}, u32[]{:S(2)}, u32[]{:S(2)}) collective-permute-start(bf16[32,4096]{1,0:T(8,128)(2,1)} %refs_4_.5), channel_id=1, source_target_pairs={{0,16},{2,18},{4,20},{6,22},{8,24},{10,26},{12,28},{14,30},{16,0},... | collective-permute-start | bytes 786440 | tf_op jit(solution)/shard_map/ppermute | solution.py:412
  8.6 5.2 %copy-done = bf16[4096,1792]{1,0:T(8,128)(2,1)S(1)} copy-done((bf16[4096,1792]{1,0:T(8,128)(2,1)S(1)}, bf16[4096,1792]{1,0:T(8,128)(2,1)}, u32[]{:S(2)}) %copy-start) | copy-done | bytes 14680088
  13.8 1.6 copy-done.6
  15.4 1.2 copy-done.8
  17.3 5.9 %partial_norms.1.nsq_a = f32[4,1792]{1,0:T(4,128)} custom-call(s32[512]{0:T(512)S(1)} %copy-done.47, bf16[4096,1792]{1,0:T(8,128)(2,1)S(1)} %copy-done, bf16[16,16,4096]{2,1,0:T(8,128)(2,1)S(1)} %copy-done.6, bf16[16,16,4096]{2,1,0:T(8,128)(2,1)S(1)} %copy-done.6, bf16[16,16,4096]{2,1,0:T(8,128)(2,1)S(1)} %copy-done.6, bf16[16,16,4096]{2,1,0:T(8,128)(2,1)S(1)} %copy-done.6, ...), custom_call_target="tpu_custom_call" | custom-call | flops 1000 | bytes 1000 | tf_op jit(solution)/shard_map/partial_norms/pallas_call | solution.py:84
  23.9 3.5 %collective-permute-done.9.nsq_b = f32[4,1792]{1,0:T(4,128)} collective-permute-done((f32[4,1792]{1,0:T(4,128)}, f32[4,1792]{1,0:T(4,128)}, u32[]{:S(2)}, u32[]{:S(2)}) %collective-permute-start.9) | collective-permute-done | bytes 28704 | tf_op jit(solution)/shard_map/ppermute | solution.py:415
  27.4 1.2 copy-done.30
  29.5 1.8 %scaled_gradient.2 = (f32[2,1792]{1,0:T(2,128)S(1)}, bf16[256,1792]{1,0:T(8,128)(2,1)S(1)}, bf16[256,64]{1,0:T(8,128)(2,1)S(1)}) custom-call(s32[512]{0:T(512)S(1)} %copy-done.48, s32[4]{0:T(128)S(1)} %pad_add_fusion.place_ref, bf16[256,1792]{1,0:T(8,128)(2,1)S(1)} %copy-done.30, f32[4,1792]{1,0:T(4,128)} %partial_norms.1.nsq_a, ...), custom_call_target="tpu_custom_call" | custom-call | flops 1000 | bytes 1000 | tf_op jit(solution)/shard_map/scaled_gradient/pallas_call | solution.py:137
  31.9 5.5 %copy-done.1 = bf16[4096,1792]{1,0:T(8,128)(2,1)S(1)} copy-done((bf16[4096,1792]{1,0:T(8,128)(2,1)S(1)}, bf16[4096,1792]{1,0:T(8,128)(2,1)}, u32[]{:S(2)}) %copy-start.1) | copy-done | bytes 14680088
  37.4 4.3 %grad_chunk.4 = (f32[128,2048]{1,0:T(8,128)S(1)}, bf16[128,2048]{1,0:T(8,128)(2,1)}) custom-call(s32[512]{0:T(512)S(1)} %copy-done.48, s32[4]{0:T(128)S(1)} %pad_add_fusion.place_ref, bf16[256,1792]{1,0:T(8,128)(2,1)S(1)} %get-tuple-element.42.sg_ref, bf16[256,64]{1,0:T(8,128)(2,1)S(1)} %get-tuple-element.43.back_ref, bf16[4096,1792]{1,0:T(8,128)(2,1)S(1)} %copy-done.1, ...), custom_call_target="tpu_custom_call" | custom-call | flops 1000 | bytes 1000 | tf_op jit(solution)/shard_map/grad_chunk/pallas_call | solution.py:195
  41.7 1.6 collective-permute-start.1
  43.8 1.5 collective-permute-start.3
  45.8 2.0 %pad_maximum_fusion = bf16[128,4096]{1,0:T(8,128)(2,1)} fusion(bf16[32,4096]{1,0:T(8,128)(2,1)S(1)} %collective-permute-done.refs_2_.refs_10_, bf16[32,4096]{1,0:T(8,128)(2,1)} %collective-permute-done.4.refs_3_.refs_8_, bf16[32,4096]{1,0:T(8,128)(2,1)S(1)} %collective-permute-done.2.refs_4_.refs_6_, bf16[32,4096]{1,0:T(8,128)(2,1)S(1)} %copy-done.32), kind=kLoop, calls=%fused_computation.3 | loop fusion | flops 4194304 | bytes 2097152 | tf_op jit(solution)/shard_map/concatenate | solution.py:426
  47.9 4.3 %grad_chunk.5 = (f32[128,2048]{1,0:T(8,128)S(1)}, bf16[128,2048]{1,0:T(8,128)(2,1)}) custom-call(s32[512]{0:T(512)S(1)} %copy-done.48, s32[4]{0:T(128)S(1)} %pad_add_fusion.place_ref, bf16[256,1792]{1,0:T(8,128)(2,1)S(1)} %get-tuple-element.42.sg_ref, bf16[256,64]{1,0:T(8,128)(2,1)S(1)} %get-tuple-element.43.back_ref, bf16[4096,1792]{1,0:T(8,128)(2,1)S(1)} %copy-done.1, ...), custom_call_target="tpu_custom_call" | custom-call | flops 1000 | bytes 1000 | tf_op jit(solution)/shard_map/grad_chunk/pallas_call | solution.py:195
  52.2 4.4 %collective-permute-done.6.refs_4_.refs_11_ = bf16[32,4096]{1,0:T(8,128)(2,1)S(1)} collective-permute-done((bf16[32,4096]{1,0:T(8,128)(2,1)S(1)}, bf16[32,4096]{1,0:T(8,128)(2,1)S(1)}, u32[]{:S(2)}, u32[]{:S(2)}) %collective-permute-start.6) | collective-permute-done | bytes 262176 | tf_op jit(solution)/shard_map/ppermute | solution.py:412
  56.5 5.6 %collective-permute-done.3.refs_3_.refs_7_ = bf16[32,4096]{1,0:T(8,128)(2,1)S(1)} collective-permute-done((bf16[32,4096]{1,0:T(8,128)(2,1)S(1)}, bf16[32,4096]{1,0:T(8,128)(2,1)S(1)}, u32[]{:S(2)}, u32[]{:S(2)}) %collective-permute-start.3) | collective-permute-done | bytes 262176 | tf_op jit(solution)/shard_map/ppermute | solution.py:412
  62.1 5.2 %collective-permute-done.5.refs_3_.refs_9_ = bf16[32,4096]{1,0:T(8,128)(2,1)S(1)} collective-permute-done((bf16[32,4096]{1,0:T(8,128)(2,1)}, bf16[32,4096]{1,0:T(8,128)(2,1)S(1)}, u32[]{:S(2)}, u32[]{:S(2)}) %collective-permute-start.5) | collective-permute-done | bytes 262176 | tf_op jit(solution)/shard_map/ppermute | solution.py:412
  67.3 1.1 pad_maximum_fusion.1
  69.3 1.2 copy-done.28
  71.4 2.3 %scaled_gradient.3 = (f32[2,1792]{1,0:T(2,128)S(1)}, bf16[256,1792]{1,0:T(8,128)(2,1)S(1)}, bf16[256,64]{1,0:T(8,128)(2,1)S(1)}) custom-call(s32[512]{0:T(512)S(1)} %copy-done.48, s32[4]{0:T(128)S(1)} %get-tuple-element.80.place_ref, bf16[256,1792]{1,0:T(8,128)(2,1)} %collective-permute-done.11.refs_3_.cot_ref, f32[4,1792]{1,0:T(4,128)} %partial_norms.1.nsq_a, ...), custom_call_target="tpu_custom_call" | custom-call | flops 1000 | bytes 1000 | tf_op jit(solution)/shard_map/scaled_gradient/pallas_call | solution.py:137
  73.7 2.2 %add_core.4 = (f32[64,2048]{1,0:T(8,128)S(1)}, bf16[64,2048]{1,0:T(8,128)(2,1)}) custom-call(f32[128,2048]{1,0:T(8,128)S(1)} %copy-done.24, bf16[128,2048]{1,0:T(8,128)(2,1)} %collective-permute-done.10.recv_ref, f32[2,1792]{1,0:T(2,128)S(1)} %get-tuple-element.47.refs_0_), custom_call_target="tpu_custom_call" | custom-call | flops 1000 | bytes 1000 | tf_op jit(solution)/shard_map/add_core/pallas_call | solution.py:229
  75.9 5.4 %copy-done.2 = bf16[4096,1792]{1,0:T(8,128)(2,1)S(1)} copy-done((bf16[4096,1792]{1,0:T(8,128)(2,1)S(1)}, bf16[4096,1792]{1,0:T(8,128)(2,1)}, u32[]{:S(2)}) %copy-start.2) | copy-done | bytes 14680088
  81.3 3.7 %grad_chunk.6 = (f32[128,2048]{1,0:T(8,128)S(1)}, bf16[128,2048]{1,0:T(8,128)(2,1)S(1)}) custom-call(s32[512]{0:T(512)S(1)} %copy-done.48, s32[4]{0:T(128)S(1)} %get-tuple-element.80.place_ref, bf16[256,1792]{1,0:T(8,128)(2,1)S(1)} %get-tuple-element.50.sg_ref, bf16[256,64]{1,0:T(8,128)(2,1)S(1)} %get-tuple-element.51.back_ref, ...), custom_call_target="tpu_custom_call" | custom-call | flops 1000 | bytes 1000 | tf_op jit(solution)/shard_map/grad_chunk/pallas_call | solution.py:195
  86.8 1.1 add_core.5
  88.7 5.4 %copy-done.3 = bf16[4096,1792]{1,0:T(8,128)(2,1)S(1)} copy-done((bf16[4096,1792]{1,0:T(8,128)(2,1)S(1)}, bf16[4096,1792]{1,0:T(8,128)(2,1)}, u32[]{:S(2)}) %copy-start.3) | copy-done | bytes 14680088
  94.0 4.3 %grad_chunk.7 = (f32[128,2048]{1,0:T(8,128)S(1)}, bf16[128,2048]{1,0:T(8,128)(2,1)}) custom-call(s32[512]{0:T(512)S(1)} %copy-done.48, s32[4]{0:T(128)S(1)} %get-tuple-element.80.place_ref, bf16[256,1792]{1,0:T(8,128)(2,1)S(1)} %get-tuple-element.50.sg_ref, bf16[256,64]{1,0:T(8,128)(2,1)S(1)} %get-tuple-element.51.back_ref, ...), custom_call_target="tpu_custom_call" | custom-call | flops 1000 | bytes 1000 | tf_op jit(solution)/shard_map/grad_chunk/pallas_call | solution.py:195
  98.4 1.5 collective-permute-start.12
  104.4 1.5 collective-permute-start.21
  106.0 5.2 %copy-done.4 = bf16[4096,1792]{1,0:T(8,128)(2,1)S(1)} copy-done((bf16[4096,1792]{1,0:T(8,128)(2,1)S(1)}, bf16[4096,1792]{1,0:T(8,128)(2,1)}, u32[]{:S(2)}) %copy-start.4) | copy-done | bytes 14680088
  115.9 1.0 copy-done.42
  116.9 9.8 %forward_group.2 = (bf16[256,1792]{1,0:T(8,128)(2,1)S(1)}, f32[2,1792]{1,0:T(2,128)S(1)}, f32[16,256]{1,0:T(8,128)S(1)}) custom-call(s32[512]{0:T(512)S(1)} %copy-done.48, s32[4]{0:T(128)S(1)} %get-tuple-element.80.place_ref, bf16[4096,1792]{1,0:T(8,128)(2,1)S(1)} %copy-done.4, bf16[256,1792]{1,0:T(8,128)(2,1)} %collective-permute-done.11.refs_3_.cot_ref, ...), custom_call_target="tpu_custom_call" | custom-call | flops 1000 | bytes 1000 | tf_op jit(solution)/shard_map/forward_group/pallas_call | solution.py:369
  127.3 1.1 add_core.7
  128.5 1.7 add_x.2
  130.3 5.2 %copy-done.5 = bf16[4096,1792]{1,0:T(8,128)(2,1)S(1)} copy-done((bf16[4096,1792]{1,0:T(8,128)(2,1)S(1)}, bf16[4096,1792]{1,0:T(8,128)(2,1)}, u32[]{:S(2)}) %copy-start.5) | copy-done | bytes 14680088
  135.5 8.7 %forward_group.3 = (f32[256,1792]{1,0:T(8,128)S(1)}, f32[2,1792]{1,0:T(2,128)S(1)}, f32[16,256]{1,0:T(8,128)S(1)}) custom-call(s32[512]{0:T(512)S(1)} %copy-done.48, s32[4]{0:T(128)S(1)} %pad_add_fusion.place_ref, bf16[4096,1792]{1,0:T(8,128)(2,1)S(1)} %copy-done.5, bf16[256,1792]{1,0:T(8,128)(2,1)S(1)} %copy-done.31, bf16[16,16,4096]{2,1,0:T(8,128)(2,1)S(1)} %copy-done.7, ...), custom_call_target="tpu_custom_call" | custom-call | flops 1000 | bytes 1000 | tf_op jit(solution)/shard_map/forward_group/pallas_call | solution.py:369
  144.2 1.7 collective-permute-start.27
  146.8 2.9 %collective-permute-done.27 = f32[4,1792]{1,0:T(4,128)S(1)} collective-permute-done((f32[4,1792]{1,0:T(4,128)S(1)}, f32[4,1792]{1,0:T(4,128)S(1)}, u32[]{:S(2)}, u32[]{:S(2)}) %collective-permute-start.27) | collective-permute-done | bytes 28704 | tf_op jit(solution)/shard_map/ppermute | solution.py:415
  152.2 1.1 collective-permute-start.20
  154.1 1.4 collective-permute-start.23
  155.5 2.0 %collective-permute-done.18.refs_1_ = bf16[32,2048]{1,0:T(8,128)(2,1)S(1)} collective-permute-done((bf16[32,2048]{1,0:T(8,128)(2,1)S(1)}, bf16[32,2048]{1,0:T(8,128)(2,1)S(1)}, u32[]{:S(2)}, u32[]{:S(2)}) %collective-permute-start.18) | collective-permute-done | bytes 131104 | tf_op jit(solution)/shard_map/ppermute | solution.py:412
  157.5 1.3 collective-permute-start.24
  158.7 7.5 %collective-permute-done.19.refs_2_ = bf16[32,2048]{1,0:T(8,128)(2,1)S(1)} collective-permute-done((bf16[32,2048]{1,0:T(8,128)(2,1)S(1)}, bf16[32,2048]{1,0:T(8,128)(2,1)S(1)}, u32[]{:S(2)}, u32[]{:S(2)}) %collective-permute-start.19) | collective-permute-done | bytes 131104 | tf_op jit(solution)/shard_map/ppermute | solution.py:412
  166.2 1.6 convolution_add_fusion
  168.2 1.4 collective-permute-done.24.refs_6_
  169.6 3.8 %collective-permute-done.25.refs_7_ = bf16[32,2048]{1,0:T(8,128)(2,1)S(1)} collective-permute-done((bf16[32,2048]{1,0:T(8,128)(2,1)S(1)}, bf16[32,2048]{1,0:T(8,128)(2,1)S(1)}, u32[]{:S(2)}, u32[]{:S(2)}) %collective-permute-start.25) | collective-permute-done | bytes 131104 | tf_op jit(solution)/shard_map/ppermute | solution.py:412
  174.3 1.1 fusion
  (159 shorter events, 24.1 us)
Async XLA Ops:
  0.6 44.7 %collective-permute-start.11 = (bf16[256,1792]{1,0:T(8,128)(2,1)}, bf16[256,1792]{1,0:T(8,128)(2,1)}, u32[]{:S(2)}, u32[]{:S(2)}) collective-permute-start(bf16[256,1792]{1,0:T(8,128)(2,1)} %cot_ref.3), channel_id=1, source_target_pairs={{0,1},{1,0},{2,3},{3,2},{4,5},{5,4},{6,7},{7,6},{8,9},{9,8},{10,11... | collective-permute-start | bytes 2752520 | tf_op jit(solution)/shard_map/ppermute | solution.py:415
  2.2 29.7 %collective-permute-start = (bf16[32,4096]{1,0:T(8,128)(2,1)}, bf16[32,4096]{1,0:T(8,128)(2,1)S(1)}, u32[]{:S(2)}, u32[]{:S(2)}) collective-permute-start(bf16[32,4096]{1,0:T(8,128)(2,1)} %refs_4_.5), channel_id=1, source_target_pairs={{0,24},{2,26},{4,28},{6,30},{8,0},{10,2},{12,4},{14,6},{16,8},{18,... | collective-permute-start | bytes 786440 | tf_op jit(solution)/shard_map/ppermute | solution.py:412
  2.7 40.6 %collective-permute-start.2 = (bf16[32,4096]{1,0:T(8,128)(2,1)}, bf16[32,4096]{1,0:T(8,128)(2,1)S(1)}, u32[]{:S(2)}, u32[]{:S(2)}) collective-permute-start(bf16[32,4096]{1,0:T(8,128)(2,1)} %refs_4_.5), channel_id=1, source_target_pairs={{0,8},{2,10},{4,12},{6,14},{8,16},{10,18},{12,20},{14,22},{16,24},... | collective-permute-start | bytes 786440 | tf_op jit(solution)/shard_map/ppermute | solution.py:412
  4.2 39.6 %collective-permute-start.4 = (bf16[32,4096]{1,0:T(8,128)(2,1)}, bf16[32,4096]{1,0:T(8,128)(2,1)}, u32[]{:S(2)}, u32[]{:S(2)}) collective-permute-start(bf16[32,4096]{1,0:T(8,128)(2,1)} %refs_4_.5), channel_id=1, source_target_pairs={{0,16},{2,18},{4,20},{6,22},{8,24},{10,26},{12,28},{14,30},{16,0},... | collective-permute-start | bytes 786440 | tf_op jit(solution)/shard_map/ppermute | solution.py:412
  17.3 10.1 %copy-start.9 = (bf16[16,16,1792]{2,1,0:T(8,128)(2,1)S(1)}, bf16[16,16,1792]{2,1,0:T(8,128)(2,1)}, u32[]{:S(2)}) copy-start(bf16[16,16,1792]{2,1,0:T(8,128)(2,1)} %refs_3_.5) | copy-start | bytes 2752516
  17.3 10.1 %copy-start.48 = (s32[512]{0:T(512)S(1)}, s32[512]{0:T(512)}, u32[]{:S(2)}) copy-start(s32[512]{0:T(512)} %tenant_ref.17) | copy-start | bytes 6148
  23.2 8.7 %copy-start.7 = (bf16[16,16,4096]{2,1,0:T(8,128)(2,1)S(1)}, bf16[16,16,4096]{2,1,0:T(8,128)(2,1)}, u32[]{:S(2)}) copy-start(bf16[16,16,4096]{2,1,0:T(8,128)(2,1)} %refs_1_.17) | copy-start | bytes 6291460
  23.2 4.2 %collective-permute-start.9 = (f32[4,1792]{1,0:T(4,128)}, f32[4,1792]{1,0:T(4,128)}, u32[]{:S(2)}, u32[]{:S(2)}) collective-permute-start(f32[4,1792]{1,0:T(4,128)} %partial_norms.1.nsq_a), channel_id=1, source_target_pairs={{0,1},{1,0},{2,3},{3,2},{4,5},{5,4},{6,7},{7,6},{8,9},{9,8},{10,11... | collective-permute-start | bytes 86024 | tf_op jit(solution)/shard_map/ppermute | solution.py:415
  31.9 16.0 %copy-start.10 = (bf16[256,1792]{1,0:T(8,128)(2,1)}, bf16[256,1792]{1,0:T(8,128)(2,1)S(1)}, u32[]{:S(2)}) copy-start(bf16[256,1792]{1,0:T(8,128)(2,1)S(1)} %get-tuple-element.42.sg_ref) | copy-start | bytes 2752516
  41.7 10.4 %copy-start.23 = (f32[128,2048]{1,0:T(8,128)}, f32[128,2048]{1,0:T(8,128)S(1)}, u32[]{:S(2)}) copy-start(f32[128,2048]{1,0:T(8,128)S(1)} %get-tuple-element.44.refs_2_.keep_ref) | copy-start | bytes 3145732
  41.7 32.0 %collective-permute-start.10 = (bf16[128,2048]{1,0:T(8,128)(2,1)}, bf16[128,2048]{1,0:T(8,128)(2,1)}, u32[]{:S(2)}, u32[]{:S(2)}) collective-permute-start(bf16[128,2048]{1,0:T(8,128)(2,1)} %get-tuple-element.45), channel_id=1, source_target_pairs={{0,2},{2,0},{4,6},{6,4},{8,10},{10,8},{12,14},{14,12},{16,18},{18,... | collective-permute-start | bytes 1572872 | tf_op jit(solution)/shard_map/ppermute | solution.py:412
  41.7 25.6 %collective-permute-start.1 = (bf16[32,4096]{1,0:T(8,128)(2,1)S(1)}, bf16[32,4096]{1,0:T(8,128)(2,1)S(1)}, u32[]{:S(2)}, u32[]{:S(2)}) collective-permute-start(bf16[32,4096]{1,0:T(8,128)(2,1)S(1)} %copy-done.32), channel_id=1, source_target_pairs={{0,4},{2,6},{4,0},{6,2},{8,12},{10,14},{12,8},{14,10},{16,20},{18,... | collective-permute-start | bytes 786440 | tf_op jit(solution)/shard_map/ppermute | solution.py:412
  43.3 13.2 %collective-permute-start.6 = (bf16[32,4096]{1,0:T(8,128)(2,1)S(1)}, bf16[32,4096]{1,0:T(8,128)(2,1)S(1)}, u32[]{:S(2)}, u32[]{:S(2)}) collective-permute-start(bf16[32,4096]{1,0:T(8,128)(2,1)S(1)} %collective-permute-done.refs_2_.refs_10_), channel_id=1, source_target_pairs={{0,4},{2,6},{4,0},{6,2},{8,12},{10,14},{12,8},{14,10},{16,20},{18,... | collective-permute-start | bytes 786440 | tf_op jit(solution)/shard_map/ppermute | solution.py:412
  43.8 18.3 %collective-permute-start.3 = (bf16[32,4096]{1,0:T(8,128)(2,1)S(1)}, bf16[32,4096]{1,0:T(8,128)(2,1)S(1)}, u32[]{:S(2)}, u32[]{:S(2)}) collective-permute-start(bf16[32,4096]{1,0:T(8,128)(2,1)S(1)} %collective-permute-done.2.refs_4_.refs_6_), channel_id=1, source_target_pairs={{0,4},{2,6},{4,0},{6,2},{8,12},{10,14},{12,8},{14,10},{16,20},{18,... | collective-permute-start | bytes 786440 | tf_op jit(solution)/shard_map/ppermute | solution.py:412
  45.3 22.0 %collective-permute-start.5 = (bf16[32,4096]{1,0:T(8,128)(2,1)}, bf16[32,4096]{1,0:T(8,128)(2,1)S(1)}, u32[]{:S(2)}, u32[]{:S(2)}) collective-permute-start(bf16[32,4096]{1,0:T(8,128)(2,1)} %collective-permute-done.4.refs_3_.refs_8_), channel_id=1, source_target_pairs={{0,4},{2,6},{4,0},{6,2},{8,12},{10,14},{12,8},{14,10},{16,20},{18,... | collective-permute-start | bytes 786440 | tf_op jit(solution)/shard_map/ppermute | solution.py:412
  52.2 16.3 %copy-start.27 = (f32[128,2048]{1,0:T(8,128)}, f32[128,2048]{1,0:T(8,128)S(1)}, u32[]{:S(2)}) copy-start(f32[128,2048]{1,0:T(8,128)S(1)} %get-tuple-element.46.refs_2_.keep_ref) | copy-start | bytes 3145732
  56.5 47.9 %collective-permute-start.7 = (bf16[128,4096]{1,0:T(8,128)(2,1)}, bf16[128,4096]{1,0:T(8,128)(2,1)}, u32[]{:S(2)}, u32[]{:S(2)}) collective-permute-start(bf16[128,4096]{1,0:T(8,128)(2,1)} %pad_maximum_fusion), channel_id=1, source_target_pairs={{0,2},{2,0},{4,6},{6,4},{8,10},{10,8},{12,14},{14,12},{16,18},{18,... | collective-permute-start | bytes 3145736 | tf_op jit(solution)/shard_map/ppermute | solution.py:412
  62.1 6.3 %copy-start.17 = (bf16[32,4096]{1,0:T(8,128)(2,1)}, bf16[32,4096]{1,0:T(8,128)(2,1)S(1)}, u32[]{:S(2)}) copy-start(bf16[32,4096]{1,0:T(8,128)(2,1)S(1)} %collective-permute-done.3.refs_3_.refs_7_) | copy-start | bytes 786436
  62.1 24.7 %collective-permute-start.14 = (bf16[128,2048]{1,0:T(8,128)(2,1)}, bf16[128,2048]{1,0:T(8,128)(2,1)}, u32[]{:S(2)}, u32[]{:S(2)}) collective-permute-start(bf16[128,2048]{1,0:T(8,128)(2,1)} %get-tuple-element.54), channel_id=1, source_target_pairs={{0,2},{2,0},{4,6},{6,4},{8,10},{10,8},{12,14},{14,12},{16,18},{18,... | collective-permute-start | bytes 1572872 | tf_op jit(solution)/shard_map/ppermute | solution.py:412
  69.1 36.8 %collective-permute-start.8 = (bf16[128,4096]{1,0:T(8,128)(2,1)}, bf16[128,4096]{1,0:T(8,128)(2,1)}, u32[]{:S(2)}, u32[]{:S(2)}) collective-permute-start(bf16[128,4096]{1,0:T(8,128)(2,1)} %pad_maximum_fusion.1), channel_id=1, source_target_pairs={{0,2},{2,0},{4,6},{6,4},{8,10},{10,8},{12,14},{14,12},{16,18},{18,... | collective-permute-start | bytes 3145736 | tf_op jit(solution)/shard_map/ppermute | solution.py:412
  73.7 14.9 %copy-start.12 = (bf16[256,1792]{1,0:T(8,128)(2,1)}, bf16[256,1792]{1,0:T(8,128)(2,1)S(1)}, u32[]{:S(2)}) copy-start(bf16[256,1792]{1,0:T(8,128)(2,1)S(1)} %get-tuple-element.50.sg_ref) | copy-start | bytes 2752516
  75.9 9.0 %copy-start.39 = (f32[64,2048]{1,0:T(8,128)}, f32[64,2048]{1,0:T(8,128)S(1)}, u32[]{:S(2)}) copy-start(f32[64,2048]{1,0:T(8,128)S(1)} %get-tuple-element.48.refs_2_.refs_0_) | copy-start | bytes 1572868
  85.0 15.0 %collective-permute-start.13 = (bf16[128,2048]{1,0:T(8,128)(2,1)S(1)}, bf16[128,2048]{1,0:T(8,128)(2,1)S(1)}, u32[]{:S(2)}, u32[]{:S(2)}) collective-permute-start(bf16[128,2048]{1,0:T(8,128)(2,1)S(1)} %get-tuple-element.53), channel_id=1, source_target_pairs={{0,2},{2,0},{4,6},{6,4},{8,10},{10,8},{12,14},{14,12},{16,18},{18,... | collective-permute-start | bytes 1572872 | tf_op jit(solution)/shard_map/ppermute | solution.py:412
  88.6 9.7 %copy-start.37 = (f32[64,2048]{1,0:T(8,128)}, f32[64,2048]{1,0:T(8,128)S(1)}, u32[]{:S(2)}) copy-start(f32[64,2048]{1,0:T(8,128)S(1)} %get-tuple-element.55.refs_2_.refs_0_) | copy-start | bytes 1572868
  98.3 29.0 %collective-permute-start.16 = (bf16[128,2048]{1,0:T(8,128)(2,1)}, bf16[128,2048]{1,0:T(8,128)(2,1)}, u32[]{:S(2)}, u32[]{:S(2)}) collective-permute-start(bf16[128,2048]{1,0:T(8,128)(2,1)} %get-tuple-element.59), channel_id=1, source_target_pairs={{0,2},{2,0},{4,6},{6,4},{8,10},{10,8},{12,14},{14,12},{16,18},{18,... | collective-permute-start | bytes 1572872 | tf_op jit(solution)/shard_map/ppermute | solution.py:412
  98.4 30.0 %collective-permute-start.12 = (bf16[64,2048]{1,0:T(8,128)(2,1)}, bf16[64,2048]{1,0:T(8,128)(2,1)}, u32[]{:S(2)}, u32[]{:S(2)}) collective-permute-start(bf16[64,2048]{1,0:T(8,128)(2,1)} %get-tuple-element.49), channel_id=1, source_target_pairs={{0,4},{2,6},{4,0},{6,2},{8,12},{10,14},{12,8},{14,10},{16,20},{18,... | collective-permute-start | bytes 786440 | tf_op jit(solution)/shard_map/ppermute | solution.py:412
  102.6 25.9 %collective-permute-start.15 = (bf16[64,2048]{1,0:T(8,128)(2,1)}, bf16[64,2048]{1,0:T(8,128)(2,1)}, u32[]{:S(2)}, u32[]{:S(2)}) collective-permute-start(bf16[64,2048]{1,0:T(8,128)(2,1)} %get-tuple-element.58), channel_id=1, source_target_pairs={{0,4},{2,6},{4,0},{6,2},{8,12},{10,14},{12,8},{14,10},{16,20},{18,... | collective-permute-start | bytes 786440 | tf_op jit(solution)/shard_map/ppermute | solution.py:412
  104.4 47.8 %collective-permute-start.21 = (bf16[64,2048]{1,0:T(8,128)(2,1)}, bf16[64,2048]{1,0:T(8,128)(2,1)S(1)}, u32[]{:S(2)}, u32[]{:S(2)}) collective-permute-start(bf16[64,2048]{1,0:T(8,128)(2,1)} %copy-done.53), channel_id=1, source_target_pairs={{0,4},{2,6},{4,0},{6,2},{8,12},{10,14},{12,8},{14,10},{16,20},{18,... | collective-permute-start | bytes 786440 | tf_op jit(solution)/shard_map/ppermute | solution.py:412
  116.9 10.4 %copy-start.26 = (f32[128,2048]{1,0:T(8,128)S(1)}, f32[128,2048]{1,0:T(8,128)}, u32[]{:S(2)}) copy-start(f32[128,2048]{1,0:T(8,128)} %copy-done.25) | copy-start | bytes 3145732
  116.9 11.6 %copy-start.40 = (f32[64,2048]{1,0:T(8,128)S(1)}, f32[64,2048]{1,0:T(8,128)}, u32[]{:S(2)}) copy-start(f32[64,2048]{1,0:T(8,128)} %copy-done.39) | copy-start | bytes 1572868
  116.9 11.6 %copy-start.43 = (f32[64,2048]{1,0:T(8,128)S(1)}, f32[64,2048]{1,0:T(8,128)}, u32[]{:S(2)}) copy-start(f32[64,2048]{1,0:T(8,128)} %copy-done.41) | copy-start | bytes 1572868
  126.8 47.5 %collective-permute-start.17 = (bf16[256,1792]{1,0:T(8,128)(2,1)S(1)}, bf16[256,1792]{1,0:T(8,128)(2,1)S(1)}, u32[]{:S(2)}, u32[]{:S(2)}) collective-permute-start(bf16[256,1792]{1,0:T(8,128)(2,1)S(1)} %get-tuple-element.64), channel_id=1, source_target_pairs={{0,1},{1,0},{2,3},{3,2},{4,5},{5,4},{6,7},{7,6},{8,9},{9,8},{10,11... | collective-permute-start | bytes 2752520 | tf_op jit(solution)/shard_map/ppermute | solution.py:415
  135.5 14.3 %copy-start.50 = (f32[2,1792]{1,0:T(2,128)S(1)}, f32[2,1792]{1,0:T(2,128)}, u32[]{:S(2)}) copy-start(f32[2,1792]{1,0:T(2,128)} %copy-done.49) | copy-start | bytes 43012
  135.5 14.3 %copy-start.52 = (f32[2,1792]{1,0:T(2,128)S(1)}, f32[2,1792]{1,0:T(2,128)}, u32[]{:S(2)}) copy-start(f32[2,1792]{1,0:T(2,128)} %copy-done.51) | copy-start | bytes 43012
  135.5 14.3 %copy-start.55 = (pred[16,4]{0,1:T(4,128)(4,1)S(1)}, pred[16,4]{0,1:T(4,128)(4,1)}, u32[]{:S(2)}) copy-start(pred[16,4]{0,1:T(4,128)(4,1)} %iota_compare_fusion.2) | copy-start | bytes 196
  135.5 14.4 %copy-start.46 = (f32[16,1792]{1,0:T(8,128)S(1)}, f32[16,1792]{1,0:T(8,128)}, u32[]{:S(2)}) copy-start(f32[16,1792]{1,0:T(8,128)} %mag_ref.3) | copy-start | bytes 344068
  135.5 16.2 %copy-start.54 = (pred[16,256]{1,0:T(8,128)(4,1)S(1)}, pred[16,256]{1,0:T(8,128)(4,1)}, u32[]{:S(2)}) copy-start(pred[16,256]{1,0:T(8,128)(4,1)} %iota_compare_fusion) | copy-start | bytes 12292
  144.1 7.5 %copy-start.13 = (bf16[256,1792]{1,0:T(8,128)(2,1)S(1)}, bf16[256,1792]{1,0:T(8,128)(2,1)}, u32[]{:S(2)}) copy-start(bf16[256,1792]{1,0:T(8,128)(2,1)} %copy-done.12) | copy-start | bytes 2752516
  144.2 5.6 %collective-permute-start.27 = (f32[4,1792]{1,0:T(4,128)S(1)}, f32[4,1792]{1,0:T(4,128)S(1)}, u32[]{:S(2)}, u32[]{:S(2)}) collective-permute-start(f32[4,1792]{1,0:T(4,128)S(1)} %pad_maximum_fusion.3), channel_id=1, source_target_pairs={{0,1},{1,0},{2,3},{3,2},{4,5},{5,4},{6,7},{7,6},{8,9},{9,8},{10,11... | collective-permute-start | bytes 86024 | tf_op jit(solution)/shard_map/ppermute | solution.py:415
  145.9 4.7 %collective-permute-start.26 = (f32[16,512]{1,0:T(8,128)S(1)}, f32[16,512]{1,0:T(8,128)S(1)}, u32[]{:S(2)}, u32[]{:S(2)}) collective-permute-start(f32[16,512]{1,0:T(8,128)S(1)} %pad_maximum_fusion.2), channel_id=1, source_target_pairs={{0,1},{1,0},{2,3},{3,2},{4,5},{5,4},{6,7},{7,6},{8,9},{9,8},{10,11... | collective-permute-start | bytes 98312 | tf_op jit(solution)/shard_map/ppermute | solution.py:415
  146.3 7.1 %collective-permute-start.22 = (bf16[64,2048]{1,0:T(8,128)(2,1)S(1)}, bf16[64,2048]{1,0:T(8,128)(2,1)S(1)}, u32[]{:S(2)}, u32[]{:S(2)}) collective-permute-start(bf16[64,2048]{1,0:T(8,128)(2,1)S(1)} %get-tuple-element.70), channel_id=1, source_target_pairs={{0,4},{2,6},{4,0},{6,2},{8,12},{10,14},{12,8},{14,10},{16,20},{18,... | collective-permute-start | bytes 786440 | tf_op jit(solution)/shard_map/ppermute | solution.py:412
  149.7 7.7 %collective-permute-start.18 = (bf16[32,2048]{1,0:T(8,128)(2,1)S(1)}, bf16[32,2048]{1,0:T(8,128)(2,1)S(1)}, u32[]{:S(2)}, u32[]{:S(2)}) collective-permute-start(bf16[32,2048]{1,0:T(8,128)(2,1)S(1)} %get-tuple-element.66), channel_id=1, source_target_pairs={{0,8},{2,10},{4,12},{6,14},{8,16},{10,18},{12,20},{14,22},{16,24},... | collective-permute-start | bytes 393224 | tf_op jit(solution)/shard_map/ppermute | solution.py:412
  150.6 15.6 %collective-permute-start.19 = (bf16[32,2048]{1,0:T(8,128)(2,1)S(1)}, bf16[32,2048]{1,0:T(8,128)(2,1)S(1)}, u32[]{:S(2)}, u32[]{:S(2)}) collective-permute-start(bf16[32,2048]{1,0:T(8,128)(2,1)S(1)} %get-tuple-element.67), channel_id=1, source_target_pairs={{0,16},{2,18},{4,20},{6,22},{8,24},{10,26},{12,28},{14,30},{16,0},... | collective-permute-start | bytes 393224 | tf_op jit(solution)/shard_map/ppermute | solution.py:412
  151.7 14.5 %copy-start.11 = (bf16[256,1792]{1,0:T(8,128)(2,1)S(1)}, bf16[256,1792]{1,0:T(8,128)(2,1)}, u32[]{:S(2)}) copy-start(bf16[256,1792]{1,0:T(8,128)(2,1)} %copy-done.10) | copy-start | bytes 2752516
  152.2 15.9 %collective-permute-start.20 = (bf16[32,2048]{1,0:T(8,128)(2,1)S(1)}, bf16[32,2048]{1,0:T(8,128)(2,1)S(1)}, u32[]{:S(2)}, u32[]{:S(2)}) collective-permute-start(bf16[32,2048]{1,0:T(8,128)(2,1)S(1)} %get-tuple-element.68), channel_id=1, source_target_pairs={{0,24},{2,26},{4,28},{6,30},{8,0},{10,2},{12,4},{14,6},{16,8},{18,... | collective-permute-start | bytes 393224 | tf_op jit(solution)/shard_map/ppermute | solution.py:412
  154.1 14.1 %collective-permute-start.23 = (bf16[32,2048]{1,0:T(8,128)(2,1)S(1)}, bf16[32,2048]{1,0:T(8,128)(2,1)S(1)}, u32[]{:S(2)}, u32[]{:S(2)}) collective-permute-start(bf16[32,2048]{1,0:T(8,128)(2,1)S(1)} %get-tuple-element.73), channel_id=1, source_target_pairs={{0,8},{2,10},{4,12},{6,14},{8,16},{10,18},{12,20},{14,22},{16,24},... | collective-permute-start | bytes 393224 | tf_op jit(solution)/shard_map/ppermute | solution.py:412
  157.5 12.2 %collective-permute-start.24 = (bf16[32,2048]{1,0:T(8,128)(2,1)S(1)}, bf16[32,2048]{1,0:T(8,128)(2,1)S(1)}, u32[]{:S(2)}, u32[]{:S(2)}) collective-permute-start(bf16[32,2048]{1,0:T(8,128)(2,1)S(1)} %get-tuple-element.74), channel_id=1, source_target_pairs={{0,16},{2,18},{4,20},{6,22},{8,24},{10,26},{12,28},{14,30},{16,0},... | collective-permute-start | bytes 393224 | tf_op jit(solution)/shard_map/ppermute | solution.py:412
  166.2 7.2 %collective-permute-start.25 = (bf16[32,2048]{1,0:T(8,128)(2,1)S(1)}, bf16[32,2048]{1,0:T(8,128)(2,1)S(1)}, u32[]{:S(2)}, u32[]{:S(2)}) collective-permute-start(bf16[32,2048]{1,0:T(8,128)(2,1)S(1)} %get-tuple-element.75), channel_id=1, source_target_pairs={{0,24},{2,26},{4,28},{6,30},{8,0},{10,2},{12,4},{14,6},{16,8},{18,... | collective-permute-start | bytes 393224 | tf_op jit(solution)/shard_map/ppermute | solution.py:412
  (36 other events, 88.8 us)

commit v3 on v2

v3 whole, which is shorter than its diff:
```python
import functools

import jax
import jax.numpy as jnp
from jax import lax
from jax.experimental import pallas as pl
from jax.experimental.pallas import tpu as pltpu
from jax.sharding import PartitionSpec as P

BLOCK = 128
EPS = 1e-06
HIGH = lax.Precision.HIGHEST
CHUNKS = 2
STEPS = 8
F32 = jnp.float32
BF16 = jnp.bfloat16
COST = pl.CostEstimate(flops=1000, bytes_accessed=1000, transcendentals=0)
LAST = (((1,), (1,)), ((), ()))
PARAMS = pltpu.CompilerParams(vmem_limit_bytes=52 * 1024 * 1024)
IN_HBM = pl.BlockSpec(memory_space=pltpu.HBM)


def order_specs(deps):
    return [pl.BlockSpec(memory_space=pl.ANY)] * len(deps)


def same_block(array):
    return pl.BlockSpec(array.shape, lambda *args: (0,) * array.ndim)


def hi_lo(value, axis):
    hi = value.astype(BF16)
    lo = (value - hi.astype(F32)).astype(BF16)
    return jnp.concatenate([hi, lo], axis=axis)


def weight_copy(w_hbm, w_ref, sem, i, first=0):
    db = w_ref.shape[0] // sem.shape[0]
    src = pl.ds(pl.multiple_of((first + i) * db, db), db)
    dst = pl.ds(pl.multiple_of(i * db, db), db)
    return pltpu.make_async_copy(w_hbm.at[src, :], w_ref.at[dst, :], sem.at[i])


def factor_copies(tenant_ref, first, hbm, ref, sem, at, columns=None):
    rank, nblk = hbm.shape[1], tenant_ref.shape[0] // BLOCK
    copies = []
    for b in range(ref.shape[0] // rank):
        src = hbm.at[tenant_ref[lax.rem(first + b, nblk) * BLOCK]]
        if columns is not None:
            src = src.at[:, columns]
        dst = ref.at[pl.ds(b * rank, rank), :]
        copies.append(pltpu.make_async_copy(src, dst, sem.at[at + b]))
    return copies


def norm_body(nblk, rank, tenant_ref, w_hbm, a_hbm, up_hbm, nsq_ref, *refs):
    w_ref, a_ref, up_ref, cross_ref, square_ref, w_sem, sem = refs
    cols = w_ref.shape[1]
    db = w_ref.shape[0] // STEPS
    copies = factor_copies(tenant_ref, 0, a_hbm, a_ref, sem, 0)
    late = factor_copies(tenant_ref, 0, up_hbm, up_ref, sem, nblk)
    for copy in copies:
        copy.start()
    for i in range(STEPS):
        weight_copy(w_hbm, w_ref, w_sem, i).start()
    for copy in late:
        copy.start()
    cross_ref[...] = jnp.zeros_like(cross_ref)
    square_ref[...] = jnp.zeros_like(square_ref)
    for copy in copies:
        copy.wait()
    step = min(db, 256)

    def block(i, carry):
        weight_copy(w_hbm, w_ref, w_sem, i).wait()
        for start in range(0, db, step):
            rows = pl.ds(pl.multiple_of(i * db + start, step), step)
            w = w_ref[rows, :]
            cross_ref[...] += jnp.dot(a_ref[:, rows], w, preferred_element_type=F32)
            wf = w.astype(F32)
            square_ref[...] += jnp.sum((wf * wf).reshape(step // 8, 8, cols), axis=0)
        return carry

    lax.fori_loop(0, STEPS, block, 0)
    for copy in late:
        copy.wait()
    gram = lax.dot_general(a_ref[...], a_ref[...], LAST, preferred_element_type=F32)
    row = lax.broadcasted_iota(jnp.int32, gram.shape, 0) // rank
    col = lax.broadcasted_iota(jnp.int32, gram.shape, 1) // rank
    gram = jnp.where(row == col, gram, 0.0)
    up = up_ref[...].astype(F32)
    quad = jnp.dot(gram, up, preferred_element_type=F32, precision=HIGH)
    mixed = (up * (2.0 * cross_ref[...] + quad)).reshape(nblk, rank, cols)
    nsq_ref[...] = jnp.sum(mixed, axis=1) + jnp.sum(square_ref[...], axis=0, keepdims=True)


def partial_norms(tenant, weight, down, up):
    depth, cols = weight.shape
    rank = down.shape[1]
    nblk = tenant.shape[0] // BLOCK
    shape = jax.ShapeDtypeStruct((nblk, cols), F32)
    return pl.pallas_call(
        functools.partial(norm_body, nblk, rank),
        out_shape=shape,
        grid_spec=pltpu.PrefetchScalarGridSpec(
            num_scalar_prefetch=1,
            grid=(1,),
            in_specs=[IN_HBM] * 3,
            out_specs=same_block(shape),
            scratch_shapes=[
                pltpu.VMEM((depth, cols), BF16),
                pltpu.VMEM((nblk * rank, depth), BF16),
                pltpu.VMEM((nblk * rank, cols), BF16),
                pltpu.VMEM((nblk * rank, cols), F32),
                pltpu.VMEM((8, cols), F32),
                pltpu.SemaphoreType.DMA((STEPS,)),
                pltpu.SemaphoreType.DMA((2 * nblk,)),
            ],
        ),
        compiler_params=PARAMS,
        cost_estimate=COST,
        name="partial_norms",
    )(tenant, weight, down, up)


def scaled_body(nb, rank, tenant_ref, place_ref, cot_ref, nsq_a, nsq_b, mag_ref, up_hbm, *refs):
    scale_ref, sg_ref, back_ref, up_ref, sem = refs[-5:]
    first = place_ref[3]
    copies = factor_copies(tenant_ref, first, up_hbm, up_ref, sem, 0)
    for copy in copies:
        copy.start()
    for i in range(nb):
        b = first + i
        total = nsq_a[pl.ds(b, 1), :] + nsq_b[pl.ds(b, 1), :]
        scale = mag_ref[pl.ds(tenant_ref[b * BLOCK], 1), :] / jnp.sqrt(total + EPS)
        scale_ref[i : i + 1, :] = scale
        rows = slice(i * BLOCK, (i + 1) * BLOCK)
        sg_ref[rows, :] = (cot_ref[rows, :].astype(F32) * scale).astype(BF16)
    for copy in copies:
        copy.wait()
    back = lax.dot_general(sg_ref[...], up_ref[...], LAST, preferred_element_type=F32)
    block = lax.broadcasted_iota(jnp.int32, back.shape, 0) // BLOCK
    owner = lax.broadcasted_iota(jnp.int32, back.shape, 1) // rank
    back_ref[...] = hi_lo(jnp.where(owner == block, back, 0.0), 1)


def scaled_gradient(tenant, place, cot, nsq_a, nsq_b, magnitude, up, deps):
    rows, cols = cot.shape
    nb = rows // BLOCK
    rank = up.shape[1]
    shapes = (
        jax.ShapeDtypeStruct((nb, cols), F32),
        jax.ShapeDtypeStruct((rows, cols), BF16),
        jax.ShapeDtypeStruct((rows, 2 * nb * rank), BF16),
    )
    return pl.pallas_call(
        functools.partial(scaled_body, nb, rank),
        out_shape=shapes,
        grid_spec=pltpu.PrefetchScalarGridSpec(
            num_scalar_prefetch=2,
            grid=(1,),
            in_specs=[same_block(a) for a in (cot, nsq_a, nsq_b, magnitude)]
            + [IN_HBM]
            + order_specs(deps),
            out_specs=[same_block(s) for s in shapes],
            scratch_shapes=[
                pltpu.VMEM((nb * rank, cols), BF16),
                pltpu.SemaphoreType.DMA((nb,)),
            ],
        ),
        compiler_params=PARAMS,
        cost_estimate=COST,
        name="scaled_gradient",
    )(tenant, place, cot, nsq_a, nsq_b, magnitude, up, *deps)


def grad_body(nb, rank, chunk, tenant_ref, place_ref, sg_ref, back_ref, w_hbm, a_hbm, *refs):
    keep_ref, send_ref, w_ref, a_ref, sgp_ref, backp_ref, w_sem, sem = refs[-8:]
    rows, size = sg_ref.shape[0], w_ref.shape[0]
    steps = w_sem.shape[0]
    db = size // steps
    piece = BLOCK // 4
    half = rows // 2
    for i in range(steps):
        weight_copy(w_hbm, w_ref, w_sem, i, chunk * steps).start()
    columns = pl.ds(chunk * size, size)
    copies = factor_copies(tenant_ref, place_ref[3], a_hbm, a_ref, sem, 0, columns)
    for copy in copies:
        copy.start()
    x, core = place_ref[1], place_ref[2]
    for fc in range(2):
        for fx in range(2):
            for b in range(nb):
                c = b * 4 + (x ^ fx) * 2 + (core ^ fc)
                src = pl.ds(pl.multiple_of(c * piece, piece), piece)
                at = ((fc * 2 + fx) * nb + b) * piece
                sgp_ref[at : at + piece, :] = sg_ref[src, :]
                backp_ref[at : at + piece, :] = back_ref[src, :]
    for copy in copies:
        copy.wait()

    def block(i, carry):
        weight_copy(w_hbm, w_ref, w_sem, i, chunk * steps).wait()
        at = pl.ds(pl.multiple_of(i * db, db), db)
        down = a_ref[:, at]
        down = jnp.concatenate([down, down], axis=0)
        part = lax.dot_general(sgp_ref[...], w_ref[at, :], LAST, preferred_element_type=F32)
        part = part + jnp.dot(backp_ref[...], down, preferred_element_type=F32)
        keep_ref[:, at] = part[:half, :]
        send_ref[:, at] = part[half:, :].astype(BF16)
        return carry

    lax.fori_loop(0, steps, block, 0)


def grad_chunk(tenant, place, sg, back, weight, down, chunk, deps):
    depth, cols = weight.shape
    rows = sg.shape[0]
    nb = rows // BLOCK
    rank = down.shape[1]
    size = depth // CHUNKS
    shapes = (
        jax.ShapeDtypeStruct((rows // 2, size), F32),
        jax.ShapeDtypeStruct((rows // 2, size), BF16),
    )
    return pl.pallas_call(
        functools.partial(grad_body, nb, rank, chunk),
        out_shape=shapes,
        grid_spec=pltpu.PrefetchScalarGridSpec(
            num_scalar_prefetch=2,
            grid=(1,),
            in_specs=[same_block(sg), same_block(back), IN_HBM, IN_HBM] + order_specs(deps),
            out_specs=[same_block(s) for s in shapes],
            scratch_shapes=[
                pltpu.VMEM((size, cols), BF16),
                pltpu.VMEM((nb * rank, size), BF16),
                pltpu.VMEM(sg.shape, BF16),
                pltpu.VMEM(back.shape, BF16),
                pltpu.SemaphoreType.DMA((STEPS // CHUNKS,)),
                pltpu.SemaphoreType.DMA((nb,)),
            ],
        ),
        compiler_params=PARAMS,
        cost_estimate=COST,
        name="grad_chunk",
    )(tenant, place, sg, back, weight, down, *deps)


def add_core_body(chunks, *refs):
    mine_ref, send_ref = refs[-2:]
    half = mine_ref.shape[0]
    for c in range(chunks):
        keep_ref, recv_ref = refs[2 * c : 2 * c + 2]
        size = keep_ref.shape[1]
        at = slice(c * size, (c + 1) * size)
        mine_ref[:, at] = keep_ref[:half, :] + recv_ref[:half, :].astype(F32)
        send_ref[:, at] = (keep_ref[half:, :] + recv_ref[half:, :].astype(F32)).astype(BF16)


def add_core(pairs, deps):
    rows, size = pairs[0][0].shape
    operands = [array for pair in pairs for array in pair]
    shape = (rows // 2, size * len(pairs))
    return pl.pallas_call(
        functools.partial(add_core_body, len(pairs)),
        out_shape=(jax.ShapeDtypeStruct(shape, F32), jax.ShapeDtypeStruct(shape, BF16)),
        in_specs=[pl.BlockSpec(memory_space=pltpu.VMEM)] * len(operands) + order_specs(deps),
        compiler_params=PARAMS,
        cost_estimate=COST,
        name="add_core",
    )(*operands, *deps)


def add_x_body(counts, nz, place_ref, *refs):
    outs, total_ref = refs[-nz - 1 : -1], refs[-1]
    piece = outs[0].shape[0]
    z = place_ref[0]
    n = 0
    for g, count in enumerate(counts):
        for c in range(count):
            keep_ref, recv_ref = refs[2 * n : 2 * n + 2]
            n += 1
            rows, size = keep_ref.shape
            first = pl.multiple_of(place_ref[3 + g] * piece, piece)
            total = keep_ref[...] + recv_ref[...].astype(F32)
            total_ref[pl.ds(first, rows), c * size : (c + 1) * size] = total
    for k in range(nz):
        at = pl.multiple_of(lax.rem(z + k, nz) * piece, piece)
        outs[k][...] = total_ref[pl.ds(at, piece), :].astype(outs[k].dtype)


def add_x(place, groups, nz, deps):
    piece = BLOCK // 4
    size = sum(pair[0].shape[1] for pair in groups[0])
    operands = [array for group in groups for pair in group for array in pair]
    shapes = tuple(jax.ShapeDtypeStruct((piece, size), BF16 if k else F32) for k in range(nz))
    return pl.pallas_call(
        functools.partial(add_x_body, [len(group) for group in groups], nz),
        out_shape=shapes,
        grid_spec=pltpu.PrefetchScalarGridSpec(
            num_scalar_prefetch=1,
            grid=(1,),
            in_specs=[same_block(a) for a in operands] + order_specs(deps),
            out_specs=[same_block(s) for s in shapes],
            scratch_shapes=[pltpu.VMEM((nz * piece, size), F32)],
        ),
        compiler_params=PARAMS,
        cost_estimate=COST,
        name="add_x",
    )(place, *operands, *deps)


def add_z_body(nz, *refs):
    out_ref = refs[-1]
    size = refs[0].shape[1]
    for chunk in range((len(refs) - 1) // nz):
        total = refs[chunk * nz][...]
        for k in range(1, nz):
            total = total + refs[chunk * nz + k][...].astype(F32)
        out_ref[:, chunk * size : (chunk + 1) * size] = total.astype(BF16)


def add_z(parts, nz):
    piece, size = parts[0].shape
    return pl.pallas_call(
        functools.partial(add_z_body, nz),
        out_shape=jax.ShapeDtypeStruct((piece, size * (len(parts) // nz)), BF16),
        in_specs=[pl.BlockSpec(memory_space=pltpu.VMEM)] * len(parts),
        compiler_params=PARAMS,
        cost_estimate=COST,
        name="add_z",
    )(*parts)


def forward_body(rank, nz, groups, tenant_ref, place_ref, *refs):
    cot_refs, refs = refs[:groups], refs[groups:]
    w_hbm, a_hbm, up_hbm = refs[:3]
    pieces = refs[3 : 2 * nz + 5]
    w_ref, a_ref, up_ref, x_ref, acc_ref, low_acc, w_sem, sem, x_sem = refs[-9:]
    tokens, cols = acc_ref.shape
    nblk = tokens // BLOCK
    outs = refs[-11 - (groups - 1) * (nblk // groups) : -9]
    part_refs, side_ref = outs[:-1], outs[-1]
    piece = BLOCK // 4
    db = w_ref.shape[0] // STEPS
    z, x, core, first = place_ref[0], place_ref[1], place_ref[2], place_ref[3]
    moves = []
    for n in range(4 * nz):
        k, fx, fc = n // 4, (n // 2) % 2, n % 2
        src = pieces[2 * nz + fx].at[pl.ds(k * piece, piece), :] if fc else pieces[2 * k + fx]
        b = lax.rem(z + (2 * nz - k) - first, nz)
        row = (b * 4 + (x ^ fx) * 2 + (core ^ fc)) * piece
        rows = pl.ds(pl.multiple_of(row, piece), piece)
        moves.append(pltpu.make_async_copy(src, x_ref.at[rows, :], x_sem.at[n]))
    moves += factor_copies(tenant_ref, first, a_hbm, a_ref, sem, 0)
    late = factor_copies(tenant_ref, first, up_hbm, up_ref, sem, nblk)
    for copy in moves:
        copy.start()
    for i in range(STEPS):
        weight_copy(w_hbm, w_ref, w_sem, i).start()
    for copy in late:
        copy.start()
    acc_ref[...] = jnp.zeros_like(acc_ref)
    low_acc[...] = jnp.zeros_like(low_acc)
    side_ref[...] = jnp.zeros_like(side_ref)
    for copy in moves:
        copy.wait()

    def block(i, carry):
        weight_copy(w_hbm, w_ref, w_sem, i).wait()
        at = pl.ds(pl.multiple_of(i * db, db), db)
        xs = x_ref[:, at]
        acc_ref[...] += jnp.dot(xs, w_ref[at, :], preferred_element_type=F32)
        low_acc[...] += lax.dot_general(a_ref[:, at], xs, LAST, preferred_element_type=F32)
        return carry

    lax.fori_loop(0, STEPS, block, 0)
    low = low_acc[...]
    owner = lax.broadcasted_iota(jnp.int32, low.shape, 0) // rank
    block_of = lax.broadcasted_iota(jnp.int32, low.shape, 1) // BLOCK
    low = jnp.where(owner == block_of, low, 0.0)
    side_ref[:rank, :tokens] = jnp.sum(low.reshape(nblk, rank, tokens), axis=0)
    hi = low.astype(BF16).astype(F32)
    lowcat = jnp.concatenate([hi, low - hi], axis=0).T.astype(BF16)
    for copy in late:
        copy.wait()
    up = up_ref[...]
    up = jnp.concatenate([up, up], axis=0)
    size = nblk // groups
    for i in range(nblk):
        rows = slice(i * BLOCK, (i + 1) * BLOCK)
        here = slice(i % size * BLOCK, (i % size + 1) * BLOCK)
        part = acc_ref[rows, :] + jnp.dot(lowcat[rows, :], up, preferred_element_type=F32)
        if i < size:
            part_refs[0][here, :] = part
        else:
            part_refs[1 + i - size][...] = part.astype(BF16)
        product = part * cot_refs[i // size][here, :].astype(F32)
        side_ref[rank + i : rank + i + 1, :cols] = jnp.sum(product, axis=0, keepdims=True)


def forward(tenant, place, weight, cots, down, up, pieces, nz, deps):
    depth, cols = weight.shape
    tokens = tenant.shape[0]
    nblk = tokens // BLOCK
    rank = down.shape[1]
    groups = len(cots)
    size = nblk // groups
    shapes = [jax.ShapeDtypeStruct((size * BLOCK, cols), F32)]
    shapes += [jax.ShapeDtypeStruct((BLOCK, cols), BF16)] * (nblk - size)
    shapes += [jax.ShapeDtypeStruct((rank + nblk, max(cols, tokens)), F32)]
    return pl.pallas_call(
        functools.partial(forward_body, rank, nz, groups),
        out_shape=shapes,
        grid_spec=pltpu.PrefetchScalarGridSpec(
            num_scalar_prefetch=2,
            grid=(1,),
            in_specs=[same_block(cot) for cot in cots]
            + [IN_HBM] * (3 + len(pieces))
            + order_specs(deps),
            out_specs=[same_block(s) for s in shapes],
            scratch_shapes=[
                pltpu.VMEM((depth, cols), BF16),
                pltpu.VMEM((nblk * rank, depth), BF16),
                pltpu.VMEM((nblk * rank, cols), BF16),
                pltpu.VMEM((tokens, depth), BF16),
                pltpu.VMEM((tokens, cols), F32),
                pltpu.VMEM((nblk * rank, tokens), F32),
                pltpu.SemaphoreType.DMA((STEPS,)),
                pltpu.SemaphoreType.DMA((2 * nblk,)),
                pltpu.SemaphoreType.DMA((4 * nz,)),
            ],
        ),
        compiler_params=PARAMS,
        cost_estimate=COST,
        name="forward",
    )(tenant, place, *cots, weight, down, up, *pieces, *deps)


def shards(inputs, weight, adapter_down_factors, adapter_up_factors, magnitude, cotangent, tenant):
    col_count, row_count = lax.axis_size("col"), lax.axis_size("row")
    nz = col_count // 4
    down, up = adapter_down_factors, adapter_up_factors
    tenant_number, rank, depth = down.shape
    cols = weight.shape[1]
    tokens = tenant.shape[0]
    nblk = tokens // BLOCK
    rows_row = tokens // row_count
    blocks_mine = rows_row // BLOCK
    col, row = lax.axis_index("col"), lax.axis_index("row")
    z, x, core = col >> 2, (col >> 1) & 1, col & 1

    def move(value, dz, fx, fc):
        perm = []
        for source in range(col_count):
            sz, sx, sc = source // 4, (source // 2) % 2, source % 2
            perm.append((source, ((sz + dz) % nz) * 4 + (sx ^ fx) * 2 + (sc ^ fc)))
        return lax.ppermute(value, "col", perm)

    def swap(value):
        return lax.ppermute(value, "row", [(0, 1), (1, 0)])

    def place(*firsts):
        return jnp.stack([z, x, core, *firsts]).astype(jnp.int32)

    pair = row_count == 2

    def once(value, other):
        return lax.optimization_barrier((value, other))[0]

    along_z = [inputs] + [move(inputs, k, 0, 0) for k in range(1, nz)]
    along_x = {0: move(once(inputs, along_z[-1]), 0, 1, 0), nz - 1: move(along_z[-1], 0, 1, 0)}

    def other_x(k, after):
        along_z[k] = once(along_z[k], after)
        along_x[k] = move(along_z[k], 0, 1, 0)

    def other_core(part):
        return move(jnp.concatenate(part, axis=0), 0, 0, 1)

    nsq = partial_norms(tenant, weight, down, up)
    if pair:
        nsq_a, nsq_b = nsq, swap(nsq)
        firsts = [row * blocks_mine, (1 - row) * blocks_mine]
        cots = [cotangent, swap(cotangent)]
    else:
        nsq_a, nsq_b = lax.psum(nsq, "row"), jnp.zeros_like(nsq)
        firsts = [0 * row]
        cots = [lax.all_gather(cotangent, "row", axis=0, tiled=True)]
    places = [place(first) for first in firsts]

    def scaled(g, deps):
        return scaled_gradient(tenant, places[g], cots[g], nsq_a, nsq_b, magnitude, up, deps)

    def grad(g, part, chunk, deps):
        return grad_chunk(tenant, places[g], part[1], part[2], weight, down, chunk, deps)

    def cross_core(made, deps):
        return add_core([(keep, move(send, 0, 0, 1)) for keep, send in made], deps)

    def cross_x(groups, deps):
        mine, *away = add_x(place(*firsts), groups, nz, deps)
        return [mine] + [move(a, k + 1, 0, 0) for k, a in enumerate(away)]

    def across_x(made):
        return made[0], move(made[1], 0, 1, 0)

    if pair:
        ours = scaled(0, [])
        made = [grad(0, ours, 0, along_z[-1:])]
        for k in range(1, nz - 2):
            other_x(k, made[0][0])
        made += [grad(0, ours, 1, [made[0][0], cots[1]])]
        other_x(nz - 2, made[1][0])
        theirs = scaled(1, [made[1][0]])
        near = [across_x(cross_core(made[:1], [theirs[0]]))]
        mine, away = cross_core(made[1:], [near[0][0]])
        near += [across_x((mine, once(away, near[0][1])))]
        far = [grad(1, theirs, 0, [mine, along_x[0], along_x[nz - 1]])]
        core_z = other_core(along_z)
        far += [grad(1, theirs, 1, [far[0][0], core_z] + [along_x[k] for k in range(1, nz - 2)])]
        along_x = [along_x[k] for k in range(nz)]
        along_x[nz - 2] = once(along_x[nz - 2], far[0][0])
        core_x = other_core(along_x)
        far = cross_core(far, along_x)
        pieces = [piece for both in zip(along_z, along_x) for piece in both] + [core_z, core_x]
        part, *away, side = forward(
            tenant, places[0], weight, cots, down, up, pieces, nz, [far[0], near[1][1]]
        )
        arrived = [swap(away[0])]
        finals = cross_x([near, [across_x(far)]], [side])
        for block in away[1:]:
            arrived.append(swap(once(block, (arrived[-1], finals[0]))))
        new = swap(once(side, (arrived[0], finals[-1])))
        low = side[:rank, :tokens] + jnp.roll(new[:rank, :tokens], rows_row, axis=1)
        dots = side[rank:, :cols] + jnp.roll(new[rank:, :cols], blocks_mine, axis=0)
        parts = [ours, theirs]
    else:
        ours = scaled(0, [])
        near = [across_x(cross_core([grad(0, ours, c, [])], [])) for c in range(CHUNKS)]
        for k in range(1, nz - 1):
            other_x(k, inputs)
        along_x = [along_x[k] for k in range(nz)]
        pieces = [piece for both in zip(along_z, along_x) for piece in both]
        pieces += [other_core(along_z), other_core(along_x)]
        part, side = forward(tenant, places[0], weight, cots, down, up, pieces, nz, [])
        finals = cross_x([near], [])
        low, dots = lax.psum((side[:rank, :tokens], side[rank:, :cols]), "row")
        parts = [ours]

    scales = jnp.concatenate([group[0] for group in parts], axis=0)

    tenants = jnp.arange(tenant_number, dtype=jnp.int32)
    block_tenant = tenant.reshape(nblk, BLOCK)[:, 0]
    size = nblk // len(parts)
    owners = jnp.concatenate(
        [lax.dynamic_slice_in_dim(block_tenant, first, size, 0) for first in firsts]
    )
    low = low.astype(BF16)
    grad_b = 0.0
    for g, group in enumerate(parts):
        owner = jnp.repeat(owners[g * size : (g + 1) * size], BLOCK)
        mine = low[:, g * size * BLOCK : (g + 1) * size * BLOCK]
        wide = jnp.where((tenants[:, None] == owner[None, :])[:, None, :], mine[None], 0)
        wide = wide.reshape(tenant_number * rank, size * BLOCK)
        grad_b = grad_b + jnp.dot(wide, group[1], preferred_element_type=F32)
    grad_b = grad_b.reshape(tenant_number, rank, cols)
    hit = (tenants[:, None] == owners[None, :])[:, :, None]
    terms = jnp.where(hit, (dots * scales)[None], 0.0)
    grad_m = 0.0
    for g in range(len(parts)):
        group = terms[:, g * size : (g + 1) * size]
        grad_m = grad_m + functools.reduce(jnp.add, [group[:, i] for i in range(size)])
    grad_inputs = add_z([once(finals[0], grad_b)] + finals[1:], nz)
    if pair:
        pre = part + jnp.concatenate(arrived, axis=0).astype(F32)
        scale_mine = parts[0][0]
    else:
        pre = lax.psum_scatter(part, "row", scatter_dimension=0, tiled=True)
        scale_mine = lax.dynamic_slice_in_dim(scales, row * blocks_mine, blocks_mine, 0)
    output = (pre.reshape(blocks_mine, BLOCK, cols) * scale_mine[:, None, :]).astype(BF16)
    output = output.reshape(rows_row, cols)
    return (output, grad_inputs, grad_b, grad_m / magnitude)


def solution(mesh):
    return jax.shard_map(
        shards,
        mesh=mesh,
        in_specs=(
            P("col", "row"),
            P("row", "col"),
            P(None, None, "row"),
            P(None, None, "col"),
            P(None, "col"),
            P("row", "col"),
            P(),
        ),
        out_specs=(P("row", "col"), P("col", "row"), P(None, None, "col"), P(None, "col")),
        check_vma=False,
    )
```

time: 178 us -> 166 us (0.933)
  the two profiles are of different devices: /device:TPU:8 before, /device:TPU:0 now
where the time goes in v3:
time: 166 us; the launch traced here: 165 us
  Pallas kernels  77.8 us (47%)
  waiting for transfers between devices  39.7 us (24%)
  starting transfers between devices  31.1 us (19%)
  local copies, waits for them, and re-layouts  9.07 us (5%)
  other arithmetic  4.51 us (3%)
  matrix products  2.07 us (1%)
    ppermute x19, waiting for transfers between devices, move(): return lax.ppermute(value, 'col', perm)  32.8 us
    pallas_call x4, Pallas kernels, grad_chunk(): pl.pallas_call(functools.partial(grad_body, nb, rank, chunk), out_shape=s...  30.7 us
    ppermute x19, starting transfers between devices, move(): return lax.ppermute(value, 'col', perm)  23.6 us
    pallas_call x1, Pallas kernels, forward(): pl.pallas_call(functools.partial(forward_body, rank, nz, groups), out_sha...  20.8 us
    pallas_call x1, Pallas kernels, partial_norms(): pl.pallas_call(functools.partial(norm_body, nblk, rank), out_shape=shape,...  10.1 us
    unnamed x44, local copies, waits for them, and re-layouts  8.75 us
    ppermute x5, starting transfers between devices, swap(): return lax.ppermute(value, 'row', [(0, 1), (1, 0)])  7.4 us
    ppermute x5, waiting for transfers between devices, swap(): return lax.ppermute(value, 'row', [(0, 1), (1, 0)])  6.89 us
  transfers between devices with their start and end apart: 24, of which 10 were waited for; matrix products, arithmetic and copies ran while one was open for 3% of the time, Pallas kernels for 47%

profile of v3, /device:TPU:0, one launch (start us, length us, event | category | flops | bytes accessed | tf_op | source)
XLA Modules:
  0.0 165.1 jit_solution(3009976325679270064)
XLA Ops:
  0.6 3.0 %collective-permute-start = (bf16[256,1792]{1,0:T(8,128)(2,1)}, bf16[256,1792]{1,0:T(8,128)(2,1)S(1)}, u32[]{:S(2)}, u32[]{:S(2)}) collective-permute-start(bf16[256,1792]{1,0:T(8,128)(2,1)} %refs_0_.1), channel_id=1, source_target_pairs={{0,1},{1,0},{2,3},{3,2},{4,5},{5,4},{6,7},{7,6},{8,9},{9,8},{10,11... | collective-permute-start | bytes 2752520 | tf_op jit(solution)/shard_map/ppermute | solution.py:461
  3.7 3.6 %collective-permute-start.1 = (bf16[32,4096]{1,0:T(8,128)(2,1)}, bf16[32,4096]{1,0:T(8,128)(2,1)S(1)}, u32[]{:S(2)}, u32[]{:S(2)}) collective-permute-start(bf16[32,4096]{1,0:T(8,128)(2,1)} %refs_5_.1), channel_id=1, source_target_pairs={{0,24},{2,26},{4,28},{6,30},{8,0},{10,2},{12,4},{14,6},{16,8},{18,... | collective-permute-start | bytes 786440 | tf_op jit(solution)/shard_map/ppermute | solution.py:458
  7.3 1.0 collective-permute-start.3
  8.3 1.2 copy-done
  9.5 0.7 copy-done.12
  10.1 10.1 %partial_norms.1.nsq_a = f32[4,1792]{1,0:T(4,128)S(1)} custom-call(s32[512]{0:T(512)S(1)} %copy-done.12, bf16[4096,1792]{1,0:T(8,128)(2,1)} %refs_2_.1, bf16[16,16,4096]{2,1,0:T(8,128)(2,1)} %refs_3_.1, bf16[16,16,1792]{2,1,0:T(8,128)(2,1)S(1)} %copy-done), custom_call_target="tpu_custom_call" | custom-call | flops 1000 | bytes 1000 | tf_op jit(solution)/shard_map/partial_norms/pallas_call | solution.py:102
  21.0 3.8 %collective-permute-done.4.nsq_b = f32[4,1792]{1,0:T(4,128)S(1)} collective-permute-done((f32[4,1792]{1,0:T(4,128)S(1)}, f32[4,1792]{1,0:T(4,128)S(1)}, u32[]{:S(2)}, u32[]{:S(2)}) %collective-permute-start.4) | collective-permute-done | bytes 28704 | tf_op jit(solution)/shard_map/ppermute | solution.py:461
  24.8 3.1 %scaled_gradient.2 = (f32[2,1792]{1,0:T(2,128)S(1)}, bf16[256,1792]{1,0:T(8,128)(2,1)S(1)}, bf16[256,64]{1,0:T(8,128)(2,1)S(1)}) custom-call(s32[512]{0:T(512)S(1)} %copy-done.13, s32[4]{0:T(128)S(1)} %pad_add_fusion.place_ref, bf16[256,1792]{1,0:T(8,128)(2,1)} %refs_0_.1, f32[4,1792]{1,0:T(4,128)S(1)} %partial_norms.1.nsq_a, ...), custom_call_target="tpu_custom_call" | custom-call | flops 1000 | bytes 1000 | tf_op jit(solution)/shard_map/scaled_gradient/pallas_call | solution.py:156
  27.9 7.4 %grad_chunk.4 = (f32[128,2048]{1,0:T(8,128)}, bf16[128,2048]{1,0:T(8,128)(2,1)S(1)}) custom-call(s32[512]{0:T(512)S(1)} %copy-done.13, s32[4]{0:T(128)S(1)} %pad_add_fusion.place_ref, bf16[256,1792]{1,0:T(8,128)(2,1)S(1)} %get-tuple-element.41.sg_ref, bf16[256,64]{1,0:T(8,128)(2,1)S(1)} %get-tuple-element.42.back_ref, bf16[4096,1792]{1,0:T(8,128)(2,1)} %refs_2_.1, ...), custom_call_target="tpu_custom_call" | custom-call | flops 1000 | bytes 1000 | tf_op jit(solution)/shard_map/grad_chunk/pallas_call | solution.py:226
  35.5 0.9 copy-done.16
  36.4 7.4 %grad_chunk.5 = (f32[128,2048]{1,0:T(8,128)}, bf16[128,2048]{1,0:T(8,128)(2,1)S(1)}) custom-call(s32[512]{0:T(512)S(1)} %copy-done.13, s32[4]{0:T(128)S(1)} %pad_add_fusion.place_ref, bf16[256,1792]{1,0:T(8,128)(2,1)S(1)} %get-tuple-element.41.sg_ref, bf16[256,64]{1,0:T(8,128)(2,1)S(1)} %get-tuple-element.42.back_ref, bf16[4096,1792]{1,0:T(8,128)(2,1)} %refs_2_.1, ...), custom_call_target="tpu_custom_call" | custom-call | flops 1000 | bytes 1000 | tf_op jit(solution)/shard_map/grad_chunk/pallas_call | solution.py:226
  44.3 1.1 pad_maximum_fusion
  45.5 1.8 %collective-permute-start.2 = (bf16[32,4096]{1,0:T(8,128)(2,1)S(1)}, bf16[32,4096]{1,0:T(8,128)(2,1)S(1)}, u32[]{:S(2)}, u32[]{:S(2)}) collective-permute-start(bf16[32,4096]{1,0:T(8,128)(2,1)S(1)} %copy-done.6), channel_id=1, source_target_pairs={{0,4},{2,6},{4,0},{6,2},{8,12},{10,14},{12,8},{14,10},{16,20},{18,... | collective-permute-start | bytes 786440 | tf_op jit(solution)/shard_map/ppermute | solution.py:458
  47.6 1.7 %collective-permute-start.7 = (bf16[32,4096]{1,0:T(8,128)(2,1)}, bf16[32,4096]{1,0:T(8,128)(2,1)S(1)}, u32[]{:S(2)}, u32[]{:S(2)}) collective-permute-start(bf16[32,4096]{1,0:T(8,128)(2,1)} %collective-permute-done.6.refs_9_), channel_id=1, source_target_pairs={{0,4},{2,6},{4,0},{6,2},{8,12},{10,14},{12,8},{14,10},{16,20},{18,... | collective-permute-start | bytes 786440 | tf_op jit(solution)/shard_map/ppermute | solution.py:458
  49.6 3.1 %scaled_gradient.3 = (f32[2,1792]{1,0:T(2,128)S(1)}, bf16[256,1792]{1,0:T(8,128)(2,1)S(1)}, bf16[256,64]{1,0:T(8,128)(2,1)S(1)}) custom-call(s32[512]{0:T(512)S(1)} %copy-done.13, s32[4]{0:T(128)S(1)} %get-tuple-element.78.place_ref, bf16[256,1792]{1,0:T(8,128)(2,1)} %copy-done.16, f32[4,1792]{1,0:T(4,128)S(1)} %partial_norms.1.nsq_a, ...), custom_call_target="tpu_custom_call" | custom-call | flops 1000 | bytes 1000 | tf_op jit(solution)/shard_map/scaled_gradient/pallas_call | solution.py:156
  52.7 0.9 copy-done.1
  53.6 1.3 add_core.3
  54.9 2.2 %add_core.4 = (f32[64,2048]{1,0:T(8,128)S(1)}, bf16[64,2048]{1,0:T(8,128)(2,1)}) custom-call(f32[128,2048]{1,0:T(8,128)} %get-tuple-element.45.refs_0_, bf16[128,2048]{1,0:T(8,128)(2,1)S(1)} %collective-permute-done.8.refs_1_, f32[64,2048]{1,0:T(8,128)S(1)} %get-tuple-element.52.refs_2_.refs_0_), custom_call_target="tpu_custom_call" | custom-call | flops 1000 | bytes 1000 | tf_op jit(solution)/shard_map/add_core/pallas_call | solution.py:264
  57.1 3.2 %collective-permute-done.10.refs_2_.refs_7_.refs_12_ = bf16[32,4096]{1,0:T(8,128)(2,1)S(1)} collective-permute-done((bf16[32,4096]{1,0:T(8,128)(2,1)S(1)}, bf16[32,4096]{1,0:T(8,128)(2,1)S(1)}, u32[]{:S(2)}, u32[]{:S(2)}) %collective-permute-start.10) | collective-permute-done | bytes 262176 | tf_op jit(solution)/shard_map/ppermute | solution.py:458
  60.3 8.6 %grad_chunk.6 = (f32[128,2048]{1,0:T(8,128)}, bf16[128,2048]{1,0:T(8,128)(2,1)S(1)}) custom-call(s32[512]{0:T(512)S(1)} %copy-done.13, s32[4]{0:T(128)S(1)} %get-tuple-element.78.place_ref, bf16[256,1792]{1,0:T(8,128)(2,1)} %copy-done.1, bf16[256,64]{1,0:T(8,128)(2,1)S(1)} %get-tuple-element.48.back_ref, bf16[4096,1792]{1,0:T(8,128)(2,1)} %refs_2_.1, ...), custom_call_target="tpu_custom_call" | custom-call | flops 1000 | bytes 1000 | tf_op jit(solution)/shard_map/grad_chunk/pallas_call | solution.py:226
  68.9 0.8 copy-done.4
  69.7 1.4 collective-permute-done.5.refs_2_.refs_5_.refs_8_
  71.1 1.1 pad_maximum_fusion.1
  72.7 1.0 copy-done.17
  73.6 7.3 %grad_chunk.7 = (f32[128,2048]{1,0:T(8,128)}, bf16[128,2048]{1,0:T(8,128)(2,1)S(1)}) custom-call(s32[512]{0:T(512)S(1)} %copy-done.13, s32[4]{0:T(128)S(1)} %get-tuple-element.78.place_ref, bf16[256,1792]{1,0:T(8,128)(2,1)S(1)} %copy-done.2, bf16[256,64]{1,0:T(8,128)(2,1)S(1)} %get-tuple-element.48.back_ref, bf16[4096,1792]{1,0:T(8,128)(2,1)} %refs_2_.1, ...), custom_call_target="tpu_custom_call" | custom-call | flops 1000 | bytes 1000 | tf_op jit(solution)/shard_map/grad_chunk/pallas_call | solution.py:226
  81.1 1.8 %collective-permute-start.15 = (bf16[64,2048]{1,0:T(8,128)(2,1)S(1)}, bf16[64,2048]{1,0:T(8,128)(2,1)S(1)}, u32[]{:S(2)}, u32[]{:S(2)}) collective-permute-start(bf16[64,2048]{1,0:T(8,128)(2,1)S(1)} %get-tuple-element.61), channel_id=1, source_target_pairs={{0,4},{2,6},{4,0},{6,2},{8,12},{10,14},{12,8},{14,10},{16,20},{18,... | collective-permute-start | bytes 786440 | tf_op jit(solution)/shard_map/ppermute | solution.py:458
  83.8 3.2 %add_core.5 = (f32[64,4096]{1,0:T(8,128)}, bf16[64,4096]{1,0:T(8,128)(2,1)}) custom-call(f32[128,2048]{1,0:T(8,128)} %get-tuple-element.54.refs_0_, bf16[128,2048]{1,0:T(8,128)(2,1)} %copy-done.19, f32[128,2048]{1,0:T(8,128)} %get-tuple-element.57.refs_2_, bf16[128,2048]{1,0:T(8,128)(2,1)} %copy-done.20, ...), custom_call_target="tpu_custom_call" | custom-call | flops 1000 | bytes 1000 | tf_op jit(solution)/shard_map/add_core/pallas_call | solution.py:264
  87.0 1.7 %collective-permute-start.18 = (bf16[64,4096]{1,0:T(8,128)(2,1)}, bf16[64,4096]{1,0:T(8,128)(2,1)}, u32[]{:S(2)}, u32[]{:S(2)}) collective-permute-start(bf16[64,4096]{1,0:T(8,128)(2,1)} %get-tuple-element.66), channel_id=1, source_target_pairs={{0,4},{2,6},{4,0},{6,2},{8,12},{10,14},{12,8},{14,10},{16,20},{18,... | collective-permute-start | bytes 1572872 | tf_op jit(solution)/shard_map/ppermute | solution.py:458
  88.7 1.1 collective-permute-done.15.refs_1_
  89.8 0.7 copy-done.10
  90.5 1.7 %collective-permute-start.16 = (bf16[64,2048]{1,0:T(8,128)(2,1)}, bf16[64,2048]{1,0:T(8,128)(2,1)S(1)}, u32[]{:S(2)}, u32[]{:S(2)}) collective-permute-start(bf16[64,2048]{1,0:T(8,128)(2,1)} %get-tuple-element.62), channel_id=1, source_target_pairs={{0,4},{2,6},{4,0},{6,2},{8,12},{10,14},{12,8},{14,10},{16,20},{18,... | collective-permute-start | bytes 786440 | tf_op jit(solution)/shard_map/ppermute | solution.py:458
  92.5 14.3 %collective-permute-done.16.refs_16_.refs_3_ = bf16[64,2048]{1,0:T(8,128)(2,1)S(1)} collective-permute-done((bf16[64,2048]{1,0:T(8,128)(2,1)}, bf16[64,2048]{1,0:T(8,128)(2,1)S(1)}, u32[]{:S(2)}, u32[]{:S(2)}) %collective-permute-start.16) | collective-permute-done | bytes 262176 | tf_op jit(solution)/shard_map/ppermute | solution.py:458
  106.9 0.7 copy-done.7
  107.6 20.8 %forward.1 = (f32[256,1792]{1,0:T(8,128)}, bf16[128,1792]{1,0:T(8,128)(2,1)}, bf16[128,1792]{1,0:T(8,128)(2,1)}, f32[20,1792]{1,0:T(8,128)S(1)}) custom-call(s32[512]{0:T(512)S(1)} %copy-done.13, s32[4]{0:T(128)S(1)} %pad_add_fusion.place_ref, bf16[256,1792]{1,0:T(8,128)(2,1)} %refs_0_.1, bf16[256,1792]{1,0:T(8,128)(2,1)} %copy-done.16, ...), custom_call_target="tpu_custom_call" | custom-call | flops 1000 | bytes 1000 | tf_op jit(solution)/shard_map/forward/pallas_call | solution.py:412
  128.4 1.7 %collective-permute-start.17 = (bf16[128,1792]{1,0:T(8,128)(2,1)}, bf16[128,1792]{1,0:T(8,128)(2,1)S(1)}, u32[]{:S(2)}, u32[]{:S(2)}) collective-permute-start(bf16[128,1792]{1,0:T(8,128)(2,1)} %get-tuple-element.64), channel_id=1, source_target_pairs={{0,1},{1,0},{2,3},{3,2},{4,5},{5,4},{6,7},{7,6},{8,9},{9,8},{10,11... | collective-permute-start | bytes 1376264 | tf_op jit(solution)/shard_map/ppermute | solution.py:461
  130.1 0.9 copy-done.8
  131.1 2.6 %add_x.1 = (f32[32,4096]{1,0:T(8,128)S(1)}, bf16[32,4096]{1,0:T(8,128)(2,1)S(1)}, bf16[32,4096]{1,0:T(8,128)(2,1)S(1)}, bf16[32,4096]{1,0:T(8,128)(2,1)S(1)}) custom-call(s32[5]{0:T(128)S(1)} %stack.39.place_ref, f32[64,2048]{1,0:T(8,128)} %copy-done.5, bf16[64,2048]{1,0:T(8,128)(2,1)S(1)} %copy-done.11, f32[64,2048]{1,0:T(8,128)} %copy-done.4, ...), custom_call_target="tpu_custom_call" | custom-call | flops 1000 | bytes 1000 | tf_op jit(solution)/shard_map/add_x/pallas_call | solution.py:297
  133.6 3.7 %collective-permute-start.20 = (bf16[32,4096]{1,0:T(8,128)(2,1)S(1)}, bf16[32,4096]{1,0:T(8,128)(2,1)S(1)}, u32[]{:S(2)}, u32[]{:S(2)}) collective-permute-start(bf16[32,4096]{1,0:T(8,128)(2,1)S(1)} %get-tuple-element.71), channel_id=1, source_target_pairs={{0,24},{2,26},{4,28},{6,30},{8,0},{10,2},{12,4},{14,6},{16,8},{18,... | collective-permute-start | bytes 786440 | tf_op jit(solution)/shard_map/ppermute | solution.py:458
  137.4 3.0 %collective-permute-done.17 = bf16[128,1792]{1,0:T(8,128)(2,1)S(1)} collective-permute-done((bf16[128,1792]{1,0:T(8,128)(2,1)}, bf16[128,1792]{1,0:T(8,128)(2,1)S(1)}, u32[]{:S(2)}, u32[]{:S(2)}) %collective-permute-start.17) | collective-permute-done | bytes 458784 | tf_op jit(solution)/shard_map/ppermute | solution.py:461
  140.4 1.6 collective-permute-done.20.refs_3_
  142.7 1.0 collective-permute-start.22
  143.7 3.8 %collective-permute-start.23 = (bf16[32,4096]{1,0:T(8,128)(2,1)S(1)}, bf16[32,4096]{1,0:T(8,128)(2,1)S(1)}, u32[]{:S(2)}, u32[]{:S(2)}) collective-permute-start(bf16[32,4096]{1,0:T(8,128)(2,1)S(1)} %get-tuple-element.75), channel_id=1, source_target_pairs={{0,16},{2,18},{4,20},{6,22},{8,24},{10,26},{12,28},{14,30},{16,0},... | collective-permute-start | bytes 786440 | tf_op jit(solution)/shard_map/ppermute | solution.py:458
  147.5 1.6 collective-permute-start.19
  149.7 1.7 %convolution_add_fusion = f32[256,1792]{1,0:T(8,128)} fusion(f32[256,1792]{1,0:T(8,128)S(1)} %fusion.9, bf16[256,256]{1,0:T(8,128)(2,1)S(1)} %bitcast.28, bf16[256,1792]{1,0:T(8,128)(2,1)S(1)} %get-tuple-element.41.sg_ref), kind=kOutput, calls=%fused_computation | convolution fusion | flops 235339776 | bytes 4718592 | tf_op jit(solution)/shard_map/dot_general | solution.py:566
  151.4 2.7 %collective-permute-done.22.refs_1_ = bf16[32,4096]{1,0:T(8,128)(2,1)S(1)} collective-permute-done((bf16[32,4096]{1,0:T(8,128)(2,1)S(1)}, bf16[32,4096]{1,0:T(8,128)(2,1)S(1)}, u32[]{:S(2)}, u32[]{:S(2)}) %collective-permute-start.22) | collective-permute-done | bytes 262176 | tf_op jit(solution)/shard_map/ppermute | solution.py:458
  154.1 8.3 %collective-permute-done.23.refs_2_ = bf16[32,4096]{1,0:T(8,128)(2,1)S(1)} collective-permute-done((bf16[32,4096]{1,0:T(8,128)(2,1)S(1)}, bf16[32,4096]{1,0:T(8,128)(2,1)S(1)}, u32[]{:S(2)}, u32[]{:S(2)}) %collective-permute-start.23) | collective-permute-done | bytes 262176 | tf_op jit(solution)/shard_map/ppermute | solution.py:458
  162.5 0.8 add_z.1
  164.0 1.1 fusion
  (80 shorter events, 6.1 us)
Async XLA Ops:
  0.6 34.8 %collective-permute-start = (bf16[256,1792]{1,0:T(8,128)(2,1)}, bf16[256,1792]{1,0:T(8,128)(2,1)S(1)}, u32[]{:S(2)}, u32[]{:S(2)}) collective-permute-start(bf16[256,1792]{1,0:T(8,128)(2,1)} %refs_0_.1), channel_id=1, source_target_pairs={{0,1},{1,0},{2,3},{3,2},{4,5},{5,4},{6,7},{7,6},{8,9},{9,8},{10,11... | collective-permute-start | bytes 2752520 | tf_op jit(solution)/shard_map/ppermute | solution.py:461
  3.7 24.3 %collective-permute-start.1 = (bf16[32,4096]{1,0:T(8,128)(2,1)}, bf16[32,4096]{1,0:T(8,128)(2,1)S(1)}, u32[]{:S(2)}, u32[]{:S(2)}) collective-permute-start(bf16[32,4096]{1,0:T(8,128)(2,1)} %refs_5_.1), channel_id=1, source_target_pairs={{0,24},{2,26},{4,28},{6,30},{8,0},{10,2},{12,4},{14,6},{16,8},{18,... | collective-permute-start | bytes 786440 | tf_op jit(solution)/shard_map/ppermute | solution.py:458
  7.3 36.5 %collective-permute-start.6 = (bf16[32,4096]{1,0:T(8,128)(2,1)}, bf16[32,4096]{1,0:T(8,128)(2,1)}, u32[]{:S(2)}, u32[]{:S(2)}) collective-permute-start(bf16[32,4096]{1,0:T(8,128)(2,1)} %refs_5_.1), channel_id=1, source_target_pairs={{0,16},{2,18},{4,20},{6,22},{8,24},{10,26},{12,28},{14,30},{16,0},... | collective-permute-start | bytes 786440 | tf_op jit(solution)/shard_map/ppermute | solution.py:458
  7.3 28.1 %collective-permute-start.3 = (bf16[32,4096]{1,0:T(8,128)(2,1)}, bf16[32,4096]{1,0:T(8,128)(2,1)}, u32[]{:S(2)}, u32[]{:S(2)}) collective-permute-start(bf16[32,4096]{1,0:T(8,128)(2,1)} %refs_5_.1), channel_id=1, source_target_pairs={{0,8},{2,10},{4,12},{6,14},{8,16},{10,18},{12,20},{14,22},{16,24},... | collective-permute-start | bytes 786440 | tf_op jit(solution)/shard_map/ppermute | solution.py:458
  8.3 1.2 copy-start
  9.5 0.7 copy-start.12
  10.1 14.7 %copy-start.9 = (f32[16,1792]{1,0:T(8,128)S(1)}, f32[16,1792]{1,0:T(8,128)}, u32[]{:S(2)}) copy-start(f32[16,1792]{1,0:T(8,128)} %mag_ref.3) | copy-start | bytes 344068
  10.1 14.7 %copy-start.13 = (s32[512]{0:T(512)S(1)}, s32[512]{0:T(512)}, u32[]{:S(2)}) copy-start(s32[512]{0:T(512)} %tenant_ref.15) | copy-start | bytes 6148
  20.3 4.6 %collective-permute-start.4 = (f32[4,1792]{1,0:T(4,128)S(1)}, f32[4,1792]{1,0:T(4,128)S(1)}, u32[]{:S(2)}, u32[]{:S(2)}) collective-permute-start(f32[4,1792]{1,0:T(4,128)S(1)} %partial_norms.1.nsq_a), channel_id=1, source_target_pairs={{0,1},{1,0},{2,3},{3,2},{4,5},{5,4},{6,7},{7,6},{8,9},{9,8},{10,11... | collective-permute-start | bytes 86024 | tf_op jit(solution)/shard_map/ppermute | solution.py:461
  27.9 7.4 %copy-start.14 = (f32[2,1792]{1,0:T(2,128)}, f32[2,1792]{1,0:T(2,128)S(1)}, u32[]{:S(2)}) copy-start(f32[2,1792]{1,0:T(2,128)S(1)} %get-tuple-element.70) | copy-start | bytes 43012
  35.4 9.0 %copy-start.6 = (bf16[32,4096]{1,0:T(8,128)(2,1)S(1)}, bf16[32,4096]{1,0:T(8,128)(2,1)}, u32[]{:S(2)}) copy-start(bf16[32,4096]{1,0:T(8,128)(2,1)} %refs_5_.1) | copy-start | bytes 786436
  35.4 12.2 %collective-permute-start.9 = (bf16[128,2048]{1,0:T(8,128)(2,1)S(1)}, bf16[128,2048]{1,0:T(8,128)(2,1)S(1)}, u32[]{:S(2)}, u32[]{:S(2)}) collective-permute-start(bf16[128,2048]{1,0:T(8,128)(2,1)S(1)} %get-tuple-element.50), channel_id=1, source_target_pairs={{0,2},{2,0},{4,6},{6,4},{8,10},{10,8},{12,14},{14,12},{16,18},{18,... | collective-permute-start | bytes 1572872 | tf_op jit(solution)/shard_map/ppermute | solution.py:458
  35.5 0.9 copy-start.16
  43.8 5.5 %collective-permute-start.8 = (bf16[128,2048]{1,0:T(8,128)(2,1)S(1)}, bf16[128,2048]{1,0:T(8,128)(2,1)S(1)}, u32[]{:S(2)}, u32[]{:S(2)}) collective-permute-start(bf16[128,2048]{1,0:T(8,128)(2,1)S(1)} %get-tuple-element.49), channel_id=1, source_target_pairs={{0,2},{2,0},{4,6},{6,4},{8,10},{10,8},{12,14},{14,12},{16,18},{18,... | collective-permute-start | bytes 1572872 | tf_op jit(solution)/shard_map/ppermute | solution.py:458
  45.4 27.3 %collective-permute-start.11 = (bf16[128,4096]{1,0:T(8,128)(2,1)S(1)}, bf16[128,4096]{1,0:T(8,128)(2,1)S(1)}, u32[]{:S(2)}, u32[]{:S(2)}) collective-permute-start(bf16[128,4096]{1,0:T(8,128)(2,1)S(1)} %pad_maximum_fusion), channel_id=1, source_target_pairs={{0,2},{2,0},{4,6},{6,4},{8,10},{10,8},{12,14},{14,12},{16,18},{18,... | collective-permute-start | bytes 3145736 | tf_op jit(solution)/shard_map/ppermute | solution.py:458
  45.5 11.6 %collective-permute-start.2 = (bf16[32,4096]{1,0:T(8,128)(2,1)S(1)}, bf16[32,4096]{1,0:T(8,128)(2,1)S(1)}, u32[]{:S(2)}, u32[]{:S(2)}) collective-permute-start(bf16[32,4096]{1,0:T(8,128)(2,1)S(1)} %copy-done.6), channel_id=1, source_target_pairs={{0,4},{2,6},{4,0},{6,2},{8,12},{10,14},{12,8},{14,10},{16,20},{18,... | collective-permute-start | bytes 786440 | tf_op jit(solution)/shard_map/ppermute | solution.py:458
  47.3 13.0 %collective-permute-start.10 = (bf16[32,4096]{1,0:T(8,128)(2,1)S(1)}, bf16[32,4096]{1,0:T(8,128)(2,1)S(1)}, u32[]{:S(2)}, u32[]{:S(2)}) collective-permute-start(bf16[32,4096]{1,0:T(8,128)(2,1)S(1)} %collective-permute-done.1.refs_0_.refs_11_), channel_id=1, source_target_pairs={{0,4},{2,6},{4,0},{6,2},{8,12},{10,14},{12,8},{14,10},{16,20},{18,... | collective-permute-start | bytes 786440 | tf_op jit(solution)/shard_map/ppermute | solution.py:458
  47.6 22.1 %collective-permute-start.7 = (bf16[32,4096]{1,0:T(8,128)(2,1)}, bf16[32,4096]{1,0:T(8,128)(2,1)S(1)}, u32[]{:S(2)}, u32[]{:S(2)}) collective-permute-start(bf16[32,4096]{1,0:T(8,128)(2,1)} %collective-permute-done.6.refs_9_), channel_id=1, source_target_pairs={{0,4},{2,6},{4,0},{6,2},{8,12},{10,14},{12,8},{14,10},{16,20},{18,... | collective-permute-start | bytes 786440 | tf_op jit(solution)/shard_map/ppermute | solution.py:458
  49.3 21.8 %collective-permute-start.5 = (bf16[32,4096]{1,0:T(8,128)(2,1)}, bf16[32,4096]{1,0:T(8,128)(2,1)S(1)}, u32[]{:S(2)}, u32[]{:S(2)}) collective-permute-start(bf16[32,4096]{1,0:T(8,128)(2,1)} %collective-permute-done.3.refs_7_), channel_id=1, source_target_pairs={{0,4},{2,6},{4,0},{6,2},{8,12},{10,14},{12,8},{14,10},{16,20},{18,... | collective-permute-start | bytes 786440 | tf_op jit(solution)/shard_map/ppermute | solution.py:458
  52.7 0.9 copy-start.1
  54.9 13.9 %copy-start.5 = (f32[64,2048]{1,0:T(8,128)}, f32[64,2048]{1,0:T(8,128)S(1)}, u32[]{:S(2)}) copy-start(f32[64,2048]{1,0:T(8,128)S(1)} %get-tuple-element.52.refs_2_.refs_0_) | copy-start | bytes 1572868
  60.3 22.7 %copy-start.3 = (bf16[32,4096]{1,0:T(8,128)(2,1)}, bf16[32,4096]{1,0:T(8,128)(2,1)S(1)}, u32[]{:S(2)}) copy-start(bf16[32,4096]{1,0:T(8,128)(2,1)S(1)} %collective-permute-done.10.refs_2_.refs_7_.refs_12_) | copy-start | bytes 786436
  68.9 0.8 copy-start.4
  69.7 4.0 %copy-start.2 = (bf16[256,1792]{1,0:T(8,128)(2,1)S(1)}, bf16[256,1792]{1,0:T(8,128)(2,1)}, u32[]{:S(2)}) copy-start(bf16[256,1792]{1,0:T(8,128)(2,1)} %copy-done.1) | copy-start | bytes 2752516
  72.2 34.7 %collective-permute-start.12 = (bf16[128,4096]{1,0:T(8,128)(2,1)}, bf16[128,4096]{1,0:T(8,128)(2,1)}, u32[]{:S(2)}, u32[]{:S(2)}) collective-permute-start(bf16[128,4096]{1,0:T(8,128)(2,1)} %pad_maximum_fusion.1), channel_id=1, source_target_pairs={{0,2},{2,0},{4,6},{6,4},{8,10},{10,8},{12,14},{14,12},{16,18},{18,... | collective-permute-start | bytes 3145736 | tf_op jit(solution)/shard_map/ppermute | solution.py:458
  72.2 10.7 %collective-permute-start.13 = (bf16[128,2048]{1,0:T(8,128)(2,1)S(1)}, bf16[128,2048]{1,0:T(8,128)(2,1)S(1)}, u32[]{:S(2)}, u32[]{:S(2)}) collective-permute-start(bf16[128,2048]{1,0:T(8,128)(2,1)S(1)} %get-tuple-element.56), channel_id=1, source_target_pairs={{0,2},{2,0},{4,6},{6,4},{8,10},{10,8},{12,14},{14,12},{16,18},{18,... | collective-permute-start | bytes 1572872 | tf_op jit(solution)/shard_map/ppermute | solution.py:458
  72.7 1.0 copy-start.17
  81.0 2.0 %collective-permute-start.14 = (bf16[128,2048]{1,0:T(8,128)(2,1)S(1)}, bf16[128,2048]{1,0:T(8,128)(2,1)S(1)}, u32[]{:S(2)}, u32[]{:S(2)}) collective-permute-start(bf16[128,2048]{1,0:T(8,128)(2,1)S(1)} %get-tuple-element.58), channel_id=1, source_target_pairs={{0,2},{2,0},{4,6},{6,4},{8,10},{10,8},{12,14},{14,12},{16,18},{18,... | collective-permute-start | bytes 1572872 | tf_op jit(solution)/shard_map/ppermute | solution.py:458
  81.1 8.7 %collective-permute-start.15 = (bf16[64,2048]{1,0:T(8,128)(2,1)S(1)}, bf16[64,2048]{1,0:T(8,128)(2,1)S(1)}, u32[]{:S(2)}, u32[]{:S(2)}) collective-permute-start(bf16[64,2048]{1,0:T(8,128)(2,1)S(1)} %get-tuple-element.61), channel_id=1, source_target_pairs={{0,4},{2,6},{4,0},{6,2},{8,12},{10,14},{12,8},{14,10},{16,20},{18,... | collective-permute-start | bytes 786440 | tf_op jit(solution)/shard_map/ppermute | solution.py:458
  82.8 0.8 copy-start.19
  83.0 0.9 copy-start.20
  87.0 43.1 %collective-permute-start.18 = (bf16[64,4096]{1,0:T(8,128)(2,1)}, bf16[64,4096]{1,0:T(8,128)(2,1)}, u32[]{:S(2)}, u32[]{:S(2)}) collective-permute-start(bf16[64,4096]{1,0:T(8,128)(2,1)} %get-tuple-element.66), channel_id=1, source_target_pairs={{0,4},{2,6},{4,0},{6,2},{8,12},{10,14},{12,8},{14,10},{16,20},{18,... | collective-permute-start | bytes 1572872 | tf_op jit(solution)/shard_map/ppermute | solution.py:458
  89.8 0.7 copy-start.10
  90.5 16.3 %collective-permute-start.16 = (bf16[64,2048]{1,0:T(8,128)(2,1)}, bf16[64,2048]{1,0:T(8,128)(2,1)S(1)}, u32[]{:S(2)}, u32[]{:S(2)}) collective-permute-start(bf16[64,2048]{1,0:T(8,128)(2,1)} %get-tuple-element.62), channel_id=1, source_target_pairs={{0,4},{2,6},{4,0},{6,2},{8,12},{10,14},{12,8},{14,10},{16,20},{18,... | collective-permute-start | bytes 786440 | tf_op jit(solution)/shard_map/ppermute | solution.py:458
  106.8 0.7 copy-start.7
  107.6 22.5 %copy-start.11 = (bf16[64,2048]{1,0:T(8,128)(2,1)S(1)}, bf16[64,2048]{1,0:T(8,128)(2,1)}, u32[]{:S(2)}) copy-start(bf16[64,2048]{1,0:T(8,128)(2,1)} %copy-done.10) | copy-start | bytes 786436
  128.4 12.0 %collective-permute-start.17 = (bf16[128,1792]{1,0:T(8,128)(2,1)}, bf16[128,1792]{1,0:T(8,128)(2,1)S(1)}, u32[]{:S(2)}, u32[]{:S(2)}) collective-permute-start(bf16[128,1792]{1,0:T(8,128)(2,1)} %get-tuple-element.64), channel_id=1, source_target_pairs={{0,1},{1,0},{2,3},{3,2},{4,5},{5,4},{6,7},{7,6},{8,9},{9,8},{10,11... | collective-permute-start | bytes 1376264 | tf_op jit(solution)/shard_map/ppermute | solution.py:461
  130.1 1.0 copy-start.8
  131.1 16.5 %copy-start.21 = (bf16[128,1792]{1,0:T(8,128)(2,1)S(1)}, bf16[128,1792]{1,0:T(8,128)(2,1)}, u32[]{:S(2)}) copy-start(bf16[128,1792]{1,0:T(8,128)(2,1)} %get-tuple-element.69) | copy-start | bytes 1376260
  133.6 15.9 %copy-start.15 = (f32[2,1792]{1,0:T(2,128)S(1)}, f32[2,1792]{1,0:T(2,128)}, u32[]{:S(2)}) copy-start(f32[2,1792]{1,0:T(2,128)} %copy-done.14) | copy-start | bytes 43012
  133.6 8.4 %collective-permute-start.20 = (bf16[32,4096]{1,0:T(8,128)(2,1)S(1)}, bf16[32,4096]{1,0:T(8,128)(2,1)S(1)}, u32[]{:S(2)}, u32[]{:S(2)}) collective-permute-start(bf16[32,4096]{1,0:T(8,128)(2,1)S(1)} %get-tuple-element.71), channel_id=1, source_target_pairs={{0,24},{2,26},{4,28},{6,30},{8,0},{10,2},{12,4},{14,6},{16,8},{18,... | collective-permute-start | bytes 786440 | tf_op jit(solution)/shard_map/ppermute | solution.py:458
  142.1 7.0 %collective-permute-start.21 = (f32[20,1792]{1,0:T(8,128)S(1)}, f32[20,1792]{1,0:T(8,128)S(1)}, u32[]{:S(2)}, u32[]{:S(2)}) collective-permute-start(f32[20,1792]{1,0:T(8,128)S(1)} %get-tuple-element.72.refs_6_), channel_id=1, source_target_pairs={{0,1},{1,0},{2,3},{3,2},{4,5},{5,4},{6,7},{7,6},{8,9},{9,8},{10,11... | collective-permute-start | bytes 430088 | tf_op jit(solution)/shard_map/ppermute | solution.py:461
  142.7 11.5 %collective-permute-start.22 = (bf16[32,4096]{1,0:T(8,128)(2,1)S(1)}, bf16[32,4096]{1,0:T(8,128)(2,1)S(1)}, u32[]{:S(2)}, u32[]{:S(2)}) collective-permute-start(bf16[32,4096]{1,0:T(8,128)(2,1)S(1)} %get-tuple-element.74), channel_id=1, source_target_pairs={{0,8},{2,10},{4,12},{6,14},{8,16},{10,18},{12,20},{14,22},{16,24},... | collective-permute-start | bytes 786440 | tf_op jit(solution)/shard_map/ppermute | solution.py:458
  143.7 18.8 %collective-permute-start.23 = (bf16[32,4096]{1,0:T(8,128)(2,1)S(1)}, bf16[32,4096]{1,0:T(8,128)(2,1)S(1)}, u32[]{:S(2)}, u32[]{:S(2)}) collective-permute-start(bf16[32,4096]{1,0:T(8,128)(2,1)S(1)} %get-tuple-element.75), channel_id=1, source_target_pairs={{0,16},{2,18},{4,20},{6,22},{8,24},{10,26},{12,28},{14,30},{16,0},... | collective-permute-start | bytes 786440 | tf_op jit(solution)/shard_map/ppermute | solution.py:458
  147.5 16.5 %collective-permute-start.19 = (bf16[128,1792]{1,0:T(8,128)(2,1)S(1)}, bf16[128,1792]{1,0:T(8,128)(2,1)S(1)}, u32[]{:S(2)}, u32[]{:S(2)}) collective-permute-start(bf16[128,1792]{1,0:T(8,128)(2,1)S(1)} %copy-done.21), channel_id=1, source_target_pairs={{0,1},{1,0},{2,3},{3,2},{4,5},{5,4},{6,7},{7,6},{8,9},{9,8},{10,11... | collective-permute-start | bytes 1376264 | tf_op jit(solution)/shard_map/ppermute | solution.py:461
  151.4 12.6 %copy-start.18 = (f32[256,1792]{1,0:T(8,128)S(1)}, f32[256,1792]{1,0:T(8,128)}, u32[]{:S(2)}) copy-start(f32[256,1792]{1,0:T(8,128)} %get-tuple-element.63) | copy-start | bytes 5505028

commit v4 on v3

v4 whole, which is shorter than its diff:
```python
import functools

import jax
import jax.numpy as jnp
from jax import lax
from jax.experimental import pallas as pl
from jax.experimental.pallas import tpu as pltpu
from jax.sharding import PartitionSpec as P

BLOCK = 128
EPS = 1e-06
HIGH = lax.Precision.HIGHEST
STEPS = 8
PARTS = 16
AHEAD = 6
F32 = jnp.float32
BF16 = jnp.bfloat16
COST = pl.CostEstimate(flops=1000, bytes_accessed=1000, transcendentals=0)
LAST = (((1,), (1,)), ((), ()))
PARAMS = pltpu.CompilerParams(vmem_limit_bytes=52 * 1024 * 1024)
IN_HBM = pl.BlockSpec(memory_space=pltpu.HBM)


def order_specs(deps):
    return [pl.BlockSpec(memory_space=pl.ANY)] * len(deps)


def same_block(array):
    return pl.BlockSpec(array.shape, lambda *args: (0,) * array.ndim)


def hi_lo(value, axis):
    hi = value.astype(BF16)
    lo = (value - hi.astype(F32)).astype(BF16)
    return jnp.concatenate([hi, lo], axis=axis)


def weight_copy(w_hbm, w_ref, sem, i):
    size = w_ref.shape[0] // PARTS
    rows = pl.ds(pl.multiple_of(i * size, size), size)
    return pltpu.make_async_copy(w_hbm.at[rows, :], w_ref.at[rows, :], sem.at[i])


def weight_block(w_hbm, w_ref, sem, i, steps):
    count = PARTS // steps
    for n in range(count):
        weight_copy(w_hbm, w_ref, sem, i * count + n).wait()
    for n in range(count):
        later = i * count + n + AHEAD

        @pl.when(later < PARTS)
        def _():
            weight_copy(w_hbm, w_ref, sem, later).start()


def factor_copies(tenant_ref, first, hbm, ref, sem, at):
    rank, nblk = hbm.shape[1], tenant_ref.shape[0] // BLOCK
    copies = []
    for b in range(ref.shape[0] // rank):
        src = hbm.at[tenant_ref[lax.rem(first + b, nblk) * BLOCK]]
        dst = ref.at[pl.ds(b * rank, rank), :]
        copies.append(pltpu.make_async_copy(src, dst, sem.at[at + b]))
    return copies


def norm_body(nblk, rank, tenant_ref, w_hbm, a_hbm, up_hbm, nsq_ref, *refs):
    w_ref, a_ref, up_ref, cross_ref, square_ref, w_sem, sem = refs
    cols = w_ref.shape[1]
    db = w_ref.shape[0] // STEPS
    copies = factor_copies(tenant_ref, 0, a_hbm, a_ref, sem, 0)
    late = factor_copies(tenant_ref, 0, up_hbm, up_ref, sem, nblk)
    for copy in copies:
        copy.start()
    for i in range(AHEAD):
        weight_copy(w_hbm, w_ref, w_sem, i).start()
    for copy in late:
        copy.start()
    cross_ref[...] = jnp.zeros_like(cross_ref)
    square_ref[...] = jnp.zeros_like(square_ref)
    for copy in copies:
        copy.wait()
    step = min(db, 256)

    def block(i, carry):
        weight_block(w_hbm, w_ref, w_sem, i, STEPS)
        squares = square_ref[...]
        for start in range(0, db, step):
            rows = pl.ds(pl.multiple_of(i * db + start, step), step)
            w = w_ref[rows, :]
            cross_ref[...] += jnp.dot(a_ref[:, rows], w, preferred_element_type=F32)
            for at in range(0, step, 16):
                wf = w[at : at + 16, :].astype(F32)
                squares = squares + wf[:8] * wf[:8] + wf[8:] * wf[8:]
        square_ref[...] = squares
        return carry

    lax.fori_loop(0, STEPS, block, 0)
    for copy in late:
        copy.wait()
    gram = lax.dot_general(a_ref[...], a_ref[...], LAST, preferred_element_type=F32)
    row = lax.broadcasted_iota(jnp.int32, gram.shape, 0) // rank
    col = lax.broadcasted_iota(jnp.int32, gram.shape, 1) // rank
    gram = jnp.where(row == col, gram, 0.0)
    up = up_ref[...].astype(F32)
    quad = jnp.dot(gram, up, preferred_element_type=F32, precision=HIGH)
    mixed = (up * (2.0 * cross_ref[...] + quad)).reshape(nblk, rank, cols)
    nsq_ref[...] = jnp.sum(mixed, axis=1) + jnp.sum(square_ref[...], axis=0, keepdims=True)


def partial_norms(tenant, weight, down, up):
    depth, cols = weight.shape
    rank = down.shape[1]
    nblk = tenant.shape[0] // BLOCK
    shape = jax.ShapeDtypeStruct((nblk, cols), F32)
    return pl.pallas_call(
        functools.partial(norm_body, nblk, rank),
        out_shape=shape,
        grid_spec=pltpu.PrefetchScalarGridSpec(
            num_scalar_prefetch=1,
            grid=(1,),
            in_specs=[IN_HBM] * 3,
            out_specs=same_block(shape),
            scratch_shapes=[
                pltpu.VMEM((depth, cols), BF16),
                pltpu.VMEM((nblk * rank, depth), BF16),
                pltpu.VMEM((nblk * rank, cols), BF16),
                pltpu.VMEM((nblk * rank, cols), F32),
                pltpu.VMEM((8, cols), F32),
                pltpu.SemaphoreType.DMA((PARTS,)),
                pltpu.SemaphoreType.DMA((2 * nblk,)),
            ],
        ),
        compiler_params=PARAMS,
        cost_estimate=COST,
        name="partial_norms",
    )(tenant, weight, down, up)


def grad_body(nb, rank, tenant_ref, place_ref, cot_ref, nsq_a, nsq_b, mag_ref, *refs):
    w_hbm, a_hbm, up_hbm = refs[:3]
    scale_ref, sg_ref, keep_ref, send_ref = refs[-11:-7]
    w_ref, a_ref, up_ref, sgp_ref, backp_ref, w_sem, sem = refs[-7:]
    rows, db = sg_ref.shape[0], keep_ref.shape[1]
    piece = BLOCK // 4
    half = rows // 2
    step = pl.program_id(0)
    x, core, first = place_ref[1], place_ref[2], place_ref[3]

    @pl.when(step == 0)
    def _():
        copies = factor_copies(tenant_ref, first, up_hbm, up_ref, sem, 0)
        copies += factor_copies(tenant_ref, first, a_hbm, a_ref, sem, nb)
        for copy in copies:
            copy.start()
        for i in range(AHEAD):
            weight_copy(w_hbm, w_ref, w_sem, i).start()
        for b in range(nb):
            at = first + b
            total = nsq_a[pl.ds(at, 1), :] + nsq_b[pl.ds(at, 1), :]
            scale = mag_ref[pl.ds(tenant_ref[at * BLOCK], 1), :] / jnp.sqrt(total + EPS)
            scale_ref[b : b + 1, :] = scale
            here = slice(b * BLOCK, (b + 1) * BLOCK)
            sg_ref[here, :] = (cot_ref[here, :].astype(F32) * scale).astype(BF16)
        for fc in range(2):
            for fx in range(2):
                for b in range(nb):
                    c = b * 4 + (x ^ fx) * 2 + (core ^ fc)
                    src = pl.ds(pl.multiple_of(c * piece, piece), piece)
                    at = ((fc * 2 + fx) * nb + b) * piece
                    sgp_ref[at : at + piece, :] = sg_ref[src, :]
        for copy in copies:
            copy.wait()
        back = lax.dot_general(sgp_ref[...], up_ref[...], LAST, preferred_element_type=F32)
        block = lax.broadcasted_iota(jnp.int32, back.shape, 0) // piece % nb
        owner = lax.broadcasted_iota(jnp.int32, back.shape, 1) // rank
        backp_ref[...] = hi_lo(jnp.where(owner == block, back, 0.0), 1)

    weight_block(w_hbm, w_ref, w_sem, step, STEPS)
    at = pl.ds(pl.multiple_of(step * db, db), db)
    down = a_ref[:, at]
    down = jnp.concatenate([down, down], axis=0)
    part = lax.dot_general(sgp_ref[...], w_ref[at, :], LAST, preferred_element_type=F32)
    part = part + jnp.dot(backp_ref[...], down, preferred_element_type=F32)
    keep_ref[...] = part[:half, :]
    send_ref[...] = part[half:, :].astype(BF16)


def input_gradient(tenant, place, cot, nsq_a, nsq_b, magnitude, weight, down, up, deps):
    depth, cols = weight.shape
    rows = cot.shape[0]
    nb = rows // BLOCK
    rank = down.shape[1]
    db = depth // STEPS
    shapes = (
        jax.ShapeDtypeStruct((nb, cols), F32),
        jax.ShapeDtypeStruct((rows, cols), BF16),
        jax.ShapeDtypeStruct((rows // 2, depth), F32),
        jax.ShapeDtypeStruct((rows // 2, depth), BF16),
    )
    return pl.pallas_call(
        functools.partial(grad_body, nb, rank),
        out_shape=shapes,
        grid_spec=pltpu.PrefetchScalarGridSpec(
            num_scalar_prefetch=2,
            grid=(STEPS,),
            in_specs=[same_block(a) for a in (cot, nsq_a, nsq_b, magnitude)]
            + [IN_HBM] * 3
            + order_specs(deps),
            out_specs=[same_block(s) for s in shapes[:2]]
            + [pl.BlockSpec((rows // 2, db), lambda i, t, p: (0, i))] * 2,
            scratch_shapes=[
                pltpu.VMEM((depth, cols), BF16),
                pltpu.VMEM((nb * rank, depth), BF16),
                pltpu.VMEM((nb * rank, cols), BF16),
                pltpu.VMEM((rows, cols), BF16),
                pltpu.VMEM((rows, 2 * nb * rank), BF16),
                pltpu.SemaphoreType.DMA((PARTS,)),
                pltpu.SemaphoreType.DMA((2 * nb,)),
            ],
        ),
        compiler_params=PARAMS,
        cost_estimate=COST,
        name="input_gradient",
    )(tenant, place, cot, nsq_a, nsq_b, magnitude, weight, down, up, *deps)


def add_core_body(keep_ref, recv_ref, *refs):
    mine_ref, send_ref = refs[-2:]
    half = mine_ref.shape[0]
    mine_ref[...] = keep_ref[:half, :] + recv_ref[:half, :].astype(F32)
    send_ref[...] = (keep_ref[half:, :] + recv_ref[half:, :].astype(F32)).astype(BF16)


def add_core(keep, recv, deps):
    rows, size = keep.shape
    block = size // 2
    return pl.pallas_call(
        add_core_body,
        out_shape=(
            jax.ShapeDtypeStruct((rows // 2, size), F32),
            jax.ShapeDtypeStruct((rows // 2, size), BF16),
        ),
        grid=(2,),
        in_specs=[pl.BlockSpec((rows, block), lambda i: (0, i))] * 2 + order_specs(deps),
        out_specs=[pl.BlockSpec((rows // 2, block), lambda i: (0, i))] * 2,
        compiler_params=PARAMS,
        cost_estimate=COST,
        name="add_core",
    )(keep, recv, *deps)


def add_x_body(groups, nz, place_ref, *refs):
    outs, total_ref = refs[-nz - 1 : -1], refs[-1]
    piece = outs[0].shape[0]
    z = place_ref[0]
    for g in range(groups):
        keep_ref, recv_ref = refs[2 * g : 2 * g + 2]
        first = pl.multiple_of(place_ref[3 + g] * piece, piece)
        total = keep_ref[...] + recv_ref[...].astype(F32)
        total_ref[pl.ds(first, keep_ref.shape[0]), :] = total
    for k in range(nz):
        at = pl.multiple_of(lax.rem(z + k, nz) * piece, piece)
        outs[k][...] = total_ref[pl.ds(at, piece), :].astype(outs[k].dtype)


def add_x(place, pairs, nz, deps):
    piece = BLOCK // 4
    size = pairs[0][0].shape[1]
    block = size // 2
    operands = [array for pair in pairs for array in pair]

    def spec(array):
        return pl.BlockSpec((array.shape[0], block), lambda i, p: (0, i))

    shapes = tuple(jax.ShapeDtypeStruct((piece, size), BF16 if k else F32) for k in range(nz))
    return pl.pallas_call(
        functools.partial(add_x_body, len(pairs), nz),
        out_shape=shapes,
        grid_spec=pltpu.PrefetchScalarGridSpec(
            num_scalar_prefetch=1,
            grid=(2,),
            in_specs=[spec(a) for a in operands] + order_specs(deps),
            out_specs=[spec(s) for s in shapes],
            scratch_shapes=[pltpu.VMEM((nz * piece, block), F32)],
        ),
        compiler_params=PARAMS,
        cost_estimate=COST,
        name="add_x",
    )(place, *operands, *deps)


def add_z_body(*refs):
    total = refs[0][...]
    for ref in refs[1:-1]:
        total = total + ref[...].astype(F32)
    refs[-1][...] = total.astype(BF16)


def add_z(parts):
    return pl.pallas_call(
        add_z_body,
        out_shape=jax.ShapeDtypeStruct(parts[0].shape, BF16),
        in_specs=[pl.BlockSpec(memory_space=pltpu.VMEM)] * len(parts),
        compiler_params=PARAMS,
        cost_estimate=COST,
        name="add_z",
    )(*parts)


def forward_body(rank, nz, groups, tenant_ref, place_ref, *refs):
    cot_refs, refs = refs[:groups], refs[groups:]
    w_hbm, a_hbm, up_hbm = refs[:3]
    pieces = refs[3 : 2 * nz + 5]
    w_ref, a_ref, up_ref, x_ref, acc_ref, low_acc, w_sem, sem, x_sem = refs[-9:]
    tokens, cols = acc_ref.shape
    nblk = tokens // BLOCK
    outs = refs[-11 - (groups - 1) * (nblk // groups) : -9]
    part_refs, side_ref = outs[:-1], outs[-1]
    piece = BLOCK // 4
    depth = w_ref.shape[0]
    steps = STEPS // 2
    db = depth // steps
    z, x, core, first = place_ref[0], place_ref[1], place_ref[2], place_ref[3]
    moves = [[], []]
    for n in range(4 * nz):
        k, fx, fc = n // 4, (n // 2) % 2, n % 2
        src = pieces[2 * nz + fx].at[pl.ds(k * piece, piece), :] if fc else pieces[2 * k + fx].at[:, :]
        b = lax.rem(z + (2 * nz - k) - first, nz)
        row = (b * 4 + (x ^ fx) * 2 + (core ^ fc)) * piece
        rows = pl.ds(pl.multiple_of(row, piece), piece)
        for h in range(2):
            at = pl.ds(h * depth // 2, depth // 2)
            copy = pltpu.make_async_copy(src.at[:, at], x_ref.at[rows, at], x_sem.at[h, n])
            moves[h].append(copy)
    moves[0] += factor_copies(tenant_ref, first, a_hbm, a_ref, sem, 0)
    late = factor_copies(tenant_ref, first, up_hbm, up_ref, sem, nblk)
    for copy in moves[0]:
        copy.start()
    for i in range(AHEAD):
        weight_copy(w_hbm, w_ref, w_sem, i).start()
    for copy in moves[1] + late:
        copy.start()
    acc_ref[...] = jnp.zeros_like(acc_ref)
    low_acc[...] = jnp.zeros_like(low_acc)
    side_ref[...] = jnp.zeros_like(side_ref)

    def block(i, carry):
        for h in range(2):

            @pl.when(i == h * (steps // 2))
            def _():
                for copy in moves[h]:
                    copy.wait()

        weight_block(w_hbm, w_ref, w_sem, i, steps)
        at = pl.ds(pl.multiple_of(i * db, db), db)
        xs = x_ref[:, at]
        acc_ref[...] += jnp.dot(xs, w_ref[at, :], preferred_element_type=F32)
        low_acc[...] += lax.dot_general(a_ref[:, at], xs, LAST, preferred_element_type=F32)
        return carry

    lax.fori_loop(0, steps, block, 0)
    low = low_acc[...]
    owner = lax.broadcasted_iota(jnp.int32, low.shape, 0) // rank
    block_of = lax.broadcasted_iota(jnp.int32, low.shape, 1) // BLOCK
    low = jnp.where(owner == block_of, low, 0.0)
    side_ref[:rank, :tokens] = jnp.sum(low.reshape(nblk, rank, tokens), axis=0)
    hi = low.astype(BF16).astype(F32)
    lowcat = jnp.concatenate([hi, low - hi], axis=0).T.astype(BF16)
    for copy in late:
        copy.wait()
    up = up_ref[...]
    up = jnp.concatenate([up, up], axis=0)
    size = nblk // groups
    for i in range(nblk):
        rows = slice(i * BLOCK, (i + 1) * BLOCK)
        here = slice(i % size * BLOCK, (i % size + 1) * BLOCK)
        part = acc_ref[rows, :] + jnp.dot(lowcat[rows, :], up, preferred_element_type=F32)
        if i < size:
            part_refs[0][here, :] = part
        else:
            part_refs[1 + i - size][:BLOCK, :] = part.astype(BF16)
        product = part * cot_refs[i // size][here, :].astype(F32)
        side_ref[rank + i : rank + i + 1, :cols] = jnp.sum(product, axis=0, keepdims=True)
    if groups > 1:
        out = part_refs[1]
        out[BLOCK:, :] = jnp.zeros((out.shape[0] - BLOCK, cols), BF16)
        low, dots = side_ref[:rank, :tokens], side_ref[rank:, :cols]
        packed = []
        for n in range(3):
            out[BLOCK : BLOCK + rank, n * tokens : (n + 1) * tokens] = low.astype(BF16)
            low = low - low.astype(BF16).astype(F32)
            packed.append(dots.astype(BF16).astype(F32))
            dots = dots - packed[-1]
        packed.append(jnp.zeros((out.shape[0] - BLOCK - rank - 3 * nblk, cols), F32))
        out[BLOCK + rank :, :] = jnp.concatenate(packed, axis=0).astype(BF16)


def forward(tenant, place, weight, cots, down, up, pieces, nz, deps):
    depth, cols = weight.shape
    tokens = tenant.shape[0]
    nblk = tokens // BLOCK
    rank = down.shape[1]
    groups = len(cots)
    size = nblk // groups
    shapes = [jax.ShapeDtypeStruct((size * BLOCK, cols), F32)]
    for i in range(nblk - size):
        extra = 0 if i else -(-(rank + 3 * nblk) // 16) * 16
        shapes += [jax.ShapeDtypeStruct((BLOCK + extra, cols), BF16)]
    shapes += [jax.ShapeDtypeStruct((rank + nblk, max(cols, tokens)), F32)]
    return pl.pallas_call(
        functools.partial(forward_body, rank, nz, groups),
        out_shape=shapes,
        grid_spec=pltpu.PrefetchScalarGridSpec(
            num_scalar_prefetch=2,
            grid=(1,),
            in_specs=[same_block(cot) for cot in cots]
            + [IN_HBM] * (3 + len(pieces))
            + order_specs(deps),
            out_specs=[same_block(s) for s in shapes],
            scratch_shapes=[
                pltpu.VMEM((depth, cols), BF16),
                pltpu.VMEM((nblk * rank, depth), BF16),
                pltpu.VMEM((nblk * rank, cols), BF16),
                pltpu.VMEM((tokens, depth), BF16),
                pltpu.VMEM((tokens, cols), F32),
                pltpu.VMEM((nblk * rank, tokens), F32),
                pltpu.SemaphoreType.DMA((PARTS,)),
                pltpu.SemaphoreType.DMA((2 * nblk,)),
                pltpu.SemaphoreType.DMA((2, 4 * nz)),
            ],
        ),
        compiler_params=PARAMS,
        cost_estimate=COST,
        name="forward",
    )(tenant, place, *cots, weight, down, up, *pieces, *deps)


def shards(inputs, weight, adapter_down_factors, adapter_up_factors, magnitude, cotangent, tenant):
    col_count, row_count = lax.axis_size("col"), lax.axis_size("row")
    nz = col_count // 4
    down, up = adapter_down_factors, adapter_up_factors
    tenant_number, rank, depth = down.shape
    cols = weight.shape[1]
    tokens = tenant.shape[0]
    nblk = tokens // BLOCK
    rows_row = tokens // row_count
    blocks_mine = rows_row // BLOCK
    col, row = lax.axis_index("col"), lax.axis_index("row")
    z, x, core = col >> 2, (col >> 1) & 1, col & 1

    def move(value, dz, fx, fc):
        perm = []
        for source in range(col_count):
            sz, sx, sc = source // 4, (source // 2) % 2, source % 2
            perm.append((source, ((sz + dz) % nz) * 4 + (sx ^ fx) * 2 + (sc ^ fc)))
        return lax.ppermute(value, "col", perm)

    def swap(value):
        return lax.ppermute(value, "row", [(0, 1), (1, 0)])

    def place(*firsts):
        return jnp.stack([z, x, core, *firsts]).astype(jnp.int32)

    pair = row_count == 2 and 3 * tokens <= cols

    def once(value, other):
        return lax.optimization_barrier((value, other))[0]

    along_z = [inputs] + [move(inputs, k, 0, 0) for k in range(1, nz)]
    along_x = {0: move(inputs, 0, 1, 0)}

    def other_x(k, after):
        along_z[k] = once(along_z[k], after)
        along_x[k] = move(along_z[k], 0, 1, 0)

    def other_core(part):
        return move(jnp.concatenate(part, axis=0), 0, 0, 1)

    nsq = partial_norms(tenant, weight, down, up)
    if pair:
        nsq_a, nsq_b = nsq, swap(once(nsq, along_x[0]))
        firsts = [row * blocks_mine, (1 - row) * blocks_mine]
        cots = [cotangent, swap(cotangent)]
    else:
        nsq_a, nsq_b = lax.psum(nsq, "row"), jnp.zeros_like(nsq)
        firsts = [0 * row]
        cots = [lax.all_gather(cotangent, "row", axis=0, tiled=True)]
    places = [place(first) for first in firsts]

    def gradient(g, deps):
        return input_gradient(
            tenant, places[g], cots[g], nsq_a, nsq_b, magnitude, weight, down, up, deps
        )

    def cross_core(made, deps):
        return add_core(made[2], move(made[3], 0, 0, 1), deps)

    def cross_x(pairs, deps):
        mine, *away = add_x(place(*firsts), pairs, nz, deps)
        return [mine] + [move(block, k + 1, 0, 0) for k, block in enumerate(away)]

    def across_x(made):
        return made[0], move(made[1], 0, 1, 0)

    if pair:
        other_x(nz - 1, nsq)
        for k in range(1, nz - 2):
            other_x(k, nsq_b)
        ours = gradient(0, [cots[1]])
        other_x(nz - 2, ours[0])
        core_z = other_core(along_z)
        near = across_x(cross_core(ours, []))
        theirs = gradient(1, [near[0], core_z, along_x[nz - 2]])
        along_x = [along_x[k] for k in range(nz)]
        core_x = other_core(along_x)
        far = cross_core(theirs, [core_x])
        pieces = [piece for both in zip(along_z, along_x) for piece in both] + [core_z, core_x]
        part, first, *away, side = forward(
            tenant, places[0], weight, cots, down, up, pieces, nz, [far[0]]
        )
        first = swap(first)
        arrived = [first[:BLOCK]] + [swap(once(block, first)) for block in away]
        finals = cross_x([near, across_x(far)], [side])
        first = once(first, (finals[nz // 2], finals[nz - 1]))[BLOCK:].astype(F32)
        low = [first[:rank, i * tokens : (i + 1) * tokens] for i in range(3)]
        dots = [first[rank + i * nblk : rank + (i + 1) * nblk] for i in range(3)]
        low = side[:rank, :tokens] + jnp.roll(low[0] + low[1] + low[2], rows_row, axis=1)
        dots = side[rank:, :cols] + jnp.roll(dots[0] + dots[1] + dots[2], blocks_mine, axis=0)
        parts = [ours, theirs]
    else:
        ours = gradient(0, [])
        near = across_x(cross_core(ours, []))
        for k in range(1, nz):
            other_x(k, inputs)
        along_x = [along_x[k] for k in range(nz)]
        pieces = [piece for both in zip(along_z, along_x) for piece in both]
        pieces += [other_core(along_z), other_core(along_x)]
        part, side = forward(tenant, places[0], weight, cots, down, up, pieces, nz, [])
        finals = cross_x([near], [])
        low, dots = lax.psum((side[:rank, :tokens], side[rank:, :cols]), "row")
        parts = [ours]

    scales = jnp.concatenate([group[0] for group in parts], axis=0)

    tenants = jnp.arange(tenant_number, dtype=jnp.int32)
    block_tenant = tenant.reshape(nblk, BLOCK)[:, 0]
    size = nblk // len(parts)
    owners = jnp.concatenate(
        [lax.dynamic_slice_in_dim(block_tenant, first, size, 0) for first in firsts]
    )
    low = low.astype(BF16)
    grad_b = 0.0
    for g, group in enumerate(parts):
        owner = jnp.repeat(owners[g * size : (g + 1) * size], BLOCK)
        mine = low[:, g * size * BLOCK : (g + 1) * size * BLOCK]
        wide = jnp.where((tenants[:, None] == owner[None, :])[:, None, :], mine[None], 0)
        wide = wide.reshape(tenant_number * rank, size * BLOCK)
        grad_b = grad_b + jnp.dot(wide, group[1], preferred_element_type=F32)
    grad_b = grad_b.reshape(tenant_number, rank, cols)
    hit = (tenants[:, None] == owners[None, :])[:, :, None]
    terms = jnp.where(hit, (dots * scales)[None], 0.0)
    grad_m = 0.0
    for g in range(len(parts)):
        group = terms[:, g * size : (g + 1) * size]
        grad_m = grad_m + functools.reduce(jnp.add, [group[:, i] for i in range(size)])
    grad_inputs = add_z([once(finals[0], grad_b)] + finals[1:])
    if pair:
        pre = part + jnp.concatenate(arrived, axis=0).astype(F32)
        scale_mine = parts[0][0]
    else:
        pre = lax.psum_scatter(part, "row", scatter_dimension=0, tiled=True)
        scale_mine = lax.dynamic_slice_in_dim(scales, row * blocks_mine, blocks_mine, 0)
    output = (pre.reshape(blocks_mine, BLOCK, cols) * scale_mine[:, None, :]).astype(BF16)
    output = output.reshape(rows_row, cols)
    return (output, grad_inputs, grad_b, grad_m / magnitude)


def solution(mesh):
    return jax.shard_map(
        shards,
        mesh=mesh,
        in_specs=(
            P("col", "row"),
            P("row", "col"),
            P(None, None, "row"),
            P(None, None, "col"),
            P(None, "col"),
            P("row", "col"),
            P(),
        ),
        out_specs=(P("row", "col"), P("col", "row"), P(None, None, "col"), P(None, "col")),
        check_vma=False,
    )
```

time: 166 us -> 136 us (0.82)
  the two profiles are of different devices: /device:TPU:0 before, /device:TPU:8 now
where the time goes in v4:
time: 136 us
  Pallas kernels  55.6 us (41%)
  waiting for transfers between devices  48.3 us (36%)
  starting transfers between devices  18.1 us (13%)
  local copies, waits for them, and re-layouts  7.17 us (5%)
  other arithmetic  3.51 us (3%)
  matrix products  2.05 us (2%)
    ppermute x16, waiting for transfers between devices, move(): return lax.ppermute(value, 'col', perm)  41.3 us
    pallas_call x2, Pallas kernels, input_gradient(): pl.pallas_call(functools.partial(grad_body, nb, rank), out_shape=shapes,...  21.2 us
    pallas_call x1, Pallas kernels, forward(): pl.pallas_call(functools.partial(forward_body, rank, nz, groups), out_sha...  17.1 us
    ppermute x16, starting transfers between devices, move(): return lax.ppermute(value, 'col', perm)  14.9 us
    pallas_call x1, Pallas kernels, partial_norms(): pl.pallas_call(functools.partial(norm_body, nblk, rank), out_shape=shape,...  9.25 us
    ppermute x4, waiting for transfers between devices, swap(): return lax.ppermute(value, 'row', [(0, 1), (1, 0)])  6.99 us
    unnamed x34, local copies, waits for them, and re-layouts  6.84 us
    pallas_call x2, Pallas kernels, add_core(): pl.pallas_call(add_core_body, out_shape=(jax.ShapeDtypeStruct((rows // 2,...  4.63 us
  transfers between devices with their start and end apart: 20, of which 10 were waited for; matrix products, arithmetic and copies ran while one was open for 4% of the time, Pallas kernels for 41%

profile of v4, /device:TPU:8, one launch (start us, length us, event | category | flops | bytes accessed | tf_op | source)
XLA Modules:
  0.0 135.7 jit_solution(881974024332453493)
XLA Ops:
  0.6 1.6 %collective-permute-start = (bf16[256,1792]{1,0:T(8,128)(2,1)}, bf16[256,1792]{1,0:T(8,128)(2,1)}, u32[]{:S(2)}, u32[]{:S(2)}) collective-permute-start(bf16[256,1792]{1,0:T(8,128)(2,1)} %refs_0_.5), channel_id=1, source_target_pairs={{0,1},{1,0},{2,3},{3,2},{4,5},{5,4},{6,7},{7,6},{8,9},{9,8},{10,11... | collective-permute-start | bytes 2752520 | tf_op jit(solution)/shard_map/ppermute | solution.py:460
  2.2 1.5 %collective-permute-start.1 = (bf16[32,4096]{1,0:T(8,128)(2,1)}, bf16[32,4096]{1,0:T(8,128)(2,1)S(1)}, u32[]{:S(2)}, u32[]{:S(2)}) collective-permute-start(bf16[32,4096]{1,0:T(8,128)(2,1)} %refs_5_.1), channel_id=1, source_target_pairs={{0,4},{2,6},{4,0},{6,2},{8,12},{10,14},{12,8},{14,10},{16,20},{18,... | collective-permute-start | bytes 786440 | tf_op jit(solution)/shard_map/ppermute | solution.py:457
  3.7 2.6 %collective-permute-start.5 = (bf16[32,4096]{1,0:T(8,128)(2,1)}, bf16[32,4096]{1,0:T(8,128)(2,1)S(1)}, u32[]{:S(2)}, u32[]{:S(2)}) collective-permute-start(bf16[32,4096]{1,0:T(8,128)(2,1)} %refs_5_.1), channel_id=1, source_target_pairs={{0,16},{2,18},{4,20},{6,22},{8,24},{10,26},{12,28},{14,30},{16,0},... | collective-permute-start | bytes 786440 | tf_op jit(solution)/shard_map/ppermute | solution.py:457
  6.3 2.0 %collective-permute-start.7 = (bf16[32,4096]{1,0:T(8,128)(2,1)}, bf16[32,4096]{1,0:T(8,128)(2,1)S(1)}, u32[]{:S(2)}, u32[]{:S(2)}) collective-permute-start(bf16[32,4096]{1,0:T(8,128)(2,1)} %refs_5_.1), channel_id=1, source_target_pairs={{0,24},{2,26},{4,28},{6,30},{8,0},{10,2},{12,4},{14,6},{16,8},{18,... | collective-permute-start | bytes 786440 | tf_op jit(solution)/shard_map/ppermute | solution.py:457
  8.4 1.2 copy-done
  9.6 0.7 copy-done.8
  10.3 9.2 %partial_norms.1.nsq_a = f32[4,1792]{1,0:T(4,128)S(1)} custom-call(s32[512]{0:T(512)S(1)} %copy-done.8, bf16[4096,1792]{1,0:T(8,128)(2,1)} %refs_2_.5, bf16[16,16,4096]{2,1,0:T(8,128)(2,1)} %refs_3_.1, bf16[16,16,1792]{2,1,0:T(8,128)(2,1)S(1)} %copy-done), custom_call_target="tpu_custom_call" | custom-call | flops 1000 | bytes 1000 | tf_op jit(solution)/shard_map/partial_norms/pallas_call | solution.py:115
  19.5 0.6 collective-permute-start.3
  20.2 8.0 %collective-permute-done.7.refs_11_ = bf16[32,4096]{1,0:T(8,128)(2,1)S(1)} collective-permute-done((bf16[32,4096]{1,0:T(8,128)(2,1)}, bf16[32,4096]{1,0:T(8,128)(2,1)S(1)}, u32[]{:S(2)}, u32[]{:S(2)}) %collective-permute-start.7) | collective-permute-done | bytes 262176 | tf_op jit(solution)/shard_map/ppermute | solution.py:457
  28.2 0.2 collective-permute-done.2.refs_7_
  28.4 9.9 %input_gradient.2 = (f32[2,1792]{1,0:T(2,128)S(1)}, bf16[256,1792]{1,0:T(8,128)(2,1)S(1)}, f32[128,4096]{1,0:T(8,128)}, bf16[128,4096]{1,0:T(8,128)(2,1)}) custom-call(s32[512]{0:T(512)S(1)} %copy-done.9, s32[4]{0:T(128)S(1)} %pad_add_fusion.place_ref, bf16[256,1792]{1,0:T(8,128)(2,1)S(1)} %copy-done.3, f32[4,1792]{1,0:T(4,128)S(1)} %partial_norms.1.nsq_a, ...), custom_call_target="tpu_custom_call" | custom-call | flops 1000 | bytes 1000 | tf_op jit(solution)/shard_map/input_gradient/pallas_call | solution.py:200
  38.4 0.1 pad_maximum_fusion
  38.5 0.5 collective-permute-start.9
  39.1 0.5 collective-permute-start.8
  39.6 1.5 %collective-permute-start.4 = (bf16[32,4096]{1,0:T(8,128)(2,1)S(1)}, bf16[32,4096]{1,0:T(8,128)(2,1)S(1)}, u32[]{:S(2)}, u32[]{:S(2)}) collective-permute-start(bf16[32,4096]{1,0:T(8,128)(2,1)S(1)} %collective-permute-done.2.refs_7_), channel_id=1, source_target_pairs={{0,4},{2,6},{4,0},{6,2},{8,12},{10,14},{12,8},{14,10},{16,20},{18,... | collective-permute-start | bytes 786440 | tf_op jit(solution)/shard_map/ppermute | solution.py:457
  41.1 0.5 collective-permute-start.6
  41.6 6.6 %collective-permute-done.8.refs_12_ = bf16[32,4096]{1,0:T(8,128)(2,1)S(1)} collective-permute-done((bf16[32,4096]{1,0:T(8,128)(2,1)S(1)}, bf16[32,4096]{1,0:T(8,128)(2,1)S(1)}, u32[]{:S(2)}, u32[]{:S(2)}) %collective-permute-start.8) | collective-permute-done | bytes 262176 | tf_op jit(solution)/shard_map/ppermute | solution.py:457
  48.2 5.6 %collective-permute-done.4.refs_8_ = bf16[32,4096]{1,0:T(8,128)(2,1)S(1)} collective-permute-done((bf16[32,4096]{1,0:T(8,128)(2,1)S(1)}, bf16[32,4096]{1,0:T(8,128)(2,1)S(1)}, u32[]{:S(2)}, u32[]{:S(2)}) %collective-permute-start.4) | collective-permute-done | bytes 262176 | tf_op jit(solution)/shard_map/ppermute | solution.py:457
  53.9 4.7 %collective-permute-done.6.refs_5_.refs_10_ = bf16[32,4096]{1,0:T(8,128)(2,1)S(1)} collective-permute-done((bf16[32,4096]{1,0:T(8,128)(2,1)S(1)}, bf16[32,4096]{1,0:T(8,128)(2,1)S(1)}, u32[]{:S(2)}, u32[]{:S(2)}) %collective-permute-start.6) | collective-permute-done | bytes 262176 | tf_op jit(solution)/shard_map/ppermute | solution.py:457
  58.6 1.1 pad_maximum_fusion.1
  59.7 1.0 copy-done.15
  60.7 2.0 %add_core.2 = (f32[64,4096]{1,0:T(8,128)S(1)}, bf16[64,4096]{1,0:T(8,128)(2,1)S(1)}) custom-call(f32[128,4096]{1,0:T(8,128)} %get-tuple-element.36.keep_ref, bf16[128,4096]{1,0:T(8,128)(2,1)} %copy-done.15), custom_call_target="tpu_custom_call" | custom-call | flops 1000 | bytes 1000 | tf_op jit(solution)/shard_map/add_core/pallas_call | solution.py:237
  62.7 1.0 copy-done.1
  63.6 1.0 copy-done.11
  64.7 11.3 %input_gradient.3 = (f32[2,1792]{1,0:T(2,128)S(1)}, bf16[256,1792]{1,0:T(8,128)(2,1)S(1)}, f32[128,4096]{1,0:T(8,128)}, bf16[128,4096]{1,0:T(8,128)(2,1)}) custom-call(s32[512]{0:T(512)S(1)} %copy-done.9, s32[4]{0:T(128)S(1)} %get-tuple-element.60.place_ref, bf16[256,1792]{1,0:T(8,128)(2,1)} %collective-permute-done.refs_3_.cot_ref.refs_1_, ...), custom_call_target="tpu_custom_call" | custom-call | flops 1000 | bytes 1000 | tf_op jit(solution)/shard_map/input_gradient/pallas_call | solution.py:200
  75.9 0.9 copy-done.6
  76.8 0.5 collective-permute-start.12
  77.4 0.1 dynamic-slice_reduce_fusion.1
  77.5 0.6 collective-permute-start.15
  78.1 1.9 %collective-permute-done.12.recv_ref = bf16[128,4096]{1,0:T(8,128)(2,1)} collective-permute-done((bf16[128,4096]{1,0:T(8,128)(2,1)}, bf16[128,4096]{1,0:T(8,128)(2,1)}, u32[]{:S(2)}, u32[]{:S(2)}) %collective-permute-start.12) | collective-permute-done | bytes 1048608 | tf_op jit(solution)/shard_map/ppermute | solution.py:457
  80.0 2.6 %add_core.3 = (f32[64,4096]{1,0:T(8,128)S(1)}, bf16[64,4096]{1,0:T(8,128)(2,1)}) custom-call(f32[128,4096]{1,0:T(8,128)} %get-tuple-element.39.keep_ref, bf16[128,4096]{1,0:T(8,128)(2,1)} %collective-permute-done.12.recv_ref, bf16[128,4096]{1,0:T(8,128)(2,1)} %collective-permute-done.10.refs_0_.refs_14_), custom_call_target="tpu_custom_call" | custom-call | flops 1000 | bytes 1000 | tf_op jit(solution)/shard_map/add_core/pallas_call | solution.py:237
  82.6 1.0 copy-done.2
  83.6 0.5 collective-permute-start.16
  84.2 17.1 %forward.1 = (f32[256,1792]{1,0:T(8,128)}, bf16[160,1792]{1,0:T(8,128)(2,1)}, bf16[128,1792]{1,0:T(8,128)(2,1)}, f32[20,1792]{1,0:T(8,128)S(1)}) custom-call(s32[512]{0:T(512)S(1)} %copy-done.9, s32[4]{0:T(128)S(1)} %pad_add_fusion.place_ref, bf16[256,1792]{1,0:T(8,128)(2,1)} %refs_0_.5, bf16[256,1792]{1,0:T(8,128)(2,1)} %collective-permute-done.refs_3_.cot_ref.refs_1_, ...), custom_call_target="tpu_custom_call" | custom-call | flops 1000 | bytes 1000 | tf_op jit(solution)/shard_map/forward/pallas_call | solution.py:411
  101.4 0.6 collective-permute-start.13
  102.1 0.8 collective-permute-done.16.refs_3_
  103.0 2.6 %add_x.1 = (f32[32,4096]{1,0:T(8,128)S(1)}, bf16[32,4096]{1,0:T(8,128)(2,1)S(1)}, bf16[32,4096]{1,0:T(8,128)(2,1)S(1)}, bf16[32,4096]{1,0:T(8,128)(2,1)S(1)}) custom-call(s32[5]{0:T(128)S(1)} %stack.39.place_ref, f32[64,4096]{1,0:T(8,128)} %copy-done.1, bf16[64,4096]{1,0:T(8,128)(2,1)} %collective-permute-done.15.refs_1_, f32[64,4096]{1,0:T(8,128)} %copy-done.2, ...), custom_call_target="tpu_custom_call" | custom-call | flops 1000 | bytes 1000 | tf_op jit(solution)/shard_map/add_x/pallas_call | solution.py:276
  105.7 3.8 %collective-permute-start.18 = (bf16[32,4096]{1,0:T(8,128)(2,1)S(1)}, bf16[32,4096]{1,0:T(8,128)(2,1)S(1)}, u32[]{:S(2)}, u32[]{:S(2)}) collective-permute-start(bf16[32,4096]{1,0:T(8,128)(2,1)S(1)} %get-tuple-element.51), channel_id=1, source_target_pairs={{0,24},{2,26},{4,28},{6,30},{8,0},{10,2},{12,4},{14,6},{16,8},{18,... | collective-permute-start | bytes 786440 | tf_op jit(solution)/shard_map/ppermute | solution.py:457
  109.6 7.0 %collective-permute-done.13 = bf16[160,1792]{1,0:T(8,128)(2,1)S(1)} collective-permute-done((bf16[160,1792]{1,0:T(8,128)(2,1)}, bf16[160,1792]{1,0:T(8,128)(2,1)S(1)}, u32[]{:S(2)}, u32[]{:S(2)}) %collective-permute-start.13) | collective-permute-done | bytes 573472 | tf_op jit(solution)/shard_map/ppermute | solution.py:460
  116.6 0.5 collective-permute-start.14
  117.1 6.5 %collective-permute-done.17.refs_2_ = bf16[32,4096]{1,0:T(8,128)(2,1)S(1)} collective-permute-done((bf16[32,4096]{1,0:T(8,128)(2,1)S(1)}, bf16[32,4096]{1,0:T(8,128)(2,1)S(1)}, u32[]{:S(2)}, u32[]{:S(2)}) %collective-permute-start.17) | collective-permute-done | bytes 262176 | tf_op jit(solution)/shard_map/ppermute | solution.py:457
  123.7 6.9 %collective-permute-done.18.refs_3_ = bf16[32,4096]{1,0:T(8,128)(2,1)S(1)} collective-permute-done((bf16[32,4096]{1,0:T(8,128)(2,1)S(1)}, bf16[32,4096]{1,0:T(8,128)(2,1)S(1)}, u32[]{:S(2)}, u32[]{:S(2)}) %collective-permute-start.18) | collective-permute-done | bytes 262176 | tf_op jit(solution)/shard_map/ppermute | solution.py:457
  130.7 0.1 broadcast_select_fusion
  130.9 0.4 fusion.9
  131.3 1.6 %convolution_add_fusion = f32[256,1792]{1,0:T(8,128)} fusion(f32[256,1792]{1,0:T(8,128)S(1)} %fusion.9, bf16[256,256]{1,0:T(8,128)(2,1)S(1)} %bitcast.28, bf16[256,1792]{1,0:T(8,128)(2,1)S(1)} %get-tuple-element.53), kind=kOutput, calls=%fused_computation | convolution fusion | flops 235339776 | bytes 4718592 | tf_op jit(solution)/shard_map/dot_general | solution.py:559
  133.0 0.8 add_z.1
  133.8 0.7 fusion.3
  134.6 1.1 fusion
  (62 shorter events, 1.0 us)
Async XLA Ops:
  0.6 27.7 %collective-permute-start = (bf16[256,1792]{1,0:T(8,128)(2,1)}, bf16[256,1792]{1,0:T(8,128)(2,1)}, u32[]{:S(2)}, u32[]{:S(2)}) collective-permute-start(bf16[256,1792]{1,0:T(8,128)(2,1)} %refs_0_.5), channel_id=1, source_target_pairs={{0,1},{1,0},{2,3},{3,2},{4,5},{5,4},{6,7},{7,6},{8,9},{9,8},{10,11... | collective-permute-start | bytes 2752520 | tf_op jit(solution)/shard_map/ppermute | solution.py:460
  2.2 17.3 %collective-permute-start.1 = (bf16[32,4096]{1,0:T(8,128)(2,1)}, bf16[32,4096]{1,0:T(8,128)(2,1)S(1)}, u32[]{:S(2)}, u32[]{:S(2)}) collective-permute-start(bf16[32,4096]{1,0:T(8,128)(2,1)} %refs_5_.1), channel_id=1, source_target_pairs={{0,4},{2,6},{4,0},{6,2},{8,12},{10,14},{12,8},{14,10},{16,20},{18,... | collective-permute-start | bytes 786440 | tf_op jit(solution)/shard_map/ppermute | solution.py:457
  3.7 34.7 %collective-permute-start.5 = (bf16[32,4096]{1,0:T(8,128)(2,1)}, bf16[32,4096]{1,0:T(8,128)(2,1)S(1)}, u32[]{:S(2)}, u32[]{:S(2)}) collective-permute-start(bf16[32,4096]{1,0:T(8,128)(2,1)} %refs_5_.1), channel_id=1, source_target_pairs={{0,16},{2,18},{4,20},{6,22},{8,24},{10,26},{12,28},{14,30},{16,0},... | collective-permute-start | bytes 786440 | tf_op jit(solution)/shard_map/ppermute | solution.py:457
  6.3 22.1 %collective-permute-start.2 = (bf16[32,4096]{1,0:T(8,128)(2,1)}, bf16[32,4096]{1,0:T(8,128)(2,1)S(1)}, u32[]{:S(2)}, u32[]{:S(2)}) collective-permute-start(bf16[32,4096]{1,0:T(8,128)(2,1)} %refs_5_.1), channel_id=1, source_target_pairs={{0,8},{2,10},{4,12},{6,14},{8,16},{10,18},{12,20},{14,22},{16,24},... | collective-permute-start | bytes 786440 | tf_op jit(solution)/shard_map/ppermute | solution.py:457
  6.3 21.9 %collective-permute-start.7 = (bf16[32,4096]{1,0:T(8,128)(2,1)}, bf16[32,4096]{1,0:T(8,128)(2,1)S(1)}, u32[]{:S(2)}, u32[]{:S(2)}) collective-permute-start(bf16[32,4096]{1,0:T(8,128)(2,1)} %refs_5_.1), channel_id=1, source_target_pairs={{0,24},{2,26},{4,28},{6,30},{8,0},{10,2},{12,4},{14,6},{16,8},{18,... | collective-permute-start | bytes 786440 | tf_op jit(solution)/shard_map/ppermute | solution.py:457
  8.4 1.2 copy-start
  9.6 0.7 copy-start.8
  10.3 18.1 %copy-start.3 = (bf16[256,1792]{1,0:T(8,128)(2,1)S(1)}, bf16[256,1792]{1,0:T(8,128)(2,1)}, u32[]{:S(2)}) copy-start(bf16[256,1792]{1,0:T(8,128)(2,1)} %refs_0_.5) | copy-start | bytes 2752516
  10.3 18.1 %copy-start.5 = (f32[16,1792]{1,0:T(8,128)S(1)}, f32[16,1792]{1,0:T(8,128)}, u32[]{:S(2)}) copy-start(f32[16,1792]{1,0:T(8,128)} %mag_ref.3) | copy-start | bytes 344068
  10.3 18.1 %copy-start.9 = (s32[512]{0:T(512)S(1)}, s32[512]{0:T(512)}, u32[]{:S(2)}) copy-start(s32[512]{0:T(512)} %tenant_ref.7) | copy-start | bytes 6148
  19.5 8.8 %collective-permute-start.3 = (f32[4,1792]{1,0:T(4,128)S(1)}, f32[4,1792]{1,0:T(4,128)S(1)}, u32[]{:S(2)}, u32[]{:S(2)}) collective-permute-start(f32[4,1792]{1,0:T(4,128)S(1)} %partial_norms.1.nsq_a), channel_id=1, source_target_pairs={{0,1},{1,0},{2,3},{3,2},{4,5},{5,4},{6,7},{7,6},{8,9},{9,8},{10,11... | collective-permute-start | bytes 86024 | tf_op jit(solution)/shard_map/ppermute | solution.py:460
  20.2 18.2 %copy-start.4 = (bf16[32,4096]{1,0:T(8,128)(2,1)S(1)}, bf16[32,4096]{1,0:T(8,128)(2,1)}, u32[]{:S(2)}) copy-start(bf16[32,4096]{1,0:T(8,128)(2,1)} %refs_5_.1) | copy-start | bytes 786436
  38.3 21.3 %collective-permute-start.11 = (bf16[128,4096]{1,0:T(8,128)(2,1)}, bf16[128,4096]{1,0:T(8,128)(2,1)S(1)}, u32[]{:S(2)}, u32[]{:S(2)}) collective-permute-start(bf16[128,4096]{1,0:T(8,128)(2,1)} %get-tuple-element.37), channel_id=1, source_target_pairs={{0,2},{2,0},{4,6},{6,4},{8,10},{10,8},{12,14},{14,12},{16,18},{18,... | collective-permute-start | bytes 3145736 | tf_op jit(solution)/shard_map/ppermute | solution.py:457
  38.5 25.1 %collective-permute-start.9 = (bf16[128,4096]{1,0:T(8,128)(2,1)S(1)}, bf16[128,4096]{1,0:T(8,128)(2,1)S(1)}, u32[]{:S(2)}, u32[]{:S(2)}) collective-permute-start(bf16[128,4096]{1,0:T(8,128)(2,1)S(1)} %pad_maximum_fusion), channel_id=1, source_target_pairs={{0,2},{2,0},{4,6},{6,4},{8,10},{10,8},{12,14},{14,12},{16,18},{18,... | collective-permute-start | bytes 3145736 | tf_op jit(solution)/shard_map/ppermute | solution.py:457
  39.1 9.2 %collective-permute-start.8 = (bf16[32,4096]{1,0:T(8,128)(2,1)S(1)}, bf16[32,4096]{1,0:T(8,128)(2,1)S(1)}, u32[]{:S(2)}, u32[]{:S(2)}) collective-permute-start(bf16[32,4096]{1,0:T(8,128)(2,1)S(1)} %collective-permute-done.7.refs_11_), channel_id=1, source_target_pairs={{0,4},{2,6},{4,0},{6,2},{8,12},{10,14},{12,8},{14,10},{16,20},{18,... | collective-permute-start | bytes 786440 | tf_op jit(solution)/shard_map/ppermute | solution.py:457
  39.6 14.2 %collective-permute-start.4 = (bf16[32,4096]{1,0:T(8,128)(2,1)S(1)}, bf16[32,4096]{1,0:T(8,128)(2,1)S(1)}, u32[]{:S(2)}, u32[]{:S(2)}) collective-permute-start(bf16[32,4096]{1,0:T(8,128)(2,1)S(1)} %collective-permute-done.2.refs_7_), channel_id=1, source_target_pairs={{0,4},{2,6},{4,0},{6,2},{8,12},{10,14},{12,8},{14,10},{16,20},{18,... | collective-permute-start | bytes 786440 | tf_op jit(solution)/shard_map/ppermute | solution.py:457
  41.1 17.5 %collective-permute-start.6 = (bf16[32,4096]{1,0:T(8,128)(2,1)S(1)}, bf16[32,4096]{1,0:T(8,128)(2,1)S(1)}, u32[]{:S(2)}, u32[]{:S(2)}) collective-permute-start(bf16[32,4096]{1,0:T(8,128)(2,1)S(1)} %collective-permute-done.5.refs_9_), channel_id=1, source_target_pairs={{0,4},{2,6},{4,0},{6,2},{8,12},{10,14},{12,8},{14,10},{16,20},{18,... | collective-permute-start | bytes 786440 | tf_op jit(solution)/shard_map/ppermute | solution.py:457
  48.2 14.4 %copy-start.14 = (bf16[32,4096]{1,0:T(8,128)(2,1)}, bf16[32,4096]{1,0:T(8,128)(2,1)S(1)}, u32[]{:S(2)}) copy-start(bf16[32,4096]{1,0:T(8,128)(2,1)S(1)} %collective-permute-done.8.refs_12_) | copy-start | bytes 786436
  59.7 18.4 %collective-permute-start.10 = (bf16[128,4096]{1,0:T(8,128)(2,1)}, bf16[128,4096]{1,0:T(8,128)(2,1)}, u32[]{:S(2)}, u32[]{:S(2)}) collective-permute-start(bf16[128,4096]{1,0:T(8,128)(2,1)} %pad_maximum_fusion.1), channel_id=1, source_target_pairs={{0,2},{2,0},{4,6},{6,4},{8,10},{10,8},{12,14},{14,12},{16,18},{18,... | collective-permute-start | bytes 3145736 | tf_op jit(solution)/shard_map/ppermute | solution.py:457
  59.7 1.0 copy-start.15
  62.7 1.0 copy-start.1
  63.6 12.3 %copy-start.10 = (bf16[64,4096]{1,0:T(8,128)(2,1)}, bf16[64,4096]{1,0:T(8,128)(2,1)S(1)}, u32[]{:S(2)}) copy-start(bf16[64,4096]{1,0:T(8,128)(2,1)S(1)} %get-tuple-element.46) | copy-start | bytes 1572868
  63.6 1.0 copy-start.11
  75.9 0.9 copy-start.6
  76.8 3.1 %collective-permute-start.12 = (bf16[128,4096]{1,0:T(8,128)(2,1)}, bf16[128,4096]{1,0:T(8,128)(2,1)}, u32[]{:S(2)}, u32[]{:S(2)}) collective-permute-start(bf16[128,4096]{1,0:T(8,128)(2,1)} %get-tuple-element.40), channel_id=1, source_target_pairs={{0,2},{2,0},{4,6},{6,4},{8,10},{10,8},{12,14},{14,12},{16,18},{18,... | collective-permute-start | bytes 3145736 | tf_op jit(solution)/shard_map/ppermute | solution.py:457
  77.5 24.6 %collective-permute-start.15 = (bf16[64,4096]{1,0:T(8,128)(2,1)}, bf16[64,4096]{1,0:T(8,128)(2,1)}, u32[]{:S(2)}, u32[]{:S(2)}) collective-permute-start(bf16[64,4096]{1,0:T(8,128)(2,1)} %copy-done.10), channel_id=1, source_target_pairs={{0,4},{2,6},{4,0},{6,2},{8,12},{10,14},{12,8},{14,10},{16,20},{18,... | collective-permute-start | bytes 1572872 | tf_op jit(solution)/shard_map/ppermute | solution.py:457
  82.6 1.0 copy-start.2
  83.6 19.3 %collective-permute-start.16 = (bf16[64,4096]{1,0:T(8,128)(2,1)}, bf16[64,4096]{1,0:T(8,128)(2,1)}, u32[]{:S(2)}, u32[]{:S(2)}) collective-permute-start(bf16[64,4096]{1,0:T(8,128)(2,1)} %get-tuple-element.47), channel_id=1, source_target_pairs={{0,4},{2,6},{4,0},{6,2},{8,12},{10,14},{12,8},{14,10},{16,20},{18,... | collective-permute-start | bytes 1572872 | tf_op jit(solution)/shard_map/ppermute | solution.py:457
  101.4 15.2 %collective-permute-start.13 = (bf16[160,1792]{1,0:T(8,128)(2,1)}, bf16[160,1792]{1,0:T(8,128)(2,1)S(1)}, u32[]{:S(2)}, u32[]{:S(2)}) collective-permute-start(bf16[160,1792]{1,0:T(8,128)(2,1)} %get-tuple-element.43), channel_id=1, source_target_pairs={{0,1},{1,0},{2,3},{3,2},{4,5},{5,4},{6,7},{7,6},{8,9},{9,8},{10,11... | collective-permute-start | bytes 1720328 | tf_op jit(solution)/shard_map/ppermute | solution.py:460
  102.0 14.6 %copy-start.16 = (bf16[128,1792]{1,0:T(8,128)(2,1)S(1)}, bf16[128,1792]{1,0:T(8,128)(2,1)}, u32[]{:S(2)}) copy-start(bf16[128,1792]{1,0:T(8,128)(2,1)} %get-tuple-element.45) | copy-start | bytes 1376260
  102.9 27.9 %copy-start.7 = (bf16[256,1792]{1,0:T(8,128)(2,1)S(1)}, bf16[256,1792]{1,0:T(8,128)(2,1)}, u32[]{:S(2)}) copy-start(bf16[256,1792]{1,0:T(8,128)(2,1)} %copy-done.6) | copy-start | bytes 2752516
  105.6 18.1 %collective-permute-start.17 = (bf16[32,4096]{1,0:T(8,128)(2,1)S(1)}, bf16[32,4096]{1,0:T(8,128)(2,1)S(1)}, u32[]{:S(2)}, u32[]{:S(2)}) collective-permute-start(bf16[32,4096]{1,0:T(8,128)(2,1)S(1)} %get-tuple-element.50), channel_id=1, source_target_pairs={{0,16},{2,18},{4,20},{6,22},{8,24},{10,26},{12,28},{14,30},{16,0},... | collective-permute-start | bytes 786440 | tf_op jit(solution)/shard_map/ppermute | solution.py:457
  105.7 24.9 %collective-permute-start.18 = (bf16[32,4096]{1,0:T(8,128)(2,1)S(1)}, bf16[32,4096]{1,0:T(8,128)(2,1)S(1)}, u32[]{:S(2)}, u32[]{:S(2)}) collective-permute-start(bf16[32,4096]{1,0:T(8,128)(2,1)S(1)} %get-tuple-element.51), channel_id=1, source_target_pairs={{0,24},{2,26},{4,28},{6,30},{8,0},{10,2},{12,4},{14,6},{16,8},{18,... | collective-permute-start | bytes 786440 | tf_op jit(solution)/shard_map/ppermute | solution.py:457
  109.6 23.4 %collective-permute-start.19 = (bf16[32,4096]{1,0:T(8,128)(2,1)S(1)}, bf16[32,4096]{1,0:T(8,128)(2,1)S(1)}, u32[]{:S(2)}, u32[]{:S(2)}) collective-permute-start(bf16[32,4096]{1,0:T(8,128)(2,1)S(1)} %get-tuple-element.56), channel_id=1, source_target_pairs={{0,8},{2,10},{4,12},{6,14},{8,16},{10,18},{12,20},{14,22},{16,24},... | collective-permute-start | bytes 786440 | tf_op jit(solution)/shard_map/ppermute | solution.py:457
  116.6 14.7 %copy-start.13 = (bf16[160,1792]{1,0:T(8,128)(2,1)}, bf16[160,1792]{1,0:T(8,128)(2,1)S(1)}, u32[]{:S(2)}) copy-start(bf16[160,1792]{1,0:T(8,128)(2,1)S(1)} %collective-permute-done.13) | copy-start | bytes 1720324
  116.6 17.9 %collective-permute-start.14 = (bf16[128,1792]{1,0:T(8,128)(2,1)S(1)}, bf16[128,1792]{1,0:T(8,128)(2,1)S(1)}, u32[]{:S(2)}, u32[]{:S(2)}) collective-permute-start(bf16[128,1792]{1,0:T(8,128)(2,1)S(1)} %copy-done.16), channel_id=1, source_target_pairs={{0,1},{1,0},{2,3},{3,2},{4,5},{5,4},{6,7},{7,6},{8,9},{9,8},{10,11... | collective-permute-start | bytes 1376264 | tf_op jit(solution)/shard_map/ppermute | solution.py:460
  131.3 3.2 %slice-start = ((bf16[160,1792]{1,0:T(8,128)(2,1)}), bf16[128,1792]{1,0:T(8,128)(2,1)S(1)}, s32[]{:S(2)}) async-start(bf16[160,1792]{1,0:T(8,128)(2,1)} %copy-done.13), calls=%async_computation | async-start | bytes 917504 | tf_op jit(solution)/shard_map/slice | solution.py:523
  133.0 1.6 %copy-start.12 = (f32[256,1792]{1,0:T(8,128)S(1)}, f32[256,1792]{1,0:T(8,128)}, u32[]{:S(2)}) copy-start(f32[256,1792]{1,0:T(8,128)} %get-tuple-element.42) | copy-start | bytes 5505028

commit v5 on v4

--- a/solution.py
+++ b/solution.py
@@ -307,50 +307,52 @@
     )(*parts)
 
 
-def forward_body(rank, nz, groups, tenant_ref, place_ref, *refs):
-    cot_refs, refs = refs[:groups], refs[groups:]
-    w_hbm, a_hbm, up_hbm = refs[:3]
-    pieces = refs[3 : 2 * nz + 5]
+def forward_body(nb, rank, nz, tenant_ref, place_ref, cot_ref, w_hbm, a_hbm, up_hbm, *refs):
+    pieces = refs[: 2 * nz + 2]
+    part_ref, dot_ref, low_ref = refs[-12:-9]
     w_ref, a_ref, up_ref, x_ref, acc_ref, low_acc, w_sem, sem, x_sem = refs[-9:]
-    tokens, cols = acc_ref.shape
-    nblk = tokens // BLOCK
-    outs = refs[-11 - (groups - 1) * (nblk // groups) : -9]
-    part_refs, side_ref = outs[:-1], outs[-1]
+    rows, cols = acc_ref.shape
     piece = BLOCK // 4
     depth = w_ref.shape[0]
     steps = STEPS // 2
     db = depth // steps
     z, x, core, first = place_ref[0], place_ref[1], place_ref[2], place_ref[3]
-    moves = [[], []]
-    for n in range(4 * nz):
-        k, fx, fc = n // 4, (n // 2) % 2, n % 2
-        src = pieces[2 * nz + fx].at[pl.ds(k * piece, piece), :] if fc else pieces[2 * k + fx].at[:, :]
-        b = lax.rem(z + (2 * nz - k) - first, nz)
-        row = (b * 4 + (x ^ fx) * 2 + (core ^ fc)) * piece
-        rows = pl.ds(pl.multiple_of(row, piece), piece)
-        for h in range(2):
-            at = pl.ds(h * depth // 2, depth // 2)
-            copy = pltpu.make_async_copy(src.at[:, at], x_ref.at[rows, at], x_sem.at[h, n])
-            moves[h].append(copy)
-    moves[0] += factor_copies(tenant_ref, first, a_hbm, a_ref, sem, 0)
-    late = factor_copies(tenant_ref, first, up_hbm, up_ref, sem, nblk)
-    for copy in moves[0]:
+
+    def each(h, act):
+        at = pl.ds(h * depth // 2, depth // 2)
+        for n in range(4 * nz):
+            k, fx, fc = n // 4, (n // 2) % 2, n % 2
+            src = pieces[2 * nz + fx] if fc else pieces[2 * k + fx]
+            src = src.at[pl.ds(k * piece if fc else 0, piece), at]
+            b = lax.rem(z + (nz - k), nz) - first
+
+            @pl.when(jnp.logical_and(b >= 0, b < nb))
+            def _():
+                row = (b * 4 + (x ^ fx) * 2 + (core ^ fc)) * piece
+                dst = pl.ds(pl.multiple_of(row, piece), piece)
+                act(pltpu.make_async_copy(src, x_ref.at[dst, at], x_sem.at[h, n]))
+
+    copies = factor_copies(tenant_ref, first, a_hbm, a_ref, sem, 0)
+    late = factor_copies(tenant_ref, first, up_hbm, up_ref, sem, nb)
+    each(0, lambda copy: copy.start())
+    for copy in copies:
         copy.start()
     for i in range(AHEAD):
         weight_copy(w_hbm, w_ref, w_sem, i).start()
-    for copy in moves[1] + late:
+    each(1, lambda copy: copy.start())
+    for copy in late:
         copy.start()
     acc_ref[...] = jnp.zeros_like(acc_ref)
     low_acc[...] = jnp.zeros_like(low_acc)
-    side_ref[...] = jnp.zeros_like(side_ref)
+    for copy in copies:
+        copy.wait()
 
     def block(i, carry):
         for h in range(2):
 
             @pl.when(i == h * (steps // 2))
             def _():
-                for copy in moves[h]:
-                    copy.wait()
+                each(h, lambda copy: copy.wait())
 
         weight_block(w_hbm, w_ref, w_sem, i, steps)
         at = pl.ds(pl.multiple_of(i * db, db), db)
@@ -364,76 +366,55 @@
     owner = lax.broadcasted_iota(jnp.int32, low.shape, 0) // rank
     block_of = lax.broadcasted_iota(jnp.int32, low.shape, 1) // BLOCK
     low = jnp.where(owner == block_of, low, 0.0)
-    side_ref[:rank, :tokens] = jnp.sum(low.reshape(nblk, rank, tokens), axis=0)
+    low_ref[...] = jnp.sum(low.reshape(nb, rank, rows), axis=0)
     hi = low.astype(BF16).astype(F32)
     lowcat = jnp.concatenate([hi, low - hi], axis=0).T.astype(BF16)
     for copy in late:
         copy.wait()
     up = up_ref[...]
     up = jnp.concatenate([up, up], axis=0)
-    size = nblk // groups
-    for i in range(nblk):
-        rows = slice(i * BLOCK, (i + 1) * BLOCK)
-        here = slice(i % size * BLOCK, (i % size + 1) * BLOCK)
-        part = acc_ref[rows, :] + jnp.dot(lowcat[rows, :], up, preferred_element_type=F32)
-        if i < size:
-            part_refs[0][here, :] = part
-        else:
-            part_refs[1 + i - size][:BLOCK, :] = part.astype(BF16)
-        product = part * cot_refs[i // size][here, :].astype(F32)
-        side_ref[rank + i : rank + i + 1, :cols] = jnp.sum(product, axis=0, keepdims=True)
-    if groups > 1:
-        out = part_refs[1]
-        out[BLOCK:, :] = jnp.zeros((out.shape[0] - BLOCK, cols), BF16)
-        low, dots = side_ref[:rank, :tokens], side_ref[rank:, :cols]
-        packed = []
-        for n in range(3):
-            out[BLOCK : BLOCK + rank, n * tokens : (n + 1) * tokens] = low.astype(BF16)
-            low = low - low.astype(BF16).astype(F32)
-            packed.append(dots.astype(BF16).astype(F32))
-            dots = dots - packed[-1]
-        packed.append(jnp.zeros((out.shape[0] - BLOCK - rank - 3 * nblk, cols), F32))
-        out[BLOCK + rank :, :] = jnp.concatenate(packed, axis=0).astype(BF16)
-
-
-def forward(tenant, place, weight, cots, down, up, pieces, nz, deps):
+    for i in range(nb):
+        here = slice(i * BLOCK, (i + 1) * BLOCK)
+        part = acc_ref[here, :] + jnp.dot(lowcat[here, :], up, preferred_element_type=F32)
+        part_ref[here, :] = part.astype(part_ref.dtype)
+        product = part * cot_ref[here, :].astype(F32)
+        dot_ref[i : i + 1, :] = jnp.sum(product, axis=0, keepdims=True)
+
+
+def forward(tenant, place, weight, cot, down, up, pieces, nz, out_dtype, deps):
     depth, cols = weight.shape
-    tokens = tenant.shape[0]
-    nblk = tokens // BLOCK
+    rows = cot.shape[0]
+    nb = rows // BLOCK
     rank = down.shape[1]
-    groups = len(cots)
-    size = nblk // groups
-    shapes = [jax.ShapeDtypeStruct((size * BLOCK, cols), F32)]
-    for i in range(nblk - size):
-        extra = 0 if i else -(-(rank + 3 * nblk) // 16) * 16
-        shapes += [jax.ShapeDtypeStruct((BLOCK + extra, cols), BF16)]
-    shapes += [jax.ShapeDtypeStruct((rank + nblk, max(cols, tokens)), F32)]
+    shapes = (
+        jax.ShapeDtypeStruct((rows, cols), out_dtype),
+        jax.ShapeDtypeStruct((nb, cols), F32),
+        jax.ShapeDtypeStruct((rank, rows), F32),
+    )
     return pl.pallas_call(
-        functools.partial(forward_body, rank, nz, groups),
+        functools.partial(forward_body, nb, rank, nz),
         out_shape=shapes,
         grid_spec=pltpu.PrefetchScalarGridSpec(
             num_scalar_prefetch=2,
             grid=(1,),
-            in_specs=[same_block(cot) for cot in cots]
-            + [IN_HBM] * (3 + len(pieces))
-            + order_specs(deps),
+            in_specs=[same_block(cot)] + [IN_HBM] * (3 + len(pieces)) + order_specs(deps),
             out_specs=[same_block(s) for s in shapes],
             scratch_shapes=[
                 pltpu.VMEM((depth, cols), BF16),
-                pltpu.VMEM((nblk * rank, depth), BF16),
-                pltpu.VMEM((nblk * rank, cols), BF16),
-                pltpu.VMEM((tokens, depth), BF16),
-                pltpu.VMEM((tokens, cols), F32),
-                pltpu.VMEM((nblk * rank, tokens), F32),
+                pltpu.VMEM((nb * rank, depth), BF16),
+                pltpu.VMEM((nb * rank, cols), BF16),
+                pltpu.VMEM((rows, depth), BF16),
+                pltpu.VMEM((rows, cols), F32),
+                pltpu.VMEM((nb * rank, rows), F32),
                 pltpu.SemaphoreType.DMA((PARTS,)),
-                pltpu.SemaphoreType.DMA((2 * nblk,)),
+                pltpu.SemaphoreType.DMA((2 * nb,)),
                 pltpu.SemaphoreType.DMA((2, 4 * nz)),
             ],
         ),
         compiler_params=PARAMS,
         cost_estimate=COST,
         name="forward",
-    )(tenant, place, *cots, weight, down, up, *pieces, *deps)
+    )(tenant, place, cot, weight, down, up, *pieces, *deps)
 
 
 def shards(inputs, weight, adapter_down_factors, adapter_up_factors, magnitude, cotangent, tenant):
@@ -462,7 +443,7 @@
     def place(*firsts):
         return jnp.stack([z, x, core, *firsts]).astype(jnp.int32)
 
-    pair = row_count == 2 and 3 * tokens <= cols
+    pair = row_count == 2
 
     def once(value, other):
         return lax.optimization_barrier((value, other))[0]
@@ -504,29 +485,32 @@
         return made[0], move(made[1], 0, 1, 0)
 
     if pair:
-        other_x(nz - 1, nsq)
-        for k in range(1, nz - 2):
-            other_x(k, nsq_b)
         ours = gradient(0, [cots[1]])
-        other_x(nz - 2, ours[0])
+        for k in [nz - 1] + list(range(1, nz - 1)):
+            other_x(k, ours[0])
         core_z = other_core(along_z)
         near = across_x(cross_core(ours, []))
-        theirs = gradient(1, [near[0], core_z, along_x[nz - 2]])
+        theirs = gradient(1, [near[0], core_z])
         along_x = [along_x[k] for k in range(nz)]
+        along_x[nz - 2] = once(along_x[nz - 2], theirs[0])
         core_x = other_core(along_x)
         far = cross_core(theirs, [core_x])
         pieces = [piece for both in zip(along_z, along_x) for piece in both] + [core_z, core_x]
-        part, first, *away, side = forward(
-            tenant, places[0], weight, cots, down, up, pieces, nz, [far[0]]
-        )
-        first = swap(first)
-        arrived = [first[:BLOCK]] + [swap(once(block, first)) for block in away]
-        finals = cross_x([near, across_x(far)], [side])
-        first = once(first, (finals[nz // 2], finals[nz - 1]))[BLOCK:].astype(F32)
-        low = [first[:rank, i * tokens : (i + 1) * tokens] for i in range(3)]
-        dots = [first[rank + i * nblk : rank + (i + 1) * nblk] for i in range(3)]
-        low = side[:rank, :tokens] + jnp.roll(low[0] + low[1] + low[2], rows_row, axis=1)
-        dots = side[rank:, :cols] + jnp.roll(dots[0] + dots[1] + dots[2], blocks_mine, axis=0)
+
+        def project(g, out_dtype, deps):
+            return forward(
+                tenant, places[g], weight, cots[g], down, up, pieces, nz, out_dtype, deps
+            )
+
+        away, dots_away, low_away = project(1, BF16, [far[0]])
+        arrived = swap(away)
+        finals = cross_x([near, across_x(far)], [dots_away])
+        part, dots_here, low_here = project(0, F32, [finals[0]])
+        dots = jnp.concatenate([dots_here, dots_away], axis=0)
+        low = jnp.concatenate([low_here, low_away], axis=1)
+        late = (finals[nz // 2], finals[nz - 1])
+        dots = dots + jnp.roll(swap(once(dots, late)), blocks_mine, axis=0)
+        low = low + jnp.roll(swap(once(low, late)), rows_row, axis=1)
         parts = [ours, theirs]
     else:
         ours = gradient(0, [])
@@ -536,9 +520,11 @@
         along_x = [along_x[k] for k in range(nz)]
         pieces = [piece for both in zip(along_z, along_x) for piece in both]
         pieces += [other_core(along_z), other_core(along_x)]
-        part, side = forward(tenant, places[0], weight, cots, down, up, pieces, nz, [])
+        part, dots, low = forward(
+            tenant, places[0], weight, cots[0], down, up, pieces, nz, F32, []
+        )
         finals = cross_x([near], [])
-        low, dots = lax.psum((side[:rank, :tokens], side[rank:, :cols]), "row")
+        low, dots = lax.psum((low, dots), "row")
         parts = [ours]
 
     scales = jnp.concatenate([group[0] for group in parts], axis=0)
@@ -566,7 +552,7 @@
         grad_m = grad_m + functools.reduce(jnp.add, [group[:, i] for i in range(size)])
     grad_inputs = add_z([once(finals[0], grad_b)] + finals[1:])
     if pair:
-        pre = part + jnp.concatenate(arrived, axis=0).astype(F32)
+        pre = part + arrived.astype(F32)
         scale_mine = parts[0][0]
     else:
         pre = lax.psum_scatter(part, "row", scatter_dimension=0, tiled=True)

time: 136 us -> 119 us (0.88)
  waiting for transfers between devices: 48.3 us -> 17.2 us
  Pallas kernels: 55.6 us -> 62.3 us
  starting transfers between devices: 18.1 us -> 24.1 us
  local copies, waits for them, and re-layouts: 7.17 us -> 8.81 us
    ppermute x16, waiting for transfers between devices: 41.3 us -> 11.9 us  [move(): return lax.ppermute(value, 'col', perm)]
    pallas_call x1 -> x2, Pallas kernels: 17.1 us -> 25 us  [forward(): pl.pallas_call(functools.partial(forward_body, nb, rank, nz), out_shape=s...]
    ppermute x16, starting transfers between devices: 14.9 us -> 18.4 us  [move(): return lax.ppermute(value, 'col', perm)]
    ppermute x4 -> x5, starting transfers between devices: 3.24 us -> 5.74 us  [swap(): return lax.ppermute(value, 'row', [(0, 1), (1, 0)])]
    ppermute x4 -> x5, waiting for transfers between devices: 6.99 us -> 5.27 us  [swap(): return lax.ppermute(value, 'row', [(0, 1), (1, 0)])]
    unnamed x34 -> x41, local copies, waits for them, and re-layouts: 6.84 us -> 8.49 us
  transfers between devices with their start and end apart: 20 -> 21, of which waited for: 10 -> 7; matrix products, arithmetic and copies ran while one was open for 4% -> 3% of each run, Pallas kernels for 41% -> 52%
where the time goes in v5:
time: 119 us
  Pallas kernels  62.3 us (52%)
  starting transfers between devices  24.1 us (20%)
  waiting for transfers between devices  17.2 us (14%)
  local copies, waits for them, and re-layouts  8.81 us (7%)
  other arithmetic  3.47 us (3%)
  matrix products  2.05 us (2%)
    pallas_call x2, Pallas kernels, forward(): pl.pallas_call(functools.partial(forward_body, nb, rank, nz), out_shape=s...  25 us
    pallas_call x2, Pallas kernels, input_gradient(): pl.pallas_call(functools.partial(grad_body, nb, rank), out_shape=shapes,...  20 us
    ppermute x16, starting transfers between devices, move(): return lax.ppermute(value, 'col', perm)  18.4 us
    ppermute x16, waiting for transfers between devices, move(): return lax.ppermute(value, 'col', perm)  11.9 us
    pallas_call x1, Pallas kernels, partial_norms(): pl.pallas_call(functools.partial(norm_body, nblk, rank), out_shape=shape,...  9.25 us
    unnamed x41, local copies, waits for them, and re-layouts  8.49 us
    ppermute x5, starting transfers between devices, swap(): return lax.ppermute(value, 'row', [(0, 1), (1, 0)])  5.74 us
    ppermute x5, waiting for transfers between devices, swap(): return lax.ppermute(value, 'row', [(0, 1), (1, 0)])  5.27 us
  transfers between devices with their start and end apart: 21, of which 7 were waited for; matrix products, arithmetic and copies ran while one was open for 3% of the time, Pallas kernels for 52%

profile of v5, /device:TPU:8, one launch (start us, length us, event | category | flops | bytes accessed | tf_op | source)
XLA Modules:
  0.0 118.9 jit_solution(3063544639576276906)
XLA Ops:
  0.6 1.6 %collective-permute-start.3 = (bf16[256,1792]{1,0:T(8,128)(2,1)}, bf16[256,1792]{1,0:T(8,128)(2,1)S(1)}, u32[]{:S(2)}, u32[]{:S(2)}) collective-permute-start(bf16[256,1792]{1,0:T(8,128)(2,1)} %cot_ref.3), channel_id=1, source_target_pairs={{0,1},{1,0},{2,3},{3,2},{4,5},{5,4},{6,7},{7,6},{8,9},{9,8},{10,11... | collective-permute-start | bytes 2752520 | tf_op jit(solution)/shard_map/ppermute | solution.py:441
  2.2 1.5 %collective-permute-start = (bf16[32,4096]{1,0:T(8,128)(2,1)}, bf16[32,4096]{1,0:T(8,128)(2,1)S(1)}, u32[]{:S(2)}, u32[]{:S(2)}) collective-permute-start(bf16[32,4096]{1,0:T(8,128)(2,1)} %refs_0_.7), channel_id=1, source_target_pairs={{0,4},{2,6},{4,0},{6,2},{8,12},{10,14},{12,8},{14,10},{16,20},{18,... | collective-permute-start | bytes 786440 | tf_op jit(solution)/shard_map/ppermute | solution.py:438
  3.7 1.6 %collective-permute-start.1 = (bf16[32,4096]{1,0:T(8,128)(2,1)}, bf16[32,4096]{1,0:T(8,128)(2,1)S(1)}, u32[]{:S(2)}, u32[]{:S(2)}) collective-permute-start(bf16[32,4096]{1,0:T(8,128)(2,1)} %refs_0_.7), channel_id=1, source_target_pairs={{0,8},{2,10},{4,12},{6,14},{8,16},{10,18},{12,20},{14,22},{16,24},... | collective-permute-start | bytes 786440 | tf_op jit(solution)/shard_map/ppermute | solution.py:438
  5.3 1.2 %collective-permute-start.5 = (bf16[32,4096]{1,0:T(8,128)(2,1)}, bf16[32,4096]{1,0:T(8,128)(2,1)S(1)}, u32[]{:S(2)}, u32[]{:S(2)}) collective-permute-start(bf16[32,4096]{1,0:T(8,128)(2,1)} %refs_0_.7), channel_id=1, source_target_pairs={{0,16},{2,18},{4,20},{6,22},{8,24},{10,26},{12,28},{14,30},{16,0},... | collective-permute-start | bytes 786440 | tf_op jit(solution)/shard_map/ppermute | solution.py:438
  6.5 1.8 %collective-permute-start.8 = (bf16[32,4096]{1,0:T(8,128)(2,1)}, bf16[32,4096]{1,0:T(8,128)(2,1)S(1)}, u32[]{:S(2)}, u32[]{:S(2)}) collective-permute-start(bf16[32,4096]{1,0:T(8,128)(2,1)} %refs_0_.7), channel_id=1, source_target_pairs={{0,24},{2,26},{4,28},{6,30},{8,0},{10,2},{12,4},{14,6},{16,8},{18,... | collective-permute-start | bytes 786440 | tf_op jit(solution)/shard_map/ppermute | solution.py:438
  8.4 1.2 copy-done
  9.6 0.7 copy-done.14
  10.3 9.2 %partial_norms.1.nsq_a = f32[4,1792]{1,0:T(4,128)S(1)} custom-call(s32[512]{0:T(512)S(1)} %copy-done.14, bf16[4096,1792]{1,0:T(8,128)(2,1)} %w_hbm.5, bf16[16,16,4096]{2,1,0:T(8,128)(2,1)} %a_hbm.5, bf16[16,16,1792]{2,1,0:T(8,128)(2,1)S(1)} %copy-done), custom_call_target="tpu_custom_call" | custom-call | flops 1000 | bytes 1000 | tf_op jit(solution)/shard_map/partial_norms/pallas_call | solution.py:115
  19.5 0.6 collective-permute-start.2
  20.2 3.4 %collective-permute-done.2.nsq_b = f32[4,1792]{1,0:T(4,128)S(1)} collective-permute-done((f32[4,1792]{1,0:T(4,128)S(1)}, f32[4,1792]{1,0:T(4,128)S(1)}, u32[]{:S(2)}, u32[]{:S(2)}) %collective-permute-start.2) | collective-permute-done | bytes 28704 | tf_op jit(solution)/shard_map/ppermute | solution.py:441
  23.6 0.9 copy-done.1
  24.5 9.9 %input_gradient.2 = (f32[2,1792]{1,0:T(2,128)S(1)}, bf16[256,1792]{1,0:T(8,128)(2,1)S(1)}, f32[128,4096]{1,0:T(8,128)}, bf16[128,4096]{1,0:T(8,128)(2,1)}) custom-call(s32[512]{0:T(512)S(1)} %copy-done.15, s32[4]{0:T(128)S(1)} %pad_add_fusion.place_ref, bf16[256,1792]{1,0:T(8,128)(2,1)S(1)} %copy-done.5, f32[4,1792]{1,0:T(4,128)S(1)} %partial_norms.1.nsq_a, ...), custom_call_target="tpu_custom_call" | custom-call | flops 1000 | bytes 1000 | tf_op jit(solution)/shard_map/input_gradient/pallas_call | solution.py:200
  34.7 0.5 collective-permute-start.9
  35.3 1.5 %collective-permute-start.6 = (bf16[32,4096]{1,0:T(8,128)(2,1)S(1)}, bf16[32,4096]{1,0:T(8,128)(2,1)S(1)}, u32[]{:S(2)}, u32[]{:S(2)}) collective-permute-start(bf16[32,4096]{1,0:T(8,128)(2,1)S(1)} %collective-permute-done.5.refs_4_), channel_id=1, source_target_pairs={{0,4},{2,6},{4,0},{6,2},{8,12},{10,14},{12,8},{14,10},{16,20},{18,... | collective-permute-start | bytes 786440 | tf_op jit(solution)/shard_map/ppermute | solution.py:438
  36.8 0.5 collective-permute-start.4
  37.3 1.5 %collective-permute-start.10 = (bf16[32,4096]{1,0:T(8,128)(2,1)S(1)}, bf16[32,4096]{1,0:T(8,128)(2,1)S(1)}, u32[]{:S(2)}, u32[]{:S(2)}) collective-permute-start(bf16[32,4096]{1,0:T(8,128)(2,1)S(1)} %collective-permute-done.8.refs_6_), channel_id=1, source_target_pairs={{0,4},{2,6},{4,0},{6,2},{8,12},{10,14},{12,8},{14,10},{16,20},{18,... | collective-permute-start | bytes 786440 | tf_op jit(solution)/shard_map/ppermute | solution.py:438
  38.8 1.0 copy-done.19
  39.8 2.0 %add_core.2 = (f32[64,4096]{1,0:T(8,128)S(1)}, bf16[64,4096]{1,0:T(8,128)(2,1)S(1)}) custom-call(f32[128,4096]{1,0:T(8,128)} %get-tuple-element.38.keep_ref, bf16[128,4096]{1,0:T(8,128)(2,1)} %copy-done.19), custom_call_target="tpu_custom_call" | custom-call | flops 1000 | bytes 1000 | tf_op jit(solution)/shard_map/add_core/pallas_call | solution.py:237
  41.8 1.0 copy-done.3
  42.7 1.0 copy-done.16
  43.7 10.1 %input_gradient.3 = (f32[2,1792]{1,0:T(2,128)S(1)}, bf16[256,1792]{1,0:T(8,128)(2,1)S(1)}, f32[128,4096]{1,0:T(8,128)}, bf16[128,4096]{1,0:T(8,128)(2,1)}) custom-call(s32[512]{0:T(512)S(1)} %copy-done.15, s32[4]{0:T(128)S(1)} %get-tuple-element.66.place_ref, bf16[256,1792]{1,0:T(8,128)(2,1)S(1)} %copy-done.2, f32[4,1792]{1,0:T(4,128)S(1)} %partial_norms.1.nsq_a, ...), custom_call_target="tpu_custom_call" | custom-call | flops 1000 | bytes 1000 | tf_op jit(solution)/shard_map/input_gradient/pallas_call | solution.py:200
  53.8 0.9 copy-done.12
  54.8 1.1 pad_maximum_fusion.1
  55.9 0.5 collective-permute-start.13
  56.7 1.5 %collective-permute-start.12 = (bf16[64,4096]{1,0:T(8,128)(2,1)S(1)}, bf16[64,4096]{1,0:T(8,128)(2,1)S(1)}, u32[]{:S(2)}, u32[]{:S(2)}) collective-permute-start(bf16[64,4096]{1,0:T(8,128)(2,1)S(1)} %get-tuple-element.44), channel_id=1, source_target_pairs={{0,4},{2,6},{4,0},{6,2},{8,12},{10,14},{12,8},{14,10},{16,20},{18,... | collective-permute-start | bytes 1572872 | tf_op jit(solution)/shard_map/ppermute | solution.py:438
  58.2 0.7 collective-permute-done.11.refs_0_.refs_9_
  58.9 1.5 %collective-permute-done.13.recv_ref = bf16[128,4096]{1,0:T(8,128)(2,1)} collective-permute-done((bf16[128,4096]{1,0:T(8,128)(2,1)}, bf16[128,4096]{1,0:T(8,128)(2,1)}, u32[]{:S(2)}, u32[]{:S(2)}) %collective-permute-start.13) | collective-permute-done | bytes 1048608 | tf_op jit(solution)/shard_map/ppermute | solution.py:438
  60.4 2.7 %add_core.3 = (f32[64,4096]{1,0:T(8,128)S(1)}, bf16[64,4096]{1,0:T(8,128)(2,1)}) custom-call(f32[128,4096]{1,0:T(8,128)} %get-tuple-element.45.keep_ref, bf16[128,4096]{1,0:T(8,128)(2,1)} %collective-permute-done.13.recv_ref, bf16[128,4096]{1,0:T(8,128)(2,1)} %collective-permute-done.11.refs_0_.refs_9_), custom_call_target="tpu_custom_call" | custom-call | flops 1000 | bytes 1000 | tf_op jit(solution)/shard_map/add_core/pallas_call | solution.py:237
  63.1 1.0 copy-done.4
  64.1 1.5 %collective-permute-start.14 = (bf16[64,4096]{1,0:T(8,128)(2,1)}, bf16[64,4096]{1,0:T(8,128)(2,1)}, u32[]{:S(2)}, u32[]{:S(2)}) collective-permute-start(bf16[64,4096]{1,0:T(8,128)(2,1)} %get-tuple-element.48), channel_id=1, source_target_pairs={{0,4},{2,6},{4,0},{6,2},{8,12},{10,14},{12,8},{14,10},{16,20},{18,... | collective-permute-start | bytes 1572872 | tf_op jit(solution)/shard_map/ppermute | solution.py:438
  65.7 12.4 %forward.2 = (bf16[256,1792]{1,0:T(8,128)(2,1)}, f32[2,1792]{1,0:T(2,128)S(1)}, f32[16,256]{1,0:T(8,128)S(1)}) custom-call(s32[512]{0:T(512)S(1)} %copy-done.15, s32[4]{0:T(128)S(1)} %get-tuple-element.66.place_ref, bf16[256,1792]{1,0:T(8,128)(2,1)} %copy-done.1, bf16[4096,1792]{1,0:T(8,128)(2,1)} %w_hbm.5, bf16[16,16,4096]{2,1,0:T(8,128)(2,1)} %a_hbm.5, ...), custom_call_target="tpu_custom_call" | custom-call | flops 1000 | bytes 1000 | tf_op jit(solution)/shard_map/forward/pallas_call | solution.py:394
  78.1 1.6 %collective-permute-start.15 = (bf16[256,1792]{1,0:T(8,128)(2,1)}, bf16[256,1792]{1,0:T(8,128)(2,1)S(1)}, u32[]{:S(2)}, u32[]{:S(2)}) collective-permute-start(bf16[256,1792]{1,0:T(8,128)(2,1)} %get-tuple-element.52), channel_id=1, source_target_pairs={{0,1},{1,0},{2,3},{3,2},{4,5},{5,4},{6,7},{7,6},{8,9},{9,8},{10,11... | collective-permute-start | bytes 2752520 | tf_op jit(solution)/shard_map/ppermute | solution.py:441
  79.7 2.2 %collective-permute-done.14.refs_3_ = bf16[64,4096]{1,0:T(8,128)(2,1)} collective-permute-done((bf16[64,4096]{1,0:T(8,128)(2,1)}, bf16[64,4096]{1,0:T(8,128)(2,1)}, u32[]{:S(2)}, u32[]{:S(2)}) %collective-permute-start.14) | collective-permute-done | bytes 524320 | tf_op jit(solution)/shard_map/ppermute | solution.py:438
  81.8 2.5 %add_x.1 = (f32[32,4096]{1,0:T(8,128)S(1)}, bf16[32,4096]{1,0:T(8,128)(2,1)S(1)}, bf16[32,4096]{1,0:T(8,128)(2,1)S(1)}, bf16[32,4096]{1,0:T(8,128)(2,1)S(1)}) custom-call(s32[5]{0:T(128)S(1)} %stack.39.place_ref, f32[64,4096]{1,0:T(8,128)} %copy-done.3, bf16[64,4096]{1,0:T(8,128)(2,1)S(1)} %collective-permute-done.12.refs_1_, f32[64,4096]{1,0:T(8,128)} %copy-done.4, ...), custom_call_target="tpu_custom_call" | custom-call | flops 1000 | bytes 1000 | tf_op jit(solution)/shard_map/add_x/pallas_call | solution.py:276
  84.3 0.8 copy-done.7
  85.1 2.6 %collective-permute-start.16 = (bf16[32,4096]{1,0:T(8,128)(2,1)S(1)}, bf16[32,4096]{1,0:T(8,128)(2,1)S(1)}, u32[]{:S(2)}, u32[]{:S(2)}) collective-permute-start(bf16[32,4096]{1,0:T(8,128)(2,1)S(1)} %get-tuple-element.55), channel_id=1, source_target_pairs={{0,16},{2,18},{4,20},{6,22},{8,24},{10,26},{12,28},{14,30},{16,0},... | collective-permute-start | bytes 786440 | tf_op jit(solution)/shard_map/ppermute | solution.py:438
  87.7 0.4 collective-permute-start.17
  88.2 12.7 %forward.3 = (f32[256,1792]{1,0:T(8,128)}, f32[2,1792]{1,0:T(2,128)S(1)}, f32[16,256]{1,0:T(8,128)S(1)}) custom-call(s32[512]{0:T(512)S(1)} %copy-done.15, s32[4]{0:T(128)S(1)} %pad_add_fusion.place_ref, bf16[256,1792]{1,0:T(8,128)(2,1)} %cot_ref.3, bf16[4096,1792]{1,0:T(8,128)(2,1)} %w_hbm.5, bf16[16,16,4096]{2,1,0:T(8,128)(2,1)} %a_hbm.5, ...), custom_call_target="tpu_custom_call" | custom-call | flops 1000 | bytes 1000 | tf_op jit(solution)/shard_map/forward/pallas_call | solution.py:394
  100.8 1.6 %collective-permute-start.19 = (bf16[32,4096]{1,0:T(8,128)(2,1)S(1)}, bf16[32,4096]{1,0:T(8,128)(2,1)S(1)}, u32[]{:S(2)}, u32[]{:S(2)}) collective-permute-start(bf16[32,4096]{1,0:T(8,128)(2,1)S(1)} %get-tuple-element.61), channel_id=1, source_target_pairs={{0,8},{2,10},{4,12},{6,14},{8,16},{10,18},{12,20},{14,22},{16,24},... | collective-permute-start | bytes 786440 | tf_op jit(solution)/shard_map/ppermute | solution.py:438
  102.5 1.4 %collective-permute-done.16.refs_2_ = bf16[32,4096]{1,0:T(8,128)(2,1)S(1)} collective-permute-done((bf16[32,4096]{1,0:T(8,128)(2,1)S(1)}, bf16[32,4096]{1,0:T(8,128)(2,1)S(1)}, u32[]{:S(2)}, u32[]{:S(2)}) %collective-permute-start.16) | collective-permute-done | bytes 262176 | tf_op jit(solution)/shard_map/ppermute | solution.py:438
  103.8 6.2 %collective-permute-done.17.refs_3_ = bf16[32,4096]{1,0:T(8,128)(2,1)S(1)} collective-permute-done((bf16[32,4096]{1,0:T(8,128)(2,1)S(1)}, bf16[32,4096]{1,0:T(8,128)(2,1)S(1)}, u32[]{:S(2)}, u32[]{:S(2)}) %collective-permute-start.17) | collective-permute-done | bytes 262176 | tf_op jit(solution)/shard_map/ppermute | solution.py:438
  110.0 2.0 %collective-permute-start.18 = (f32[16,512]{1,0:T(8,128)S(1)}, f32[16,512]{1,0:T(8,128)S(1)}, u32[]{:S(2)}, u32[]{:S(2)}) collective-permute-start(f32[16,512]{1,0:T(8,128)S(1)} %constant_dynamic-update-slice_fusion), channel_id=1, source_target_pairs={{0,1},{1,0},{2,3},{3,2},{4,5},{5,4},{6,7},{7,6},{8,9},{9,8},{10,11... | collective-permute-start | bytes 98312 | tf_op jit(solution)/shard_map/ppermute | solution.py:441
  112.0 1.8 %collective-permute-done.20 = f32[4,1792]{1,0:T(4,128)S(1)} collective-permute-done((f32[4,1792]{1,0:T(4,128)S(1)}, f32[4,1792]{1,0:T(4,128)S(1)}, u32[]{:S(2)}, u32[]{:S(2)}) %collective-permute-start.20) | collective-permute-done | bytes 28704 | tf_op jit(solution)/shard_map/ppermute | solution.py:441
  114.1 0.7 fusion.3
  114.9 0.4 fusion.9
  115.3 1.6 %convolution_add_fusion = f32[256,1792]{1,0:T(8,128)} fusion(f32[256,1792]{1,0:T(8,128)S(1)} %fusion.9, bf16[256,256]{1,0:T(8,128)(2,1)S(1)} %bitcast.29, bf16[256,1792]{1,0:T(8,128)(2,1)S(1)} %copy-done.11), kind=kOutput, calls=%fused_computation | convolution fusion | flops 235339776 | bytes 4718592 | tf_op jit(solution)/shard_map/dot_general | solution.py:545
  116.9 0.8 add_z.1
  117.8 1.1 fusion
  (69 shorter events, 1.1 us)
Async XLA Ops:
  0.6 23.0 %collective-permute-start.3 = (bf16[256,1792]{1,0:T(8,128)(2,1)}, bf16[256,1792]{1,0:T(8,128)(2,1)S(1)}, u32[]{:S(2)}, u32[]{:S(2)}) collective-permute-start(bf16[256,1792]{1,0:T(8,128)(2,1)} %cot_ref.3), channel_id=1, source_target_pairs={{0,1},{1,0},{2,3},{3,2},{4,5},{5,4},{6,7},{7,6},{8,9},{9,8},{10,11... | collective-permute-start | bytes 2752520 | tf_op jit(solution)/shard_map/ppermute | solution.py:441
  2.2 17.3 %collective-permute-start = (bf16[32,4096]{1,0:T(8,128)(2,1)}, bf16[32,4096]{1,0:T(8,128)(2,1)S(1)}, u32[]{:S(2)}, u32[]{:S(2)}) collective-permute-start(bf16[32,4096]{1,0:T(8,128)(2,1)} %refs_0_.7), channel_id=1, source_target_pairs={{0,4},{2,6},{4,0},{6,2},{8,12},{10,14},{12,8},{14,10},{16,20},{18,... | collective-permute-start | bytes 786440 | tf_op jit(solution)/shard_map/ppermute | solution.py:438
  3.7 30.8 %collective-permute-start.1 = (bf16[32,4096]{1,0:T(8,128)(2,1)}, bf16[32,4096]{1,0:T(8,128)(2,1)S(1)}, u32[]{:S(2)}, u32[]{:S(2)}) collective-permute-start(bf16[32,4096]{1,0:T(8,128)(2,1)} %refs_0_.7), channel_id=1, source_target_pairs={{0,8},{2,10},{4,12},{6,14},{8,16},{10,18},{12,20},{14,22},{16,24},... | collective-permute-start | bytes 786440 | tf_op jit(solution)/shard_map/ppermute | solution.py:438
  5.3 29.2 %collective-permute-start.5 = (bf16[32,4096]{1,0:T(8,128)(2,1)}, bf16[32,4096]{1,0:T(8,128)(2,1)S(1)}, u32[]{:S(2)}, u32[]{:S(2)}) collective-permute-start(bf16[32,4096]{1,0:T(8,128)(2,1)} %refs_0_.7), channel_id=1, source_target_pairs={{0,16},{2,18},{4,20},{6,22},{8,24},{10,26},{12,28},{14,30},{16,0},... | collective-permute-start | bytes 786440 | tf_op jit(solution)/shard_map/ppermute | solution.py:438
  6.5 28.1 %collective-permute-start.8 = (bf16[32,4096]{1,0:T(8,128)(2,1)}, bf16[32,4096]{1,0:T(8,128)(2,1)S(1)}, u32[]{:S(2)}, u32[]{:S(2)}) collective-permute-start(bf16[32,4096]{1,0:T(8,128)(2,1)} %refs_0_.7), channel_id=1, source_target_pairs={{0,24},{2,26},{4,28},{6,30},{8,0},{10,2},{12,4},{14,6},{16,8},{18,... | collective-permute-start | bytes 786440 | tf_op jit(solution)/shard_map/ppermute | solution.py:438
  8.4 1.2 copy-start
  9.6 0.7 copy-start.14
  10.3 14.3 %copy-start.5 = (bf16[256,1792]{1,0:T(8,128)(2,1)S(1)}, bf16[256,1792]{1,0:T(8,128)(2,1)}, u32[]{:S(2)}) copy-start(bf16[256,1792]{1,0:T(8,128)(2,1)} %cot_ref.3) | copy-start | bytes 2752516
  10.3 14.3 %copy-start.9 = (f32[16,1792]{1,0:T(8,128)S(1)}, f32[16,1792]{1,0:T(8,128)}, u32[]{:S(2)}) copy-start(f32[16,1792]{1,0:T(8,128)} %mag_ref.3) | copy-start | bytes 344068
  10.3 14.3 %copy-start.15 = (s32[512]{0:T(512)S(1)}, s32[512]{0:T(512)}, u32[]{:S(2)}) copy-start(s32[512]{0:T(512)} %tenant_ref.9) | copy-start | bytes 6148
  19.5 4.1 %collective-permute-start.2 = (f32[4,1792]{1,0:T(4,128)S(1)}, f32[4,1792]{1,0:T(4,128)S(1)}, u32[]{:S(2)}, u32[]{:S(2)}) collective-permute-start(f32[4,1792]{1,0:T(4,128)S(1)} %partial_norms.1.nsq_a), channel_id=1, source_target_pairs={{0,1},{1,0},{2,3},{3,2},{4,5},{5,4},{6,7},{7,6},{8,9},{9,8},{10,11... | collective-permute-start | bytes 86024 | tf_op jit(solution)/shard_map/ppermute | solution.py:441
  20.2 14.4 %copy-start.6 = (bf16[32,4096]{1,0:T(8,128)(2,1)S(1)}, bf16[32,4096]{1,0:T(8,128)(2,1)}, u32[]{:S(2)}) copy-start(bf16[32,4096]{1,0:T(8,128)(2,1)} %refs_0_.7) | copy-start | bytes 786436
  23.6 0.9 copy-start.1
  34.5 4.3 %copy-start.10 = (bf16[256,1792]{1,0:T(8,128)(2,1)}, bf16[256,1792]{1,0:T(8,128)(2,1)S(1)}, u32[]{:S(2)}) copy-start(bf16[256,1792]{1,0:T(8,128)(2,1)S(1)} %get-tuple-element.58) | copy-start | bytes 2752516
  34.5 4.3 %collective-permute-start.7 = (bf16[128,4096]{1,0:T(8,128)(2,1)}, bf16[128,4096]{1,0:T(8,128)(2,1)S(1)}, u32[]{:S(2)}, u32[]{:S(2)}) collective-permute-start(bf16[128,4096]{1,0:T(8,128)(2,1)} %get-tuple-element.39), channel_id=1, source_target_pairs={{0,2},{2,0},{4,6},{6,4},{8,10},{10,8},{12,14},{14,12},{16,18},{18,... | collective-permute-start | bytes 3145736 | tf_op jit(solution)/shard_map/ppermute | solution.py:438
  34.7 9.0 %copy-start.2 = (bf16[256,1792]{1,0:T(8,128)(2,1)S(1)}, bf16[256,1792]{1,0:T(8,128)(2,1)}, u32[]{:S(2)}) copy-start(bf16[256,1792]{1,0:T(8,128)(2,1)} %copy-done.1) | copy-start | bytes 2752516
  34.7 8.0 %collective-permute-start.9 = (bf16[128,4096]{1,0:T(8,128)(2,1)S(1)}, bf16[128,4096]{1,0:T(8,128)(2,1)S(1)}, u32[]{:S(2)}, u32[]{:S(2)}) collective-permute-start(bf16[128,4096]{1,0:T(8,128)(2,1)S(1)} %pad_maximum_fusion), channel_id=1, source_target_pairs={{0,2},{2,0},{4,6},{6,4},{8,10},{10,8},{12,14},{14,12},{16,18},{18,... | collective-permute-start | bytes 3145736 | tf_op jit(solution)/shard_map/ppermute | solution.py:438
  35.3 19.5 %collective-permute-start.6 = (bf16[32,4096]{1,0:T(8,128)(2,1)S(1)}, bf16[32,4096]{1,0:T(8,128)(2,1)S(1)}, u32[]{:S(2)}, u32[]{:S(2)}) collective-permute-start(bf16[32,4096]{1,0:T(8,128)(2,1)S(1)} %collective-permute-done.5.refs_4_), channel_id=1, source_target_pairs={{0,4},{2,6},{4,0},{6,2},{8,12},{10,14},{12,8},{14,10},{16,20},{18,... | collective-permute-start | bytes 786440 | tf_op jit(solution)/shard_map/ppermute | solution.py:438
  36.8 18.0 %collective-permute-start.4 = (bf16[32,4096]{1,0:T(8,128)(2,1)S(1)}, bf16[32,4096]{1,0:T(8,128)(2,1)S(1)}, u32[]{:S(2)}, u32[]{:S(2)}) collective-permute-start(bf16[32,4096]{1,0:T(8,128)(2,1)S(1)} %collective-permute-done.1.refs_2_), channel_id=1, source_target_pairs={{0,4},{2,6},{4,0},{6,2},{8,12},{10,14},{12,8},{14,10},{16,20},{18,... | collective-permute-start | bytes 786440 | tf_op jit(solution)/shard_map/ppermute | solution.py:438
  37.3 17.5 %collective-permute-start.10 = (bf16[32,4096]{1,0:T(8,128)(2,1)S(1)}, bf16[32,4096]{1,0:T(8,128)(2,1)S(1)}, u32[]{:S(2)}, u32[]{:S(2)}) collective-permute-start(bf16[32,4096]{1,0:T(8,128)(2,1)S(1)} %collective-permute-done.8.refs_6_), channel_id=1, source_target_pairs={{0,4},{2,6},{4,0},{6,2},{8,12},{10,14},{12,8},{14,10},{16,20},{18,... | collective-permute-start | bytes 786440 | tf_op jit(solution)/shard_map/ppermute | solution.py:438
  38.8 1.0 copy-start.19
  41.8 1.0 copy-start.3
  42.7 1.0 copy-start.16
  53.8 1.0 copy-start.12
  54.8 8.3 %copy-start.17 = (bf16[32,4096]{1,0:T(8,128)(2,1)}, bf16[32,4096]{1,0:T(8,128)(2,1)S(1)}, u32[]{:S(2)}) copy-start(bf16[32,4096]{1,0:T(8,128)(2,1)S(1)} %collective-permute-done.10.refs_7_) | copy-start | bytes 786436
  55.9 3.0 %collective-permute-start.11 = (bf16[128,4096]{1,0:T(8,128)(2,1)}, bf16[128,4096]{1,0:T(8,128)(2,1)}, u32[]{:S(2)}, u32[]{:S(2)}) collective-permute-start(bf16[128,4096]{1,0:T(8,128)(2,1)} %pad_maximum_fusion.1), channel_id=1, source_target_pairs={{0,2},{2,0},{4,6},{6,4},{8,10},{10,8},{12,14},{14,12},{16,18},{18,... | collective-permute-start | bytes 3145736 | tf_op jit(solution)/shard_map/ppermute | solution.py:438
  55.9 4.5 %collective-permute-start.13 = (bf16[128,4096]{1,0:T(8,128)(2,1)}, bf16[128,4096]{1,0:T(8,128)(2,1)}, u32[]{:S(2)}, u32[]{:S(2)}) collective-permute-start(bf16[128,4096]{1,0:T(8,128)(2,1)} %get-tuple-element.46), channel_id=1, source_target_pairs={{0,2},{2,0},{4,6},{6,4},{8,10},{10,8},{12,14},{14,12},{16,18},{18,... | collective-permute-start | bytes 3145736 | tf_op jit(solution)/shard_map/ppermute | solution.py:438
  56.7 23.0 %collective-permute-start.12 = (bf16[64,4096]{1,0:T(8,128)(2,1)S(1)}, bf16[64,4096]{1,0:T(8,128)(2,1)S(1)}, u32[]{:S(2)}, u32[]{:S(2)}) collective-permute-start(bf16[64,4096]{1,0:T(8,128)(2,1)S(1)} %get-tuple-element.44), channel_id=1, source_target_pairs={{0,4},{2,6},{4,0},{6,2},{8,12},{10,14},{12,8},{14,10},{16,20},{18,... | collective-permute-start | bytes 1572872 | tf_op jit(solution)/shard_map/ppermute | solution.py:438
  63.1 1.0 copy-start.4
  64.1 17.8 %collective-permute-start.14 = (bf16[64,4096]{1,0:T(8,128)(2,1)}, bf16[64,4096]{1,0:T(8,128)(2,1)}, u32[]{:S(2)}, u32[]{:S(2)}) collective-permute-start(bf16[64,4096]{1,0:T(8,128)(2,1)} %get-tuple-element.48), channel_id=1, source_target_pairs={{0,4},{2,6},{4,0},{6,2},{8,12},{10,14},{12,8},{14,10},{16,20},{18,... | collective-permute-start | bytes 1572872 | tf_op jit(solution)/shard_map/ppermute | solution.py:438
  78.1 39.6 %collective-permute-start.15 = (bf16[256,1792]{1,0:T(8,128)(2,1)}, bf16[256,1792]{1,0:T(8,128)(2,1)S(1)}, u32[]{:S(2)}, u32[]{:S(2)}) collective-permute-start(bf16[256,1792]{1,0:T(8,128)(2,1)} %get-tuple-element.52), channel_id=1, source_target_pairs={{0,1},{1,0},{2,3},{3,2},{4,5},{5,4},{6,7},{7,6},{8,9},{9,8},{10,11... | collective-permute-start | bytes 2752520 | tf_op jit(solution)/shard_map/ppermute | solution.py:441
  84.3 0.8 copy-start.7
  85.1 18.7 %collective-permute-start.16 = (bf16[32,4096]{1,0:T(8,128)(2,1)S(1)}, bf16[32,4096]{1,0:T(8,128)(2,1)S(1)}, u32[]{:S(2)}, u32[]{:S(2)}) collective-permute-start(bf16[32,4096]{1,0:T(8,128)(2,1)S(1)} %get-tuple-element.55), channel_id=1, source_target_pairs={{0,16},{2,18},{4,20},{6,22},{8,24},{10,26},{12,28},{14,30},{16,0},... | collective-permute-start | bytes 786440 | tf_op jit(solution)/shard_map/ppermute | solution.py:438
  87.7 22.3 %collective-permute-start.17 = (bf16[32,4096]{1,0:T(8,128)(2,1)S(1)}, bf16[32,4096]{1,0:T(8,128)(2,1)S(1)}, u32[]{:S(2)}, u32[]{:S(2)}) collective-permute-start(bf16[32,4096]{1,0:T(8,128)(2,1)S(1)} %get-tuple-element.56), channel_id=1, source_target_pairs={{0,24},{2,26},{4,28},{6,30},{8,0},{10,2},{12,4},{14,6},{16,8},{18,... | collective-permute-start | bytes 786440 | tf_op jit(solution)/shard_map/ppermute | solution.py:438
  100.8 14.0 %copy-start.13 = (bf16[256,1792]{1,0:T(8,128)(2,1)S(1)}, bf16[256,1792]{1,0:T(8,128)(2,1)}, u32[]{:S(2)}) copy-start(bf16[256,1792]{1,0:T(8,128)(2,1)} %copy-done.12) | copy-start | bytes 2752516
  100.8 16.1 %collective-permute-start.19 = (bf16[32,4096]{1,0:T(8,128)(2,1)S(1)}, bf16[32,4096]{1,0:T(8,128)(2,1)S(1)}, u32[]{:S(2)}, u32[]{:S(2)}) collective-permute-start(bf16[32,4096]{1,0:T(8,128)(2,1)S(1)} %get-tuple-element.61), channel_id=1, source_target_pairs={{0,8},{2,10},{4,12},{6,14},{8,16},{10,18},{12,20},{14,22},{16,24},... | collective-permute-start | bytes 786440 | tf_op jit(solution)/shard_map/ppermute | solution.py:438
  110.0 3.9 %collective-permute-start.20 = (f32[4,1792]{1,0:T(4,128)S(1)}, f32[4,1792]{1,0:T(4,128)S(1)}, u32[]{:S(2)}, u32[]{:S(2)}) collective-permute-start(f32[4,1792]{1,0:T(4,128)S(1)} %pad_maximum_fusion.2), channel_id=1, source_target_pairs={{0,1},{1,0},{2,3},{3,2},{4,5},{5,4},{6,7},{7,6},{8,9},{9,8},{10,11... | collective-permute-start | bytes 86024 | tf_op jit(solution)/shard_map/ppermute | solution.py:441
  110.0 4.7 %collective-permute-start.18 = (f32[16,512]{1,0:T(8,128)S(1)}, f32[16,512]{1,0:T(8,128)S(1)}, u32[]{:S(2)}, u32[]{:S(2)}) collective-permute-start(f32[16,512]{1,0:T(8,128)S(1)} %constant_dynamic-update-slice_fusion), channel_id=1, source_target_pairs={{0,1},{1,0},{2,3},{3,2},{4,5},{5,4},{6,7},{7,6},{8,9},{9,8},{10,11... | collective-permute-start | bytes 98312 | tf_op jit(solution)/shard_map/ppermute | solution.py:441
  114.1 1.2 %copy-start.11 = (bf16[256,1792]{1,0:T(8,128)(2,1)S(1)}, bf16[256,1792]{1,0:T(8,128)(2,1)}, u32[]{:S(2)}) copy-start(bf16[256,1792]{1,0:T(8,128)(2,1)} %copy-done.10) | copy-start | bytes 2752516
  115.3 1.7 %copy-start.8 = (f32[32,4096]{1,0:T(8,128)S(1)}, f32[32,4096]{1,0:T(8,128)}, u32[]{:S(2)}) copy-start(f32[32,4096]{1,0:T(8,128)} %copy-done.7) | copy-start | bytes 1572868
  115.3 2.5 %copy-start.18 = (f32[256,1792]{1,0:T(8,128)S(1)}, f32[256,1792]{1,0:T(8,128)}, u32[]{:S(2)}) copy-start(f32[256,1792]{1,0:T(8,128)} %get-tuple-element.51) | copy-start | bytes 5505028

commit v6 on v5

--- a/solution.py
+++ b/solution.py
@@ -18,6 +18,7 @@
 COST = pl.CostEstimate(flops=1000, bytes_accessed=1000, transcendentals=0)
 LAST = (((1,), (1,)), ((), ()))
 PARAMS = pltpu.CompilerParams(vmem_limit_bytes=52 * 1024 * 1024)
+SMALL = pltpu.CompilerParams(vmem_limit_bytes=12 * 1024 * 1024)
 IN_HBM = pl.BlockSpec(memory_space=pltpu.HBM)
 
 
@@ -136,8 +137,11 @@
     )(tenant, weight, down, up)
 
 
-def grad_body(nb, rank, tenant_ref, place_ref, cot_ref, nsq_a, nsq_b, mag_ref, *refs):
+def grad_body(nb, rank, adds, tenant_ref, place_ref, cot_ref, nsq_a, nsq_b, mag_ref, *refs):
     w_hbm, a_hbm, up_hbm = refs[:3]
+    if adds:
+        add_core_body(*refs[3:5], *refs[-9:-7])
+        refs = refs[:-9] + refs[-7:]
     scale_ref, sg_ref, keep_ref, send_ref = refs[-11:-7]
     w_ref, a_ref, up_ref, sgp_ref, backp_ref, w_sem, sem = refs[-7:]
     rows, db = sg_ref.shape[0], keep_ref.shape[1]
@@ -185,7 +189,7 @@
     send_ref[...] = part[half:, :].astype(BF16)
 
 
-def input_gradient(tenant, place, cot, nsq_a, nsq_b, magnitude, weight, down, up, deps):
+def input_gradient(tenant, place, cot, nsq_a, nsq_b, magnitude, weight, down, up, add, deps):
     depth, cols = weight.shape
     rows = cot.shape[0]
     nb = rows // BLOCK
@@ -197,17 +201,23 @@
         jax.ShapeDtypeStruct((rows // 2, depth), F32),
         jax.ShapeDtypeStruct((rows // 2, depth), BF16),
     )
+    if add:
+        shapes += tuple(jax.ShapeDtypeStruct((rows // 4, depth), t) for t in (F32, BF16))
+
+    def columns(array):
+        return pl.BlockSpec((array.shape[0], db), lambda i, t, p: (0, i))
+
     return pl.pallas_call(
-        functools.partial(grad_body, nb, rank),
+        functools.partial(grad_body, nb, rank, len(add)),
         out_shape=shapes,
         grid_spec=pltpu.PrefetchScalarGridSpec(
             num_scalar_prefetch=2,
             grid=(STEPS,),
             in_specs=[same_block(a) for a in (cot, nsq_a, nsq_b, magnitude)]
             + [IN_HBM] * 3
+            + [columns(a) for a in add]
             + order_specs(deps),
-            out_specs=[same_block(s) for s in shapes[:2]]
-            + [pl.BlockSpec((rows // 2, db), lambda i, t, p: (0, i))] * 2,
+            out_specs=[same_block(s) for s in shapes[:2]] + [columns(s) for s in shapes[2:]],
             scratch_shapes=[
                 pltpu.VMEM((depth, cols), BF16),
                 pltpu.VMEM((nb * rank, depth), BF16),
@@ -221,7 +231,7 @@
         compiler_params=PARAMS,
         cost_estimate=COST,
         name="input_gradient",
-    )(tenant, place, cot, nsq_a, nsq_b, magnitude, weight, down, up, *deps)
+    )(tenant, place, cot, nsq_a, nsq_b, magnitude, weight, down, up, *add, *deps)
 
 
 def add_core_body(keep_ref, recv_ref, *refs):
@@ -243,7 +253,7 @@
         grid=(2,),
         in_specs=[pl.BlockSpec((rows, block), lambda i: (0, i))] * 2 + order_specs(deps),
         out_specs=[pl.BlockSpec((rows // 2, block), lambda i: (0, i))] * 2,
-        compiler_params=PARAMS,
+        compiler_params=SMALL,
         cost_estimate=COST,
         name="add_core",
     )(keep, recv, *deps)
@@ -283,7 +293,7 @@
             out_specs=[spec(s) for s in shapes],
             scratch_shapes=[pltpu.VMEM((nz * piece, block), F32)],
         ),
-        compiler_params=PARAMS,
+        compiler_params=SMALL,
         cost_estimate=COST,
         name="add_x",
     )(place, *operands, *deps)
@@ -301,7 +311,7 @@
         add_z_body,
         out_shape=jax.ShapeDtypeStruct(parts[0].shape, BF16),
         in_specs=[pl.BlockSpec(memory_space=pltpu.VMEM)] * len(parts),
-        compiler_params=PARAMS,
+        compiler_params=SMALL,
         cost_estimate=COST,
         name="add_z",
     )(*parts)
@@ -314,7 +324,7 @@
     rows, cols = acc_ref.shape
     piece = BLOCK // 4
     depth = w_ref.shape[0]
-    steps = STEPS // 2
+    steps = STEPS
     db = depth // steps
     z, x, core, first = place_ref[0], place_ref[1], place_ref[2], place_ref[3]
 
@@ -469,9 +479,9 @@
         cots = [lax.all_gather(cotangent, "row", axis=0, tiled=True)]
     places = [place(first) for first in firsts]
 
-    def gradient(g, deps):
+    def gradient(g, add, deps):
         return input_gradient(
-            tenant, places[g], cots[g], nsq_a, nsq_b, magnitude, weight, down, up, deps
+            tenant, places[g], cots[g], nsq_a, nsq_b, magnitude, weight, down, up, add, deps
         )
 
     def cross_core(made, deps):
@@ -485,12 +495,12 @@
         return made[0], move(made[1], 0, 1, 0)
 
     if pair:
-        ours = gradient(0, [cots[1]])
+        ours = gradient(0, [], [cots[1]])
         for k in [nz - 1] + list(range(1, nz - 1)):
             other_x(k, ours[0])
         core_z = other_core(along_z)
-        near = across_x(cross_core(ours, []))
-        theirs = gradient(1, [near[0], core_z])
+        theirs = gradient(1, [ours[2], move(ours[3], 0, 0, 1)], [core_z])
+        near = across_x(theirs[4:])
         along_x = [along_x[k] for k in range(nz)]
         along_x[nz - 2] = once(along_x[nz - 2], theirs[0])
         core_x = other_core(along_x)
@@ -513,7 +523,7 @@
         low = low + jnp.roll(swap(once(low, late)), rows_row, axis=1)
         parts = [ours, theirs]
     else:
-        ours = gradient(0, [])
+        ours = gradient(0, [], [])
         near = across_x(cross_core(ours, []))
         for k in range(1, nz):
             other_x(k, inputs)

time: 119 us -> 115 us (0.966); the launches traced: 119 us -> 113 us
  waiting for transfers between devices: 17.2 us -> 11.2 us
    ppermute x16, waiting for transfers between devices: 11.9 us -> 5.27 us  [move(): return lax.ppermute(value, 'col', perm)]
    pallas_call x2, Pallas kernels: 20 us -> 23.1 us  [input_gradient(): pl.pallas_call(functools.partial(grad_body, nb, rank, len(add)), out_shap...]
    pallas_call x2 -> x1, Pallas kernels: 4.69 us -> 2.12 us  [add_core(): pl.pallas_call(add_core_body, out_shape=(jax.ShapeDtypeStruct((rows // 2,...]
    unnamed x41 -> x47, local copies, waits for them, and re-layouts: 8.49 us -> 9.68 us
  transfers between devices with their start and end apart: 21 -> 21, of which waited for: 7 -> 8; matrix products, arithmetic and copies ran while one was open for 3% -> 3% of each run, Pallas kernels for 52% -> 55%
where the time goes in v6:
time: 115 us; the launch traced here: 113 us
  Pallas kernels  62 us (54%)
  starting transfers between devices  23.6 us (21%)
  waiting for transfers between devices  11.2 us (10%)
  local copies, waits for them, and re-layouts  10 us (9%)
  other arithmetic  3.52 us (3%)
  matrix products  2.05 us (2%)
    pallas_call x2, Pallas kernels, forward(): pl.pallas_call(functools.partial(forward_body, nb, rank, nz), out_shape=s...  24.7 us
    pallas_call x2, Pallas kernels, input_gradient(): pl.pallas_call(functools.partial(grad_body, nb, rank, len(add)), out_shap...  23.1 us
    ppermute x16, starting transfers between devices, move(): return lax.ppermute(value, 'col', perm)  17.9 us
    unnamed x47, local copies, waits for them, and re-layouts  9.68 us
    pallas_call x1, Pallas kernels, partial_norms(): pl.pallas_call(functools.partial(norm_body, nblk, rank), out_shape=shape,...  9.25 us
    ppermute x5, waiting for transfers between devices, swap(): return lax.ppermute(value, 'row', [(0, 1), (1, 0)])  5.98 us
    ppermute x5, starting transfers between devices, swap(): return lax.ppermute(value, 'row', [(0, 1), (1, 0)])  5.75 us
    ppermute x16, waiting for transfers between devices, move(): return lax.ppermute(value, 'col', perm)  5.27 us
  transfers between devices with their start and end apart: 21, of which 8 were waited for; matrix products, arithmetic and copies ran while one was open for 3% of the time, Pallas kernels for 55%

profile of v6, /device:TPU:8, one launch (start us, length us, event | category | flops | bytes accessed | tf_op | source)
XLA Modules:
  0.0 113.4 jit_solution(11929078044174680480)
XLA Ops:
  0.6 1.6 %collective-permute-start.3 = (bf16[256,1792]{1,0:T(8,128)(2,1)}, bf16[256,1792]{1,0:T(8,128)(2,1)}, u32[]{:S(2)}, u32[]{:S(2)}) collective-permute-start(bf16[256,1792]{1,0:T(8,128)(2,1)} %cot_ref.3), channel_id=1, source_target_pairs={{0,1},{1,0},{2,3},{3,2},{4,5},{5,4},{6,7},{7,6},{8,9},{9,8},{10,11... | collective-permute-start | bytes 2752520 | tf_op jit(solution)/shard_map/ppermute | solution.py:451
  2.2 1.5 %collective-permute-start = (bf16[32,4096]{1,0:T(8,128)(2,1)}, bf16[32,4096]{1,0:T(8,128)(2,1)S(1)}, u32[]{:S(2)}, u32[]{:S(2)}) collective-permute-start(bf16[32,4096]{1,0:T(8,128)(2,1)} %refs_0_.7), channel_id=1, source_target_pairs={{0,4},{2,6},{4,0},{6,2},{8,12},{10,14},{12,8},{14,10},{16,20},{18,... | collective-permute-start | bytes 786440 | tf_op jit(solution)/shard_map/ppermute | solution.py:448
  3.7 2.6 %collective-permute-start.5 = (bf16[32,4096]{1,0:T(8,128)(2,1)}, bf16[32,4096]{1,0:T(8,128)(2,1)S(1)}, u32[]{:S(2)}, u32[]{:S(2)}) collective-permute-start(bf16[32,4096]{1,0:T(8,128)(2,1)} %refs_0_.7), channel_id=1, source_target_pairs={{0,16},{2,18},{4,20},{6,22},{8,24},{10,26},{12,28},{14,30},{16,0},... | collective-permute-start | bytes 786440 | tf_op jit(solution)/shard_map/ppermute | solution.py:448
  6.3 0.4 collective-permute-start.8
  6.7 1.6 %collective-permute-start.1 = (bf16[32,4096]{1,0:T(8,128)(2,1)}, bf16[32,4096]{1,0:T(8,128)(2,1)S(1)}, u32[]{:S(2)}, u32[]{:S(2)}) collective-permute-start(bf16[32,4096]{1,0:T(8,128)(2,1)} %refs_0_.7), channel_id=1, source_target_pairs={{0,8},{2,10},{4,12},{6,14},{8,16},{10,18},{12,20},{14,22},{16,24},... | collective-permute-start | bytes 786440 | tf_op jit(solution)/shard_map/ppermute | solution.py:448
  8.4 1.2 %copy-done = bf16[16,16,1792]{2,1,0:T(8,128)(2,1)S(1)} copy-done((bf16[16,16,1792]{2,1,0:T(8,128)(2,1)S(1)}, bf16[16,16,1792]{2,1,0:T(8,128)(2,1)}, u32[]{:S(2)}) %copy-start) | copy-done | bytes 917528
  9.6 0.7 copy-done.15
  10.3 9.2 %partial_norms.1.nsq_a = f32[4,1792]{1,0:T(4,128)S(1)} custom-call(s32[512]{0:T(512)S(1)} %copy-done.15, bf16[4096,1792]{1,0:T(8,128)(2,1)} %w_hbm.5, bf16[16,16,4096]{2,1,0:T(8,128)(2,1)} %a_hbm.5, bf16[16,16,1792]{2,1,0:T(8,128)(2,1)S(1)} %copy-done), custom_call_target="tpu_custom_call" | custom-call | flops 1000 | bytes 1000 | tf_op jit(solution)/shard_map/partial_norms/pallas_call | solution.py:116
  19.5 0.6 collective-permute-start.2
  20.2 3.4 %collective-permute-done.2.nsq_b = f32[4,1792]{1,0:T(4,128)S(1)} collective-permute-done((f32[4,1792]{1,0:T(4,128)S(1)}, f32[4,1792]{1,0:T(4,128)S(1)}, u32[]{:S(2)}, u32[]{:S(2)}) %collective-permute-start.2) | collective-permute-done | bytes 28704 | tf_op jit(solution)/shard_map/ppermute | solution.py:451
  23.6 9.9 %input_gradient.2 = (f32[2,1792]{1,0:T(2,128)S(1)}, bf16[256,1792]{1,0:T(8,128)(2,1)S(1)}, f32[128,4096]{1,0:T(8,128)}, bf16[128,4096]{1,0:T(8,128)(2,1)}) custom-call(s32[512]{0:T(512)S(1)} %copy-done.16, s32[4]{0:T(128)S(1)} %pad_add_fusion.place_ref, bf16[256,1792]{1,0:T(8,128)(2,1)S(1)} %copy-done.4, f32[4,1792]{1,0:T(4,128)S(1)} %partial_norms.1.nsq_a, ...), custom_call_target="tpu_custom_call" | custom-call | flops 1000 | bytes 1000 | tf_op jit(solution)/shard_map/input_gradient/pallas_call | solution.py:210
  33.8 1.3 %copy-done.22 = bf16[128,4096]{1,0:T(8,128)(2,1)S(1)} copy-done((bf16[128,4096]{1,0:T(8,128)(2,1)S(1)}, bf16[128,4096]{1,0:T(8,128)(2,1)}, u32[]{:S(2)}) %copy-start.22) | copy-done | bytes 1048600
  35.1 1.5 %collective-permute-start.6 = (bf16[32,4096]{1,0:T(8,128)(2,1)S(1)}, bf16[32,4096]{1,0:T(8,128)(2,1)S(1)}, u32[]{:S(2)}, u32[]{:S(2)}) collective-permute-start(bf16[32,4096]{1,0:T(8,128)(2,1)S(1)} %collective-permute-done.5.refs_4_), channel_id=1, source_target_pairs={{0,4},{2,6},{4,0},{6,2},{8,12},{10,14},{12,8},{14,10},{16,20},{18,... | collective-permute-start | bytes 786440 | tf_op jit(solution)/shard_map/ppermute | solution.py:448
  36.6 0.5 collective-permute-start.10
  37.2 1.5 %collective-permute-start.4 = (bf16[32,4096]{1,0:T(8,128)(2,1)S(1)}, bf16[32,4096]{1,0:T(8,128)(2,1)S(1)}, u32[]{:S(2)}, u32[]{:S(2)}) collective-permute-start(bf16[32,4096]{1,0:T(8,128)(2,1)S(1)} %collective-permute-done.1.refs_2_), channel_id=1, source_target_pairs={{0,4},{2,6},{4,0},{6,2},{8,12},{10,14},{12,8},{14,10},{16,20},{18,... | collective-permute-start | bytes 786440 | tf_op jit(solution)/shard_map/ppermute | solution.py:448
  38.7 1.0 copy-done.18
  39.6 0.4 copy-done.21
  40.0 13.2 %input_gradient.3 = (f32[2,1792]{1,0:T(2,128)S(1)}, bf16[256,1792]{1,0:T(8,128)(2,1)S(1)}, f32[128,4096]{1,0:T(8,128)}, bf16[128,4096]{1,0:T(8,128)(2,1)}, f32[6...) custom-call(s32[512]{0:T(512)S(1)} %copy-done.16, s32[4]{0:T(128)S(1)} %get-tuple-element.66.place_ref, ...), custom_call_target="tpu_custom_call" | custom-call | flops 1000 | bytes 1000 | tf_op jit(solution)/shard_map/input_gradient/pallas_call | solution.py:210
  53.2 0.9 copy-done.13
  54.2 0.8 copy-done.17
  55.1 1.1 pad_maximum_fusion.1
  56.2 0.5 collective-permute-start.13
  57.0 1.5 %collective-permute-start.12 = (bf16[64,4096]{1,0:T(8,128)(2,1)}, bf16[64,4096]{1,0:T(8,128)(2,1)}, u32[]{:S(2)}, u32[]{:S(2)}) collective-permute-start(bf16[64,4096]{1,0:T(8,128)(2,1)} %copy-done.17), channel_id=1, source_target_pairs={{0,4},{2,6},{4,0},{6,2},{8,12},{10,14},{12,8},{14,10},{16,20},{18,... | collective-permute-start | bytes 1572872 | tf_op jit(solution)/shard_map/ppermute | solution.py:448
  58.5 1.7 %collective-permute-done.11.refs_0_.refs_9_ = bf16[128,4096]{1,0:T(8,128)(2,1)S(1)} collective-permute-done((bf16[128,4096]{1,0:T(8,128)(2,1)}, bf16[128,4096]{1,0:T(8,128)(2,1)S(1)}, u32[]{:S(2)}, u32[]{:S(2)}) %collective-permute-start.11) | collective-permute-done | bytes 1048608 | tf_op jit(solution)/shard_map/ppermute | solution.py:448
  60.2 0.5 collective-permute-done.13.recv_ref
  60.7 1.6 %copy-done.8 = f32[128,4096]{1,0:T(8,128)S(1)} copy-done((f32[128,4096]{1,0:T(8,128)S(1)}, f32[128,4096]{1,0:T(8,128)}, u32[]{:S(2)}) %copy-start.8) | copy-done | bytes 2097176
  62.3 2.1 %add_core.1 = (f32[64,4096]{1,0:T(8,128)S(1)}, bf16[64,4096]{1,0:T(8,128)(2,1)}) custom-call(f32[128,4096]{1,0:T(8,128)S(1)} %copy-done.8, bf16[128,4096]{1,0:T(8,128)(2,1)} %collective-permute-done.13.recv_ref, bf16[128,4096]{1,0:T(8,128)(2,1)S(1)} %collective-permute-done.11.refs_0_.refs_9_), custom_call_target="tpu_custom_call" | custom-call | flops 1000 | bytes 1000 | tf_op jit(solution)/shard_map/add_core/pallas_call | solution.py:247
  64.4 1.0 copy-done.2
  65.4 1.5 %collective-permute-start.14 = (bf16[64,4096]{1,0:T(8,128)(2,1)}, bf16[64,4096]{1,0:T(8,128)(2,1)S(1)}, u32[]{:S(2)}, u32[]{:S(2)}) collective-permute-start(bf16[64,4096]{1,0:T(8,128)(2,1)} %get-tuple-element.48), channel_id=1, source_target_pairs={{0,4},{2,6},{4,0},{6,2},{8,12},{10,14},{12,8},{14,10},{16,20},{18,... | collective-permute-start | bytes 1572872 | tf_op jit(solution)/shard_map/ppermute | solution.py:448
  67.1 12.3 %forward.2 = (bf16[256,1792]{1,0:T(8,128)(2,1)}, f32[2,1792]{1,0:T(2,128)S(1)}, f32[16,256]{1,0:T(8,128)S(1)}) custom-call(s32[512]{0:T(512)S(1)} %copy-done.16, s32[4]{0:T(128)S(1)} %get-tuple-element.66.place_ref, bf16[256,1792]{1,0:T(8,128)(2,1)} %collective-permute-done.3.refs_3_.cot_ref, bf16[4096,1792]{1,0:T(8,128)(2,1)} %w_hbm.5, ...), custom_call_target="tpu_custom_call" | custom-call | flops 1000 | bytes 1000 | tf_op jit(solution)/shard_map/forward/pallas_call | solution.py:404
  79.3 1.6 %collective-permute-start.15 = (bf16[256,1792]{1,0:T(8,128)(2,1)}, bf16[256,1792]{1,0:T(8,128)(2,1)S(1)}, u32[]{:S(2)}, u32[]{:S(2)}) collective-permute-start(bf16[256,1792]{1,0:T(8,128)(2,1)} %get-tuple-element.52), channel_id=1, source_target_pairs={{0,1},{1,0},{2,3},{3,2},{4,5},{5,4},{6,7},{7,6},{8,9},{9,8},{10,11... | collective-permute-start | bytes 2752520 | tf_op jit(solution)/shard_map/ppermute | solution.py:451
  80.9 1.4 %collective-permute-done.14.refs_3_ = bf16[64,4096]{1,0:T(8,128)(2,1)S(1)} collective-permute-done((bf16[64,4096]{1,0:T(8,128)(2,1)}, bf16[64,4096]{1,0:T(8,128)(2,1)S(1)}, u32[]{:S(2)}, u32[]{:S(2)}) %collective-permute-start.14) | collective-permute-done | bytes 524320 | tf_op jit(solution)/shard_map/ppermute | solution.py:448
  82.3 2.0 %add_x.1 = (f32[32,4096]{1,0:T(8,128)S(1)}, bf16[32,4096]{1,0:T(8,128)(2,1)S(1)}, bf16[32,4096]{1,0:T(8,128)(2,1)S(1)}, bf16[32,4096]{1,0:T(8,128)(2,1)S(1)}) custom-call(s32[5]{0:T(128)S(1)} %stack.39.place_ref, f32[64,4096]{1,0:T(8,128)S(1)} %copy-done.9, bf16[64,4096]{1,0:T(8,128)(2,1)} %collective-permute-done.12.refs_1_, f32[64,4096]{1,0:T(8,128)S(1)} %copy-done.3, ...), custom_call_target="tpu_custom_call" | custom-call | flops 1000 | bytes 1000 | tf_op jit(solution)/shard_map/add_x/pallas_call | solution.py:286
  84.3 0.8 copy-done.6
  85.1 2.6 %collective-permute-start.16 = (bf16[32,4096]{1,0:T(8,128)(2,1)S(1)}, bf16[32,4096]{1,0:T(8,128)(2,1)S(1)}, u32[]{:S(2)}, u32[]{:S(2)}) collective-permute-start(bf16[32,4096]{1,0:T(8,128)(2,1)S(1)} %get-tuple-element.55), channel_id=1, source_target_pairs={{0,16},{2,18},{4,20},{6,22},{8,24},{10,26},{12,28},{14,30},{16,0},... | collective-permute-start | bytes 786440 | tf_op jit(solution)/shard_map/ppermute | solution.py:448
  87.7 0.4 collective-permute-start.17
  88.1 12.5 %forward.3 = (f32[256,1792]{1,0:T(8,128)}, f32[2,1792]{1,0:T(2,128)S(1)}, f32[16,256]{1,0:T(8,128)S(1)}) custom-call(s32[512]{0:T(512)S(1)} %copy-done.16, s32[4]{0:T(128)S(1)} %pad_add_fusion.place_ref, bf16[256,1792]{1,0:T(8,128)(2,1)} %cot_ref.3, bf16[4096,1792]{1,0:T(8,128)(2,1)} %w_hbm.5, bf16[16,16,4096]{2,1,0:T(8,128)(2,1)} %a_hbm.5, ...), custom_call_target="tpu_custom_call" | custom-call | flops 1000 | bytes 1000 | tf_op jit(solution)/shard_map/forward/pallas_call | solution.py:404
  100.6 1.6 %collective-permute-start.19 = (bf16[32,4096]{1,0:T(8,128)(2,1)S(1)}, bf16[32,4096]{1,0:T(8,128)(2,1)S(1)}, u32[]{:S(2)}, u32[]{:S(2)}) collective-permute-start(bf16[32,4096]{1,0:T(8,128)(2,1)S(1)} %get-tuple-element.61), channel_id=1, source_target_pairs={{0,8},{2,10},{4,12},{6,14},{8,16},{10,18},{12,20},{14,22},{16,24},... | collective-permute-start | bytes 786440 | tf_op jit(solution)/shard_map/ppermute | solution.py:448
  102.3 1.5 %collective-permute-done.16.refs_2_ = bf16[32,4096]{1,0:T(8,128)(2,1)S(1)} collective-permute-done((bf16[32,4096]{1,0:T(8,128)(2,1)S(1)}, bf16[32,4096]{1,0:T(8,128)(2,1)S(1)}, u32[]{:S(2)}, u32[]{:S(2)}) %collective-permute-start.16) | collective-permute-done | bytes 262176 | tf_op jit(solution)/shard_map/ppermute | solution.py:448
  103.8 1.5 %collective-permute-start.20 = (f32[4,1792]{1,0:T(4,128)S(1)}, f32[4,1792]{1,0:T(4,128)S(1)}, u32[]{:S(2)}, u32[]{:S(2)}) collective-permute-start(f32[4,1792]{1,0:T(4,128)S(1)} %pad_maximum_fusion.2), channel_id=1, source_target_pairs={{0,1},{1,0},{2,3},{3,2},{4,5},{5,4},{6,7},{7,6},{8,9},{9,8},{10,11... | collective-permute-start | bytes 86024 | tf_op jit(solution)/shard_map/ppermute | solution.py:451
  105.3 0.5 collective-permute-start.18
  105.9 2.0 %collective-permute-done.20 = f32[4,1792]{1,0:T(4,128)S(1)} collective-permute-done((f32[4,1792]{1,0:T(4,128)S(1)}, f32[4,1792]{1,0:T(4,128)S(1)}, u32[]{:S(2)}, u32[]{:S(2)}) %collective-permute-start.20) | collective-permute-done | bytes 28704 | tf_op jit(solution)/shard_map/ppermute | solution.py:451
  108.0 0.7 fusion.3
  108.7 0.6 collective-permute-done.18
  109.4 0.4 fusion.9
  109.8 1.6 %convolution_add_fusion = f32[256,1792]{1,0:T(8,128)} fusion(f32[256,1792]{1,0:T(8,128)S(1)} %fusion.9, bf16[256,256]{1,0:T(8,128)(2,1)S(1)} %bitcast.29, bf16[256,1792]{1,0:T(8,128)(2,1)S(1)} %copy-done.12), kind=kOutput, calls=%fused_computation | convolution fusion | flops 235339776 | bytes 4718592 | tf_op jit(solution)/shard_map/dot_general | solution.py:555
  111.5 0.8 add_z.1
  112.3 1.1 fusion
  (74 shorter events, 1.3 us)
Async XLA Ops:
  0.6 23.0 %collective-permute-start.3 = (bf16[256,1792]{1,0:T(8,128)(2,1)}, bf16[256,1792]{1,0:T(8,128)(2,1)}, u32[]{:S(2)}, u32[]{:S(2)}) collective-permute-start(bf16[256,1792]{1,0:T(8,128)(2,1)} %cot_ref.3), channel_id=1, source_target_pairs={{0,1},{1,0},{2,3},{3,2},{4,5},{5,4},{6,7},{7,6},{8,9},{9,8},{10,11... | collective-permute-start | bytes 2752520 | tf_op jit(solution)/shard_map/ppermute | solution.py:451
  2.2 17.3 %collective-permute-start = (bf16[32,4096]{1,0:T(8,128)(2,1)}, bf16[32,4096]{1,0:T(8,128)(2,1)S(1)}, u32[]{:S(2)}, u32[]{:S(2)}) collective-permute-start(bf16[32,4096]{1,0:T(8,128)(2,1)} %refs_0_.7), channel_id=1, source_target_pairs={{0,4},{2,6},{4,0},{6,2},{8,12},{10,14},{12,8},{14,10},{16,20},{18,... | collective-permute-start | bytes 786440 | tf_op jit(solution)/shard_map/ppermute | solution.py:448
  3.7 29.9 %collective-permute-start.5 = (bf16[32,4096]{1,0:T(8,128)(2,1)}, bf16[32,4096]{1,0:T(8,128)(2,1)S(1)}, u32[]{:S(2)}, u32[]{:S(2)}) collective-permute-start(bf16[32,4096]{1,0:T(8,128)(2,1)} %refs_0_.7), channel_id=1, source_target_pairs={{0,16},{2,18},{4,20},{6,22},{8,24},{10,26},{12,28},{14,30},{16,0},... | collective-permute-start | bytes 786440 | tf_op jit(solution)/shard_map/ppermute | solution.py:448
  6.3 27.3 %collective-permute-start.8 = (bf16[32,4096]{1,0:T(8,128)(2,1)}, bf16[32,4096]{1,0:T(8,128)(2,1)S(1)}, u32[]{:S(2)}, u32[]{:S(2)}) collective-permute-start(bf16[32,4096]{1,0:T(8,128)(2,1)} %refs_0_.7), channel_id=1, source_target_pairs={{0,24},{2,26},{4,28},{6,30},{8,0},{10,2},{12,4},{14,6},{16,8},{18,... | collective-permute-start | bytes 786440 | tf_op jit(solution)/shard_map/ppermute | solution.py:448
  6.7 26.9 %collective-permute-start.1 = (bf16[32,4096]{1,0:T(8,128)(2,1)}, bf16[32,4096]{1,0:T(8,128)(2,1)S(1)}, u32[]{:S(2)}, u32[]{:S(2)}) collective-permute-start(bf16[32,4096]{1,0:T(8,128)(2,1)} %refs_0_.7), channel_id=1, source_target_pairs={{0,8},{2,10},{4,12},{6,14},{8,16},{10,18},{12,20},{14,22},{16,24},... | collective-permute-start | bytes 786440 | tf_op jit(solution)/shard_map/ppermute | solution.py:448
  8.4 1.2 %copy-start = (bf16[16,16,1792]{2,1,0:T(8,128)(2,1)S(1)}, bf16[16,16,1792]{2,1,0:T(8,128)(2,1)}, u32[]{:S(2)}) copy-start(bf16[16,16,1792]{2,1,0:T(8,128)(2,1)} %up_hbm.5) | copy-start | bytes 2752516
  9.6 0.7 copy-start.15
  10.3 13.4 %copy-start.4 = (bf16[256,1792]{1,0:T(8,128)(2,1)S(1)}, bf16[256,1792]{1,0:T(8,128)(2,1)}, u32[]{:S(2)}) copy-start(bf16[256,1792]{1,0:T(8,128)(2,1)} %cot_ref.3) | copy-start | bytes 2752516
  10.3 13.4 %copy-start.10 = (f32[16,1792]{1,0:T(8,128)S(1)}, f32[16,1792]{1,0:T(8,128)}, u32[]{:S(2)}) copy-start(f32[16,1792]{1,0:T(8,128)} %mag_ref.3) | copy-start | bytes 344068
  10.3 13.4 %copy-start.16 = (s32[512]{0:T(512)S(1)}, s32[512]{0:T(512)}, u32[]{:S(2)}) copy-start(s32[512]{0:T(512)} %tenant_ref.9) | copy-start | bytes 6148
  19.5 4.1 %collective-permute-start.2 = (f32[4,1792]{1,0:T(4,128)S(1)}, f32[4,1792]{1,0:T(4,128)S(1)}, u32[]{:S(2)}, u32[]{:S(2)}) collective-permute-start(f32[4,1792]{1,0:T(4,128)S(1)} %partial_norms.1.nsq_a), channel_id=1, source_target_pairs={{0,1},{1,0},{2,3},{3,2},{4,5},{5,4},{6,7},{7,6},{8,9},{9,8},{10,11... | collective-permute-start | bytes 86024 | tf_op jit(solution)/shard_map/ppermute | solution.py:451
  20.2 13.4 %copy-start.5 = (bf16[32,4096]{1,0:T(8,128)(2,1)S(1)}, bf16[32,4096]{1,0:T(8,128)(2,1)}, u32[]{:S(2)}) copy-start(bf16[32,4096]{1,0:T(8,128)(2,1)} %refs_0_.7) | copy-start | bytes 786436
  33.6 3.1 %copy-start.11 = (bf16[256,1792]{1,0:T(8,128)(2,1)}, bf16[256,1792]{1,0:T(8,128)(2,1)S(1)}, u32[]{:S(2)}) copy-start(bf16[256,1792]{1,0:T(8,128)(2,1)S(1)} %get-tuple-element.58) | copy-start | bytes 2752516
  33.6 1.6 %copy-start.22 = (bf16[128,4096]{1,0:T(8,128)(2,1)S(1)}, bf16[128,4096]{1,0:T(8,128)(2,1)}, u32[]{:S(2)}) copy-start(bf16[128,4096]{1,0:T(8,128)(2,1)} %get-tuple-element.39) | copy-start | bytes 3145732
  33.7 4.9 %collective-permute-start.9 = (bf16[128,4096]{1,0:T(8,128)(2,1)S(1)}, bf16[128,4096]{1,0:T(8,128)(2,1)S(1)}, u32[]{:S(2)}, u32[]{:S(2)}) collective-permute-start(bf16[128,4096]{1,0:T(8,128)(2,1)S(1)} %pad_maximum_fusion), channel_id=1, source_target_pairs={{0,2},{2,0},{4,6},{6,4},{8,10},{10,8},{12,14},{14,12},{16,18},{18,... | collective-permute-start | bytes 3145736 | tf_op jit(solution)/shard_map/ppermute | solution.py:448
  35.1 3.5 %collective-permute-start.7 = (bf16[128,4096]{1,0:T(8,128)(2,1)S(1)}, bf16[128,4096]{1,0:T(8,128)(2,1)S(1)}, u32[]{:S(2)}, u32[]{:S(2)}) collective-permute-start(bf16[128,4096]{1,0:T(8,128)(2,1)S(1)} %copy-done.22), channel_id=1, source_target_pairs={{0,2},{2,0},{4,6},{6,4},{8,10},{10,8},{12,14},{14,12},{16,18},{18,... | collective-permute-start | bytes 3145736 | tf_op jit(solution)/shard_map/ppermute | solution.py:448
  35.1 19.8 %collective-permute-start.6 = (bf16[32,4096]{1,0:T(8,128)(2,1)S(1)}, bf16[32,4096]{1,0:T(8,128)(2,1)S(1)}, u32[]{:S(2)}, u32[]{:S(2)}) collective-permute-start(bf16[32,4096]{1,0:T(8,128)(2,1)S(1)} %collective-permute-done.5.refs_4_), channel_id=1, source_target_pairs={{0,4},{2,6},{4,0},{6,2},{8,12},{10,14},{12,8},{14,10},{16,20},{18,... | collective-permute-start | bytes 786440 | tf_op jit(solution)/shard_map/ppermute | solution.py:448
  36.6 18.3 %collective-permute-start.10 = (bf16[32,4096]{1,0:T(8,128)(2,1)S(1)}, bf16[32,4096]{1,0:T(8,128)(2,1)S(1)}, u32[]{:S(2)}, u32[]{:S(2)}) collective-permute-start(bf16[32,4096]{1,0:T(8,128)(2,1)S(1)} %collective-permute-done.8.refs_6_), channel_id=1, source_target_pairs={{0,4},{2,6},{4,0},{6,2},{8,12},{10,14},{12,8},{14,10},{16,20},{18,... | collective-permute-start | bytes 786440 | tf_op jit(solution)/shard_map/ppermute | solution.py:448
  37.2 17.9 %collective-permute-start.4 = (bf16[32,4096]{1,0:T(8,128)(2,1)S(1)}, bf16[32,4096]{1,0:T(8,128)(2,1)S(1)}, u32[]{:S(2)}, u32[]{:S(2)}) collective-permute-start(bf16[32,4096]{1,0:T(8,128)(2,1)S(1)} %collective-permute-done.1.refs_2_), channel_id=1, source_target_pairs={{0,4},{2,6},{4,0},{6,2},{8,12},{10,14},{12,8},{14,10},{16,20},{18,... | collective-permute-start | bytes 786440 | tf_op jit(solution)/shard_map/ppermute | solution.py:448
  38.7 1.0 copy-start.18
  38.7 1.3 %copy-start.21 = (bf16[128,4096]{1,0:T(8,128)(2,1)}, bf16[128,4096]{1,0:T(8,128)(2,1)S(1)}, u32[]{:S(2)}) copy-start(bf16[128,4096]{1,0:T(8,128)(2,1)S(1)} %collective-permute-done.7.refs_4_) | copy-start | bytes 3145732
  53.2 0.9 copy-start.13
  54.2 0.8 copy-start.17
  55.0 9.4 %copy-start.19 = (bf16[32,4096]{1,0:T(8,128)(2,1)}, bf16[32,4096]{1,0:T(8,128)(2,1)S(1)}, u32[]{:S(2)}) copy-start(bf16[32,4096]{1,0:T(8,128)(2,1)S(1)} %collective-permute-done.10.refs_7_) | copy-start | bytes 786436
  56.2 4.0 %collective-permute-start.11 = (bf16[128,4096]{1,0:T(8,128)(2,1)}, bf16[128,4096]{1,0:T(8,128)(2,1)S(1)}, u32[]{:S(2)}, u32[]{:S(2)}) collective-permute-start(bf16[128,4096]{1,0:T(8,128)(2,1)} %pad_maximum_fusion.1), channel_id=1, source_target_pairs={{0,2},{2,0},{4,6},{6,4},{8,10},{10,8},{12,14},{14,12},{16,18},{18,... | collective-permute-start | bytes 3145736 | tf_op jit(solution)/shard_map/ppermute | solution.py:448
  56.2 4.5 %collective-permute-start.13 = (bf16[128,4096]{1,0:T(8,128)(2,1)}, bf16[128,4096]{1,0:T(8,128)(2,1)}, u32[]{:S(2)}, u32[]{:S(2)}) collective-permute-start(bf16[128,4096]{1,0:T(8,128)(2,1)} %get-tuple-element.46), channel_id=1, source_target_pairs={{0,2},{2,0},{4,6},{6,4},{8,10},{10,8},{12,14},{14,12},{16,18},{18,... | collective-permute-start | bytes 3145736 | tf_op jit(solution)/shard_map/ppermute | solution.py:448
  57.0 23.9 %collective-permute-start.12 = (bf16[64,4096]{1,0:T(8,128)(2,1)}, bf16[64,4096]{1,0:T(8,128)(2,1)}, u32[]{:S(2)}, u32[]{:S(2)}) collective-permute-start(bf16[64,4096]{1,0:T(8,128)(2,1)} %copy-done.17), channel_id=1, source_target_pairs={{0,4},{2,6},{4,0},{6,2},{8,12},{10,14},{12,8},{14,10},{16,20},{18,... | collective-permute-start | bytes 1572872 | tf_op jit(solution)/shard_map/ppermute | solution.py:448
  60.2 4.2 %copy-start.1 = (bf16[128,4096]{1,0:T(8,128)(2,1)}, bf16[128,4096]{1,0:T(8,128)(2,1)S(1)}, u32[]{:S(2)}) copy-start(bf16[128,4096]{1,0:T(8,128)(2,1)S(1)} %collective-permute-done.11.refs_0_.refs_9_) | copy-start | bytes 3145732
  60.7 1.6 %copy-start.8 = (f32[128,4096]{1,0:T(8,128)S(1)}, f32[128,4096]{1,0:T(8,128)}, u32[]{:S(2)}) copy-start(f32[128,4096]{1,0:T(8,128)} %get-tuple-element.45.keep_ref) | copy-start | bytes 6291460
  64.4 1.0 copy-start.2
  65.4 16.9 %collective-permute-start.14 = (bf16[64,4096]{1,0:T(8,128)(2,1)}, bf16[64,4096]{1,0:T(8,128)(2,1)S(1)}, u32[]{:S(2)}, u32[]{:S(2)}) collective-permute-start(bf16[64,4096]{1,0:T(8,128)(2,1)} %get-tuple-element.48), channel_id=1, source_target_pairs={{0,4},{2,6},{4,0},{6,2},{8,12},{10,14},{12,8},{14,10},{16,20},{18,... | collective-permute-start | bytes 1572872 | tf_op jit(solution)/shard_map/ppermute | solution.py:448
  67.0 15.2 %copy-start.3 = (f32[64,4096]{1,0:T(8,128)S(1)}, f32[64,4096]{1,0:T(8,128)}, u32[]{:S(2)}) copy-start(f32[64,4096]{1,0:T(8,128)} %copy-done.2) | copy-start | bytes 3145732
  67.1 15.2 %copy-start.9 = (f32[64,4096]{1,0:T(8,128)S(1)}, f32[64,4096]{1,0:T(8,128)}, u32[]{:S(2)}) copy-start(f32[64,4096]{1,0:T(8,128)} %get-tuple-element.43.refs_0_) | copy-start | bytes 3145732
  79.3 32.9 %collective-permute-start.15 = (bf16[256,1792]{1,0:T(8,128)(2,1)}, bf16[256,1792]{1,0:T(8,128)(2,1)S(1)}, u32[]{:S(2)}, u32[]{:S(2)}) collective-permute-start(bf16[256,1792]{1,0:T(8,128)(2,1)} %get-tuple-element.52), channel_id=1, source_target_pairs={{0,1},{1,0},{2,3},{3,2},{4,5},{5,4},{6,7},{7,6},{8,9},{9,8},{10,11... | collective-permute-start | bytes 2752520 | tf_op jit(solution)/shard_map/ppermute | solution.py:451
  84.3 0.8 copy-start.6
  85.1 18.7 %collective-permute-start.16 = (bf16[32,4096]{1,0:T(8,128)(2,1)S(1)}, bf16[32,4096]{1,0:T(8,128)(2,1)S(1)}, u32[]{:S(2)}, u32[]{:S(2)}) collective-permute-start(bf16[32,4096]{1,0:T(8,128)(2,1)S(1)} %get-tuple-element.55), channel_id=1, source_target_pairs={{0,16},{2,18},{4,20},{6,22},{8,24},{10,26},{12,28},{14,30},{16,0},... | collective-permute-start | bytes 786440 | tf_op jit(solution)/shard_map/ppermute | solution.py:448
  87.7 16.1 %collective-permute-start.17 = (bf16[32,4096]{1,0:T(8,128)(2,1)S(1)}, bf16[32,4096]{1,0:T(8,128)(2,1)S(1)}, u32[]{:S(2)}, u32[]{:S(2)}) collective-permute-start(bf16[32,4096]{1,0:T(8,128)(2,1)S(1)} %get-tuple-element.56), channel_id=1, source_target_pairs={{0,24},{2,26},{4,28},{6,30},{8,0},{10,2},{12,4},{14,6},{16,8},{18,... | collective-permute-start | bytes 786440 | tf_op jit(solution)/shard_map/ppermute | solution.py:448
  100.6 8.7 %copy-start.14 = (bf16[256,1792]{1,0:T(8,128)(2,1)S(1)}, bf16[256,1792]{1,0:T(8,128)(2,1)}, u32[]{:S(2)}) copy-start(bf16[256,1792]{1,0:T(8,128)(2,1)} %copy-done.13) | copy-start | bytes 2752516
  100.6 10.8 %collective-permute-start.19 = (bf16[32,4096]{1,0:T(8,128)(2,1)S(1)}, bf16[32,4096]{1,0:T(8,128)(2,1)S(1)}, u32[]{:S(2)}, u32[]{:S(2)}) collective-permute-start(bf16[32,4096]{1,0:T(8,128)(2,1)S(1)} %get-tuple-element.61), channel_id=1, source_target_pairs={{0,8},{2,10},{4,12},{6,14},{8,16},{10,18},{12,20},{14,22},{16,24},... | collective-permute-start | bytes 786440 | tf_op jit(solution)/shard_map/ppermute | solution.py:448
  103.8 4.0 %collective-permute-start.20 = (f32[4,1792]{1,0:T(4,128)S(1)}, f32[4,1792]{1,0:T(4,128)S(1)}, u32[]{:S(2)}, u32[]{:S(2)}) collective-permute-start(f32[4,1792]{1,0:T(4,128)S(1)} %pad_maximum_fusion.2), channel_id=1, source_target_pairs={{0,1},{1,0},{2,3},{3,2},{4,5},{5,4},{6,7},{7,6},{8,9},{9,8},{10,11... | collective-permute-start | bytes 86024 | tf_op jit(solution)/shard_map/ppermute | solution.py:451
  105.3 3.9 %collective-permute-start.18 = (f32[16,512]{1,0:T(8,128)S(1)}, f32[16,512]{1,0:T(8,128)S(1)}, u32[]{:S(2)}, u32[]{:S(2)}) collective-permute-start(f32[16,512]{1,0:T(8,128)S(1)} %constant_dynamic-update-slice_fusion), channel_id=1, source_target_pairs={{0,1},{1,0},{2,3},{3,2},{4,5},{5,4},{6,7},{7,6},{8,9},{9,8},{10,11... | collective-permute-start | bytes 98312 | tf_op jit(solution)/shard_map/ppermute | solution.py:451
  108.0 1.8 %copy-start.12 = (bf16[256,1792]{1,0:T(8,128)(2,1)S(1)}, bf16[256,1792]{1,0:T(8,128)(2,1)}, u32[]{:S(2)}) copy-start(bf16[256,1792]{1,0:T(8,128)(2,1)} %copy-done.11) | copy-start | bytes 2752516
  109.8 1.7 %copy-start.7 = (f32[32,4096]{1,0:T(8,128)S(1)}, f32[32,4096]{1,0:T(8,128)}, u32[]{:S(2)}) copy-start(f32[32,4096]{1,0:T(8,128)} %copy-done.6) | copy-start | bytes 1572868
  109.8 2.5 %copy-start.20 = (f32[256,1792]{1,0:T(8,128)S(1)}, f32[256,1792]{1,0:T(8,128)}, u32[]{:S(2)}) copy-start(f32[256,1792]{1,0:T(8,128)} %get-tuple-element.51) | copy-start | bytes 5505028

commit v7 on v6

--- a/solution.py
+++ b/solution.py
@@ -51,7 +51,7 @@
 
         @pl.when(later < PARTS)
         def _():
-            weight_copy(w_hbm, w_ref, sem, later).start()
+            weight_copy(w_hbm, w_ref, sem, later).start(priority=(n + AHEAD) % 2)
 
 
 def factor_copies(tenant_ref, first, hbm, ref, sem, at):
@@ -73,7 +73,7 @@
     for copy in copies:
         copy.start()
     for i in range(AHEAD):
-        weight_copy(w_hbm, w_ref, w_sem, i).start()
+        weight_copy(w_hbm, w_ref, w_sem, i).start(priority=i % 2)
     for copy in late:
         copy.start()
     cross_ref[...] = jnp.zeros_like(cross_ref)
@@ -157,7 +157,7 @@
         for copy in copies:
             copy.start()
         for i in range(AHEAD):
-            weight_copy(w_hbm, w_ref, w_sem, i).start()
+            weight_copy(w_hbm, w_ref, w_sem, i).start(priority=i % 2)
         for b in range(nb):
             at = first + b
             total = nsq_a[pl.ds(at, 1), :] + nsq_b[pl.ds(at, 1), :]
@@ -340,16 +340,16 @@
             def _():
                 row = (b * 4 + (x ^ fx) * 2 + (core ^ fc)) * piece
                 dst = pl.ds(pl.multiple_of(row, piece), piece)
-                act(pltpu.make_async_copy(src, x_ref.at[dst, at], x_sem.at[h, n]))
+                act(pltpu.make_async_copy(src, x_ref.at[dst, at], x_sem.at[h, n]), n % 2)
 
     copies = factor_copies(tenant_ref, first, a_hbm, a_ref, sem, 0)
     late = factor_copies(tenant_ref, first, up_hbm, up_ref, sem, nb)
-    each(0, lambda copy: copy.start())
+    each(0, lambda copy, queue: copy.start(priority=queue))
     for copy in copies:
         copy.start()
     for i in range(AHEAD):
-        weight_copy(w_hbm, w_ref, w_sem, i).start()
-    each(1, lambda copy: copy.start())
+        weight_copy(w_hbm, w_ref, w_sem, i).start(priority=i % 2)
+    each(1, lambda copy, queue: copy.start(priority=queue))
     for copy in late:
         copy.start()
     acc_ref[...] = jnp.zeros_like(acc_ref)
@@ -362,7 +362,7 @@
 
             @pl.when(i == h * (steps // 2))
             def _():
-                each(h, lambda copy: copy.wait())
+                each(h, lambda copy, queue: copy.wait())
 
         weight_block(w_hbm, w_ref, w_sem, i, steps)
         at = pl.ds(pl.multiple_of(i * db, db), db)

time: 115 us -> 119 us (1.035)
  waiting for transfers between devices: 11.2 us -> 18 us
  Pallas kernels: 62 us -> 60.2 us
    ppermute x16, waiting for transfers between devices: 5.27 us -> 11.7 us  [move(): return lax.ppermute(value, 'col', perm)]
  transfers between devices with their start and end apart: 21 -> 21, of which waited for: 8 -> 9; matrix products, arithmetic and copies ran while one was open for 3% -> 3% of each run, Pallas kernels for 55% -> 51%
where the time goes in v7:
time: 119 us; the launch traced here: 118 us
  Pallas kernels  60.2 us (51%)
  starting transfers between devices  23.5 us (20%)
  waiting for transfers between devices  18 us (15%)
  local copies, waits for them, and re-layouts  10 us (8%)
  other arithmetic  3.52 us (3%)
  matrix products  2.05 us (2%)
    pallas_call x2, Pallas kernels, forward(): pl.pallas_call(functools.partial(forward_body, nb, rank, nz), out_shape=s...  24.4 us
    pallas_call x2, Pallas kernels, input_gradient(): pl.pallas_call(functools.partial(grad_body, nb, rank, len(add)), out_shap...  21.9 us
    ppermute x16, starting transfers between devices, move(): return lax.ppermute(value, 'col', perm)  17.9 us
    ppermute x16, waiting for transfers between devices, move(): return lax.ppermute(value, 'col', perm)  11.7 us
    unnamed x47, local copies, waits for them, and re-layouts  9.68 us
    pallas_call x1, Pallas kernels, partial_norms(): pl.pallas_call(functools.partial(norm_body, nblk, rank), out_shape=shape,...  9.01 us
    ppermute x5, waiting for transfers between devices, swap(): return lax.ppermute(value, 'row', [(0, 1), (1, 0)])  6.25 us
    ppermute x5, starting transfers between devices, swap(): return lax.ppermute(value, 'row', [(0, 1), (1, 0)])  5.66 us
  transfers between devices with their start and end apart: 21, of which 9 were waited for; matrix products, arithmetic and copies ran while one was open for 3% of the time, Pallas kernels for 51%

profile of v7, /device:TPU:8, one launch (start us, length us, event | category | flops | bytes accessed | tf_op | source)
XLA Modules:
  0.0 118.3 jit_solution(3915806997495613790)
XLA Ops:
  0.6 1.6 %collective-permute-start.3 = (bf16[256,1792]{1,0:T(8,128)(2,1)}, bf16[256,1792]{1,0:T(8,128)(2,1)}, u32[]{:S(2)}, u32[]{:S(2)}) collective-permute-start(bf16[256,1792]{1,0:T(8,128)(2,1)} %cot_ref.3), channel_id=1, source_target_pairs={{0,1},{1,0},{2,3},{3,2},{4,5},{5,4},{6,7},{7,6},{8,9},{9,8},{10,11... | collective-permute-start | bytes 2752520 | tf_op jit(solution)/shard_map/ppermute | solution.py:451
  2.2 1.5 %collective-permute-start = (bf16[32,4096]{1,0:T(8,128)(2,1)}, bf16[32,4096]{1,0:T(8,128)(2,1)S(1)}, u32[]{:S(2)}, u32[]{:S(2)}) collective-permute-start(bf16[32,4096]{1,0:T(8,128)(2,1)} %refs_0_.7), channel_id=1, source_target_pairs={{0,4},{2,6},{4,0},{6,2},{8,12},{10,14},{12,8},{14,10},{16,20},{18,... | collective-permute-start | bytes 786440 | tf_op jit(solution)/shard_map/ppermute | solution.py:448
  3.7 2.6 %collective-permute-start.5 = (bf16[32,4096]{1,0:T(8,128)(2,1)}, bf16[32,4096]{1,0:T(8,128)(2,1)S(1)}, u32[]{:S(2)}, u32[]{:S(2)}) collective-permute-start(bf16[32,4096]{1,0:T(8,128)(2,1)} %refs_0_.7), channel_id=1, source_target_pairs={{0,16},{2,18},{4,20},{6,22},{8,24},{10,26},{12,28},{14,30},{16,0},... | collective-permute-start | bytes 786440 | tf_op jit(solution)/shard_map/ppermute | solution.py:448
  6.3 0.4 collective-permute-start.8
  6.7 1.6 %collective-permute-start.1 = (bf16[32,4096]{1,0:T(8,128)(2,1)}, bf16[32,4096]{1,0:T(8,128)(2,1)S(1)}, u32[]{:S(2)}, u32[]{:S(2)}) collective-permute-start(bf16[32,4096]{1,0:T(8,128)(2,1)} %refs_0_.7), channel_id=1, source_target_pairs={{0,8},{2,10},{4,12},{6,14},{8,16},{10,18},{12,20},{14,22},{16,24},... | collective-permute-start | bytes 786440 | tf_op jit(solution)/shard_map/ppermute | solution.py:448
  8.4 1.2 copy-done
  9.6 0.7 copy-done.15
  10.3 9.0 %partial_norms.1.nsq_a = f32[4,1792]{1,0:T(4,128)S(1)} custom-call(s32[512]{0:T(512)S(1)} %copy-done.15, bf16[4096,1792]{1,0:T(8,128)(2,1)} %w_hbm.5, bf16[16,16,4096]{2,1,0:T(8,128)(2,1)} %a_hbm.5, bf16[16,16,1792]{2,1,0:T(8,128)(2,1)S(1)} %copy-done), custom_call_target="tpu_custom_call" | custom-call | flops 1000 | bytes 1000 | tf_op jit(solution)/shard_map/partial_norms/pallas_call | solution.py:116
  19.3 0.6 collective-permute-start.2
  19.9 3.7 %collective-permute-done.2.nsq_b = f32[4,1792]{1,0:T(4,128)S(1)} collective-permute-done((f32[4,1792]{1,0:T(4,128)S(1)}, f32[4,1792]{1,0:T(4,128)S(1)}, u32[]{:S(2)}, u32[]{:S(2)}) %collective-permute-start.2) | collective-permute-done | bytes 28704 | tf_op jit(solution)/shard_map/ppermute | solution.py:451
  23.6 9.4 %input_gradient.2 = (f32[2,1792]{1,0:T(2,128)S(1)}, bf16[256,1792]{1,0:T(8,128)(2,1)S(1)}, f32[128,4096]{1,0:T(8,128)}, bf16[128,4096]{1,0:T(8,128)(2,1)}) custom-call(s32[512]{0:T(512)S(1)} %copy-done.16, s32[4]{0:T(128)S(1)} %pad_add_fusion.place_ref, bf16[256,1792]{1,0:T(8,128)(2,1)S(1)} %copy-done.4, f32[4,1792]{1,0:T(4,128)S(1)} %partial_norms.1.nsq_a, ...), custom_call_target="tpu_custom_call" | custom-call | flops 1000 | bytes 1000 | tf_op jit(solution)/shard_map/input_gradient/pallas_call | solution.py:210
  33.3 1.3 %copy-done.22 = bf16[128,4096]{1,0:T(8,128)(2,1)S(1)} copy-done((bf16[128,4096]{1,0:T(8,128)(2,1)S(1)}, bf16[128,4096]{1,0:T(8,128)(2,1)}, u32[]{:S(2)}) %copy-start.22) | copy-done | bytes 1048600
  34.6 1.5 %collective-permute-start.6 = (bf16[32,4096]{1,0:T(8,128)(2,1)S(1)}, bf16[32,4096]{1,0:T(8,128)(2,1)S(1)}, u32[]{:S(2)}, u32[]{:S(2)}) collective-permute-start(bf16[32,4096]{1,0:T(8,128)(2,1)S(1)} %collective-permute-done.5.refs_4_), channel_id=1, source_target_pairs={{0,4},{2,6},{4,0},{6,2},{8,12},{10,14},{12,8},{14,10},{16,20},{18,... | collective-permute-start | bytes 786440 | tf_op jit(solution)/shard_map/ppermute | solution.py:448
  36.1 0.5 collective-permute-start.10
  36.6 1.5 %collective-permute-start.4 = (bf16[32,4096]{1,0:T(8,128)(2,1)S(1)}, bf16[32,4096]{1,0:T(8,128)(2,1)S(1)}, u32[]{:S(2)}, u32[]{:S(2)}) collective-permute-start(bf16[32,4096]{1,0:T(8,128)(2,1)S(1)} %collective-permute-done.1.refs_2_), channel_id=1, source_target_pairs={{0,4},{2,6},{4,0},{6,2},{8,12},{10,14},{12,8},{14,10},{16,20},{18,... | collective-permute-start | bytes 786440 | tf_op jit(solution)/shard_map/ppermute | solution.py:448
  38.2 1.0 copy-done.18
  39.5 12.5 %input_gradient.3 = (f32[2,1792]{1,0:T(2,128)S(1)}, bf16[256,1792]{1,0:T(8,128)(2,1)S(1)}, f32[128,4096]{1,0:T(8,128)}, bf16[128,4096]{1,0:T(8,128)(2,1)}, f32[6...) custom-call(s32[512]{0:T(512)S(1)} %copy-done.16, s32[4]{0:T(128)S(1)} %get-tuple-element.66.place_ref, ...), custom_call_target="tpu_custom_call" | custom-call | flops 1000 | bytes 1000 | tf_op jit(solution)/shard_map/input_gradient/pallas_call | solution.py:210
  52.0 0.9 copy-done.13
  53.0 0.8 copy-done.17
  53.8 0.8 collective-permute-done.4.refs_3_
  54.6 1.1 pad_maximum_fusion.1
  55.7 0.5 collective-permute-start.13
  56.5 1.5 %collective-permute-start.12 = (bf16[64,4096]{1,0:T(8,128)(2,1)}, bf16[64,4096]{1,0:T(8,128)(2,1)}, u32[]{:S(2)}, u32[]{:S(2)}) collective-permute-start(bf16[64,4096]{1,0:T(8,128)(2,1)} %copy-done.17), channel_id=1, source_target_pairs={{0,4},{2,6},{4,0},{6,2},{8,12},{10,14},{12,8},{14,10},{16,20},{18,... | collective-permute-start | bytes 1572872 | tf_op jit(solution)/shard_map/ppermute | solution.py:448
  58.0 1.7 %collective-permute-done.11.refs_0_.refs_9_ = bf16[128,4096]{1,0:T(8,128)(2,1)S(1)} collective-permute-done((bf16[128,4096]{1,0:T(8,128)(2,1)}, bf16[128,4096]{1,0:T(8,128)(2,1)S(1)}, u32[]{:S(2)}, u32[]{:S(2)}) %collective-permute-start.11) | collective-permute-done | bytes 1048608 | tf_op jit(solution)/shard_map/ppermute | solution.py:448
  59.7 0.5 collective-permute-done.13.recv_ref
  60.2 1.6 %copy-done.8 = f32[128,4096]{1,0:T(8,128)S(1)} copy-done((f32[128,4096]{1,0:T(8,128)S(1)}, f32[128,4096]{1,0:T(8,128)}, u32[]{:S(2)}) %copy-start.8) | copy-done | bytes 2097176
  61.8 2.1 %add_core.1 = (f32[64,4096]{1,0:T(8,128)S(1)}, bf16[64,4096]{1,0:T(8,128)(2,1)}) custom-call(f32[128,4096]{1,0:T(8,128)S(1)} %copy-done.8, bf16[128,4096]{1,0:T(8,128)(2,1)} %collective-permute-done.13.recv_ref, bf16[128,4096]{1,0:T(8,128)(2,1)S(1)} %collective-permute-done.11.refs_0_.refs_9_), custom_call_target="tpu_custom_call" | custom-call | flops 1000 | bytes 1000 | tf_op jit(solution)/shard_map/add_core/pallas_call | solution.py:247
  63.9 1.0 copy-done.2
  64.8 1.5 %collective-permute-start.14 = (bf16[64,4096]{1,0:T(8,128)(2,1)}, bf16[64,4096]{1,0:T(8,128)(2,1)S(1)}, u32[]{:S(2)}, u32[]{:S(2)}) collective-permute-start(bf16[64,4096]{1,0:T(8,128)(2,1)} %get-tuple-element.48), channel_id=1, source_target_pairs={{0,4},{2,6},{4,0},{6,2},{8,12},{10,14},{12,8},{14,10},{16,20},{18,... | collective-permute-start | bytes 1572872 | tf_op jit(solution)/shard_map/ppermute | solution.py:448
  66.5 12.1 %forward.2 = (bf16[256,1792]{1,0:T(8,128)(2,1)}, f32[2,1792]{1,0:T(2,128)S(1)}, f32[16,256]{1,0:T(8,128)S(1)}) custom-call(s32[512]{0:T(512)S(1)} %copy-done.16, s32[4]{0:T(128)S(1)} %get-tuple-element.66.place_ref, bf16[256,1792]{1,0:T(8,128)(2,1)} %collective-permute-done.3.refs_3_.cot_ref, bf16[4096,1792]{1,0:T(8,128)(2,1)} %w_hbm.5, ...), custom_call_target="tpu_custom_call" | custom-call | flops 1000 | bytes 1000 | tf_op jit(solution)/shard_map/forward/pallas_call | solution.py:404
  78.6 1.5 %collective-permute-start.15 = (bf16[256,1792]{1,0:T(8,128)(2,1)}, bf16[256,1792]{1,0:T(8,128)(2,1)S(1)}, u32[]{:S(2)}, u32[]{:S(2)}) collective-permute-start(bf16[256,1792]{1,0:T(8,128)(2,1)} %get-tuple-element.52), channel_id=1, source_target_pairs={{0,1},{1,0},{2,3},{3,2},{4,5},{5,4},{6,7},{7,6},{8,9},{9,8},{10,11... | collective-permute-start | bytes 2752520 | tf_op jit(solution)/shard_map/ppermute | solution.py:451
  80.1 1.6 %collective-permute-done.14.refs_3_ = bf16[64,4096]{1,0:T(8,128)(2,1)S(1)} collective-permute-done((bf16[64,4096]{1,0:T(8,128)(2,1)}, bf16[64,4096]{1,0:T(8,128)(2,1)S(1)}, u32[]{:S(2)}, u32[]{:S(2)}) %collective-permute-start.14) | collective-permute-done | bytes 524320 | tf_op jit(solution)/shard_map/ppermute | solution.py:448
  81.8 2.0 %add_x.1 = (f32[32,4096]{1,0:T(8,128)S(1)}, bf16[32,4096]{1,0:T(8,128)(2,1)S(1)}, bf16[32,4096]{1,0:T(8,128)(2,1)S(1)}, bf16[32,4096]{1,0:T(8,128)(2,1)S(1)}) custom-call(s32[5]{0:T(128)S(1)} %stack.39.place_ref, f32[64,4096]{1,0:T(8,128)S(1)} %copy-done.9, bf16[64,4096]{1,0:T(8,128)(2,1)} %collective-permute-done.12.refs_1_, f32[64,4096]{1,0:T(8,128)S(1)} %copy-done.3, ...), custom_call_target="tpu_custom_call" | custom-call | flops 1000 | bytes 1000 | tf_op jit(solution)/shard_map/add_x/pallas_call | solution.py:286
  83.8 0.8 copy-done.6
  84.6 2.6 %collective-permute-start.16 = (bf16[32,4096]{1,0:T(8,128)(2,1)S(1)}, bf16[32,4096]{1,0:T(8,128)(2,1)S(1)}, u32[]{:S(2)}, u32[]{:S(2)}) collective-permute-start(bf16[32,4096]{1,0:T(8,128)(2,1)S(1)} %get-tuple-element.55), channel_id=1, source_target_pairs={{0,16},{2,18},{4,20},{6,22},{8,24},{10,26},{12,28},{14,30},{16,0},... | collective-permute-start | bytes 786440 | tf_op jit(solution)/shard_map/ppermute | solution.py:448
  87.2 0.4 collective-permute-start.17
  87.6 12.3 %forward.3 = (f32[256,1792]{1,0:T(8,128)}, f32[2,1792]{1,0:T(2,128)S(1)}, f32[16,256]{1,0:T(8,128)S(1)}) custom-call(s32[512]{0:T(512)S(1)} %copy-done.16, s32[4]{0:T(128)S(1)} %pad_add_fusion.place_ref, bf16[256,1792]{1,0:T(8,128)(2,1)} %cot_ref.3, bf16[4096,1792]{1,0:T(8,128)(2,1)} %w_hbm.5, bf16[16,16,4096]{2,1,0:T(8,128)(2,1)} %a_hbm.5, ...), custom_call_target="tpu_custom_call" | custom-call | flops 1000 | bytes 1000 | tf_op jit(solution)/shard_map/forward/pallas_call | solution.py:404
  99.9 1.6 %collective-permute-start.19 = (bf16[32,4096]{1,0:T(8,128)(2,1)S(1)}, bf16[32,4096]{1,0:T(8,128)(2,1)S(1)}, u32[]{:S(2)}, u32[]{:S(2)}) collective-permute-start(bf16[32,4096]{1,0:T(8,128)(2,1)S(1)} %get-tuple-element.61), channel_id=1, source_target_pairs={{0,8},{2,10},{4,12},{6,14},{8,16},{10,18},{12,20},{14,22},{16,24},... | collective-permute-start | bytes 786440 | tf_op jit(solution)/shard_map/ppermute | solution.py:448
  101.5 1.7 %collective-permute-done.16.refs_2_ = bf16[32,4096]{1,0:T(8,128)(2,1)S(1)} collective-permute-done((bf16[32,4096]{1,0:T(8,128)(2,1)S(1)}, bf16[32,4096]{1,0:T(8,128)(2,1)S(1)}, u32[]{:S(2)}, u32[]{:S(2)}) %collective-permute-start.16) | collective-permute-done | bytes 262176 | tf_op jit(solution)/shard_map/ppermute | solution.py:448
  103.3 5.4 %collective-permute-done.17.refs_3_ = bf16[32,4096]{1,0:T(8,128)(2,1)S(1)} collective-permute-done((bf16[32,4096]{1,0:T(8,128)(2,1)S(1)}, bf16[32,4096]{1,0:T(8,128)(2,1)S(1)}, u32[]{:S(2)}, u32[]{:S(2)}) %collective-permute-start.17) | collective-permute-done | bytes 262176 | tf_op jit(solution)/shard_map/ppermute | solution.py:448
  108.7 1.6 %collective-permute-start.20 = (f32[4,1792]{1,0:T(4,128)S(1)}, f32[4,1792]{1,0:T(4,128)S(1)}, u32[]{:S(2)}, u32[]{:S(2)}) collective-permute-start(f32[4,1792]{1,0:T(4,128)S(1)} %pad_maximum_fusion.2), channel_id=1, source_target_pairs={{0,1},{1,0},{2,3},{3,2},{4,5},{5,4},{6,7},{7,6},{8,9},{9,8},{10,11... | collective-permute-start | bytes 86024 | tf_op jit(solution)/shard_map/ppermute | solution.py:451
  110.2 0.5 collective-permute-start.18
  110.7 1.8 %collective-permute-done.20 = f32[4,1792]{1,0:T(4,128)S(1)} collective-permute-done((f32[4,1792]{1,0:T(4,128)S(1)}, f32[4,1792]{1,0:T(4,128)S(1)}, u32[]{:S(2)}, u32[]{:S(2)}) %collective-permute-start.20) | collective-permute-done | bytes 28704 | tf_op jit(solution)/shard_map/ppermute | solution.py:451
  112.7 0.7 fusion.3
  113.4 0.7 collective-permute-done.18
  114.7 1.6 %convolution_add_fusion = f32[256,1792]{1,0:T(8,128)} fusion(f32[256,1792]{1,0:T(8,128)S(1)} %fusion.9, bf16[256,256]{1,0:T(8,128)(2,1)S(1)} %bitcast.29, bf16[256,1792]{1,0:T(8,128)(2,1)S(1)} %copy-done.12), kind=kOutput, calls=%fused_computation | convolution fusion | flops 235339776 | bytes 4718592 | tf_op jit(solution)/shard_map/dot_general | solution.py:555
  116.3 0.8 add_z.1
  117.1 1.1 fusion
  (74 shorter events, 1.9 us)
Async XLA Ops:
  0.6 23.0 %collective-permute-start.3 = (bf16[256,1792]{1,0:T(8,128)(2,1)}, bf16[256,1792]{1,0:T(8,128)(2,1)}, u32[]{:S(2)}, u32[]{:S(2)}) collective-permute-start(bf16[256,1792]{1,0:T(8,128)(2,1)} %cot_ref.3), channel_id=1, source_target_pairs={{0,1},{1,0},{2,3},{3,2},{4,5},{5,4},{6,7},{7,6},{8,9},{9,8},{10,11... | collective-permute-start | bytes 2752520 | tf_op jit(solution)/shard_map/ppermute | solution.py:451
  2.2 17.1 %collective-permute-start = (bf16[32,4096]{1,0:T(8,128)(2,1)}, bf16[32,4096]{1,0:T(8,128)(2,1)S(1)}, u32[]{:S(2)}, u32[]{:S(2)}) collective-permute-start(bf16[32,4096]{1,0:T(8,128)(2,1)} %refs_0_.7), channel_id=1, source_target_pairs={{0,4},{2,6},{4,0},{6,2},{8,12},{10,14},{12,8},{14,10},{16,20},{18,... | collective-permute-start | bytes 786440 | tf_op jit(solution)/shard_map/ppermute | solution.py:448
  3.7 29.4 %collective-permute-start.5 = (bf16[32,4096]{1,0:T(8,128)(2,1)}, bf16[32,4096]{1,0:T(8,128)(2,1)S(1)}, u32[]{:S(2)}, u32[]{:S(2)}) collective-permute-start(bf16[32,4096]{1,0:T(8,128)(2,1)} %refs_0_.7), channel_id=1, source_target_pairs={{0,16},{2,18},{4,20},{6,22},{8,24},{10,26},{12,28},{14,30},{16,0},... | collective-permute-start | bytes 786440 | tf_op jit(solution)/shard_map/ppermute | solution.py:448
  6.3 26.8 %collective-permute-start.8 = (bf16[32,4096]{1,0:T(8,128)(2,1)}, bf16[32,4096]{1,0:T(8,128)(2,1)S(1)}, u32[]{:S(2)}, u32[]{:S(2)}) collective-permute-start(bf16[32,4096]{1,0:T(8,128)(2,1)} %refs_0_.7), channel_id=1, source_target_pairs={{0,24},{2,26},{4,28},{6,30},{8,0},{10,2},{12,4},{14,6},{16,8},{18,... | collective-permute-start | bytes 786440 | tf_op jit(solution)/shard_map/ppermute | solution.py:448
  6.7 26.3 %collective-permute-start.1 = (bf16[32,4096]{1,0:T(8,128)(2,1)}, bf16[32,4096]{1,0:T(8,128)(2,1)S(1)}, u32[]{:S(2)}, u32[]{:S(2)}) collective-permute-start(bf16[32,4096]{1,0:T(8,128)(2,1)} %refs_0_.7), channel_id=1, source_target_pairs={{0,8},{2,10},{4,12},{6,14},{8,16},{10,18},{12,20},{14,22},{16,24},... | collective-permute-start | bytes 786440 | tf_op jit(solution)/shard_map/ppermute | solution.py:448
  8.4 1.2 copy-start
  9.6 0.7 copy-start.15
  10.3 13.4 %copy-start.4 = (bf16[256,1792]{1,0:T(8,128)(2,1)S(1)}, bf16[256,1792]{1,0:T(8,128)(2,1)}, u32[]{:S(2)}) copy-start(bf16[256,1792]{1,0:T(8,128)(2,1)} %cot_ref.3) | copy-start | bytes 2752516
  10.3 13.4 %copy-start.10 = (f32[16,1792]{1,0:T(8,128)S(1)}, f32[16,1792]{1,0:T(8,128)}, u32[]{:S(2)}) copy-start(f32[16,1792]{1,0:T(8,128)} %mag_ref.3) | copy-start | bytes 344068
  10.3 13.4 %copy-start.16 = (s32[512]{0:T(512)S(1)}, s32[512]{0:T(512)}, u32[]{:S(2)}) copy-start(s32[512]{0:T(512)} %tenant_ref.9) | copy-start | bytes 6148
  19.3 4.3 %collective-permute-start.2 = (f32[4,1792]{1,0:T(4,128)S(1)}, f32[4,1792]{1,0:T(4,128)S(1)}, u32[]{:S(2)}, u32[]{:S(2)}) collective-permute-start(f32[4,1792]{1,0:T(4,128)S(1)} %partial_norms.1.nsq_a), channel_id=1, source_target_pairs={{0,1},{1,0},{2,3},{3,2},{4,5},{5,4},{6,7},{7,6},{8,9},{9,8},{10,11... | collective-permute-start | bytes 86024 | tf_op jit(solution)/shard_map/ppermute | solution.py:451
  19.9 13.2 %copy-start.5 = (bf16[32,4096]{1,0:T(8,128)(2,1)S(1)}, bf16[32,4096]{1,0:T(8,128)(2,1)}, u32[]{:S(2)}) copy-start(bf16[32,4096]{1,0:T(8,128)(2,1)} %refs_0_.7) | copy-start | bytes 786436
  33.0 3.1 %copy-start.11 = (bf16[256,1792]{1,0:T(8,128)(2,1)}, bf16[256,1792]{1,0:T(8,128)(2,1)S(1)}, u32[]{:S(2)}) copy-start(bf16[256,1792]{1,0:T(8,128)(2,1)S(1)} %get-tuple-element.58) | copy-start | bytes 2752516
  33.1 1.6 %copy-start.22 = (bf16[128,4096]{1,0:T(8,128)(2,1)S(1)}, bf16[128,4096]{1,0:T(8,128)(2,1)}, u32[]{:S(2)}) copy-start(bf16[128,4096]{1,0:T(8,128)(2,1)} %get-tuple-element.39) | copy-start | bytes 3145732
  33.2 4.9 %collective-permute-start.9 = (bf16[128,4096]{1,0:T(8,128)(2,1)S(1)}, bf16[128,4096]{1,0:T(8,128)(2,1)S(1)}, u32[]{:S(2)}, u32[]{:S(2)}) collective-permute-start(bf16[128,4096]{1,0:T(8,128)(2,1)S(1)} %pad_maximum_fusion), channel_id=1, source_target_pairs={{0,2},{2,0},{4,6},{6,4},{8,10},{10,8},{12,14},{14,12},{16,18},{18,... | collective-permute-start | bytes 3145736 | tf_op jit(solution)/shard_map/ppermute | solution.py:448
  34.6 3.5 %collective-permute-start.7 = (bf16[128,4096]{1,0:T(8,128)(2,1)S(1)}, bf16[128,4096]{1,0:T(8,128)(2,1)S(1)}, u32[]{:S(2)}, u32[]{:S(2)}) collective-permute-start(bf16[128,4096]{1,0:T(8,128)(2,1)S(1)} %copy-done.22), channel_id=1, source_target_pairs={{0,2},{2,0},{4,6},{6,4},{8,10},{10,8},{12,14},{14,12},{16,18},{18,... | collective-permute-start | bytes 3145736 | tf_op jit(solution)/shard_map/ppermute | solution.py:448
  34.6 19.2 %collective-permute-start.6 = (bf16[32,4096]{1,0:T(8,128)(2,1)S(1)}, bf16[32,4096]{1,0:T(8,128)(2,1)S(1)}, u32[]{:S(2)}, u32[]{:S(2)}) collective-permute-start(bf16[32,4096]{1,0:T(8,128)(2,1)S(1)} %collective-permute-done.5.refs_4_), channel_id=1, source_target_pairs={{0,4},{2,6},{4,0},{6,2},{8,12},{10,14},{12,8},{14,10},{16,20},{18,... | collective-permute-start | bytes 786440 | tf_op jit(solution)/shard_map/ppermute | solution.py:448
  36.1 17.7 %collective-permute-start.10 = (bf16[32,4096]{1,0:T(8,128)(2,1)S(1)}, bf16[32,4096]{1,0:T(8,128)(2,1)S(1)}, u32[]{:S(2)}, u32[]{:S(2)}) collective-permute-start(bf16[32,4096]{1,0:T(8,128)(2,1)S(1)} %collective-permute-done.8.refs_6_), channel_id=1, source_target_pairs={{0,4},{2,6},{4,0},{6,2},{8,12},{10,14},{12,8},{14,10},{16,20},{18,... | collective-permute-start | bytes 786440 | tf_op jit(solution)/shard_map/ppermute | solution.py:448
  36.6 17.9 %collective-permute-start.4 = (bf16[32,4096]{1,0:T(8,128)(2,1)S(1)}, bf16[32,4096]{1,0:T(8,128)(2,1)S(1)}, u32[]{:S(2)}, u32[]{:S(2)}) collective-permute-start(bf16[32,4096]{1,0:T(8,128)(2,1)S(1)} %collective-permute-done.1.refs_2_), channel_id=1, source_target_pairs={{0,4},{2,6},{4,0},{6,2},{8,12},{10,14},{12,8},{14,10},{16,20},{18,... | collective-permute-start | bytes 786440 | tf_op jit(solution)/shard_map/ppermute | solution.py:448
  38.1 1.0 copy-start.18
  38.2 1.3 %copy-start.21 = (bf16[128,4096]{1,0:T(8,128)(2,1)}, bf16[128,4096]{1,0:T(8,128)(2,1)S(1)}, u32[]{:S(2)}) copy-start(bf16[128,4096]{1,0:T(8,128)(2,1)S(1)} %collective-permute-done.7.refs_4_) | copy-start | bytes 3145732
  52.0 0.9 copy-start.13
  53.0 0.8 copy-start.17
  53.8 10.1 %copy-start.19 = (bf16[32,4096]{1,0:T(8,128)(2,1)}, bf16[32,4096]{1,0:T(8,128)(2,1)S(1)}, u32[]{:S(2)}) copy-start(bf16[32,4096]{1,0:T(8,128)(2,1)S(1)} %collective-permute-done.10.refs_7_) | copy-start | bytes 786436
  55.7 4.0 %collective-permute-start.11 = (bf16[128,4096]{1,0:T(8,128)(2,1)}, bf16[128,4096]{1,0:T(8,128)(2,1)S(1)}, u32[]{:S(2)}, u32[]{:S(2)}) collective-permute-start(bf16[128,4096]{1,0:T(8,128)(2,1)} %pad_maximum_fusion.1), channel_id=1, source_target_pairs={{0,2},{2,0},{4,6},{6,4},{8,10},{10,8},{12,14},{14,12},{16,18},{18,... | collective-permute-start | bytes 3145736 | tf_op jit(solution)/shard_map/ppermute | solution.py:448
  55.7 4.5 %collective-permute-start.13 = (bf16[128,4096]{1,0:T(8,128)(2,1)}, bf16[128,4096]{1,0:T(8,128)(2,1)}, u32[]{:S(2)}, u32[]{:S(2)}) collective-permute-start(bf16[128,4096]{1,0:T(8,128)(2,1)} %get-tuple-element.46), channel_id=1, source_target_pairs={{0,2},{2,0},{4,6},{6,4},{8,10},{10,8},{12,14},{14,12},{16,18},{18,... | collective-permute-start | bytes 3145736 | tf_op jit(solution)/shard_map/ppermute | solution.py:448
  56.5 23.7 %collective-permute-start.12 = (bf16[64,4096]{1,0:T(8,128)(2,1)}, bf16[64,4096]{1,0:T(8,128)(2,1)}, u32[]{:S(2)}, u32[]{:S(2)}) collective-permute-start(bf16[64,4096]{1,0:T(8,128)(2,1)} %copy-done.17), channel_id=1, source_target_pairs={{0,4},{2,6},{4,0},{6,2},{8,12},{10,14},{12,8},{14,10},{16,20},{18,... | collective-permute-start | bytes 1572872 | tf_op jit(solution)/shard_map/ppermute | solution.py:448
  59.7 4.2 %copy-start.1 = (bf16[128,4096]{1,0:T(8,128)(2,1)}, bf16[128,4096]{1,0:T(8,128)(2,1)S(1)}, u32[]{:S(2)}) copy-start(bf16[128,4096]{1,0:T(8,128)(2,1)S(1)} %collective-permute-done.11.refs_0_.refs_9_) | copy-start | bytes 3145732
  60.2 1.6 %copy-start.8 = (f32[128,4096]{1,0:T(8,128)S(1)}, f32[128,4096]{1,0:T(8,128)}, u32[]{:S(2)}) copy-start(f32[128,4096]{1,0:T(8,128)} %get-tuple-element.45.keep_ref) | copy-start | bytes 6291460
  63.9 1.0 copy-start.2
  64.8 16.9 %collective-permute-start.14 = (bf16[64,4096]{1,0:T(8,128)(2,1)}, bf16[64,4096]{1,0:T(8,128)(2,1)S(1)}, u32[]{:S(2)}, u32[]{:S(2)}) collective-permute-start(bf16[64,4096]{1,0:T(8,128)(2,1)} %get-tuple-element.48), channel_id=1, source_target_pairs={{0,4},{2,6},{4,0},{6,2},{8,12},{10,14},{12,8},{14,10},{16,20},{18,... | collective-permute-start | bytes 1572872 | tf_op jit(solution)/shard_map/ppermute | solution.py:448
  66.5 15.2 %copy-start.3 = (f32[64,4096]{1,0:T(8,128)S(1)}, f32[64,4096]{1,0:T(8,128)}, u32[]{:S(2)}) copy-start(f32[64,4096]{1,0:T(8,128)} %copy-done.2) | copy-start | bytes 3145732
  66.5 15.2 %copy-start.9 = (f32[64,4096]{1,0:T(8,128)S(1)}, f32[64,4096]{1,0:T(8,128)}, u32[]{:S(2)}) copy-start(f32[64,4096]{1,0:T(8,128)} %get-tuple-element.43.refs_0_) | copy-start | bytes 3145732
  78.6 38.5 %collective-permute-start.15 = (bf16[256,1792]{1,0:T(8,128)(2,1)}, bf16[256,1792]{1,0:T(8,128)(2,1)S(1)}, u32[]{:S(2)}, u32[]{:S(2)}) collective-permute-start(bf16[256,1792]{1,0:T(8,128)(2,1)} %get-tuple-element.52), channel_id=1, source_target_pairs={{0,1},{1,0},{2,3},{3,2},{4,5},{5,4},{6,7},{7,6},{8,9},{9,8},{10,11... | collective-permute-start | bytes 2752520 | tf_op jit(solution)/shard_map/ppermute | solution.py:451
  83.8 0.8 copy-start.6
  84.6 18.7 %collective-permute-start.16 = (bf16[32,4096]{1,0:T(8,128)(2,1)S(1)}, bf16[32,4096]{1,0:T(8,128)(2,1)S(1)}, u32[]{:S(2)}, u32[]{:S(2)}) collective-permute-start(bf16[32,4096]{1,0:T(8,128)(2,1)S(1)} %get-tuple-element.55), channel_id=1, source_target_pairs={{0,16},{2,18},{4,20},{6,22},{8,24},{10,26},{12,28},{14,30},{16,0},... | collective-permute-start | bytes 786440 | tf_op jit(solution)/shard_map/ppermute | solution.py:448
  87.2 21.5 %collective-permute-start.17 = (bf16[32,4096]{1,0:T(8,128)(2,1)S(1)}, bf16[32,4096]{1,0:T(8,128)(2,1)S(1)}, u32[]{:S(2)}, u32[]{:S(2)}) collective-permute-start(bf16[32,4096]{1,0:T(8,128)(2,1)S(1)} %get-tuple-element.56), channel_id=1, source_target_pairs={{0,24},{2,26},{4,28},{6,30},{8,0},{10,2},{12,4},{14,6},{16,8},{18,... | collective-permute-start | bytes 786440 | tf_op jit(solution)/shard_map/ppermute | solution.py:448
  99.9 14.3 %copy-start.14 = (bf16[256,1792]{1,0:T(8,128)(2,1)S(1)}, bf16[256,1792]{1,0:T(8,128)(2,1)}, u32[]{:S(2)}) copy-start(bf16[256,1792]{1,0:T(8,128)(2,1)} %copy-done.13) | copy-start | bytes 2752516
  99.9 16.4 %collective-permute-start.19 = (bf16[32,4096]{1,0:T(8,128)(2,1)S(1)}, bf16[32,4096]{1,0:T(8,128)(2,1)S(1)}, u32[]{:S(2)}, u32[]{:S(2)}) collective-permute-start(bf16[32,4096]{1,0:T(8,128)(2,1)S(1)} %get-tuple-element.61), channel_id=1, source_target_pairs={{0,8},{2,10},{4,12},{6,14},{8,16},{10,18},{12,20},{14,22},{16,24},... | collective-permute-start | bytes 786440 | tf_op jit(solution)/shard_map/ppermute | solution.py:448
  108.7 3.9 %collective-permute-start.20 = (f32[4,1792]{1,0:T(4,128)S(1)}, f32[4,1792]{1,0:T(4,128)S(1)}, u32[]{:S(2)}, u32[]{:S(2)}) collective-permute-start(f32[4,1792]{1,0:T(4,128)S(1)} %pad_maximum_fusion.2), channel_id=1, source_target_pairs={{0,1},{1,0},{2,3},{3,2},{4,5},{5,4},{6,7},{7,6},{8,9},{9,8},{10,11... | collective-permute-start | bytes 86024 | tf_op jit(solution)/shard_map/ppermute | solution.py:451
  110.2 3.9 %collective-permute-start.18 = (f32[16,512]{1,0:T(8,128)S(1)}, f32[16,512]{1,0:T(8,128)S(1)}, u32[]{:S(2)}, u32[]{:S(2)}) collective-permute-start(f32[16,512]{1,0:T(8,128)S(1)} %constant_dynamic-update-slice_fusion), channel_id=1, source_target_pairs={{0,1},{1,0},{2,3},{3,2},{4,5},{5,4},{6,7},{7,6},{8,9},{9,8},{10,11... | collective-permute-start | bytes 98312 | tf_op jit(solution)/shard_map/ppermute | solution.py:451
  112.7 1.9 %copy-start.12 = (bf16[256,1792]{1,0:T(8,128)(2,1)S(1)}, bf16[256,1792]{1,0:T(8,128)(2,1)}, u32[]{:S(2)}) copy-start(bf16[256,1792]{1,0:T(8,128)(2,1)} %copy-done.11) | copy-start | bytes 2752516
  114.6 1.7 %copy-start.7 = (f32[32,4096]{1,0:T(8,128)S(1)}, f32[32,4096]{1,0:T(8,128)}, u32[]{:S(2)}) copy-start(f32[32,4096]{1,0:T(8,128)} %copy-done.6) | copy-start | bytes 1572868
  114.7 2.5 %copy-start.20 = (f32[256,1792]{1,0:T(8,128)S(1)}, f32[256,1792]{1,0:T(8,128)}, u32[]{:S(2)}) copy-start(f32[256,1792]{1,0:T(8,128)} %get-tuple-element.51) | copy-start | bytes 5505028

commit v8 on v7

--- a/solution.py
+++ b/solution.py
@@ -179,11 +179,11 @@
         owner = lax.broadcasted_iota(jnp.int32, back.shape, 1) // rank
         backp_ref[...] = hi_lo(jnp.where(owner == block, back, 0.0), 1)
 
-    weight_block(w_hbm, w_ref, w_sem, step, STEPS)
+    weight_block(w_hbm, w_ref, w_sem, step, w_ref.shape[0] // db)
     at = pl.ds(pl.multiple_of(step * db, db), db)
     down = a_ref[:, at]
     down = jnp.concatenate([down, down], axis=0)
-    part = lax.dot_general(sgp_ref[...], w_ref[at, :], LAST, preferred_element_type=F32)
+    part = lax.dot_general(w_ref[at, :], sgp_ref[...], LAST, preferred_element_type=F32).T
     part = part + jnp.dot(backp_ref[...], down, preferred_element_type=F32)
     keep_ref[...] = part[:half, :]
     send_ref[...] = part[half:, :].astype(BF16)
@@ -194,7 +194,8 @@
     rows = cot.shape[0]
     nb = rows // BLOCK
     rank = down.shape[1]
-    db = depth // STEPS
+    steps = STEPS // 2
+    db = depth // steps
     shapes = (
         jax.ShapeDtypeStruct((nb, cols), F32),
         jax.ShapeDtypeStruct((rows, cols), BF16),
@@ -212,7 +213,7 @@
         out_shape=shapes,
         grid_spec=pltpu.PrefetchScalarGridSpec(
             num_scalar_prefetch=2,
-            grid=(STEPS,),
+            grid=(steps,),
             in_specs=[same_block(a) for a in (cot, nsq_a, nsq_b, magnitude)]
             + [IN_HBM] * 3
             + [columns(a) for a in add]

time: 119 us -> 120 us (level)
  no operation moved by 1% of the time
where the time goes in v8:
time: 120 us; the launch traced here: 119 us
  Pallas kernels  61.1 us (51%)
  starting transfers between devices  23.5 us (20%)
  waiting for transfers between devices  18.2 us (15%)
  local copies, waits for them, and re-layouts  10 us (8%)
  other arithmetic  3.52 us (3%)
  matrix products  2.05 us (2%)
    pallas_call x2, Pallas kernels, forward(): pl.pallas_call(functools.partial(forward_body, nb, rank, nz), out_shape=s...  24.4 us
    pallas_call x2, Pallas kernels, input_gradient(): pl.pallas_call(functools.partial(grad_body, nb, rank, len(add)), out_shap...  22.8 us
    ppermute x16, starting transfers between devices, move(): return lax.ppermute(value, 'col', perm)  17.9 us
    ppermute x16, waiting for transfers between devices, move(): return lax.ppermute(value, 'col', perm)  12 us
    unnamed x47, local copies, waits for them, and re-layouts  9.68 us
    pallas_call x1, Pallas kernels, partial_norms(): pl.pallas_call(functools.partial(norm_body, nblk, rank), out_shape=shape,...  9.01 us
    ppermute x5, waiting for transfers between devices, swap(): return lax.ppermute(value, 'row', [(0, 1), (1, 0)])  6.26 us
    ppermute x5, starting transfers between devices, swap(): return lax.ppermute(value, 'row', [(0, 1), (1, 0)])  5.68 us
  transfers between devices with their start and end apart: 21, of which 9 were waited for; matrix products, arithmetic and copies ran while one was open for 3% of the time, Pallas kernels for 51%

profile of v8, /device:TPU:8, one launch (start us, length us, event | category | flops | bytes accessed | tf_op | source)
XLA Modules:
  0.0 119.4 jit_solution(190414179147649448)
XLA Ops:
  0.6 1.6 %collective-permute-start.3 = (bf16[256,1792]{1,0:T(8,128)(2,1)}, bf16[256,1792]{1,0:T(8,128)(2,1)}, u32[]{:S(2)}, u32[]{:S(2)}) collective-permute-start(bf16[256,1792]{1,0:T(8,128)(2,1)} %cot_ref.3), channel_id=1, source_target_pairs={{0,1},{1,0},{2,3},{3,2},{4,5},{5,4},{6,7},{7,6},{8,9},{9,8},{10,11... | collective-permute-start | bytes 2752520 | tf_op jit(solution)/shard_map/ppermute | solution.py:452
  2.2 1.5 %collective-permute-start = (bf16[32,4096]{1,0:T(8,128)(2,1)}, bf16[32,4096]{1,0:T(8,128)(2,1)S(1)}, u32[]{:S(2)}, u32[]{:S(2)}) collective-permute-start(bf16[32,4096]{1,0:T(8,128)(2,1)} %refs_0_.7), channel_id=1, source_target_pairs={{0,4},{2,6},{4,0},{6,2},{8,12},{10,14},{12,8},{14,10},{16,20},{18,... | collective-permute-start | bytes 786440 | tf_op jit(solution)/shard_map/ppermute | solution.py:449
  3.7 2.6 %collective-permute-start.5 = (bf16[32,4096]{1,0:T(8,128)(2,1)}, bf16[32,4096]{1,0:T(8,128)(2,1)S(1)}, u32[]{:S(2)}, u32[]{:S(2)}) collective-permute-start(bf16[32,4096]{1,0:T(8,128)(2,1)} %refs_0_.7), channel_id=1, source_target_pairs={{0,16},{2,18},{4,20},{6,22},{8,24},{10,26},{12,28},{14,30},{16,0},... | collective-permute-start | bytes 786440 | tf_op jit(solution)/shard_map/ppermute | solution.py:449
  6.3 0.4 collective-permute-start.8
  6.7 1.6 %collective-permute-start.1 = (bf16[32,4096]{1,0:T(8,128)(2,1)}, bf16[32,4096]{1,0:T(8,128)(2,1)S(1)}, u32[]{:S(2)}, u32[]{:S(2)}) collective-permute-start(bf16[32,4096]{1,0:T(8,128)(2,1)} %refs_0_.7), channel_id=1, source_target_pairs={{0,8},{2,10},{4,12},{6,14},{8,16},{10,18},{12,20},{14,22},{16,24},... | collective-permute-start | bytes 786440 | tf_op jit(solution)/shard_map/ppermute | solution.py:449
  8.4 1.2 copy-done
  9.6 0.7 copy-done.15
  10.3 9.0 %partial_norms.1.nsq_a = f32[4,1792]{1,0:T(4,128)S(1)} custom-call(s32[512]{0:T(512)S(1)} %copy-done.15, bf16[4096,1792]{1,0:T(8,128)(2,1)} %w_hbm.5, bf16[16,16,4096]{2,1,0:T(8,128)(2,1)} %a_hbm.5, bf16[16,16,1792]{2,1,0:T(8,128)(2,1)S(1)} %copy-done), custom_call_target="tpu_custom_call" | custom-call | flops 1000 | bytes 1000 | tf_op jit(solution)/shard_map/partial_norms/pallas_call | solution.py:116
  19.3 0.6 collective-permute-start.2
  19.9 3.7 %collective-permute-done.2.nsq_b = f32[4,1792]{1,0:T(4,128)S(1)} collective-permute-done((f32[4,1792]{1,0:T(4,128)S(1)}, f32[4,1792]{1,0:T(4,128)S(1)}, u32[]{:S(2)}, u32[]{:S(2)}) %collective-permute-start.2) | collective-permute-done | bytes 28704 | tf_op jit(solution)/shard_map/ppermute | solution.py:452
  23.6 10.5 %input_gradient.2 = (f32[2,1792]{1,0:T(2,128)S(1)}, bf16[256,1792]{1,0:T(8,128)(2,1)S(1)}, f32[128,4096]{1,0:T(8,128)}, bf16[128,4096]{1,0:T(8,128)(2,1)}) custom-call(s32[512]{0:T(512)S(1)} %copy-done.16, s32[4]{0:T(128)S(1)} %pad_add_fusion.place_ref, bf16[256,1792]{1,0:T(8,128)(2,1)S(1)} %copy-done.4, f32[4,1792]{1,0:T(4,128)S(1)} %partial_norms.1.nsq_a, ...), custom_call_target="tpu_custom_call" | custom-call | flops 1000 | bytes 1000 | tf_op jit(solution)/shard_map/input_gradient/pallas_call | solution.py:211
  34.4 1.3 %copy-done.22 = bf16[128,4096]{1,0:T(8,128)(2,1)S(1)} copy-done((bf16[128,4096]{1,0:T(8,128)(2,1)S(1)}, bf16[128,4096]{1,0:T(8,128)(2,1)}, u32[]{:S(2)}) %copy-start.22) | copy-done | bytes 1048600
  35.7 1.5 %collective-permute-start.6 = (bf16[32,4096]{1,0:T(8,128)(2,1)S(1)}, bf16[32,4096]{1,0:T(8,128)(2,1)S(1)}, u32[]{:S(2)}, u32[]{:S(2)}) collective-permute-start(bf16[32,4096]{1,0:T(8,128)(2,1)S(1)} %collective-permute-done.5.refs_4_), channel_id=1, source_target_pairs={{0,4},{2,6},{4,0},{6,2},{8,12},{10,14},{12,8},{14,10},{16,20},{18,... | collective-permute-start | bytes 786440 | tf_op jit(solution)/shard_map/ppermute | solution.py:449
  37.2 0.5 collective-permute-start.10
  37.8 1.5 %collective-permute-start.4 = (bf16[32,4096]{1,0:T(8,128)(2,1)S(1)}, bf16[32,4096]{1,0:T(8,128)(2,1)S(1)}, u32[]{:S(2)}, u32[]{:S(2)}) collective-permute-start(bf16[32,4096]{1,0:T(8,128)(2,1)S(1)} %collective-permute-done.1.refs_2_), channel_id=1, source_target_pairs={{0,4},{2,6},{4,0},{6,2},{8,12},{10,14},{12,8},{14,10},{16,20},{18,... | collective-permute-start | bytes 786440 | tf_op jit(solution)/shard_map/ppermute | solution.py:449
  39.3 1.0 copy-done.18
  40.6 12.3 %input_gradient.3 = (f32[2,1792]{1,0:T(2,128)S(1)}, bf16[256,1792]{1,0:T(8,128)(2,1)S(1)}, f32[128,4096]{1,0:T(8,128)}, bf16[128,4096]{1,0:T(8,128)(2,1)}, f32[6...) custom-call(s32[512]{0:T(512)S(1)} %copy-done.16, s32[4]{0:T(128)S(1)} %get-tuple-element.66.place_ref, ...), custom_call_target="tpu_custom_call" | custom-call | flops 1000 | bytes 1000 | tf_op jit(solution)/shard_map/input_gradient/pallas_call | solution.py:211
  52.9 0.9 copy-done.13
  53.9 0.8 copy-done.17
  54.7 1.0 collective-permute-done.4.refs_3_
  55.7 1.1 pad_maximum_fusion.1
  56.8 0.5 collective-permute-start.13
  57.6 1.5 %collective-permute-start.12 = (bf16[64,4096]{1,0:T(8,128)(2,1)}, bf16[64,4096]{1,0:T(8,128)(2,1)}, u32[]{:S(2)}, u32[]{:S(2)}) collective-permute-start(bf16[64,4096]{1,0:T(8,128)(2,1)} %copy-done.17), channel_id=1, source_target_pairs={{0,4},{2,6},{4,0},{6,2},{8,12},{10,14},{12,8},{14,10},{16,20},{18,... | collective-permute-start | bytes 1572872 | tf_op jit(solution)/shard_map/ppermute | solution.py:449
  59.1 1.7 %collective-permute-done.11.refs_0_.refs_9_ = bf16[128,4096]{1,0:T(8,128)(2,1)S(1)} collective-permute-done((bf16[128,4096]{1,0:T(8,128)(2,1)}, bf16[128,4096]{1,0:T(8,128)(2,1)S(1)}, u32[]{:S(2)}, u32[]{:S(2)}) %collective-permute-start.11) | collective-permute-done | bytes 1048608 | tf_op jit(solution)/shard_map/ppermute | solution.py:449
  60.8 0.5 collective-permute-done.13.recv_ref
  61.3 1.6 %copy-done.8 = f32[128,4096]{1,0:T(8,128)S(1)} copy-done((f32[128,4096]{1,0:T(8,128)S(1)}, f32[128,4096]{1,0:T(8,128)}, u32[]{:S(2)}) %copy-start.8) | copy-done | bytes 2097176
  62.9 2.1 %add_core.1 = (f32[64,4096]{1,0:T(8,128)S(1)}, bf16[64,4096]{1,0:T(8,128)(2,1)}) custom-call(f32[128,4096]{1,0:T(8,128)S(1)} %copy-done.8, bf16[128,4096]{1,0:T(8,128)(2,1)} %collective-permute-done.13.recv_ref, bf16[128,4096]{1,0:T(8,128)(2,1)S(1)} %collective-permute-done.11.refs_0_.refs_9_), custom_call_target="tpu_custom_call" | custom-call | flops 1000 | bytes 1000 | tf_op jit(solution)/shard_map/add_core/pallas_call | solution.py:248
  65.0 1.0 copy-done.2
  66.0 1.5 %collective-permute-start.14 = (bf16[64,4096]{1,0:T(8,128)(2,1)}, bf16[64,4096]{1,0:T(8,128)(2,1)S(1)}, u32[]{:S(2)}, u32[]{:S(2)}) collective-permute-start(bf16[64,4096]{1,0:T(8,128)(2,1)} %get-tuple-element.48), channel_id=1, source_target_pairs={{0,4},{2,6},{4,0},{6,2},{8,12},{10,14},{12,8},{14,10},{16,20},{18,... | collective-permute-start | bytes 1572872 | tf_op jit(solution)/shard_map/ppermute | solution.py:449
  67.7 12.1 %forward.2 = (bf16[256,1792]{1,0:T(8,128)(2,1)}, f32[2,1792]{1,0:T(2,128)S(1)}, f32[16,256]{1,0:T(8,128)S(1)}) custom-call(s32[512]{0:T(512)S(1)} %copy-done.16, s32[4]{0:T(128)S(1)} %get-tuple-element.66.place_ref, bf16[256,1792]{1,0:T(8,128)(2,1)} %collective-permute-done.3.refs_3_.cot_ref, bf16[4096,1792]{1,0:T(8,128)(2,1)} %w_hbm.5, ...), custom_call_target="tpu_custom_call" | custom-call | flops 1000 | bytes 1000 | tf_op jit(solution)/shard_map/forward/pallas_call | solution.py:405
  79.8 1.5 %collective-permute-start.15 = (bf16[256,1792]{1,0:T(8,128)(2,1)}, bf16[256,1792]{1,0:T(8,128)(2,1)S(1)}, u32[]{:S(2)}, u32[]{:S(2)}) collective-permute-start(bf16[256,1792]{1,0:T(8,128)(2,1)} %get-tuple-element.52), channel_id=1, source_target_pairs={{0,1},{1,0},{2,3},{3,2},{4,5},{5,4},{6,7},{7,6},{8,9},{9,8},{10,11... | collective-permute-start | bytes 2752520 | tf_op jit(solution)/shard_map/ppermute | solution.py:452
  81.3 1.6 %collective-permute-done.14.refs_3_ = bf16[64,4096]{1,0:T(8,128)(2,1)S(1)} collective-permute-done((bf16[64,4096]{1,0:T(8,128)(2,1)}, bf16[64,4096]{1,0:T(8,128)(2,1)S(1)}, u32[]{:S(2)}, u32[]{:S(2)}) %collective-permute-start.14) | collective-permute-done | bytes 524320 | tf_op jit(solution)/shard_map/ppermute | solution.py:449
  82.9 2.0 %add_x.1 = (f32[32,4096]{1,0:T(8,128)S(1)}, bf16[32,4096]{1,0:T(8,128)(2,1)S(1)}, bf16[32,4096]{1,0:T(8,128)(2,1)S(1)}, bf16[32,4096]{1,0:T(8,128)(2,1)S(1)}) custom-call(s32[5]{0:T(128)S(1)} %stack.39.place_ref, f32[64,4096]{1,0:T(8,128)S(1)} %copy-done.9, bf16[64,4096]{1,0:T(8,128)(2,1)} %collective-permute-done.12.refs_1_, f32[64,4096]{1,0:T(8,128)S(1)} %copy-done.3, ...), custom_call_target="tpu_custom_call" | custom-call | flops 1000 | bytes 1000 | tf_op jit(solution)/shard_map/add_x/pallas_call | solution.py:287
  84.9 0.8 copy-done.6
  85.7 2.6 %collective-permute-start.16 = (bf16[32,4096]{1,0:T(8,128)(2,1)S(1)}, bf16[32,4096]{1,0:T(8,128)(2,1)S(1)}, u32[]{:S(2)}, u32[]{:S(2)}) collective-permute-start(bf16[32,4096]{1,0:T(8,128)(2,1)S(1)} %get-tuple-element.55), channel_id=1, source_target_pairs={{0,16},{2,18},{4,20},{6,22},{8,24},{10,26},{12,28},{14,30},{16,0},... | collective-permute-start | bytes 786440 | tf_op jit(solution)/shard_map/ppermute | solution.py:449
  88.3 0.5 collective-permute-start.17
  88.7 12.3 %forward.3 = (f32[256,1792]{1,0:T(8,128)}, f32[2,1792]{1,0:T(2,128)S(1)}, f32[16,256]{1,0:T(8,128)S(1)}) custom-call(s32[512]{0:T(512)S(1)} %copy-done.16, s32[4]{0:T(128)S(1)} %pad_add_fusion.place_ref, bf16[256,1792]{1,0:T(8,128)(2,1)} %cot_ref.3, bf16[4096,1792]{1,0:T(8,128)(2,1)} %w_hbm.5, bf16[16,16,4096]{2,1,0:T(8,128)(2,1)} %a_hbm.5, ...), custom_call_target="tpu_custom_call" | custom-call | flops 1000 | bytes 1000 | tf_op jit(solution)/shard_map/forward/pallas_call | solution.py:405
  101.0 1.6 %collective-permute-start.19 = (bf16[32,4096]{1,0:T(8,128)(2,1)S(1)}, bf16[32,4096]{1,0:T(8,128)(2,1)S(1)}, u32[]{:S(2)}, u32[]{:S(2)}) collective-permute-start(bf16[32,4096]{1,0:T(8,128)(2,1)S(1)} %get-tuple-element.61), channel_id=1, source_target_pairs={{0,8},{2,10},{4,12},{6,14},{8,16},{10,18},{12,20},{14,22},{16,24},... | collective-permute-start | bytes 786440 | tf_op jit(solution)/shard_map/ppermute | solution.py:449
  102.7 1.8 %collective-permute-done.16.refs_2_ = bf16[32,4096]{1,0:T(8,128)(2,1)S(1)} collective-permute-done((bf16[32,4096]{1,0:T(8,128)(2,1)S(1)}, bf16[32,4096]{1,0:T(8,128)(2,1)S(1)}, u32[]{:S(2)}, u32[]{:S(2)}) %collective-permute-start.16) | collective-permute-done | bytes 262176 | tf_op jit(solution)/shard_map/ppermute | solution.py:449
  104.4 5.4 %collective-permute-done.17.refs_3_ = bf16[32,4096]{1,0:T(8,128)(2,1)S(1)} collective-permute-done((bf16[32,4096]{1,0:T(8,128)(2,1)S(1)}, bf16[32,4096]{1,0:T(8,128)(2,1)S(1)}, u32[]{:S(2)}, u32[]{:S(2)}) %collective-permute-start.17) | collective-permute-done | bytes 262176 | tf_op jit(solution)/shard_map/ppermute | solution.py:449
  109.8 1.6 %collective-permute-start.20 = (f32[4,1792]{1,0:T(4,128)S(1)}, f32[4,1792]{1,0:T(4,128)S(1)}, u32[]{:S(2)}, u32[]{:S(2)}) collective-permute-start(f32[4,1792]{1,0:T(4,128)S(1)} %pad_maximum_fusion.2), channel_id=1, source_target_pairs={{0,1},{1,0},{2,3},{3,2},{4,5},{5,4},{6,7},{7,6},{8,9},{9,8},{10,11... | collective-permute-start | bytes 86024 | tf_op jit(solution)/shard_map/ppermute | solution.py:452
  111.4 0.5 collective-permute-start.18
  111.8 1.8 %collective-permute-done.20 = f32[4,1792]{1,0:T(4,128)S(1)} collective-permute-done((f32[4,1792]{1,0:T(4,128)S(1)}, f32[4,1792]{1,0:T(4,128)S(1)}, u32[]{:S(2)}, u32[]{:S(2)}) %collective-permute-start.20) | collective-permute-done | bytes 28704 | tf_op jit(solution)/shard_map/ppermute | solution.py:452
  113.8 0.7 fusion.3
  114.5 0.8 collective-permute-done.18
  115.8 1.6 %convolution_add_fusion = f32[256,1792]{1,0:T(8,128)} fusion(f32[256,1792]{1,0:T(8,128)S(1)} %fusion.9, bf16[256,256]{1,0:T(8,128)(2,1)S(1)} %bitcast.29, bf16[256,1792]{1,0:T(8,128)(2,1)S(1)} %copy-done.12), kind=kOutput, calls=%fused_computation | convolution fusion | flops 235339776 | bytes 4718592 | tf_op jit(solution)/shard_map/dot_general | solution.py:556
  117.5 0.8 add_z.1
  118.3 1.1 fusion
  (74 shorter events, 1.9 us)
Async XLA Ops:
  0.6 23.0 %collective-permute-start.3 = (bf16[256,1792]{1,0:T(8,128)(2,1)}, bf16[256,1792]{1,0:T(8,128)(2,1)}, u32[]{:S(2)}, u32[]{:S(2)}) collective-permute-start(bf16[256,1792]{1,0:T(8,128)(2,1)} %cot_ref.3), channel_id=1, source_target_pairs={{0,1},{1,0},{2,3},{3,2},{4,5},{5,4},{6,7},{7,6},{8,9},{9,8},{10,11... | collective-permute-start | bytes 2752520 | tf_op jit(solution)/shard_map/ppermute | solution.py:452
  2.2 17.1 %collective-permute-start = (bf16[32,4096]{1,0:T(8,128)(2,1)}, bf16[32,4096]{1,0:T(8,128)(2,1)S(1)}, u32[]{:S(2)}, u32[]{:S(2)}) collective-permute-start(bf16[32,4096]{1,0:T(8,128)(2,1)} %refs_0_.7), channel_id=1, source_target_pairs={{0,4},{2,6},{4,0},{6,2},{8,12},{10,14},{12,8},{14,10},{16,20},{18,... | collective-permute-start | bytes 786440 | tf_op jit(solution)/shard_map/ppermute | solution.py:449
  3.7 30.5 %collective-permute-start.5 = (bf16[32,4096]{1,0:T(8,128)(2,1)}, bf16[32,4096]{1,0:T(8,128)(2,1)S(1)}, u32[]{:S(2)}, u32[]{:S(2)}) collective-permute-start(bf16[32,4096]{1,0:T(8,128)(2,1)} %refs_0_.7), channel_id=1, source_target_pairs={{0,16},{2,18},{4,20},{6,22},{8,24},{10,26},{12,28},{14,30},{16,0},... | collective-permute-start | bytes 786440 | tf_op jit(solution)/shard_map/ppermute | solution.py:449
  6.3 27.9 %collective-permute-start.8 = (bf16[32,4096]{1,0:T(8,128)(2,1)}, bf16[32,4096]{1,0:T(8,128)(2,1)S(1)}, u32[]{:S(2)}, u32[]{:S(2)}) collective-permute-start(bf16[32,4096]{1,0:T(8,128)(2,1)} %refs_0_.7), channel_id=1, source_target_pairs={{0,24},{2,26},{4,28},{6,30},{8,0},{10,2},{12,4},{14,6},{16,8},{18,... | collective-permute-start | bytes 786440 | tf_op jit(solution)/shard_map/ppermute | solution.py:449
  6.7 27.5 %collective-permute-start.1 = (bf16[32,4096]{1,0:T(8,128)(2,1)}, bf16[32,4096]{1,0:T(8,128)(2,1)S(1)}, u32[]{:S(2)}, u32[]{:S(2)}) collective-permute-start(bf16[32,4096]{1,0:T(8,128)(2,1)} %refs_0_.7), channel_id=1, source_target_pairs={{0,8},{2,10},{4,12},{6,14},{8,16},{10,18},{12,20},{14,22},{16,24},... | collective-permute-start | bytes 786440 | tf_op jit(solution)/shard_map/ppermute | solution.py:449
  8.4 1.2 copy-start
  9.6 0.7 copy-start.15
  10.3 13.4 %copy-start.4 = (bf16[256,1792]{1,0:T(8,128)(2,1)S(1)}, bf16[256,1792]{1,0:T(8,128)(2,1)}, u32[]{:S(2)}) copy-start(bf16[256,1792]{1,0:T(8,128)(2,1)} %cot_ref.3) | copy-start | bytes 2752516
  10.3 13.4 %copy-start.10 = (f32[16,1792]{1,0:T(8,128)S(1)}, f32[16,1792]{1,0:T(8,128)}, u32[]{:S(2)}) copy-start(f32[16,1792]{1,0:T(8,128)} %mag_ref.3) | copy-start | bytes 344068
  10.3 13.4 %copy-start.16 = (s32[512]{0:T(512)S(1)}, s32[512]{0:T(512)}, u32[]{:S(2)}) copy-start(s32[512]{0:T(512)} %tenant_ref.9) | copy-start | bytes 6148
  19.3 4.3 %collective-permute-start.2 = (f32[4,1792]{1,0:T(4,128)S(1)}, f32[4,1792]{1,0:T(4,128)S(1)}, u32[]{:S(2)}, u32[]{:S(2)}) collective-permute-start(f32[4,1792]{1,0:T(4,128)S(1)} %partial_norms.1.nsq_a), channel_id=1, source_target_pairs={{0,1},{1,0},{2,3},{3,2},{4,5},{5,4},{6,7},{7,6},{8,9},{9,8},{10,11... | collective-permute-start | bytes 86024 | tf_op jit(solution)/shard_map/ppermute | solution.py:452
  19.9 14.3 %copy-start.5 = (bf16[32,4096]{1,0:T(8,128)(2,1)S(1)}, bf16[32,4096]{1,0:T(8,128)(2,1)}, u32[]{:S(2)}) copy-start(bf16[32,4096]{1,0:T(8,128)(2,1)} %refs_0_.7) | copy-start | bytes 786436
  34.2 3.1 %copy-start.11 = (bf16[256,1792]{1,0:T(8,128)(2,1)}, bf16[256,1792]{1,0:T(8,128)(2,1)S(1)}, u32[]{:S(2)}) copy-start(bf16[256,1792]{1,0:T(8,128)(2,1)S(1)} %get-tuple-element.58) | copy-start | bytes 2752516
  34.2 1.6 %copy-start.22 = (bf16[128,4096]{1,0:T(8,128)(2,1)S(1)}, bf16[128,4096]{1,0:T(8,128)(2,1)}, u32[]{:S(2)}) copy-start(bf16[128,4096]{1,0:T(8,128)(2,1)} %get-tuple-element.39) | copy-start | bytes 3145732
  34.3 4.9 %collective-permute-start.9 = (bf16[128,4096]{1,0:T(8,128)(2,1)S(1)}, bf16[128,4096]{1,0:T(8,128)(2,1)S(1)}, u32[]{:S(2)}, u32[]{:S(2)}) collective-permute-start(bf16[128,4096]{1,0:T(8,128)(2,1)S(1)} %pad_maximum_fusion), channel_id=1, source_target_pairs={{0,2},{2,0},{4,6},{6,4},{8,10},{10,8},{12,14},{14,12},{16,18},{18,... | collective-permute-start | bytes 3145736 | tf_op jit(solution)/shard_map/ppermute | solution.py:449
  35.7 3.5 %collective-permute-start.7 = (bf16[128,4096]{1,0:T(8,128)(2,1)S(1)}, bf16[128,4096]{1,0:T(8,128)(2,1)S(1)}, u32[]{:S(2)}, u32[]{:S(2)}) collective-permute-start(bf16[128,4096]{1,0:T(8,128)(2,1)S(1)} %copy-done.22), channel_id=1, source_target_pairs={{0,2},{2,0},{4,6},{6,4},{8,10},{10,8},{12,14},{14,12},{16,18},{18,... | collective-permute-start | bytes 3145736 | tf_op jit(solution)/shard_map/ppermute | solution.py:449
  35.7 18.9 %collective-permute-start.6 = (bf16[32,4096]{1,0:T(8,128)(2,1)S(1)}, bf16[32,4096]{1,0:T(8,128)(2,1)S(1)}, u32[]{:S(2)}, u32[]{:S(2)}) collective-permute-start(bf16[32,4096]{1,0:T(8,128)(2,1)S(1)} %collective-permute-done.5.refs_4_), channel_id=1, source_target_pairs={{0,4},{2,6},{4,0},{6,2},{8,12},{10,14},{12,8},{14,10},{16,20},{18,... | collective-permute-start | bytes 786440 | tf_op jit(solution)/shard_map/ppermute | solution.py:449
  37.2 17.4 %collective-permute-start.10 = (bf16[32,4096]{1,0:T(8,128)(2,1)S(1)}, bf16[32,4096]{1,0:T(8,128)(2,1)S(1)}, u32[]{:S(2)}, u32[]{:S(2)}) collective-permute-start(bf16[32,4096]{1,0:T(8,128)(2,1)S(1)} %collective-permute-done.8.refs_6_), channel_id=1, source_target_pairs={{0,4},{2,6},{4,0},{6,2},{8,12},{10,14},{12,8},{14,10},{16,20},{18,... | collective-permute-start | bytes 786440 | tf_op jit(solution)/shard_map/ppermute | solution.py:449
  37.8 17.9 %collective-permute-start.4 = (bf16[32,4096]{1,0:T(8,128)(2,1)S(1)}, bf16[32,4096]{1,0:T(8,128)(2,1)S(1)}, u32[]{:S(2)}, u32[]{:S(2)}) collective-permute-start(bf16[32,4096]{1,0:T(8,128)(2,1)S(1)} %collective-permute-done.1.refs_2_), channel_id=1, source_target_pairs={{0,4},{2,6},{4,0},{6,2},{8,12},{10,14},{12,8},{14,10},{16,20},{18,... | collective-permute-start | bytes 786440 | tf_op jit(solution)/shard_map/ppermute | solution.py:449
  39.3 1.0 copy-start.18
  39.3 1.3 %copy-start.21 = (bf16[128,4096]{1,0:T(8,128)(2,1)}, bf16[128,4096]{1,0:T(8,128)(2,1)S(1)}, u32[]{:S(2)}) copy-start(bf16[128,4096]{1,0:T(8,128)(2,1)S(1)} %collective-permute-done.7.refs_4_) | copy-start | bytes 3145732
  52.9 0.9 copy-start.13
  53.9 0.8 copy-start.17
  54.7 10.3 %copy-start.19 = (bf16[32,4096]{1,0:T(8,128)(2,1)}, bf16[32,4096]{1,0:T(8,128)(2,1)S(1)}, u32[]{:S(2)}) copy-start(bf16[32,4096]{1,0:T(8,128)(2,1)S(1)} %collective-permute-done.10.refs_7_) | copy-start | bytes 786436
  56.8 4.0 %collective-permute-start.11 = (bf16[128,4096]{1,0:T(8,128)(2,1)}, bf16[128,4096]{1,0:T(8,128)(2,1)S(1)}, u32[]{:S(2)}, u32[]{:S(2)}) collective-permute-start(bf16[128,4096]{1,0:T(8,128)(2,1)} %pad_maximum_fusion.1), channel_id=1, source_target_pairs={{0,2},{2,0},{4,6},{6,4},{8,10},{10,8},{12,14},{14,12},{16,18},{18,... | collective-permute-start | bytes 3145736 | tf_op jit(solution)/shard_map/ppermute | solution.py:449
  56.8 4.5 %collective-permute-start.13 = (bf16[128,4096]{1,0:T(8,128)(2,1)}, bf16[128,4096]{1,0:T(8,128)(2,1)}, u32[]{:S(2)}, u32[]{:S(2)}) collective-permute-start(bf16[128,4096]{1,0:T(8,128)(2,1)} %get-tuple-element.46), channel_id=1, source_target_pairs={{0,2},{2,0},{4,6},{6,4},{8,10},{10,8},{12,14},{14,12},{16,18},{18,... | collective-permute-start | bytes 3145736 | tf_op jit(solution)/shard_map/ppermute | solution.py:449
  57.6 23.7 %collective-permute-start.12 = (bf16[64,4096]{1,0:T(8,128)(2,1)}, bf16[64,4096]{1,0:T(8,128)(2,1)}, u32[]{:S(2)}, u32[]{:S(2)}) collective-permute-start(bf16[64,4096]{1,0:T(8,128)(2,1)} %copy-done.17), channel_id=1, source_target_pairs={{0,4},{2,6},{4,0},{6,2},{8,12},{10,14},{12,8},{14,10},{16,20},{18,... | collective-permute-start | bytes 1572872 | tf_op jit(solution)/shard_map/ppermute | solution.py:449
  60.8 4.2 %copy-start.1 = (bf16[128,4096]{1,0:T(8,128)(2,1)}, bf16[128,4096]{1,0:T(8,128)(2,1)S(1)}, u32[]{:S(2)}) copy-start(bf16[128,4096]{1,0:T(8,128)(2,1)S(1)} %collective-permute-done.11.refs_0_.refs_9_) | copy-start | bytes 3145732
  61.3 1.6 %copy-start.8 = (f32[128,4096]{1,0:T(8,128)S(1)}, f32[128,4096]{1,0:T(8,128)}, u32[]{:S(2)}) copy-start(f32[128,4096]{1,0:T(8,128)} %get-tuple-element.45.keep_ref) | copy-start | bytes 6291460
  65.0 1.0 copy-start.2
  66.0 16.9 %collective-permute-start.14 = (bf16[64,4096]{1,0:T(8,128)(2,1)}, bf16[64,4096]{1,0:T(8,128)(2,1)S(1)}, u32[]{:S(2)}, u32[]{:S(2)}) collective-permute-start(bf16[64,4096]{1,0:T(8,128)(2,1)} %get-tuple-element.48), channel_id=1, source_target_pairs={{0,4},{2,6},{4,0},{6,2},{8,12},{10,14},{12,8},{14,10},{16,20},{18,... | collective-permute-start | bytes 1572872 | tf_op jit(solution)/shard_map/ppermute | solution.py:449
  67.6 15.2 %copy-start.3 = (f32[64,4096]{1,0:T(8,128)S(1)}, f32[64,4096]{1,0:T(8,128)}, u32[]{:S(2)}) copy-start(f32[64,4096]{1,0:T(8,128)} %copy-done.2) | copy-start | bytes 3145732
  67.6 15.2 %copy-start.9 = (f32[64,4096]{1,0:T(8,128)S(1)}, f32[64,4096]{1,0:T(8,128)}, u32[]{:S(2)}) copy-start(f32[64,4096]{1,0:T(8,128)} %get-tuple-element.43.refs_0_) | copy-start | bytes 3145732
  79.8 38.5 %collective-permute-start.15 = (bf16[256,1792]{1,0:T(8,128)(2,1)}, bf16[256,1792]{1,0:T(8,128)(2,1)S(1)}, u32[]{:S(2)}, u32[]{:S(2)}) collective-permute-start(bf16[256,1792]{1,0:T(8,128)(2,1)} %get-tuple-element.52), channel_id=1, source_target_pairs={{0,1},{1,0},{2,3},{3,2},{4,5},{5,4},{6,7},{7,6},{8,9},{9,8},{10,11... | collective-permute-start | bytes 2752520 | tf_op jit(solution)/shard_map/ppermute | solution.py:452
  84.9 0.8 copy-start.6
  85.7 18.7 %collective-permute-start.16 = (bf16[32,4096]{1,0:T(8,128)(2,1)S(1)}, bf16[32,4096]{1,0:T(8,128)(2,1)S(1)}, u32[]{:S(2)}, u32[]{:S(2)}) collective-permute-start(bf16[32,4096]{1,0:T(8,128)(2,1)S(1)} %get-tuple-element.55), channel_id=1, source_target_pairs={{0,16},{2,18},{4,20},{6,22},{8,24},{10,26},{12,28},{14,30},{16,0},... | collective-permute-start | bytes 786440 | tf_op jit(solution)/shard_map/ppermute | solution.py:449
  88.3 21.5 %collective-permute-start.17 = (bf16[32,4096]{1,0:T(8,128)(2,1)S(1)}, bf16[32,4096]{1,0:T(8,128)(2,1)S(1)}, u32[]{:S(2)}, u32[]{:S(2)}) collective-permute-start(bf16[32,4096]{1,0:T(8,128)(2,1)S(1)} %get-tuple-element.56), channel_id=1, source_target_pairs={{0,24},{2,26},{4,28},{6,30},{8,0},{10,2},{12,4},{14,6},{16,8},{18,... | collective-permute-start | bytes 786440 | tf_op jit(solution)/shard_map/ppermute | solution.py:449
  101.0 14.4 %copy-start.14 = (bf16[256,1792]{1,0:T(8,128)(2,1)S(1)}, bf16[256,1792]{1,0:T(8,128)(2,1)}, u32[]{:S(2)}) copy-start(bf16[256,1792]{1,0:T(8,128)(2,1)} %copy-done.13) | copy-start | bytes 2752516
  101.0 16.4 %collective-permute-start.19 = (bf16[32,4096]{1,0:T(8,128)(2,1)S(1)}, bf16[32,4096]{1,0:T(8,128)(2,1)S(1)}, u32[]{:S(2)}, u32[]{:S(2)}) collective-permute-start(bf16[32,4096]{1,0:T(8,128)(2,1)S(1)} %get-tuple-element.61), channel_id=1, source_target_pairs={{0,8},{2,10},{4,12},{6,14},{8,16},{10,18},{12,20},{14,22},{16,24},... | collective-permute-start | bytes 786440 | tf_op jit(solution)/shard_map/ppermute | solution.py:449
  109.8 3.9 %collective-permute-start.20 = (f32[4,1792]{1,0:T(4,128)S(1)}, f32[4,1792]{1,0:T(4,128)S(1)}, u32[]{:S(2)}, u32[]{:S(2)}) collective-permute-start(f32[4,1792]{1,0:T(4,128)S(1)} %pad_maximum_fusion.2), channel_id=1, source_target_pairs={{0,1},{1,0},{2,3},{3,2},{4,5},{5,4},{6,7},{7,6},{8,9},{9,8},{10,11... | collective-permute-start | bytes 86024 | tf_op jit(solution)/shard_map/ppermute | solution.py:452
  111.4 3.9 %collective-permute-start.18 = (f32[16,512]{1,0:T(8,128)S(1)}, f32[16,512]{1,0:T(8,128)S(1)}, u32[]{:S(2)}, u32[]{:S(2)}) collective-permute-start(f32[16,512]{1,0:T(8,128)S(1)} %constant_dynamic-update-slice_fusion), channel_id=1, source_target_pairs={{0,1},{1,0},{2,3},{3,2},{4,5},{5,4},{6,7},{7,6},{8,9},{9,8},{10,11... | collective-permute-start | bytes 98312 | tf_op jit(solution)/shard_map/ppermute | solution.py:452
  113.8 2.0 %copy-start.12 = (bf16[256,1792]{1,0:T(8,128)(2,1)S(1)}, bf16[256,1792]{1,0:T(8,128)(2,1)}, u32[]{:S(2)}) copy-start(bf16[256,1792]{1,0:T(8,128)(2,1)} %copy-done.11) | copy-start | bytes 2752516
  115.8 1.7 %copy-start.7 = (f32[32,4096]{1,0:T(8,128)S(1)}, f32[32,4096]{1,0:T(8,128)}, u32[]{:S(2)}) copy-start(f32[32,4096]{1,0:T(8,128)} %copy-done.6) | copy-start | bytes 1572868
  115.8 2.5 %copy-start.20 = (f32[256,1792]{1,0:T(8,128)S(1)}, f32[256,1792]{1,0:T(8,128)}, u32[]{:S(2)}) copy-start(f32[256,1792]{1,0:T(8,128)} %get-tuple-element.51) | copy-start | bytes 5505028

commit v9 on v7

--- a/solution.py
+++ b/solution.py
@@ -494,6 +494,10 @@
     def across_x(made):
         return made[0], move(made[1], 0, 1, 0)
 
+    def scaled_output(pre, scale):
+        out = pre.reshape(blocks_mine, BLOCK, cols) * scale[:, None, :]
+        return out.astype(BF16).reshape(rows_row, cols)
+
     if pair:
         ours = gradient(0, [], [cots[1]])
         for k in [nz - 1] + list(range(1, nz - 1)):
@@ -518,9 +522,11 @@
         part, dots_here, low_here = project(0, F32, [finals[0]])
         dots = jnp.concatenate([dots_here, dots_away], axis=0)
         low = jnp.concatenate([low_here, low_away], axis=1)
-        late = (finals[nz // 2], finals[nz - 1])
-        dots = dots + jnp.roll(swap(once(dots, late)), blocks_mine, axis=0)
-        low = low + jnp.roll(swap(once(low, late)), rows_row, axis=1)
+        output = scaled_output(part + arrived.astype(F32), ours[0])
+        new_dots = swap(once(dots, finals[nz // 2]))
+        new_low = once(swap(once(low, finals[nz - 1])), output)
+        dots = dots + jnp.roll(new_dots, blocks_mine, axis=0)
+        low = low + jnp.roll(new_low, rows_row, axis=1)
         parts = [ours, theirs]
     else:
         ours = gradient(0, [], [])
@@ -561,14 +567,10 @@
         group = terms[:, g * size : (g + 1) * size]
         grad_m = grad_m + functools.reduce(jnp.add, [group[:, i] for i in range(size)])
     grad_inputs = add_z([once(finals[0], grad_b)] + finals[1:])
-    if pair:
-        pre = part + arrived.astype(F32)
-        scale_mine = parts[0][0]
-    else:
+    if not pair:
         pre = lax.psum_scatter(part, "row", scatter_dimension=0, tiled=True)
         scale_mine = lax.dynamic_slice_in_dim(scales, row * blocks_mine, blocks_mine, 0)
-    output = (pre.reshape(blocks_mine, BLOCK, cols) * scale_mine[:, None, :]).astype(BF16)
-    output = output.reshape(rows_row, cols)
+        output = scaled_output(pre, scale_mine)
     return (output, grad_inputs, grad_b, grad_m / magnitude)
 
 

time: 119 us -> 118 us (level)
  waiting for transfers between devices: 18 us -> 13.9 us
  other arithmetic: 3.52 us -> 5.04 us
    ppermute x5, waiting for transfers between devices: 6.25 us -> 3.67 us  [swap(): return lax.ppermute(value, 'row', [(0, 1), (1, 0)])]
    convert_element_type x1, other arithmetic: 1.13 us -> 2.71 us  [scaled_output(): return out.astype(BF16).reshape(rows_row, cols)]
    ppermute x16, waiting for transfers between devices: 11.7 us -> 10.2 us  [move(): return lax.ppermute(value, 'col', perm)]
    unnamed x47 -> x45, local copies, waits for them, and re-layouts: 9.68 us -> 10.3 us
  transfers between devices with their start and end apart: 21 -> 21, of which waited for: 9 -> 7; matrix products, arithmetic and copies ran while one was open for 3% -> 5% of each run, Pallas kernels for 51% -> 51%
where the time goes in v9:
time: 118 us; the launch traced here: 117 us
  Pallas kernels  60.3 us (51%)
  starting transfers between devices  24.6 us (21%)
  waiting for transfers between devices  13.9 us (12%)
  local copies, waits for them, and re-layouts  10.6 us (9%)
  other arithmetic  5.04 us (4%)
  matrix products  2.05 us (2%)
    pallas_call x2, Pallas kernels, forward(): pl.pallas_call(functools.partial(forward_body, nb, rank, nz), out_shape=s...  24.4 us
    pallas_call x2, Pallas kernels, input_gradient(): pl.pallas_call(functools.partial(grad_body, nb, rank, len(add)), out_shap...  22 us
    ppermute x16, starting transfers between devices, move(): return lax.ppermute(value, 'col', perm)  17.9 us
    unnamed x45, local copies, waits for them, and re-layouts  10.3 us
    ppermute x16, waiting for transfers between devices, move(): return lax.ppermute(value, 'col', perm)  10.2 us
    pallas_call x1, Pallas kernels, partial_norms(): pl.pallas_call(functools.partial(norm_body, nblk, rank), out_shape=shape,...  9.01 us
    ppermute x5, starting transfers between devices, swap(): return lax.ppermute(value, 'row', [(0, 1), (1, 0)])  6.75 us
    ppermute x5, waiting for transfers between devices, swap(): return lax.ppermute(value, 'row', [(0, 1), (1, 0)])  3.67 us
  transfers between devices with their start and end apart: 21, of which 7 were waited for; matrix products, arithmetic and copies ran while one was open for 5% of the time, Pallas kernels for 51%

profile of v9, /device:TPU:8, one launch (start us, length us, event | category | flops | bytes accessed | tf_op | source)
XLA Modules:
  0.0 117.5 jit_solution(4417658726001590244)
XLA Ops:
  0.6 1.6 %collective-permute-start.3 = (bf16[256,1792]{1,0:T(8,128)(2,1)}, bf16[256,1792]{1,0:T(8,128)(2,1)}, u32[]{:S(2)}, u32[]{:S(2)}) collective-permute-start(bf16[256,1792]{1,0:T(8,128)(2,1)} %cot_ref.3), channel_id=1, source_target_pairs={{0,1},{1,0},{2,3},{3,2},{4,5},{5,4},{6,7},{7,6},{8,9},{9,8},{10,11... | collective-permute-start | bytes 2752520 | tf_op jit(solution)/shard_map/ppermute | solution.py:451
  2.2 1.5 %collective-permute-start = (bf16[32,4096]{1,0:T(8,128)(2,1)}, bf16[32,4096]{1,0:T(8,128)(2,1)S(1)}, u32[]{:S(2)}, u32[]{:S(2)}) collective-permute-start(bf16[32,4096]{1,0:T(8,128)(2,1)} %refs_0_.7), channel_id=1, source_target_pairs={{0,4},{2,6},{4,0},{6,2},{8,12},{10,14},{12,8},{14,10},{16,20},{18,... | collective-permute-start | bytes 786440 | tf_op jit(solution)/shard_map/ppermute | solution.py:448
  3.7 2.6 %collective-permute-start.5 = (bf16[32,4096]{1,0:T(8,128)(2,1)}, bf16[32,4096]{1,0:T(8,128)(2,1)S(1)}, u32[]{:S(2)}, u32[]{:S(2)}) collective-permute-start(bf16[32,4096]{1,0:T(8,128)(2,1)} %refs_0_.7), channel_id=1, source_target_pairs={{0,16},{2,18},{4,20},{6,22},{8,24},{10,26},{12,28},{14,30},{16,0},... | collective-permute-start | bytes 786440 | tf_op jit(solution)/shard_map/ppermute | solution.py:448
  6.3 0.4 collective-permute-start.8
  6.7 1.6 %collective-permute-start.1 = (bf16[32,4096]{1,0:T(8,128)(2,1)}, bf16[32,4096]{1,0:T(8,128)(2,1)S(1)}, u32[]{:S(2)}, u32[]{:S(2)}) collective-permute-start(bf16[32,4096]{1,0:T(8,128)(2,1)} %refs_0_.7), channel_id=1, source_target_pairs={{0,8},{2,10},{4,12},{6,14},{8,16},{10,18},{12,20},{14,22},{16,24},... | collective-permute-start | bytes 786440 | tf_op jit(solution)/shard_map/ppermute | solution.py:448
  8.4 1.2 %copy-done = bf16[16,16,1792]{2,1,0:T(8,128)(2,1)S(1)} copy-done((bf16[16,16,1792]{2,1,0:T(8,128)(2,1)S(1)}, bf16[16,16,1792]{2,1,0:T(8,128)(2,1)}, u32[]{:S(2)}) %copy-start) | copy-done | bytes 917528
  9.6 0.7 copy-done.15
  10.3 9.0 %partial_norms.1.nsq_a = f32[4,1792]{1,0:T(4,128)S(1)} custom-call(s32[512]{0:T(512)S(1)} %copy-done.15, bf16[4096,1792]{1,0:T(8,128)(2,1)} %w_hbm.5, bf16[16,16,4096]{2,1,0:T(8,128)(2,1)} %a_hbm.5, bf16[16,16,1792]{2,1,0:T(8,128)(2,1)S(1)} %copy-done), custom_call_target="tpu_custom_call" | custom-call | flops 1000 | bytes 1000 | tf_op jit(solution)/shard_map/partial_norms/pallas_call | solution.py:116
  19.3 0.6 collective-permute-start.2
  19.9 3.7 %collective-permute-done.2.nsq_b = f32[4,1792]{1,0:T(4,128)S(1)} collective-permute-done((f32[4,1792]{1,0:T(4,128)S(1)}, f32[4,1792]{1,0:T(4,128)S(1)}, u32[]{:S(2)}, u32[]{:S(2)}) %collective-permute-start.2) | collective-permute-done | bytes 28704 | tf_op jit(solution)/shard_map/ppermute | solution.py:451
  23.6 9.4 %input_gradient.2 = (f32[2,1792]{1,0:T(2,128)S(1)}, bf16[256,1792]{1,0:T(8,128)(2,1)S(1)}, f32[128,4096]{1,0:T(8,128)}, bf16[128,4096]{1,0:T(8,128)(2,1)}) custom-call(s32[512]{0:T(512)S(1)} %copy-done.16, s32[4]{0:T(128)S(1)} %pad_add_fusion.place_ref, bf16[256,1792]{1,0:T(8,128)(2,1)S(1)} %copy-done.4, f32[4,1792]{1,0:T(4,128)S(1)} %partial_norms.1.nsq_a, ...), custom_call_target="tpu_custom_call" | custom-call | flops 1000 | bytes 1000 | tf_op jit(solution)/shard_map/input_gradient/pallas_call | solution.py:210
  33.3 1.3 %copy-done.21 = bf16[128,4096]{1,0:T(8,128)(2,1)S(1)} copy-done((bf16[128,4096]{1,0:T(8,128)(2,1)S(1)}, bf16[128,4096]{1,0:T(8,128)(2,1)}, u32[]{:S(2)}) %copy-start.21) | copy-done | bytes 1048600
  34.6 1.5 %collective-permute-start.6 = (bf16[32,4096]{1,0:T(8,128)(2,1)S(1)}, bf16[32,4096]{1,0:T(8,128)(2,1)S(1)}, u32[]{:S(2)}, u32[]{:S(2)}) collective-permute-start(bf16[32,4096]{1,0:T(8,128)(2,1)S(1)} %collective-permute-done.5.refs_4_), channel_id=1, source_target_pairs={{0,4},{2,6},{4,0},{6,2},{8,12},{10,14},{12,8},{14,10},{16,20},{18,... | collective-permute-start | bytes 786440 | tf_op jit(solution)/shard_map/ppermute | solution.py:448
  36.1 0.5 collective-permute-start.10
  36.7 1.5 %collective-permute-start.4 = (bf16[32,4096]{1,0:T(8,128)(2,1)S(1)}, bf16[32,4096]{1,0:T(8,128)(2,1)S(1)}, u32[]{:S(2)}, u32[]{:S(2)}) collective-permute-start(bf16[32,4096]{1,0:T(8,128)(2,1)S(1)} %collective-permute-done.1.refs_2_), channel_id=1, source_target_pairs={{0,4},{2,6},{4,0},{6,2},{8,12},{10,14},{12,8},{14,10},{16,20},{18,... | collective-permute-start | bytes 786440 | tf_op jit(solution)/shard_map/ppermute | solution.py:448
  38.2 1.0 copy-done.18
  39.5 12.6 %input_gradient.3 = (f32[2,1792]{1,0:T(2,128)S(1)}, bf16[256,1792]{1,0:T(8,128)(2,1)S(1)}, f32[128,4096]{1,0:T(8,128)}, bf16[128,4096]{1,0:T(8,128)(2,1)}, f32[6...) custom-call(s32[512]{0:T(512)S(1)} %copy-done.16, s32[4]{0:T(128)S(1)} %get-tuple-element.68.place_ref, ...), custom_call_target="tpu_custom_call" | custom-call | flops 1000 | bytes 1000 | tf_op jit(solution)/shard_map/input_gradient/pallas_call | solution.py:210
  52.1 0.9 copy-done.13
  53.0 0.8 copy-done.17
  53.8 0.8 collective-permute-done.4.refs_3_
  54.6 1.0 pad_maximum_fusion.1
  55.6 0.5 collective-permute-start.13
  56.4 1.5 %collective-permute-start.12 = (bf16[64,4096]{1,0:T(8,128)(2,1)}, bf16[64,4096]{1,0:T(8,128)(2,1)}, u32[]{:S(2)}, u32[]{:S(2)}) collective-permute-start(bf16[64,4096]{1,0:T(8,128)(2,1)} %copy-done.17), channel_id=1, source_target_pairs={{0,4},{2,6},{4,0},{6,2},{8,12},{10,14},{12,8},{14,10},{16,20},{18,... | collective-permute-start | bytes 1572872 | tf_op jit(solution)/shard_map/ppermute | solution.py:448
  57.9 1.7 %collective-permute-done.11.refs_0_.refs_9_ = bf16[128,4096]{1,0:T(8,128)(2,1)S(1)} collective-permute-done((bf16[128,4096]{1,0:T(8,128)(2,1)}, bf16[128,4096]{1,0:T(8,128)(2,1)S(1)}, u32[]{:S(2)}, u32[]{:S(2)}) %collective-permute-start.11) | collective-permute-done | bytes 1048608 | tf_op jit(solution)/shard_map/ppermute | solution.py:448
  59.6 0.5 collective-permute-done.13.recv_ref
  60.1 1.6 %copy-done.8 = f32[128,4096]{1,0:T(8,128)S(1)} copy-done((f32[128,4096]{1,0:T(8,128)S(1)}, f32[128,4096]{1,0:T(8,128)}, u32[]{:S(2)}) %copy-start.8) | copy-done | bytes 2097176
  61.7 2.1 %add_core.1 = (f32[64,4096]{1,0:T(8,128)S(1)}, bf16[64,4096]{1,0:T(8,128)(2,1)}) custom-call(f32[128,4096]{1,0:T(8,128)S(1)} %copy-done.8, bf16[128,4096]{1,0:T(8,128)(2,1)} %collective-permute-done.13.recv_ref, bf16[128,4096]{1,0:T(8,128)(2,1)S(1)} %collective-permute-done.11.refs_0_.refs_9_), custom_call_target="tpu_custom_call" | custom-call | flops 1000 | bytes 1000 | tf_op jit(solution)/shard_map/add_core/pallas_call | solution.py:247
  63.8 1.0 copy-done.2
  64.8 1.5 %collective-permute-start.14 = (bf16[64,4096]{1,0:T(8,128)(2,1)}, bf16[64,4096]{1,0:T(8,128)(2,1)S(1)}, u32[]{:S(2)}, u32[]{:S(2)}) collective-permute-start(bf16[64,4096]{1,0:T(8,128)(2,1)} %get-tuple-element.49), channel_id=1, source_target_pairs={{0,4},{2,6},{4,0},{6,2},{8,12},{10,14},{12,8},{14,10},{16,20},{18,... | collective-permute-start | bytes 1572872 | tf_op jit(solution)/shard_map/ppermute | solution.py:448
  66.5 12.1 %forward.2 = (bf16[256,1792]{1,0:T(8,128)(2,1)}, f32[2,1792]{1,0:T(2,128)S(1)}, f32[16,256]{1,0:T(8,128)S(1)}) custom-call(s32[512]{0:T(512)S(1)} %copy-done.16, s32[4]{0:T(128)S(1)} %get-tuple-element.68.place_ref, bf16[256,1792]{1,0:T(8,128)(2,1)} %collective-permute-done.3.refs_3_.cot_ref, bf16[4096,1792]{1,0:T(8,128)(2,1)} %w_hbm.5, ...), custom_call_target="tpu_custom_call" | custom-call | flops 1000 | bytes 1000 | tf_op jit(solution)/shard_map/forward/pallas_call | solution.py:404
  78.6 1.5 %collective-permute-start.15 = (bf16[256,1792]{1,0:T(8,128)(2,1)}, bf16[256,1792]{1,0:T(8,128)(2,1)S(1)}, u32[]{:S(2)}, u32[]{:S(2)}) collective-permute-start(bf16[256,1792]{1,0:T(8,128)(2,1)} %get-tuple-element.53), channel_id=1, source_target_pairs={{0,1},{1,0},{2,3},{3,2},{4,5},{5,4},{6,7},{7,6},{8,9},{9,8},{10,11... | collective-permute-start | bytes 2752520 | tf_op jit(solution)/shard_map/ppermute | solution.py:451
  80.1 1.6 %collective-permute-done.14.refs_3_ = bf16[64,4096]{1,0:T(8,128)(2,1)S(1)} collective-permute-done((bf16[64,4096]{1,0:T(8,128)(2,1)}, bf16[64,4096]{1,0:T(8,128)(2,1)S(1)}, u32[]{:S(2)}, u32[]{:S(2)}) %collective-permute-start.14) | collective-permute-done | bytes 524320 | tf_op jit(solution)/shard_map/ppermute | solution.py:448
  81.7 2.0 %add_x.1 = (f32[32,4096]{1,0:T(8,128)S(1)}, bf16[32,4096]{1,0:T(8,128)(2,1)S(1)}, bf16[32,4096]{1,0:T(8,128)(2,1)S(1)}, bf16[32,4096]{1,0:T(8,128)(2,1)S(1)}) custom-call(s32[5]{0:T(128)S(1)} %stack.39.place_ref, f32[64,4096]{1,0:T(8,128)S(1)} %copy-done.9, bf16[64,4096]{1,0:T(8,128)(2,1)} %collective-permute-done.12.refs_1_, f32[64,4096]{1,0:T(8,128)S(1)} %copy-done.3, ...), custom_call_target="tpu_custom_call" | custom-call | flops 1000 | bytes 1000 | tf_op jit(solution)/shard_map/add_x/pallas_call | solution.py:286
  83.8 0.8 copy-done.6
  84.6 2.6 %collective-permute-start.19 = (bf16[32,4096]{1,0:T(8,128)(2,1)S(1)}, bf16[32,4096]{1,0:T(8,128)(2,1)S(1)}, u32[]{:S(2)}, u32[]{:S(2)}) collective-permute-start(bf16[32,4096]{1,0:T(8,128)(2,1)S(1)} %get-tuple-element.63), channel_id=1, source_target_pairs={{0,16},{2,18},{4,20},{6,22},{8,24},{10,26},{12,28},{14,30},{16,0},... | collective-permute-start | bytes 786440 | tf_op jit(solution)/shard_map/ppermute | solution.py:448
  87.2 0.4 collective-permute-start.16
  87.6 12.2 %forward.3 = (f32[256,1792]{1,0:T(8,128)}, f32[2,1792]{1,0:T(2,128)S(1)}, f32[16,256]{1,0:T(8,128)S(1)}) custom-call(s32[512]{0:T(512)S(1)} %copy-done.16, s32[4]{0:T(128)S(1)} %pad_add_fusion.place_ref, bf16[256,1792]{1,0:T(8,128)(2,1)} %cot_ref.3, bf16[4096,1792]{1,0:T(8,128)(2,1)} %w_hbm.5, bf16[16,16,4096]{2,1,0:T(8,128)(2,1)} %a_hbm.5, ...), custom_call_target="tpu_custom_call" | custom-call | flops 1000 | bytes 1000 | tf_op jit(solution)/shard_map/forward/pallas_call | solution.py:404
  99.9 1.6 %collective-permute-start.18 = (bf16[32,4096]{1,0:T(8,128)(2,1)S(1)}, bf16[32,4096]{1,0:T(8,128)(2,1)S(1)}, u32[]{:S(2)}, u32[]{:S(2)}) collective-permute-start(bf16[32,4096]{1,0:T(8,128)(2,1)S(1)} %get-tuple-element.62), channel_id=1, source_target_pairs={{0,8},{2,10},{4,12},{6,14},{8,16},{10,18},{12,20},{14,22},{16,24},... | collective-permute-start | bytes 786440 | tf_op jit(solution)/shard_map/ppermute | solution.py:448
  101.5 1.8 %collective-permute-done.19.refs_2_ = bf16[32,4096]{1,0:T(8,128)(2,1)S(1)} collective-permute-done((bf16[32,4096]{1,0:T(8,128)(2,1)S(1)}, bf16[32,4096]{1,0:T(8,128)(2,1)S(1)}, u32[]{:S(2)}, u32[]{:S(2)}) %collective-permute-start.19) | collective-permute-done | bytes 262176 | tf_op jit(solution)/shard_map/ppermute | solution.py:448
  103.3 1.5 %collective-permute-start.20 = (f32[4,1792]{1,0:T(4,128)S(1)}, f32[4,1792]{1,0:T(4,128)S(1)}, u32[]{:S(2)}, u32[]{:S(2)}) collective-permute-start(f32[4,1792]{1,0:T(4,128)S(1)} %pad_maximum_fusion.2), channel_id=1, source_target_pairs={{0,1},{1,0},{2,3},{3,2},{4,5},{5,4},{6,7},{7,6},{8,9},{9,8},{10,11... | collective-permute-start | bytes 86024 | tf_op jit(solution)/shard_map/ppermute | solution.py:451
  104.8 3.8 %collective-permute-done.16.refs_3_ = bf16[32,4096]{1,0:T(8,128)(2,1)S(1)} collective-permute-done((bf16[32,4096]{1,0:T(8,128)(2,1)S(1)}, bf16[32,4096]{1,0:T(8,128)(2,1)S(1)}, u32[]{:S(2)}, u32[]{:S(2)}) %collective-permute-start.16) | collective-permute-done | bytes 262176 | tf_op jit(solution)/shard_map/ppermute | solution.py:448
  108.7 1.6 %collective-permute-start.17 = (f32[16,512]{1,0:T(8,128)S(1)}, f32[16,512]{1,0:T(8,128)S(1)}, u32[]{:S(2)}, u32[]{:S(2)}) collective-permute-start(f32[16,512]{1,0:T(8,128)S(1)} %constant_dynamic-update-slice_fusion), channel_id=1, source_target_pairs={{0,1},{1,0},{2,3},{3,2},{4,5},{5,4},{6,7},{7,6},{8,9},{9,8},{10,11... | collective-permute-start | bytes 98312 | tf_op jit(solution)/shard_map/ppermute | solution.py:451
  110.4 0.7 fusion.3
  111.1 2.7 %fusion = bf16[256,1792]{1,0:T(8,128)(2,1)} fusion(f32[256,1792]{1,0:T(8,128)} %get-tuple-element.52, bf16[256,1792]{1,0:T(8,128)(2,1)S(1)} %collective-permute-done.15, f32[2,1792]{1,0:T(2,128)S(1)} %get-tuple-element.36), kind=kLoop, calls=%fused_computation.2 | loop fusion | flops 1835008 | bytes 3684352 | tf_op jit(solution)/shard_map/convert_element_type | solution.py:499
  113.9 0.4 fusion.9
  114.3 0.7 copy-done.12
  115.0 1.6 %convolution_add_fusion = f32[256,1792]{1,0:T(8,128)} fusion(f32[256,1792]{1,0:T(8,128)S(1)} %fusion.9, bf16[256,256]{1,0:T(8,128)(2,1)S(1)} %bitcast.28, bf16[256,1792]{1,0:T(8,128)(2,1)S(1)} %copy-done.12), kind=kOutput, calls=%fused_computation | convolution fusion | flops 235339776 | bytes 4718592 | tf_op jit(solution)/shard_map/dot_general | solution.py:561
  116.6 0.8 add_z.1
  (72 shorter events, 1.4 us)
Async XLA Ops:
  0.6 23.0 %collective-permute-start.3 = (bf16[256,1792]{1,0:T(8,128)(2,1)}, bf16[256,1792]{1,0:T(8,128)(2,1)}, u32[]{:S(2)}, u32[]{:S(2)}) collective-permute-start(bf16[256,1792]{1,0:T(8,128)(2,1)} %cot_ref.3), channel_id=1, source_target_pairs={{0,1},{1,0},{2,3},{3,2},{4,5},{5,4},{6,7},{7,6},{8,9},{9,8},{10,11... | collective-permute-start | bytes 2752520 | tf_op jit(solution)/shard_map/ppermute | solution.py:451
  2.2 17.1 %collective-permute-start = (bf16[32,4096]{1,0:T(8,128)(2,1)}, bf16[32,4096]{1,0:T(8,128)(2,1)S(1)}, u32[]{:S(2)}, u32[]{:S(2)}) collective-permute-start(bf16[32,4096]{1,0:T(8,128)(2,1)} %refs_0_.7), channel_id=1, source_target_pairs={{0,4},{2,6},{4,0},{6,2},{8,12},{10,14},{12,8},{14,10},{16,20},{18,... | collective-permute-start | bytes 786440 | tf_op jit(solution)/shard_map/ppermute | solution.py:448
  3.7 29.4 %collective-permute-start.5 = (bf16[32,4096]{1,0:T(8,128)(2,1)}, bf16[32,4096]{1,0:T(8,128)(2,1)S(1)}, u32[]{:S(2)}, u32[]{:S(2)}) collective-permute-start(bf16[32,4096]{1,0:T(8,128)(2,1)} %refs_0_.7), channel_id=1, source_target_pairs={{0,16},{2,18},{4,20},{6,22},{8,24},{10,26},{12,28},{14,30},{16,0},... | collective-permute-start | bytes 786440 | tf_op jit(solution)/shard_map/ppermute | solution.py:448
  6.3 26.8 %collective-permute-start.8 = (bf16[32,4096]{1,0:T(8,128)(2,1)}, bf16[32,4096]{1,0:T(8,128)(2,1)S(1)}, u32[]{:S(2)}, u32[]{:S(2)}) collective-permute-start(bf16[32,4096]{1,0:T(8,128)(2,1)} %refs_0_.7), channel_id=1, source_target_pairs={{0,24},{2,26},{4,28},{6,30},{8,0},{10,2},{12,4},{14,6},{16,8},{18,... | collective-permute-start | bytes 786440 | tf_op jit(solution)/shard_map/ppermute | solution.py:448
  6.7 26.4 %collective-permute-start.1 = (bf16[32,4096]{1,0:T(8,128)(2,1)}, bf16[32,4096]{1,0:T(8,128)(2,1)S(1)}, u32[]{:S(2)}, u32[]{:S(2)}) collective-permute-start(bf16[32,4096]{1,0:T(8,128)(2,1)} %refs_0_.7), channel_id=1, source_target_pairs={{0,8},{2,10},{4,12},{6,14},{8,16},{10,18},{12,20},{14,22},{16,24},... | collective-permute-start | bytes 786440 | tf_op jit(solution)/shard_map/ppermute | solution.py:448
  8.4 1.2 %copy-start = (bf16[16,16,1792]{2,1,0:T(8,128)(2,1)S(1)}, bf16[16,16,1792]{2,1,0:T(8,128)(2,1)}, u32[]{:S(2)}) copy-start(bf16[16,16,1792]{2,1,0:T(8,128)(2,1)} %up_hbm.5) | copy-start | bytes 2752516
  9.6 0.7 copy-start.15
  10.3 13.4 %copy-start.4 = (bf16[256,1792]{1,0:T(8,128)(2,1)S(1)}, bf16[256,1792]{1,0:T(8,128)(2,1)}, u32[]{:S(2)}) copy-start(bf16[256,1792]{1,0:T(8,128)(2,1)} %cot_ref.3) | copy-start | bytes 2752516
  10.3 13.4 %copy-start.10 = (f32[16,1792]{1,0:T(8,128)S(1)}, f32[16,1792]{1,0:T(8,128)}, u32[]{:S(2)}) copy-start(f32[16,1792]{1,0:T(8,128)} %mag_ref.3) | copy-start | bytes 344068
  10.3 13.4 %copy-start.16 = (s32[512]{0:T(512)S(1)}, s32[512]{0:T(512)}, u32[]{:S(2)}) copy-start(s32[512]{0:T(512)} %tenant_ref.9) | copy-start | bytes 6148
  19.3 4.3 %collective-permute-start.2 = (f32[4,1792]{1,0:T(4,128)S(1)}, f32[4,1792]{1,0:T(4,128)S(1)}, u32[]{:S(2)}, u32[]{:S(2)}) collective-permute-start(f32[4,1792]{1,0:T(4,128)S(1)} %partial_norms.1.nsq_a), channel_id=1, source_target_pairs={{0,1},{1,0},{2,3},{3,2},{4,5},{5,4},{6,7},{7,6},{8,9},{9,8},{10,11... | collective-permute-start | bytes 86024 | tf_op jit(solution)/shard_map/ppermute | solution.py:451
  19.9 13.2 %copy-start.5 = (bf16[32,4096]{1,0:T(8,128)(2,1)S(1)}, bf16[32,4096]{1,0:T(8,128)(2,1)}, u32[]{:S(2)}) copy-start(bf16[32,4096]{1,0:T(8,128)(2,1)} %refs_0_.7) | copy-start | bytes 786436
  33.1 3.1 %copy-start.11 = (bf16[256,1792]{1,0:T(8,128)(2,1)}, bf16[256,1792]{1,0:T(8,128)(2,1)S(1)}, u32[]{:S(2)}) copy-start(bf16[256,1792]{1,0:T(8,128)(2,1)S(1)} %get-tuple-element.59) | copy-start | bytes 2752516
  33.1 1.6 %copy-start.21 = (bf16[128,4096]{1,0:T(8,128)(2,1)S(1)}, bf16[128,4096]{1,0:T(8,128)(2,1)}, u32[]{:S(2)}) copy-start(bf16[128,4096]{1,0:T(8,128)(2,1)} %get-tuple-element.40) | copy-start | bytes 3145732
  33.2 5.0 %collective-permute-start.9 = (bf16[128,4096]{1,0:T(8,128)(2,1)S(1)}, bf16[128,4096]{1,0:T(8,128)(2,1)S(1)}, u32[]{:S(2)}, u32[]{:S(2)}) collective-permute-start(bf16[128,4096]{1,0:T(8,128)(2,1)S(1)} %pad_maximum_fusion), channel_id=1, source_target_pairs={{0,2},{2,0},{4,6},{6,4},{8,10},{10,8},{12,14},{14,12},{16,18},{18,... | collective-permute-start | bytes 3145736 | tf_op jit(solution)/shard_map/ppermute | solution.py:448
  34.6 3.5 %collective-permute-start.7 = (bf16[128,4096]{1,0:T(8,128)(2,1)S(1)}, bf16[128,4096]{1,0:T(8,128)(2,1)S(1)}, u32[]{:S(2)}, u32[]{:S(2)}) collective-permute-start(bf16[128,4096]{1,0:T(8,128)(2,1)S(1)} %copy-done.21), channel_id=1, source_target_pairs={{0,2},{2,0},{4,6},{6,4},{8,10},{10,8},{12,14},{14,12},{16,18},{18,... | collective-permute-start | bytes 3145736 | tf_op jit(solution)/shard_map/ppermute | solution.py:448
  34.6 19.1 %collective-permute-start.6 = (bf16[32,4096]{1,0:T(8,128)(2,1)S(1)}, bf16[32,4096]{1,0:T(8,128)(2,1)S(1)}, u32[]{:S(2)}, u32[]{:S(2)}) collective-permute-start(bf16[32,4096]{1,0:T(8,128)(2,1)S(1)} %collective-permute-done.5.refs_4_), channel_id=1, source_target_pairs={{0,4},{2,6},{4,0},{6,2},{8,12},{10,14},{12,8},{14,10},{16,20},{18,... | collective-permute-start | bytes 786440 | tf_op jit(solution)/shard_map/ppermute | solution.py:448
  36.1 17.7 %collective-permute-start.10 = (bf16[32,4096]{1,0:T(8,128)(2,1)S(1)}, bf16[32,4096]{1,0:T(8,128)(2,1)S(1)}, u32[]{:S(2)}, u32[]{:S(2)}) collective-permute-start(bf16[32,4096]{1,0:T(8,128)(2,1)S(1)} %collective-permute-done.8.refs_6_), channel_id=1, source_target_pairs={{0,4},{2,6},{4,0},{6,2},{8,12},{10,14},{12,8},{14,10},{16,20},{18,... | collective-permute-start | bytes 786440 | tf_op jit(solution)/shard_map/ppermute | solution.py:448
  36.7 17.9 %collective-permute-start.4 = (bf16[32,4096]{1,0:T(8,128)(2,1)S(1)}, bf16[32,4096]{1,0:T(8,128)(2,1)S(1)}, u32[]{:S(2)}, u32[]{:S(2)}) collective-permute-start(bf16[32,4096]{1,0:T(8,128)(2,1)S(1)} %collective-permute-done.1.refs_2_), channel_id=1, source_target_pairs={{0,4},{2,6},{4,0},{6,2},{8,12},{10,14},{12,8},{14,10},{16,20},{18,... | collective-permute-start | bytes 786440 | tf_op jit(solution)/shard_map/ppermute | solution.py:448
  38.2 1.0 copy-start.18
  38.2 1.3 %copy-start.20 = (bf16[128,4096]{1,0:T(8,128)(2,1)}, bf16[128,4096]{1,0:T(8,128)(2,1)S(1)}, u32[]{:S(2)}) copy-start(bf16[128,4096]{1,0:T(8,128)(2,1)S(1)} %collective-permute-done.7.refs_4_) | copy-start | bytes 3145732
  52.0 0.9 copy-start.13
  53.0 0.8 copy-start.17
  53.8 10.0 %copy-start.19 = (bf16[32,4096]{1,0:T(8,128)(2,1)}, bf16[32,4096]{1,0:T(8,128)(2,1)S(1)}, u32[]{:S(2)}) copy-start(bf16[32,4096]{1,0:T(8,128)(2,1)S(1)} %collective-permute-done.10.refs_7_) | copy-start | bytes 786436
  55.6 4.0 %collective-permute-start.11 = (bf16[128,4096]{1,0:T(8,128)(2,1)}, bf16[128,4096]{1,0:T(8,128)(2,1)S(1)}, u32[]{:S(2)}, u32[]{:S(2)}) collective-permute-start(bf16[128,4096]{1,0:T(8,128)(2,1)} %pad_maximum_fusion.1), channel_id=1, source_target_pairs={{0,2},{2,0},{4,6},{6,4},{8,10},{10,8},{12,14},{14,12},{16,18},{18,... | collective-permute-start | bytes 3145736 | tf_op jit(solution)/shard_map/ppermute | solution.py:448
  55.6 4.5 %collective-permute-start.13 = (bf16[128,4096]{1,0:T(8,128)(2,1)}, bf16[128,4096]{1,0:T(8,128)(2,1)}, u32[]{:S(2)}, u32[]{:S(2)}) collective-permute-start(bf16[128,4096]{1,0:T(8,128)(2,1)} %get-tuple-element.47), channel_id=1, source_target_pairs={{0,2},{2,0},{4,6},{6,4},{8,10},{10,8},{12,14},{14,12},{16,18},{18,... | collective-permute-start | bytes 3145736 | tf_op jit(solution)/shard_map/ppermute | solution.py:448
  56.4 23.7 %collective-permute-start.12 = (bf16[64,4096]{1,0:T(8,128)(2,1)}, bf16[64,4096]{1,0:T(8,128)(2,1)}, u32[]{:S(2)}, u32[]{:S(2)}) collective-permute-start(bf16[64,4096]{1,0:T(8,128)(2,1)} %copy-done.17), channel_id=1, source_target_pairs={{0,4},{2,6},{4,0},{6,2},{8,12},{10,14},{12,8},{14,10},{16,20},{18,... | collective-permute-start | bytes 1572872 | tf_op jit(solution)/shard_map/ppermute | solution.py:448
  59.6 4.2 %copy-start.1 = (bf16[128,4096]{1,0:T(8,128)(2,1)}, bf16[128,4096]{1,0:T(8,128)(2,1)S(1)}, u32[]{:S(2)}) copy-start(bf16[128,4096]{1,0:T(8,128)(2,1)S(1)} %collective-permute-done.11.refs_0_.refs_9_) | copy-start | bytes 3145732
  60.1 1.6 %copy-start.8 = (f32[128,4096]{1,0:T(8,128)S(1)}, f32[128,4096]{1,0:T(8,128)}, u32[]{:S(2)}) copy-start(f32[128,4096]{1,0:T(8,128)} %get-tuple-element.46.keep_ref) | copy-start | bytes 6291460
  63.8 1.0 copy-start.2
  64.8 16.9 %collective-permute-start.14 = (bf16[64,4096]{1,0:T(8,128)(2,1)}, bf16[64,4096]{1,0:T(8,128)(2,1)S(1)}, u32[]{:S(2)}, u32[]{:S(2)}) collective-permute-start(bf16[64,4096]{1,0:T(8,128)(2,1)} %get-tuple-element.49), channel_id=1, source_target_pairs={{0,4},{2,6},{4,0},{6,2},{8,12},{10,14},{12,8},{14,10},{16,20},{18,... | collective-permute-start | bytes 1572872 | tf_op jit(solution)/shard_map/ppermute | solution.py:448
  66.5 15.3 %copy-start.3 = (f32[64,4096]{1,0:T(8,128)S(1)}, f32[64,4096]{1,0:T(8,128)}, u32[]{:S(2)}) copy-start(f32[64,4096]{1,0:T(8,128)} %copy-done.2) | copy-start | bytes 3145732
  66.5 15.2 %copy-start.9 = (f32[64,4096]{1,0:T(8,128)S(1)}, f32[64,4096]{1,0:T(8,128)}, u32[]{:S(2)}) copy-start(f32[64,4096]{1,0:T(8,128)} %get-tuple-element.44.refs_0_) | copy-start | bytes 3145732
  78.6 32.5 %collective-permute-start.15 = (bf16[256,1792]{1,0:T(8,128)(2,1)}, bf16[256,1792]{1,0:T(8,128)(2,1)S(1)}, u32[]{:S(2)}, u32[]{:S(2)}) collective-permute-start(bf16[256,1792]{1,0:T(8,128)(2,1)} %get-tuple-element.53), channel_id=1, source_target_pairs={{0,1},{1,0},{2,3},{3,2},{4,5},{5,4},{6,7},{7,6},{8,9},{9,8},{10,11... | collective-permute-start | bytes 2752520 | tf_op jit(solution)/shard_map/ppermute | solution.py:451
  83.7 0.8 copy-start.6
  84.6 18.7 %collective-permute-start.19 = (bf16[32,4096]{1,0:T(8,128)(2,1)S(1)}, bf16[32,4096]{1,0:T(8,128)(2,1)S(1)}, u32[]{:S(2)}, u32[]{:S(2)}) collective-permute-start(bf16[32,4096]{1,0:T(8,128)(2,1)S(1)} %get-tuple-element.63), channel_id=1, source_target_pairs={{0,16},{2,18},{4,20},{6,22},{8,24},{10,26},{12,28},{14,30},{16,0},... | collective-permute-start | bytes 786440 | tf_op jit(solution)/shard_map/ppermute | solution.py:448
  87.2 21.5 %collective-permute-start.16 = (bf16[32,4096]{1,0:T(8,128)(2,1)S(1)}, bf16[32,4096]{1,0:T(8,128)(2,1)S(1)}, u32[]{:S(2)}, u32[]{:S(2)}) collective-permute-start(bf16[32,4096]{1,0:T(8,128)(2,1)S(1)} %get-tuple-element.56), channel_id=1, source_target_pairs={{0,24},{2,26},{4,28},{6,30},{8,0},{10,2},{12,4},{14,6},{16,8},{18,... | collective-permute-start | bytes 786440 | tf_op jit(solution)/shard_map/ppermute | solution.py:448
  99.9 16.7 %collective-permute-start.18 = (bf16[32,4096]{1,0:T(8,128)(2,1)S(1)}, bf16[32,4096]{1,0:T(8,128)(2,1)S(1)}, u32[]{:S(2)}, u32[]{:S(2)}) collective-permute-start(bf16[32,4096]{1,0:T(8,128)(2,1)S(1)} %get-tuple-element.62), channel_id=1, source_target_pairs={{0,8},{2,10},{4,12},{6,14},{8,16},{10,18},{12,20},{14,22},{16,24},... | collective-permute-start | bytes 786440 | tf_op jit(solution)/shard_map/ppermute | solution.py:448
  103.3 6.9 %collective-permute-start.20 = (f32[4,1792]{1,0:T(4,128)S(1)}, f32[4,1792]{1,0:T(4,128)S(1)}, u32[]{:S(2)}, u32[]{:S(2)}) collective-permute-start(f32[4,1792]{1,0:T(4,128)S(1)} %pad_maximum_fusion.2), channel_id=1, source_target_pairs={{0,1},{1,0},{2,3},{3,2},{4,5},{5,4},{6,7},{7,6},{8,9},{9,8},{10,11... | collective-permute-start | bytes 86024 | tf_op jit(solution)/shard_map/ppermute | solution.py:451
  108.7 5.1 %collective-permute-start.17 = (f32[16,512]{1,0:T(8,128)S(1)}, f32[16,512]{1,0:T(8,128)S(1)}, u32[]{:S(2)}, u32[]{:S(2)}) collective-permute-start(f32[16,512]{1,0:T(8,128)S(1)} %constant_dynamic-update-slice_fusion), channel_id=1, source_target_pairs={{0,1},{1,0},{2,3},{3,2},{4,5},{5,4},{6,7},{7,6},{8,9},{9,8},{10,11... | collective-permute-start | bytes 98312 | tf_op jit(solution)/shard_map/ppermute | solution.py:451
  111.1 2.8 %copy-start.14 = (bf16[256,1792]{1,0:T(8,128)(2,1)S(1)}, bf16[256,1792]{1,0:T(8,128)(2,1)}, u32[]{:S(2)}) copy-start(bf16[256,1792]{1,0:T(8,128)(2,1)} %copy-done.13) | copy-start | bytes 2752516
  113.8 1.2 %copy-start.12 = (bf16[256,1792]{1,0:T(8,128)(2,1)S(1)}, bf16[256,1792]{1,0:T(8,128)(2,1)}, u32[]{:S(2)}) copy-start(bf16[256,1792]{1,0:T(8,128)(2,1)} %copy-done.11) | copy-start | bytes 2752516
  115.0 1.6 %copy-start.7 = (f32[32,4096]{1,0:T(8,128)S(1)}, f32[32,4096]{1,0:T(8,128)}, u32[]{:S(2)}) copy-start(f32[32,4096]{1,0:T(8,128)} %copy-done.6) | copy-start | bytes 1572868

commit v10 on v6

--- a/solution.py
+++ b/solution.py
@@ -18,7 +18,7 @@
 COST = pl.CostEstimate(flops=1000, bytes_accessed=1000, transcendentals=0)
 LAST = (((1,), (1,)), ((), ()))
 PARAMS = pltpu.CompilerParams(vmem_limit_bytes=52 * 1024 * 1024)
-SMALL = pltpu.CompilerParams(vmem_limit_bytes=12 * 1024 * 1024)
+LARGE = pltpu.CompilerParams(vmem_limit_bytes=62 * 1024 * 1024)
 IN_HBM = pl.BlockSpec(memory_space=pltpu.HBM)
 
 
@@ -131,7 +131,7 @@
                 pltpu.SemaphoreType.DMA((2 * nblk,)),
             ],
         ),
-        compiler_params=PARAMS,
+        compiler_params=LARGE,
         cost_estimate=COST,
         name="partial_norms",
     )(tenant, weight, down, up)
@@ -253,7 +253,7 @@
         grid=(2,),
         in_specs=[pl.BlockSpec((rows, block), lambda i: (0, i))] * 2 + order_specs(deps),
         out_specs=[pl.BlockSpec((rows // 2, block), lambda i: (0, i))] * 2,
-        compiler_params=SMALL,
+        compiler_params=PARAMS,
         cost_estimate=COST,
         name="add_core",
     )(keep, recv, *deps)
@@ -293,7 +293,7 @@
             out_specs=[spec(s) for s in shapes],
             scratch_shapes=[pltpu.VMEM((nz * piece, block), F32)],
         ),
-        compiler_params=SMALL,
+        compiler_params=PARAMS,
         cost_estimate=COST,
         name="add_x",
     )(place, *operands, *deps)
@@ -311,7 +311,7 @@
         add_z_body,
         out_shape=jax.ShapeDtypeStruct(parts[0].shape, BF16),
         in_specs=[pl.BlockSpec(memory_space=pltpu.VMEM)] * len(parts),
-        compiler_params=SMALL,
+        compiler_params=PARAMS,
         cost_estimate=COST,
         name="add_z",
     )(*parts)
@@ -518,9 +518,10 @@
         part, dots_here, low_here = project(0, F32, [finals[0]])
         dots = jnp.concatenate([dots_here, dots_away], axis=0)
         low = jnp.concatenate([low_here, low_away], axis=1)
-        late = (finals[nz // 2], finals[nz - 1])
-        dots = dots + jnp.roll(swap(once(dots, late)), blocks_mine, axis=0)
-        low = low + jnp.roll(swap(once(low, late)), rows_row, axis=1)
+        new_dots = swap(once(dots, finals[nz // 2]))
+        new_low = swap(once(low, finals[nz - 1]))
+        dots = dots + jnp.roll(new_dots, blocks_mine, axis=0)
+        low = low + jnp.roll(new_low, rows_row, axis=1)
         parts = [ours, theirs]
     else:
         ours = gradient(0, [], [])

time: 115 us -> 117 us (1.017)
  waiting for transfers between devices: 11.2 us -> 15.8 us
  local copies, waits for them, and re-layouts: 10 us -> 6.4 us
  Pallas kernels: 62 us -> 63.2 us
    unnamed x47 -> x35, local copies, waits for them, and re-layouts: 9.68 us -> 6.08 us
    ppermute x16, waiting for transfers between devices: 5.27 us -> 8.2 us  [move(): return lax.ppermute(value, 'col', perm)]
    ppermute x5, waiting for transfers between devices: 5.98 us -> 7.65 us  [swap(): return lax.ppermute(value, 'row', [(0, 1), (1, 0)])]
where the time goes in v10:
time: 117 us; the launch traced here: 116 us
  Pallas kernels  63.2 us (54%)
  starting transfers between devices  23.6 us (20%)
  waiting for transfers between devices  15.8 us (14%)
  local copies, waits for them, and re-layouts  6.4 us (5%)
  other arithmetic  3.5 us (3%)
  matrix products  2.05 us (2%)
    pallas_call x2, Pallas kernels, forward(): pl.pallas_call(functools.partial(forward_body, nb, rank, nz), out_shape=s...  24.7 us
    pallas_call x2, Pallas kernels, input_gradient(): pl.pallas_call(functools.partial(grad_body, nb, rank, len(add)), out_shap...  23.1 us
    ppermute x16, starting transfers between devices, move(): return lax.ppermute(value, 'col', perm)  17.9 us
    pallas_call x1, Pallas kernels, partial_norms(): pl.pallas_call(functools.partial(norm_body, nblk, rank), out_shape=shape,...  9.44 us
    ppermute x16, waiting for transfers between devices, move(): return lax.ppermute(value, 'col', perm)  8.2 us
    ppermute x5, waiting for transfers between devices, swap(): return lax.ppermute(value, 'row', [(0, 1), (1, 0)])  7.65 us
    unnamed x35, local copies, waits for them, and re-layouts  6.08 us
    ppermute x5, starting transfers between devices, swap(): return lax.ppermute(value, 'row', [(0, 1), (1, 0)])  5.75 us
  transfers between devices with their start and end apart: 21, of which 8 were waited for; matrix products, arithmetic and copies ran while one was open for 3% of the time, Pallas kernels for 55%

profile of v10, /device:TPU:8, one launch (start us, length us, event | category | flops | bytes accessed | tf_op | source)
XLA Modules:
  0.0 115.6 jit_solution(9700894977850653770)
XLA Ops:
  0.6 1.6 %collective-permute-start.3 = (bf16[256,1792]{1,0:T(8,128)(2,1)}, bf16[256,1792]{1,0:T(8,128)(2,1)}, u32[]{:S(2)}, u32[]{:S(2)}) collective-permute-start(bf16[256,1792]{1,0:T(8,128)(2,1)} %cot_ref.3), channel_id=1, source_target_pairs={{0,1},{1,0},{2,3},{3,2},{4,5},{5,4},{6,7},{7,6},{8,9},{9,8},{10,11... | collective-permute-start | bytes 2752520 | tf_op jit(solution)/shard_map/ppermute | solution.py:451
  2.2 1.5 %collective-permute-start = (bf16[32,4096]{1,0:T(8,128)(2,1)}, bf16[32,4096]{1,0:T(8,128)(2,1)S(1)}, u32[]{:S(2)}, u32[]{:S(2)}) collective-permute-start(bf16[32,4096]{1,0:T(8,128)(2,1)} %refs_0_.7), channel_id=1, source_target_pairs={{0,4},{2,6},{4,0},{6,2},{8,12},{10,14},{12,8},{14,10},{16,20},{18,... | collective-permute-start | bytes 786440 | tf_op jit(solution)/shard_map/ppermute | solution.py:448
  3.7 2.6 %collective-permute-start.5 = (bf16[32,4096]{1,0:T(8,128)(2,1)}, bf16[32,4096]{1,0:T(8,128)(2,1)S(1)}, u32[]{:S(2)}, u32[]{:S(2)}) collective-permute-start(bf16[32,4096]{1,0:T(8,128)(2,1)} %refs_0_.7), channel_id=1, source_target_pairs={{0,16},{2,18},{4,20},{6,22},{8,24},{10,26},{12,28},{14,30},{16,0},... | collective-permute-start | bytes 786440 | tf_op jit(solution)/shard_map/ppermute | solution.py:448
  6.3 0.4 collective-permute-start.8
  6.7 1.6 %collective-permute-start.1 = (bf16[32,4096]{1,0:T(8,128)(2,1)}, bf16[32,4096]{1,0:T(8,128)(2,1)S(1)}, u32[]{:S(2)}, u32[]{:S(2)}) collective-permute-start(bf16[32,4096]{1,0:T(8,128)(2,1)} %refs_0_.7), channel_id=1, source_target_pairs={{0,8},{2,10},{4,12},{6,14},{8,16},{10,18},{12,20},{14,22},{16,24},... | collective-permute-start | bytes 786440 | tf_op jit(solution)/shard_map/ppermute | solution.py:448
  8.4 9.4 %partial_norms.1.nsq_a = f32[4,1792]{1,0:T(4,128)} custom-call(s32[512]{0:T(512)} %tenant_ref.9, bf16[4096,1792]{1,0:T(8,128)(2,1)} %w_hbm.5, bf16[16,16,4096]{2,1,0:T(8,128)(2,1)} %a_hbm.5, bf16[16,16,1792]{2,1,0:T(8,128)(2,1)} %up_hbm.5), custom_call_target="tpu_custom_call" | custom-call | flops 1000 | bytes 1000 | tf_op jit(solution)/shard_map/partial_norms/pallas_call | solution.py:116
  17.9 0.6 collective-permute-start.2
  18.5 5.1 %collective-permute-done.2.nsq_b = f32[4,1792]{1,0:T(4,128)S(1)} collective-permute-done((f32[4,1792]{1,0:T(4,128)}, f32[4,1792]{1,0:T(4,128)S(1)}, u32[]{:S(2)}, u32[]{:S(2)}) %collective-permute-start.2) | collective-permute-done | bytes 28704 | tf_op jit(solution)/shard_map/ppermute | solution.py:451
  23.6 0.9 copy-done.5
  24.5 0.7 copy-done.9
  25.3 9.9 %input_gradient.2 = (f32[2,1792]{1,0:T(2,128)S(1)}, bf16[256,1792]{1,0:T(8,128)(2,1)S(1)}, f32[128,4096]{1,0:T(8,128)}, bf16[128,4096]{1,0:T(8,128)(2,1)}) custom-call(s32[512]{0:T(512)S(1)} %copy-done.10, s32[4]{0:T(128)S(1)} %pad_add_fusion.place_ref, bf16[256,1792]{1,0:T(8,128)(2,1)S(1)} %copy-done.1, f32[4,1792]{1,0:T(4,128)S(1)} %copy-done.9, ...), custom_call_target="tpu_custom_call" | custom-call | flops 1000 | bytes 1000 | tf_op jit(solution)/shard_map/input_gradient/pallas_call | solution.py:210
  35.5 1.3 %copy-done.16 = bf16[128,4096]{1,0:T(8,128)(2,1)S(1)} copy-done((bf16[128,4096]{1,0:T(8,128)(2,1)S(1)}, bf16[128,4096]{1,0:T(8,128)(2,1)}, u32[]{:S(2)}) %copy-start.16) | copy-done | bytes 1048600
  36.8 1.5 %collective-permute-start.6 = (bf16[32,4096]{1,0:T(8,128)(2,1)S(1)}, bf16[32,4096]{1,0:T(8,128)(2,1)S(1)}, u32[]{:S(2)}, u32[]{:S(2)}) collective-permute-start(bf16[32,4096]{1,0:T(8,128)(2,1)S(1)} %collective-permute-done.5.refs_4_), channel_id=1, source_target_pairs={{0,4},{2,6},{4,0},{6,2},{8,12},{10,14},{12,8},{14,10},{16,20},{18,... | collective-permute-start | bytes 786440 | tf_op jit(solution)/shard_map/ppermute | solution.py:448
  38.3 0.5 collective-permute-start.10
  38.8 1.5 %collective-permute-start.4 = (bf16[32,4096]{1,0:T(8,128)(2,1)S(1)}, bf16[32,4096]{1,0:T(8,128)(2,1)S(1)}, u32[]{:S(2)}, u32[]{:S(2)}) collective-permute-start(bf16[32,4096]{1,0:T(8,128)(2,1)S(1)} %collective-permute-done.1.refs_2_), channel_id=1, source_target_pairs={{0,4},{2,6},{4,0},{6,2},{8,12},{10,14},{12,8},{14,10},{16,20},{18,... | collective-permute-start | bytes 786440 | tf_op jit(solution)/shard_map/ppermute | solution.py:448
  40.3 1.0 copy-done.12
  41.3 0.4 copy-done.15
  41.6 13.2 %input_gradient.3 = (f32[2,1792]{1,0:T(2,128)S(1)}, bf16[256,1792]{1,0:T(8,128)(2,1)S(1)}, f32[128,4096]{1,0:T(8,128)}, bf16[128,4096]{1,0:T(8,128)(2,1)}, f32[6...) custom-call(s32[512]{0:T(512)S(1)} %copy-done.10, s32[4]{0:T(128)S(1)} %get-tuple-element.66.place_ref, ...), custom_call_target="tpu_custom_call" | custom-call | flops 1000 | bytes 1000 | tf_op jit(solution)/shard_map/input_gradient/pallas_call | solution.py:210
  54.9 1.9 %collective-permute-done.4.refs_3_ = bf16[32,4096]{1,0:T(8,128)(2,1)S(1)} collective-permute-done((bf16[32,4096]{1,0:T(8,128)(2,1)S(1)}, bf16[32,4096]{1,0:T(8,128)(2,1)S(1)}, u32[]{:S(2)}, u32[]{:S(2)}) %collective-permute-start.4) | collective-permute-done | bytes 262176 | tf_op jit(solution)/shard_map/ppermute | solution.py:448
  56.7 1.1 pad_maximum_fusion.1
  57.8 0.5 collective-permute-start.13
  58.3 0.1 dynamic-slice_reduce_fusion.1
  58.6 1.5 %collective-permute-start.12 = (bf16[64,4096]{1,0:T(8,128)(2,1)}, bf16[64,4096]{1,0:T(8,128)(2,1)S(1)}, u32[]{:S(2)}, u32[]{:S(2)}) collective-permute-start(bf16[64,4096]{1,0:T(8,128)(2,1)} %copy-done.11), channel_id=1, source_target_pairs={{0,4},{2,6},{4,0},{6,2},{8,12},{10,14},{12,8},{14,10},{16,20},{18,... | collective-permute-start | bytes 1572872 | tf_op jit(solution)/shard_map/ppermute | solution.py:448
  60.1 0.7 collective-permute-done.11.refs_0_.refs_9_
  60.8 1.5 %collective-permute-done.13.recv_ref = bf16[128,4096]{1,0:T(8,128)(2,1)} collective-permute-done((bf16[128,4096]{1,0:T(8,128)(2,1)}, bf16[128,4096]{1,0:T(8,128)(2,1)}, u32[]{:S(2)}, u32[]{:S(2)}) %collective-permute-start.13) | collective-permute-done | bytes 1048608 | tf_op jit(solution)/shard_map/ppermute | solution.py:448
  62.3 2.7 %add_core.1 = (f32[64,4096]{1,0:T(8,128)S(1)}, bf16[64,4096]{1,0:T(8,128)(2,1)}) custom-call(f32[128,4096]{1,0:T(8,128)} %get-tuple-element.45.keep_ref, bf16[128,4096]{1,0:T(8,128)(2,1)} %collective-permute-done.13.recv_ref, bf16[128,4096]{1,0:T(8,128)(2,1)} %collective-permute-done.11.refs_0_.refs_9_), custom_call_target="tpu_custom_call" | custom-call | flops 1000 | bytes 1000 | tf_op jit(solution)/shard_map/add_core/pallas_call | solution.py:247
  65.0 1.0 copy-done
  66.0 1.5 %collective-permute-start.14 = (bf16[64,4096]{1,0:T(8,128)(2,1)}, bf16[64,4096]{1,0:T(8,128)(2,1)}, u32[]{:S(2)}, u32[]{:S(2)}) collective-permute-start(bf16[64,4096]{1,0:T(8,128)(2,1)} %get-tuple-element.48), channel_id=1, source_target_pairs={{0,4},{2,6},{4,0},{6,2},{8,12},{10,14},{12,8},{14,10},{16,20},{18,... | collective-permute-start | bytes 1572872 | tf_op jit(solution)/shard_map/ppermute | solution.py:448
  67.6 12.2 %forward.2 = (bf16[256,1792]{1,0:T(8,128)(2,1)}, f32[2,1792]{1,0:T(2,128)S(1)}, f32[16,256]{1,0:T(8,128)S(1)}) custom-call(s32[512]{0:T(512)S(1)} %copy-done.10, s32[4]{0:T(128)S(1)} %get-tuple-element.66.place_ref, bf16[256,1792]{1,0:T(8,128)(2,1)} %collective-permute-done.3.refs_3_.cot_ref, bf16[4096,1792]{1,0:T(8,128)(2,1)} %w_hbm.5, ...), custom_call_target="tpu_custom_call" | custom-call | flops 1000 | bytes 1000 | tf_op jit(solution)/shard_map/forward/pallas_call | solution.py:404
  79.8 1.6 %collective-permute-start.15 = (bf16[256,1792]{1,0:T(8,128)(2,1)}, bf16[256,1792]{1,0:T(8,128)(2,1)S(1)}, u32[]{:S(2)}, u32[]{:S(2)}) collective-permute-start(bf16[256,1792]{1,0:T(8,128)(2,1)} %get-tuple-element.52), channel_id=1, source_target_pairs={{0,1},{1,0},{2,3},{3,2},{4,5},{5,4},{6,7},{7,6},{8,9},{9,8},{10,11... | collective-permute-start | bytes 2752520 | tf_op jit(solution)/shard_map/ppermute | solution.py:451
  81.4 2.6 %collective-permute-done.14.refs_3_ = bf16[64,4096]{1,0:T(8,128)(2,1)} collective-permute-done((bf16[64,4096]{1,0:T(8,128)(2,1)}, bf16[64,4096]{1,0:T(8,128)(2,1)}, u32[]{:S(2)}, u32[]{:S(2)}) %collective-permute-start.14) | collective-permute-done | bytes 524320 | tf_op jit(solution)/shard_map/ppermute | solution.py:448
  84.0 2.5 %add_x.1 = (f32[32,4096]{1,0:T(8,128)S(1)}, bf16[32,4096]{1,0:T(8,128)(2,1)S(1)}, bf16[32,4096]{1,0:T(8,128)(2,1)S(1)}, bf16[32,4096]{1,0:T(8,128)(2,1)S(1)}) custom-call(s32[5]{0:T(128)S(1)} %stack.39.place_ref, f32[64,4096]{1,0:T(8,128)} %get-tuple-element.43.refs_0_, bf16[64,4096]{1,0:T(8,128)(2,1)S(1)} %collective-permute-done.12.refs_1_, ...), custom_call_target="tpu_custom_call" | custom-call | flops 1000 | bytes 1000 | tf_op jit(solution)/shard_map/add_x/pallas_call | solution.py:286
  86.5 0.8 copy-done.3
  87.3 2.6 %collective-permute-start.19 = (bf16[32,4096]{1,0:T(8,128)(2,1)S(1)}, bf16[32,4096]{1,0:T(8,128)(2,1)S(1)}, u32[]{:S(2)}, u32[]{:S(2)}) collective-permute-start(bf16[32,4096]{1,0:T(8,128)(2,1)S(1)} %get-tuple-element.61), channel_id=1, source_target_pairs={{0,16},{2,18},{4,20},{6,22},{8,24},{10,26},{12,28},{14,30},{16,0},... | collective-permute-start | bytes 786440 | tf_op jit(solution)/shard_map/ppermute | solution.py:448
  89.9 0.4 collective-permute-start.16
  90.3 12.5 %forward.3 = (f32[256,1792]{1,0:T(8,128)}, f32[2,1792]{1,0:T(2,128)S(1)}, f32[16,256]{1,0:T(8,128)S(1)}) custom-call(s32[512]{0:T(512)S(1)} %copy-done.10, s32[4]{0:T(128)S(1)} %pad_add_fusion.place_ref, bf16[256,1792]{1,0:T(8,128)(2,1)} %cot_ref.3, bf16[4096,1792]{1,0:T(8,128)(2,1)} %w_hbm.5, bf16[16,16,4096]{2,1,0:T(8,128)(2,1)} %a_hbm.5, ...), custom_call_target="tpu_custom_call" | custom-call | flops 1000 | bytes 1000 | tf_op jit(solution)/shard_map/forward/pallas_call | solution.py:404
  102.8 1.6 %collective-permute-start.18 = (bf16[32,4096]{1,0:T(8,128)(2,1)S(1)}, bf16[32,4096]{1,0:T(8,128)(2,1)S(1)}, u32[]{:S(2)}, u32[]{:S(2)}) collective-permute-start(bf16[32,4096]{1,0:T(8,128)(2,1)S(1)} %get-tuple-element.60), channel_id=1, source_target_pairs={{0,8},{2,10},{4,12},{6,14},{8,16},{10,18},{12,20},{14,22},{16,24},... | collective-permute-start | bytes 786440 | tf_op jit(solution)/shard_map/ppermute | solution.py:448
  104.5 1.5 %collective-permute-done.19.refs_2_ = bf16[32,4096]{1,0:T(8,128)(2,1)S(1)} collective-permute-done((bf16[32,4096]{1,0:T(8,128)(2,1)S(1)}, bf16[32,4096]{1,0:T(8,128)(2,1)S(1)}, u32[]{:S(2)}, u32[]{:S(2)}) %collective-permute-start.19) | collective-permute-done | bytes 262176 | tf_op jit(solution)/shard_map/ppermute | solution.py:448
  106.0 1.5 %collective-permute-start.20 = (f32[4,1792]{1,0:T(4,128)S(1)}, f32[4,1792]{1,0:T(4,128)S(1)}, u32[]{:S(2)}, u32[]{:S(2)}) collective-permute-start(f32[4,1792]{1,0:T(4,128)S(1)} %pad_maximum_fusion.2), channel_id=1, source_target_pairs={{0,1},{1,0},{2,3},{3,2},{4,5},{5,4},{6,7},{7,6},{8,9},{9,8},{10,11... | collective-permute-start | bytes 86024 | tf_op jit(solution)/shard_map/ppermute | solution.py:451
  107.5 0.5 collective-permute-start.17
  108.0 1.9 %collective-permute-done.20 = f32[4,1792]{1,0:T(4,128)S(1)} collective-permute-done((f32[4,1792]{1,0:T(4,128)S(1)}, f32[4,1792]{1,0:T(4,128)S(1)}, u32[]{:S(2)}, u32[]{:S(2)}) %collective-permute-start.20) | collective-permute-done | bytes 28704 | tf_op jit(solution)/shard_map/ppermute | solution.py:451
  110.0 0.1 broadcast_select_fusion
  110.2 0.7 fusion.3
  110.8 0.6 collective-permute-done.17
  111.5 0.4 fusion.9
  112.0 1.6 %convolution_add_fusion = f32[256,1792]{1,0:T(8,128)} fusion(f32[256,1792]{1,0:T(8,128)S(1)} %fusion.9, bf16[256,256]{1,0:T(8,128)(2,1)S(1)} %bitcast.29, bf16[256,1792]{1,0:T(8,128)(2,1)S(1)} %copy-done.8), kind=kOutput, calls=%fused_computation | convolution fusion | flops 235339776 | bytes 4718592 | tf_op jit(solution)/shard_map/dot_general | solution.py:556
  113.6 0.8 add_z.1
  114.4 1.1 fusion
  (62 shorter events, 0.9 us)
Async XLA Ops:
  0.6 23.0 %collective-permute-start.3 = (bf16[256,1792]{1,0:T(8,128)(2,1)}, bf16[256,1792]{1,0:T(8,128)(2,1)}, u32[]{:S(2)}, u32[]{:S(2)}) collective-permute-start(bf16[256,1792]{1,0:T(8,128)(2,1)} %cot_ref.3), channel_id=1, source_target_pairs={{0,1},{1,0},{2,3},{3,2},{4,5},{5,4},{6,7},{7,6},{8,9},{9,8},{10,11... | collective-permute-start | bytes 2752520 | tf_op jit(solution)/shard_map/ppermute | solution.py:451
  2.2 15.6 %collective-permute-start = (bf16[32,4096]{1,0:T(8,128)(2,1)}, bf16[32,4096]{1,0:T(8,128)(2,1)S(1)}, u32[]{:S(2)}, u32[]{:S(2)}) collective-permute-start(bf16[32,4096]{1,0:T(8,128)(2,1)} %refs_0_.7), channel_id=1, source_target_pairs={{0,4},{2,6},{4,0},{6,2},{8,12},{10,14},{12,8},{14,10},{16,20},{18,... | collective-permute-start | bytes 786440 | tf_op jit(solution)/shard_map/ppermute | solution.py:448
  3.7 31.5 %collective-permute-start.5 = (bf16[32,4096]{1,0:T(8,128)(2,1)}, bf16[32,4096]{1,0:T(8,128)(2,1)S(1)}, u32[]{:S(2)}, u32[]{:S(2)}) collective-permute-start(bf16[32,4096]{1,0:T(8,128)(2,1)} %refs_0_.7), channel_id=1, source_target_pairs={{0,16},{2,18},{4,20},{6,22},{8,24},{10,26},{12,28},{14,30},{16,0},... | collective-permute-start | bytes 786440 | tf_op jit(solution)/shard_map/ppermute | solution.py:448
  6.3 29.0 %collective-permute-start.8 = (bf16[32,4096]{1,0:T(8,128)(2,1)}, bf16[32,4096]{1,0:T(8,128)(2,1)S(1)}, u32[]{:S(2)}, u32[]{:S(2)}) collective-permute-start(bf16[32,4096]{1,0:T(8,128)(2,1)} %refs_0_.7), channel_id=1, source_target_pairs={{0,24},{2,26},{4,28},{6,30},{8,0},{10,2},{12,4},{14,6},{16,8},{18,... | collective-permute-start | bytes 786440 | tf_op jit(solution)/shard_map/ppermute | solution.py:448
  6.7 28.5 %collective-permute-start.1 = (bf16[32,4096]{1,0:T(8,128)(2,1)}, bf16[32,4096]{1,0:T(8,128)(2,1)S(1)}, u32[]{:S(2)}, u32[]{:S(2)}) collective-permute-start(bf16[32,4096]{1,0:T(8,128)(2,1)} %refs_0_.7), channel_id=1, source_target_pairs={{0,8},{2,10},{4,12},{6,14},{8,16},{10,18},{12,20},{14,22},{16,24},... | collective-permute-start | bytes 786440 | tf_op jit(solution)/shard_map/ppermute | solution.py:448
  8.4 15.2 %copy-start.1 = (bf16[256,1792]{1,0:T(8,128)(2,1)S(1)}, bf16[256,1792]{1,0:T(8,128)(2,1)}, u32[]{:S(2)}) copy-start(bf16[256,1792]{1,0:T(8,128)(2,1)} %cot_ref.3) | copy-start | bytes 2752516
  8.4 15.2 %copy-start.10 = (s32[512]{0:T(512)S(1)}, s32[512]{0:T(512)}, u32[]{:S(2)}) copy-start(s32[512]{0:T(512)} %tenant_ref.9) | copy-start | bytes 6148
  17.9 5.7 %collective-permute-start.2 = (f32[4,1792]{1,0:T(4,128)}, f32[4,1792]{1,0:T(4,128)S(1)}, u32[]{:S(2)}, u32[]{:S(2)}) collective-permute-start(f32[4,1792]{1,0:T(4,128)} %partial_norms.1.nsq_a), channel_id=1, source_target_pairs={{0,1},{1,0},{2,3},{3,2},{4,5},{5,4},{6,7},{7,6},{8,9},{9,8},{10,11... | collective-permute-start | bytes 86024 | tf_op jit(solution)/shard_map/ppermute | solution.py:451
  18.5 16.8 %copy-start.2 = (bf16[32,4096]{1,0:T(8,128)(2,1)S(1)}, bf16[32,4096]{1,0:T(8,128)(2,1)}, u32[]{:S(2)}) copy-start(bf16[32,4096]{1,0:T(8,128)(2,1)} %refs_0_.7) | copy-start | bytes 786436
  23.6 0.9 copy-start.5
  24.5 0.7 copy-start.9
  35.2 3.1 %copy-start.7 = (bf16[256,1792]{1,0:T(8,128)(2,1)}, bf16[256,1792]{1,0:T(8,128)(2,1)S(1)}, u32[]{:S(2)}) copy-start(bf16[256,1792]{1,0:T(8,128)(2,1)S(1)} %get-tuple-element.57) | copy-start | bytes 2752516
  35.2 1.6 %copy-start.16 = (bf16[128,4096]{1,0:T(8,128)(2,1)S(1)}, bf16[128,4096]{1,0:T(8,128)(2,1)}, u32[]{:S(2)}) copy-start(bf16[128,4096]{1,0:T(8,128)(2,1)} %get-tuple-element.39) | copy-start | bytes 3145732
  35.2 6.4 %copy-start.6 = (f32[16,1792]{1,0:T(8,128)S(1)}, f32[16,1792]{1,0:T(8,128)}, u32[]{:S(2)}) copy-start(f32[16,1792]{1,0:T(8,128)} %mag_ref.3) | copy-start | bytes 344068
  35.4 4.9 %collective-permute-start.9 = (bf16[128,4096]{1,0:T(8,128)(2,1)S(1)}, bf16[128,4096]{1,0:T(8,128)(2,1)S(1)}, u32[]{:S(2)}, u32[]{:S(2)}) collective-permute-start(bf16[128,4096]{1,0:T(8,128)(2,1)S(1)} %pad_maximum_fusion), channel_id=1, source_target_pairs={{0,2},{2,0},{4,6},{6,4},{8,10},{10,8},{12,14},{14,12},{16,18},{18,... | collective-permute-start | bytes 3145736 | tf_op jit(solution)/shard_map/ppermute | solution.py:448
  36.8 3.5 %collective-permute-start.7 = (bf16[128,4096]{1,0:T(8,128)(2,1)S(1)}, bf16[128,4096]{1,0:T(8,128)(2,1)S(1)}, u32[]{:S(2)}, u32[]{:S(2)}) collective-permute-start(bf16[128,4096]{1,0:T(8,128)(2,1)S(1)} %copy-done.16), channel_id=1, source_target_pairs={{0,2},{2,0},{4,6},{6,4},{8,10},{10,8},{12,14},{14,12},{16,18},{18,... | collective-permute-start | bytes 3145736 | tf_op jit(solution)/shard_map/ppermute | solution.py:448
  36.8 18.0 %collective-permute-start.6 = (bf16[32,4096]{1,0:T(8,128)(2,1)S(1)}, bf16[32,4096]{1,0:T(8,128)(2,1)S(1)}, u32[]{:S(2)}, u32[]{:S(2)}) collective-permute-start(bf16[32,4096]{1,0:T(8,128)(2,1)S(1)} %collective-permute-done.5.refs_4_), channel_id=1, source_target_pairs={{0,4},{2,6},{4,0},{6,2},{8,12},{10,14},{12,8},{14,10},{16,20},{18,... | collective-permute-start | bytes 786440 | tf_op jit(solution)/shard_map/ppermute | solution.py:448
  38.3 16.6 %collective-permute-start.10 = (bf16[32,4096]{1,0:T(8,128)(2,1)S(1)}, bf16[32,4096]{1,0:T(8,128)(2,1)S(1)}, u32[]{:S(2)}, u32[]{:S(2)}) collective-permute-start(bf16[32,4096]{1,0:T(8,128)(2,1)S(1)} %collective-permute-done.8.refs_6_), channel_id=1, source_target_pairs={{0,4},{2,6},{4,0},{6,2},{8,12},{10,14},{12,8},{14,10},{16,20},{18,... | collective-permute-start | bytes 786440 | tf_op jit(solution)/shard_map/ppermute | solution.py:448
  38.8 17.9 %collective-permute-start.4 = (bf16[32,4096]{1,0:T(8,128)(2,1)S(1)}, bf16[32,4096]{1,0:T(8,128)(2,1)S(1)}, u32[]{:S(2)}, u32[]{:S(2)}) collective-permute-start(bf16[32,4096]{1,0:T(8,128)(2,1)S(1)} %collective-permute-done.1.refs_2_), channel_id=1, source_target_pairs={{0,4},{2,6},{4,0},{6,2},{8,12},{10,14},{12,8},{14,10},{16,20},{18,... | collective-permute-start | bytes 786440 | tf_op jit(solution)/shard_map/ppermute | solution.py:448
  40.3 1.0 copy-start.12
  40.3 1.3 %copy-start.15 = (bf16[128,4096]{1,0:T(8,128)(2,1)}, bf16[128,4096]{1,0:T(8,128)(2,1)S(1)}, u32[]{:S(2)}) copy-start(bf16[128,4096]{1,0:T(8,128)(2,1)S(1)} %collective-permute-done.7.refs_4_) | copy-start | bytes 3145732
  54.8 3.8 %copy-start.11 = (bf16[64,4096]{1,0:T(8,128)(2,1)}, bf16[64,4096]{1,0:T(8,128)(2,1)S(1)}, u32[]{:S(2)}) copy-start(bf16[64,4096]{1,0:T(8,128)(2,1)S(1)} %get-tuple-element.44) | copy-start | bytes 1572868
  54.8 1.9 %copy-start.13 = (bf16[32,4096]{1,0:T(8,128)(2,1)}, bf16[32,4096]{1,0:T(8,128)(2,1)S(1)}, u32[]{:S(2)}) copy-start(bf16[32,4096]{1,0:T(8,128)(2,1)S(1)} %collective-permute-done.10.refs_7_) | copy-start | bytes 786436
  57.8 3.0 %collective-permute-start.11 = (bf16[128,4096]{1,0:T(8,128)(2,1)}, bf16[128,4096]{1,0:T(8,128)(2,1)}, u32[]{:S(2)}, u32[]{:S(2)}) collective-permute-start(bf16[128,4096]{1,0:T(8,128)(2,1)} %pad_maximum_fusion.1), channel_id=1, source_target_pairs={{0,2},{2,0},{4,6},{6,4},{8,10},{10,8},{12,14},{14,12},{16,18},{18,... | collective-permute-start | bytes 3145736 | tf_op jit(solution)/shard_map/ppermute | solution.py:448
  57.8 4.5 %collective-permute-start.13 = (bf16[128,4096]{1,0:T(8,128)(2,1)}, bf16[128,4096]{1,0:T(8,128)(2,1)}, u32[]{:S(2)}, u32[]{:S(2)}) collective-permute-start(bf16[128,4096]{1,0:T(8,128)(2,1)} %get-tuple-element.46), channel_id=1, source_target_pairs={{0,2},{2,0},{4,6},{6,4},{8,10},{10,8},{12,14},{14,12},{16,18},{18,... | collective-permute-start | bytes 3145736 | tf_op jit(solution)/shard_map/ppermute | solution.py:448
  58.6 22.8 %collective-permute-start.12 = (bf16[64,4096]{1,0:T(8,128)(2,1)}, bf16[64,4096]{1,0:T(8,128)(2,1)S(1)}, u32[]{:S(2)}, u32[]{:S(2)}) collective-permute-start(bf16[64,4096]{1,0:T(8,128)(2,1)} %copy-done.11), channel_id=1, source_target_pairs={{0,4},{2,6},{4,0},{6,2},{8,12},{10,14},{12,8},{14,10},{16,20},{18,... | collective-permute-start | bytes 1572872 | tf_op jit(solution)/shard_map/ppermute | solution.py:448
  65.0 1.0 copy-start
  66.0 18.0 %collective-permute-start.14 = (bf16[64,4096]{1,0:T(8,128)(2,1)}, bf16[64,4096]{1,0:T(8,128)(2,1)}, u32[]{:S(2)}, u32[]{:S(2)}) collective-permute-start(bf16[64,4096]{1,0:T(8,128)(2,1)} %get-tuple-element.48), channel_id=1, source_target_pairs={{0,4},{2,6},{4,0},{6,2},{8,12},{10,14},{12,8},{14,10},{16,20},{18,... | collective-permute-start | bytes 1572872 | tf_op jit(solution)/shard_map/ppermute | solution.py:448
  79.8 34.6 %collective-permute-start.15 = (bf16[256,1792]{1,0:T(8,128)(2,1)}, bf16[256,1792]{1,0:T(8,128)(2,1)S(1)}, u32[]{:S(2)}, u32[]{:S(2)}) collective-permute-start(bf16[256,1792]{1,0:T(8,128)(2,1)} %get-tuple-element.52), channel_id=1, source_target_pairs={{0,1},{1,0},{2,3},{3,2},{4,5},{5,4},{6,7},{7,6},{8,9},{9,8},{10,11... | collective-permute-start | bytes 2752520 | tf_op jit(solution)/shard_map/ppermute | solution.py:451
  86.5 0.8 copy-start.3
  87.3 18.7 %collective-permute-start.19 = (bf16[32,4096]{1,0:T(8,128)(2,1)S(1)}, bf16[32,4096]{1,0:T(8,128)(2,1)S(1)}, u32[]{:S(2)}, u32[]{:S(2)}) collective-permute-start(bf16[32,4096]{1,0:T(8,128)(2,1)S(1)} %get-tuple-element.61), channel_id=1, source_target_pairs={{0,16},{2,18},{4,20},{6,22},{8,24},{10,26},{12,28},{14,30},{16,0},... | collective-permute-start | bytes 786440 | tf_op jit(solution)/shard_map/ppermute | solution.py:448
  89.9 17.7 %collective-permute-start.16 = (bf16[32,4096]{1,0:T(8,128)(2,1)S(1)}, bf16[32,4096]{1,0:T(8,128)(2,1)S(1)}, u32[]{:S(2)}, u32[]{:S(2)}) collective-permute-start(bf16[32,4096]{1,0:T(8,128)(2,1)S(1)} %get-tuple-element.55), channel_id=1, source_target_pairs={{0,24},{2,26},{4,28},{6,30},{8,0},{10,2},{12,4},{14,6},{16,8},{18,... | collective-permute-start | bytes 786440 | tf_op jit(solution)/shard_map/ppermute | solution.py:448
  102.8 10.8 %collective-permute-start.18 = (bf16[32,4096]{1,0:T(8,128)(2,1)S(1)}, bf16[32,4096]{1,0:T(8,128)(2,1)S(1)}, u32[]{:S(2)}, u32[]{:S(2)}) collective-permute-start(bf16[32,4096]{1,0:T(8,128)(2,1)S(1)} %get-tuple-element.60), channel_id=1, source_target_pairs={{0,8},{2,10},{4,12},{6,14},{8,16},{10,18},{12,20},{14,22},{16,24},... | collective-permute-start | bytes 786440 | tf_op jit(solution)/shard_map/ppermute | solution.py:448
  106.0 4.0 %collective-permute-start.20 = (f32[4,1792]{1,0:T(4,128)S(1)}, f32[4,1792]{1,0:T(4,128)S(1)}, u32[]{:S(2)}, u32[]{:S(2)}) collective-permute-start(f32[4,1792]{1,0:T(4,128)S(1)} %pad_maximum_fusion.2), channel_id=1, source_target_pairs={{0,1},{1,0},{2,3},{3,2},{4,5},{5,4},{6,7},{7,6},{8,9},{9,8},{10,11... | collective-permute-start | bytes 86024 | tf_op jit(solution)/shard_map/ppermute | solution.py:451
  107.5 3.9 %collective-permute-start.17 = (f32[16,512]{1,0:T(8,128)S(1)}, f32[16,512]{1,0:T(8,128)S(1)}, u32[]{:S(2)}, u32[]{:S(2)}) collective-permute-start(f32[16,512]{1,0:T(8,128)S(1)} %constant_dynamic-update-slice_fusion), channel_id=1, source_target_pairs={{0,1},{1,0},{2,3},{3,2},{4,5},{5,4},{6,7},{7,6},{8,9},{9,8},{10,11... | collective-permute-start | bytes 98312 | tf_op jit(solution)/shard_map/ppermute | solution.py:451
  110.1 1.8 %copy-start.8 = (bf16[256,1792]{1,0:T(8,128)(2,1)S(1)}, bf16[256,1792]{1,0:T(8,128)(2,1)}, u32[]{:S(2)}) copy-start(bf16[256,1792]{1,0:T(8,128)(2,1)} %copy-done.7) | copy-start | bytes 2752516
  112.0 1.7 %copy-start.4 = (f32[32,4096]{1,0:T(8,128)S(1)}, f32[32,4096]{1,0:T(8,128)}, u32[]{:S(2)}) copy-start(f32[32,4096]{1,0:T(8,128)} %copy-done.3) | copy-start | bytes 1572868
  112.0 2.5 %copy-start.14 = (f32[256,1792]{1,0:T(8,128)S(1)}, f32[256,1792]{1,0:T(8,128)}, u32[]{:S(2)}) copy-start(f32[256,1792]{1,0:T(8,128)} %get-tuple-element.51) | copy-start | bytes 5505028

commit v11 on v6

--- a/solution.py
+++ b/solution.py
@@ -518,9 +518,10 @@
         part, dots_here, low_here = project(0, F32, [finals[0]])
         dots = jnp.concatenate([dots_here, dots_away], axis=0)
         low = jnp.concatenate([low_here, low_away], axis=1)
-        late = (finals[nz // 2], finals[nz - 1])
-        dots = dots + jnp.roll(swap(once(dots, late)), blocks_mine, axis=0)
-        low = low + jnp.roll(swap(once(low, late)), rows_row, axis=1)
+        new_dots = swap(once(dots, finals[nz // 2]))
+        new_low = swap(once(low, finals[nz - 1]))
+        dots = dots + jnp.roll(new_dots, blocks_mine, axis=0)
+        low = low + jnp.roll(new_low, rows_row, axis=1)
         parts = [ours, theirs]
     else:
         ours = gradient(0, [], [])

time: 115 us -> 115 us (level)
  transfers between devices with their start and end apart: 21 -> 21, of which waited for: 8 -> 7; matrix products, arithmetic and copies ran while one was open for 3% -> 3% of each run, Pallas kernels for 55% -> 55%
where the time goes in v11:
time: 115 us; the launch traced here: 114 us
  Pallas kernels  62.7 us (55%)
  starting transfers between devices  23.3 us (20%)
  waiting for transfers between devices  11 us (10%)
  local copies, waits for them, and re-layouts  10 us (9%)
  other arithmetic  3.53 us (3%)
  matrix products  2.05 us (2%)
    pallas_call x2, Pallas kernels, forward(): pl.pallas_call(functools.partial(forward_body, nb, rank, nz), out_shape=s...  25.1 us
    pallas_call x2, Pallas kernels, input_gradient(): pl.pallas_call(functools.partial(grad_body, nb, rank, len(add)), out_shap...  23.3 us
    ppermute x16, starting transfers between devices, move(): return lax.ppermute(value, 'col', perm)  17.7 us
    unnamed x47, local copies, waits for them, and re-layouts  9.68 us
    pallas_call x1, Pallas kernels, partial_norms(): pl.pallas_call(functools.partial(norm_body, nblk, rank), out_shape=shape,...  9.41 us
    ppermute x5, waiting for transfers between devices, swap(): return lax.ppermute(value, 'row', [(0, 1), (1, 0)])  5.95 us
    ppermute x5, starting transfers between devices, swap(): return lax.ppermute(value, 'row', [(0, 1), (1, 0)])  5.58 us
    ppermute x16, waiting for transfers between devices, move(): return lax.ppermute(value, 'col', perm)  5.08 us
  transfers between devices with their start and end apart: 21, of which 7 were waited for; matrix products, arithmetic and copies ran while one was open for 3% of the time, Pallas kernels for 55%

profile of v11, /device:TPU:8, one launch (start us, length us, event | category | flops | bytes accessed | tf_op | source)
XLA Modules:
  0.0 113.6 jit_solution(11311850744179407281)
XLA Ops:
  0.6 1.6 %collective-permute-start.3 = (bf16[256,1792]{1,0:T(8,128)(2,1)}, bf16[256,1792]{1,0:T(8,128)(2,1)}, u32[]{:S(2)}, u32[]{:S(2)}) collective-permute-start(bf16[256,1792]{1,0:T(8,128)(2,1)} %cot_ref.3), channel_id=1, source_target_pairs={{0,1},{1,0},{2,3},{3,2},{4,5},{5,4},{6,7},{7,6},{8,9},{9,8},{10,11... | collective-permute-start | bytes 2752520 | tf_op jit(solution)/shard_map/ppermute | solution.py:451
  2.2 1.5 %collective-permute-start = (bf16[32,4096]{1,0:T(8,128)(2,1)}, bf16[32,4096]{1,0:T(8,128)(2,1)S(1)}, u32[]{:S(2)}, u32[]{:S(2)}) collective-permute-start(bf16[32,4096]{1,0:T(8,128)(2,1)} %refs_0_.7), channel_id=1, source_target_pairs={{0,4},{2,6},{4,0},{6,2},{8,12},{10,14},{12,8},{14,10},{16,20},{18,... | collective-permute-start | bytes 786440 | tf_op jit(solution)/shard_map/ppermute | solution.py:448
  3.7 2.6 %collective-permute-start.5 = (bf16[32,4096]{1,0:T(8,128)(2,1)}, bf16[32,4096]{1,0:T(8,128)(2,1)S(1)}, u32[]{:S(2)}, u32[]{:S(2)}) collective-permute-start(bf16[32,4096]{1,0:T(8,128)(2,1)} %refs_0_.7), channel_id=1, source_target_pairs={{0,16},{2,18},{4,20},{6,22},{8,24},{10,26},{12,28},{14,30},{16,0},... | collective-permute-start | bytes 786440 | tf_op jit(solution)/shard_map/ppermute | solution.py:448
  6.3 0.4 collective-permute-start.8
  6.7 1.6 %collective-permute-start.1 = (bf16[32,4096]{1,0:T(8,128)(2,1)}, bf16[32,4096]{1,0:T(8,128)(2,1)S(1)}, u32[]{:S(2)}, u32[]{:S(2)}) collective-permute-start(bf16[32,4096]{1,0:T(8,128)(2,1)} %refs_0_.7), channel_id=1, source_target_pairs={{0,8},{2,10},{4,12},{6,14},{8,16},{10,18},{12,20},{14,22},{16,24},... | collective-permute-start | bytes 786440 | tf_op jit(solution)/shard_map/ppermute | solution.py:448
  8.4 1.2 %copy-done = bf16[16,16,1792]{2,1,0:T(8,128)(2,1)S(1)} copy-done((bf16[16,16,1792]{2,1,0:T(8,128)(2,1)S(1)}, bf16[16,16,1792]{2,1,0:T(8,128)(2,1)}, u32[]{:S(2)}) %copy-start) | copy-done | bytes 917528
  9.6 0.7 copy-done.15
  10.3 9.4 %partial_norms.1.nsq_a = f32[4,1792]{1,0:T(4,128)S(1)} custom-call(s32[512]{0:T(512)S(1)} %copy-done.15, bf16[4096,1792]{1,0:T(8,128)(2,1)} %w_hbm.5, bf16[16,16,4096]{2,1,0:T(8,128)(2,1)} %a_hbm.5, bf16[16,16,1792]{2,1,0:T(8,128)(2,1)S(1)} %copy-done), custom_call_target="tpu_custom_call" | custom-call | flops 1000 | bytes 1000 | tf_op jit(solution)/shard_map/partial_norms/pallas_call | solution.py:116
  19.7 0.6 collective-permute-start.2
  20.4 3.3 %collective-permute-done.2.nsq_b = f32[4,1792]{1,0:T(4,128)S(1)} collective-permute-done((f32[4,1792]{1,0:T(4,128)S(1)}, f32[4,1792]{1,0:T(4,128)S(1)}, u32[]{:S(2)}, u32[]{:S(2)}) %collective-permute-start.2) | collective-permute-done | bytes 28704 | tf_op jit(solution)/shard_map/ppermute | solution.py:451
  23.7 9.9 %input_gradient.2 = (f32[2,1792]{1,0:T(2,128)S(1)}, bf16[256,1792]{1,0:T(8,128)(2,1)S(1)}, f32[128,4096]{1,0:T(8,128)}, bf16[128,4096]{1,0:T(8,128)(2,1)}) custom-call(s32[512]{0:T(512)S(1)} %copy-done.16, s32[4]{0:T(128)S(1)} %pad_add_fusion.place_ref, bf16[256,1792]{1,0:T(8,128)(2,1)S(1)} %copy-done.4, f32[4,1792]{1,0:T(4,128)S(1)} %partial_norms.1.nsq_a, ...), custom_call_target="tpu_custom_call" | custom-call | flops 1000 | bytes 1000 | tf_op jit(solution)/shard_map/input_gradient/pallas_call | solution.py:210
  33.8 1.3 %copy-done.22 = bf16[128,4096]{1,0:T(8,128)(2,1)S(1)} copy-done((bf16[128,4096]{1,0:T(8,128)(2,1)S(1)}, bf16[128,4096]{1,0:T(8,128)(2,1)}, u32[]{:S(2)}) %copy-start.22) | copy-done | bytes 1048600
  35.2 1.5 %collective-permute-start.6 = (bf16[32,4096]{1,0:T(8,128)(2,1)S(1)}, bf16[32,4096]{1,0:T(8,128)(2,1)S(1)}, u32[]{:S(2)}, u32[]{:S(2)}) collective-permute-start(bf16[32,4096]{1,0:T(8,128)(2,1)S(1)} %collective-permute-done.5.refs_4_), channel_id=1, source_target_pairs={{0,4},{2,6},{4,0},{6,2},{8,12},{10,14},{12,8},{14,10},{16,20},{18,... | collective-permute-start | bytes 786440 | tf_op jit(solution)/shard_map/ppermute | solution.py:448
  36.6 0.6 collective-permute-start.10
  37.2 1.5 %collective-permute-start.4 = (bf16[32,4096]{1,0:T(8,128)(2,1)S(1)}, bf16[32,4096]{1,0:T(8,128)(2,1)S(1)}, u32[]{:S(2)}, u32[]{:S(2)}) collective-permute-start(bf16[32,4096]{1,0:T(8,128)(2,1)S(1)} %collective-permute-done.1.refs_2_), channel_id=1, source_target_pairs={{0,4},{2,6},{4,0},{6,2},{8,12},{10,14},{12,8},{14,10},{16,20},{18,... | collective-permute-start | bytes 786440 | tf_op jit(solution)/shard_map/ppermute | solution.py:448
  38.7 1.0 copy-done.18
  39.6 0.4 copy-done.21
  40.0 13.4 %input_gradient.3 = (f32[2,1792]{1,0:T(2,128)S(1)}, bf16[256,1792]{1,0:T(8,128)(2,1)S(1)}, f32[128,4096]{1,0:T(8,128)}, bf16[128,4096]{1,0:T(8,128)(2,1)}, f32[6...) custom-call(s32[512]{0:T(512)S(1)} %copy-done.16, s32[4]{0:T(128)S(1)} %get-tuple-element.66.place_ref, ...), custom_call_target="tpu_custom_call" | custom-call | flops 1000 | bytes 1000 | tf_op jit(solution)/shard_map/input_gradient/pallas_call | solution.py:210
  53.4 0.9 copy-done.13
  54.3 0.8 copy-done.17
  55.2 1.1 pad_maximum_fusion.1
  56.3 0.5 collective-permute-start.13
  57.1 1.4 %collective-permute-start.12 = (bf16[64,4096]{1,0:T(8,128)(2,1)}, bf16[64,4096]{1,0:T(8,128)(2,1)}, u32[]{:S(2)}, u32[]{:S(2)}) collective-permute-start(bf16[64,4096]{1,0:T(8,128)(2,1)} %copy-done.17), channel_id=1, source_target_pairs={{0,4},{2,6},{4,0},{6,2},{8,12},{10,14},{12,8},{14,10},{16,20},{18,... | collective-permute-start | bytes 1572872 | tf_op jit(solution)/shard_map/ppermute | solution.py:448
  58.5 1.8 %collective-permute-done.11.refs_0_.refs_9_ = bf16[128,4096]{1,0:T(8,128)(2,1)S(1)} collective-permute-done((bf16[128,4096]{1,0:T(8,128)(2,1)}, bf16[128,4096]{1,0:T(8,128)(2,1)S(1)}, u32[]{:S(2)}, u32[]{:S(2)}) %collective-permute-start.11) | collective-permute-done | bytes 1048608 | tf_op jit(solution)/shard_map/ppermute | solution.py:448
  60.3 0.5 collective-permute-done.13.recv_ref
  60.8 1.6 %copy-done.8 = f32[128,4096]{1,0:T(8,128)S(1)} copy-done((f32[128,4096]{1,0:T(8,128)S(1)}, f32[128,4096]{1,0:T(8,128)}, u32[]{:S(2)}) %copy-start.8) | copy-done | bytes 2097176
  62.3 2.1 %add_core.1 = (f32[64,4096]{1,0:T(8,128)S(1)}, bf16[64,4096]{1,0:T(8,128)(2,1)}) custom-call(f32[128,4096]{1,0:T(8,128)S(1)} %copy-done.8, bf16[128,4096]{1,0:T(8,128)(2,1)} %collective-permute-done.13.recv_ref, bf16[128,4096]{1,0:T(8,128)(2,1)S(1)} %collective-permute-done.11.refs_0_.refs_9_), custom_call_target="tpu_custom_call" | custom-call | flops 1000 | bytes 1000 | tf_op jit(solution)/shard_map/add_core/pallas_call | solution.py:247
  64.5 1.0 copy-done.2
  65.4 1.4 %collective-permute-start.14 = (bf16[64,4096]{1,0:T(8,128)(2,1)}, bf16[64,4096]{1,0:T(8,128)(2,1)S(1)}, u32[]{:S(2)}, u32[]{:S(2)}) collective-permute-start(bf16[64,4096]{1,0:T(8,128)(2,1)} %get-tuple-element.48), channel_id=1, source_target_pairs={{0,4},{2,6},{4,0},{6,2},{8,12},{10,14},{12,8},{14,10},{16,20},{18,... | collective-permute-start | bytes 1572872 | tf_op jit(solution)/shard_map/ppermute | solution.py:448
  67.1 12.6 %forward.2 = (bf16[256,1792]{1,0:T(8,128)(2,1)}, f32[2,1792]{1,0:T(2,128)S(1)}, f32[16,256]{1,0:T(8,128)S(1)}) custom-call(s32[512]{0:T(512)S(1)} %copy-done.16, s32[4]{0:T(128)S(1)} %get-tuple-element.66.place_ref, bf16[256,1792]{1,0:T(8,128)(2,1)} %collective-permute-done.3.refs_3_.cot_ref, bf16[4096,1792]{1,0:T(8,128)(2,1)} %w_hbm.5, ...), custom_call_target="tpu_custom_call" | custom-call | flops 1000 | bytes 1000 | tf_op jit(solution)/shard_map/forward/pallas_call | solution.py:404
  79.7 1.4 %collective-permute-start.15 = (bf16[256,1792]{1,0:T(8,128)(2,1)}, bf16[256,1792]{1,0:T(8,128)(2,1)S(1)}, u32[]{:S(2)}, u32[]{:S(2)}) collective-permute-start(bf16[256,1792]{1,0:T(8,128)(2,1)} %get-tuple-element.52), channel_id=1, source_target_pairs={{0,1},{1,0},{2,3},{3,2},{4,5},{5,4},{6,7},{7,6},{8,9},{9,8},{10,11... | collective-permute-start | bytes 2752520 | tf_op jit(solution)/shard_map/ppermute | solution.py:451
  81.1 1.3 %collective-permute-done.14.refs_3_ = bf16[64,4096]{1,0:T(8,128)(2,1)S(1)} collective-permute-done((bf16[64,4096]{1,0:T(8,128)(2,1)}, bf16[64,4096]{1,0:T(8,128)(2,1)S(1)}, u32[]{:S(2)}, u32[]{:S(2)}) %collective-permute-start.14) | collective-permute-done | bytes 524320 | tf_op jit(solution)/shard_map/ppermute | solution.py:448
  82.3 2.0 %add_x.1 = (f32[32,4096]{1,0:T(8,128)S(1)}, bf16[32,4096]{1,0:T(8,128)(2,1)S(1)}, bf16[32,4096]{1,0:T(8,128)(2,1)S(1)}, bf16[32,4096]{1,0:T(8,128)(2,1)S(1)}) custom-call(s32[5]{0:T(128)S(1)} %stack.39.place_ref, f32[64,4096]{1,0:T(8,128)S(1)} %copy-done.9, bf16[64,4096]{1,0:T(8,128)(2,1)} %collective-permute-done.12.refs_1_, f32[64,4096]{1,0:T(8,128)S(1)} %copy-done.3, ...), custom_call_target="tpu_custom_call" | custom-call | flops 1000 | bytes 1000 | tf_op jit(solution)/shard_map/add_x/pallas_call | solution.py:286
  84.4 0.8 copy-done.6
  85.2 2.6 %collective-permute-start.19 = (bf16[32,4096]{1,0:T(8,128)(2,1)S(1)}, bf16[32,4096]{1,0:T(8,128)(2,1)S(1)}, u32[]{:S(2)}, u32[]{:S(2)}) collective-permute-start(bf16[32,4096]{1,0:T(8,128)(2,1)S(1)} %get-tuple-element.61), channel_id=1, source_target_pairs={{0,16},{2,18},{4,20},{6,22},{8,24},{10,26},{12,28},{14,30},{16,0},... | collective-permute-start | bytes 786440 | tf_op jit(solution)/shard_map/ppermute | solution.py:448
  87.7 0.4 collective-permute-start.16
  88.2 12.5 %forward.3 = (f32[256,1792]{1,0:T(8,128)}, f32[2,1792]{1,0:T(2,128)S(1)}, f32[16,256]{1,0:T(8,128)S(1)}) custom-call(s32[512]{0:T(512)S(1)} %copy-done.16, s32[4]{0:T(128)S(1)} %pad_add_fusion.place_ref, bf16[256,1792]{1,0:T(8,128)(2,1)} %cot_ref.3, bf16[4096,1792]{1,0:T(8,128)(2,1)} %w_hbm.5, bf16[16,16,4096]{2,1,0:T(8,128)(2,1)} %a_hbm.5, ...), custom_call_target="tpu_custom_call" | custom-call | flops 1000 | bytes 1000 | tf_op jit(solution)/shard_map/forward/pallas_call | solution.py:404
  100.7 1.6 %collective-permute-start.18 = (bf16[32,4096]{1,0:T(8,128)(2,1)S(1)}, bf16[32,4096]{1,0:T(8,128)(2,1)S(1)}, u32[]{:S(2)}, u32[]{:S(2)}) collective-permute-start(bf16[32,4096]{1,0:T(8,128)(2,1)S(1)} %get-tuple-element.60), channel_id=1, source_target_pairs={{0,8},{2,10},{4,12},{6,14},{8,16},{10,18},{12,20},{14,22},{16,24},... | collective-permute-start | bytes 786440 | tf_op jit(solution)/shard_map/ppermute | solution.py:448
  102.4 1.5 %collective-permute-done.19.refs_2_ = bf16[32,4096]{1,0:T(8,128)(2,1)S(1)} collective-permute-done((bf16[32,4096]{1,0:T(8,128)(2,1)S(1)}, bf16[32,4096]{1,0:T(8,128)(2,1)S(1)}, u32[]{:S(2)}, u32[]{:S(2)}) %collective-permute-start.19) | collective-permute-done | bytes 262176 | tf_op jit(solution)/shard_map/ppermute | solution.py:448
  103.9 1.6 %collective-permute-start.20 = (f32[4,1792]{1,0:T(4,128)S(1)}, f32[4,1792]{1,0:T(4,128)S(1)}, u32[]{:S(2)}, u32[]{:S(2)}) collective-permute-start(f32[4,1792]{1,0:T(4,128)S(1)} %pad_maximum_fusion.2), channel_id=1, source_target_pairs={{0,1},{1,0},{2,3},{3,2},{4,5},{5,4},{6,7},{7,6},{8,9},{9,8},{10,11... | collective-permute-start | bytes 86024 | tf_op jit(solution)/shard_map/ppermute | solution.py:451
  105.5 0.4 collective-permute-start.17
  105.9 1.8 %collective-permute-done.20 = f32[4,1792]{1,0:T(4,128)S(1)} collective-permute-done((f32[4,1792]{1,0:T(4,128)S(1)}, f32[4,1792]{1,0:T(4,128)S(1)}, u32[]{:S(2)}, u32[]{:S(2)}) %collective-permute-start.20) | collective-permute-done | bytes 28704 | tf_op jit(solution)/shard_map/ppermute | solution.py:451
  107.9 0.7 fusion.3
  108.6 0.8 collective-permute-done.17
  109.5 0.4 fusion.9
  110.0 1.6 %convolution_add_fusion = f32[256,1792]{1,0:T(8,128)} fusion(f32[256,1792]{1,0:T(8,128)S(1)} %fusion.9, bf16[256,256]{1,0:T(8,128)(2,1)S(1)} %bitcast.29, bf16[256,1792]{1,0:T(8,128)(2,1)S(1)} %copy-done.12), kind=kOutput, calls=%fused_computation | convolution fusion | flops 235339776 | bytes 4718592 | tf_op jit(solution)/shard_map/dot_general | solution.py:556
  111.6 0.8 add_z.1
  112.5 1.1 fusion
  (74 shorter events, 1.1 us)
Async XLA Ops:
  0.6 23.0 %collective-permute-start.3 = (bf16[256,1792]{1,0:T(8,128)(2,1)}, bf16[256,1792]{1,0:T(8,128)(2,1)}, u32[]{:S(2)}, u32[]{:S(2)}) collective-permute-start(bf16[256,1792]{1,0:T(8,128)(2,1)} %cot_ref.3), channel_id=1, source_target_pairs={{0,1},{1,0},{2,3},{3,2},{4,5},{5,4},{6,7},{7,6},{8,9},{9,8},{10,11... | collective-permute-start | bytes 2752520 | tf_op jit(solution)/shard_map/ppermute | solution.py:451
  2.2 17.5 %collective-permute-start = (bf16[32,4096]{1,0:T(8,128)(2,1)}, bf16[32,4096]{1,0:T(8,128)(2,1)S(1)}, u32[]{:S(2)}, u32[]{:S(2)}) collective-permute-start(bf16[32,4096]{1,0:T(8,128)(2,1)} %refs_0_.7), channel_id=1, source_target_pairs={{0,4},{2,6},{4,0},{6,2},{8,12},{10,14},{12,8},{14,10},{16,20},{18,... | collective-permute-start | bytes 786440 | tf_op jit(solution)/shard_map/ppermute | solution.py:448
  3.7 29.9 %collective-permute-start.5 = (bf16[32,4096]{1,0:T(8,128)(2,1)}, bf16[32,4096]{1,0:T(8,128)(2,1)S(1)}, u32[]{:S(2)}, u32[]{:S(2)}) collective-permute-start(bf16[32,4096]{1,0:T(8,128)(2,1)} %refs_0_.7), channel_id=1, source_target_pairs={{0,16},{2,18},{4,20},{6,22},{8,24},{10,26},{12,28},{14,30},{16,0},... | collective-permute-start | bytes 786440 | tf_op jit(solution)/shard_map/ppermute | solution.py:448
  6.3 27.3 %collective-permute-start.8 = (bf16[32,4096]{1,0:T(8,128)(2,1)}, bf16[32,4096]{1,0:T(8,128)(2,1)S(1)}, u32[]{:S(2)}, u32[]{:S(2)}) collective-permute-start(bf16[32,4096]{1,0:T(8,128)(2,1)} %refs_0_.7), channel_id=1, source_target_pairs={{0,24},{2,26},{4,28},{6,30},{8,0},{10,2},{12,4},{14,6},{16,8},{18,... | collective-permute-start | bytes 786440 | tf_op jit(solution)/shard_map/ppermute | solution.py:448
  6.7 26.9 %collective-permute-start.1 = (bf16[32,4096]{1,0:T(8,128)(2,1)}, bf16[32,4096]{1,0:T(8,128)(2,1)S(1)}, u32[]{:S(2)}, u32[]{:S(2)}) collective-permute-start(bf16[32,4096]{1,0:T(8,128)(2,1)} %refs_0_.7), channel_id=1, source_target_pairs={{0,8},{2,10},{4,12},{6,14},{8,16},{10,18},{12,20},{14,22},{16,24},... | collective-permute-start | bytes 786440 | tf_op jit(solution)/shard_map/ppermute | solution.py:448
  8.4 1.2 %copy-start = (bf16[16,16,1792]{2,1,0:T(8,128)(2,1)S(1)}, bf16[16,16,1792]{2,1,0:T(8,128)(2,1)}, u32[]{:S(2)}) copy-start(bf16[16,16,1792]{2,1,0:T(8,128)(2,1)} %up_hbm.5) | copy-start | bytes 2752516
  9.6 0.7 copy-start.15
  10.3 13.4 %copy-start.4 = (bf16[256,1792]{1,0:T(8,128)(2,1)S(1)}, bf16[256,1792]{1,0:T(8,128)(2,1)}, u32[]{:S(2)}) copy-start(bf16[256,1792]{1,0:T(8,128)(2,1)} %cot_ref.3) | copy-start | bytes 2752516
  10.3 13.4 %copy-start.10 = (f32[16,1792]{1,0:T(8,128)S(1)}, f32[16,1792]{1,0:T(8,128)}, u32[]{:S(2)}) copy-start(f32[16,1792]{1,0:T(8,128)} %mag_ref.3) | copy-start | bytes 344068
  10.3 13.4 %copy-start.16 = (s32[512]{0:T(512)S(1)}, s32[512]{0:T(512)}, u32[]{:S(2)}) copy-start(s32[512]{0:T(512)} %tenant_ref.9) | copy-start | bytes 6148
  19.7 3.9 %collective-permute-start.2 = (f32[4,1792]{1,0:T(4,128)S(1)}, f32[4,1792]{1,0:T(4,128)S(1)}, u32[]{:S(2)}, u32[]{:S(2)}) collective-permute-start(f32[4,1792]{1,0:T(4,128)S(1)} %partial_norms.1.nsq_a), channel_id=1, source_target_pairs={{0,1},{1,0},{2,3},{3,2},{4,5},{5,4},{6,7},{7,6},{8,9},{9,8},{10,11... | collective-permute-start | bytes 86024 | tf_op jit(solution)/shard_map/ppermute | solution.py:451
  20.3 13.3 %copy-start.5 = (bf16[32,4096]{1,0:T(8,128)(2,1)S(1)}, bf16[32,4096]{1,0:T(8,128)(2,1)}, u32[]{:S(2)}) copy-start(bf16[32,4096]{1,0:T(8,128)(2,1)} %refs_0_.7) | copy-start | bytes 786436
  33.6 3.0 %copy-start.11 = (bf16[256,1792]{1,0:T(8,128)(2,1)}, bf16[256,1792]{1,0:T(8,128)(2,1)S(1)}, u32[]{:S(2)}) copy-start(bf16[256,1792]{1,0:T(8,128)(2,1)S(1)} %get-tuple-element.57) | copy-start | bytes 2752516
  33.6 1.6 %copy-start.22 = (bf16[128,4096]{1,0:T(8,128)(2,1)S(1)}, bf16[128,4096]{1,0:T(8,128)(2,1)}, u32[]{:S(2)}) copy-start(bf16[128,4096]{1,0:T(8,128)(2,1)} %get-tuple-element.39) | copy-start | bytes 3145732
  33.8 4.9 %collective-permute-start.9 = (bf16[128,4096]{1,0:T(8,128)(2,1)S(1)}, bf16[128,4096]{1,0:T(8,128)(2,1)S(1)}, u32[]{:S(2)}, u32[]{:S(2)}) collective-permute-start(bf16[128,4096]{1,0:T(8,128)(2,1)S(1)} %pad_maximum_fusion), channel_id=1, source_target_pairs={{0,2},{2,0},{4,6},{6,4},{8,10},{10,8},{12,14},{14,12},{16,18},{18,... | collective-permute-start | bytes 3145736 | tf_op jit(solution)/shard_map/ppermute | solution.py:448
  35.2 3.5 %collective-permute-start.7 = (bf16[128,4096]{1,0:T(8,128)(2,1)S(1)}, bf16[128,4096]{1,0:T(8,128)(2,1)S(1)}, u32[]{:S(2)}, u32[]{:S(2)}) collective-permute-start(bf16[128,4096]{1,0:T(8,128)(2,1)S(1)} %copy-done.22), channel_id=1, source_target_pairs={{0,2},{2,0},{4,6},{6,4},{8,10},{10,8},{12,14},{14,12},{16,18},{18,... | collective-permute-start | bytes 3145736 | tf_op jit(solution)/shard_map/ppermute | solution.py:448
  35.2 20.0 %collective-permute-start.6 = (bf16[32,4096]{1,0:T(8,128)(2,1)S(1)}, bf16[32,4096]{1,0:T(8,128)(2,1)S(1)}, u32[]{:S(2)}, u32[]{:S(2)}) collective-permute-start(bf16[32,4096]{1,0:T(8,128)(2,1)S(1)} %collective-permute-done.5.refs_4_), channel_id=1, source_target_pairs={{0,4},{2,6},{4,0},{6,2},{8,12},{10,14},{12,8},{14,10},{16,20},{18,... | collective-permute-start | bytes 786440 | tf_op jit(solution)/shard_map/ppermute | solution.py:448
  36.6 18.5 %collective-permute-start.10 = (bf16[32,4096]{1,0:T(8,128)(2,1)S(1)}, bf16[32,4096]{1,0:T(8,128)(2,1)S(1)}, u32[]{:S(2)}, u32[]{:S(2)}) collective-permute-start(bf16[32,4096]{1,0:T(8,128)(2,1)S(1)} %collective-permute-done.8.refs_6_), channel_id=1, source_target_pairs={{0,4},{2,6},{4,0},{6,2},{8,12},{10,14},{12,8},{14,10},{16,20},{18,... | collective-permute-start | bytes 786440 | tf_op jit(solution)/shard_map/ppermute | solution.py:448
  37.2 17.9 %collective-permute-start.4 = (bf16[32,4096]{1,0:T(8,128)(2,1)S(1)}, bf16[32,4096]{1,0:T(8,128)(2,1)S(1)}, u32[]{:S(2)}, u32[]{:S(2)}) collective-permute-start(bf16[32,4096]{1,0:T(8,128)(2,1)S(1)} %collective-permute-done.1.refs_2_), channel_id=1, source_target_pairs={{0,4},{2,6},{4,0},{6,2},{8,12},{10,14},{12,8},{14,10},{16,20},{18,... | collective-permute-start | bytes 786440 | tf_op jit(solution)/shard_map/ppermute | solution.py:448
  38.7 1.0 copy-start.18
  38.7 1.3 %copy-start.21 = (bf16[128,4096]{1,0:T(8,128)(2,1)}, bf16[128,4096]{1,0:T(8,128)(2,1)S(1)}, u32[]{:S(2)}) copy-start(bf16[128,4096]{1,0:T(8,128)(2,1)S(1)} %collective-permute-done.7.refs_4_) | copy-start | bytes 3145732
  53.4 0.9 copy-start.13
  54.3 0.8 copy-start.17
  55.1 9.3 %copy-start.19 = (bf16[32,4096]{1,0:T(8,128)(2,1)}, bf16[32,4096]{1,0:T(8,128)(2,1)S(1)}, u32[]{:S(2)}) copy-start(bf16[32,4096]{1,0:T(8,128)(2,1)S(1)} %collective-permute-done.10.refs_7_) | copy-start | bytes 786436
  56.3 4.0 %collective-permute-start.11 = (bf16[128,4096]{1,0:T(8,128)(2,1)}, bf16[128,4096]{1,0:T(8,128)(2,1)S(1)}, u32[]{:S(2)}, u32[]{:S(2)}) collective-permute-start(bf16[128,4096]{1,0:T(8,128)(2,1)} %pad_maximum_fusion.1), channel_id=1, source_target_pairs={{0,2},{2,0},{4,6},{6,4},{8,10},{10,8},{12,14},{14,12},{16,18},{18,... | collective-permute-start | bytes 3145736 | tf_op jit(solution)/shard_map/ppermute | solution.py:448
  56.3 4.5 %collective-permute-start.13 = (bf16[128,4096]{1,0:T(8,128)(2,1)}, bf16[128,4096]{1,0:T(8,128)(2,1)}, u32[]{:S(2)}, u32[]{:S(2)}) collective-permute-start(bf16[128,4096]{1,0:T(8,128)(2,1)} %get-tuple-element.46), channel_id=1, source_target_pairs={{0,2},{2,0},{4,6},{6,4},{8,10},{10,8},{12,14},{14,12},{16,18},{18,... | collective-permute-start | bytes 3145736 | tf_op jit(solution)/shard_map/ppermute | solution.py:448
  57.1 24.0 %collective-permute-start.12 = (bf16[64,4096]{1,0:T(8,128)(2,1)}, bf16[64,4096]{1,0:T(8,128)(2,1)}, u32[]{:S(2)}, u32[]{:S(2)}) collective-permute-start(bf16[64,4096]{1,0:T(8,128)(2,1)} %copy-done.17), channel_id=1, source_target_pairs={{0,4},{2,6},{4,0},{6,2},{8,12},{10,14},{12,8},{14,10},{16,20},{18,... | collective-permute-start | bytes 1572872 | tf_op jit(solution)/shard_map/ppermute | solution.py:448
  60.3 4.2 %copy-start.1 = (bf16[128,4096]{1,0:T(8,128)(2,1)}, bf16[128,4096]{1,0:T(8,128)(2,1)S(1)}, u32[]{:S(2)}) copy-start(bf16[128,4096]{1,0:T(8,128)(2,1)S(1)} %collective-permute-done.11.refs_0_.refs_9_) | copy-start | bytes 3145732
  60.8 1.6 %copy-start.8 = (f32[128,4096]{1,0:T(8,128)S(1)}, f32[128,4096]{1,0:T(8,128)}, u32[]{:S(2)}) copy-start(f32[128,4096]{1,0:T(8,128)} %get-tuple-element.45.keep_ref) | copy-start | bytes 6291460
  64.5 1.0 copy-start.2
  65.4 16.9 %collective-permute-start.14 = (bf16[64,4096]{1,0:T(8,128)(2,1)}, bf16[64,4096]{1,0:T(8,128)(2,1)S(1)}, u32[]{:S(2)}, u32[]{:S(2)}) collective-permute-start(bf16[64,4096]{1,0:T(8,128)(2,1)} %get-tuple-element.48), channel_id=1, source_target_pairs={{0,4},{2,6},{4,0},{6,2},{8,12},{10,14},{12,8},{14,10},{16,20},{18,... | collective-permute-start | bytes 1572872 | tf_op jit(solution)/shard_map/ppermute | solution.py:448
  67.0 15.3 %copy-start.3 = (f32[64,4096]{1,0:T(8,128)S(1)}, f32[64,4096]{1,0:T(8,128)}, u32[]{:S(2)}) copy-start(f32[64,4096]{1,0:T(8,128)} %copy-done.2) | copy-start | bytes 3145732
  67.1 15.3 %copy-start.9 = (f32[64,4096]{1,0:T(8,128)S(1)}, f32[64,4096]{1,0:T(8,128)}, u32[]{:S(2)}) copy-start(f32[64,4096]{1,0:T(8,128)} %get-tuple-element.43.refs_0_) | copy-start | bytes 3145732
  79.7 32.8 %collective-permute-start.15 = (bf16[256,1792]{1,0:T(8,128)(2,1)}, bf16[256,1792]{1,0:T(8,128)(2,1)S(1)}, u32[]{:S(2)}, u32[]{:S(2)}) collective-permute-start(bf16[256,1792]{1,0:T(8,128)(2,1)} %get-tuple-element.52), channel_id=1, source_target_pairs={{0,1},{1,0},{2,3},{3,2},{4,5},{5,4},{6,7},{7,6},{8,9},{9,8},{10,11... | collective-permute-start | bytes 2752520 | tf_op jit(solution)/shard_map/ppermute | solution.py:451
  84.4 0.8 copy-start.6
  85.2 18.7 %collective-permute-start.19 = (bf16[32,4096]{1,0:T(8,128)(2,1)S(1)}, bf16[32,4096]{1,0:T(8,128)(2,1)S(1)}, u32[]{:S(2)}, u32[]{:S(2)}) collective-permute-start(bf16[32,4096]{1,0:T(8,128)(2,1)S(1)} %get-tuple-element.61), channel_id=1, source_target_pairs={{0,16},{2,18},{4,20},{6,22},{8,24},{10,26},{12,28},{14,30},{16,0},... | collective-permute-start | bytes 786440 | tf_op jit(solution)/shard_map/ppermute | solution.py:448
  87.7 17.8 %collective-permute-start.16 = (bf16[32,4096]{1,0:T(8,128)(2,1)S(1)}, bf16[32,4096]{1,0:T(8,128)(2,1)S(1)}, u32[]{:S(2)}, u32[]{:S(2)}) collective-permute-start(bf16[32,4096]{1,0:T(8,128)(2,1)S(1)} %get-tuple-element.55), channel_id=1, source_target_pairs={{0,24},{2,26},{4,28},{6,30},{8,0},{10,2},{12,4},{14,6},{16,8},{18,... | collective-permute-start | bytes 786440 | tf_op jit(solution)/shard_map/ppermute | solution.py:448
  100.7 8.8 %copy-start.14 = (bf16[256,1792]{1,0:T(8,128)(2,1)S(1)}, bf16[256,1792]{1,0:T(8,128)(2,1)}, u32[]{:S(2)}) copy-start(bf16[256,1792]{1,0:T(8,128)(2,1)} %copy-done.13) | copy-start | bytes 2752516
  100.7 10.9 %collective-permute-start.18 = (bf16[32,4096]{1,0:T(8,128)(2,1)S(1)}, bf16[32,4096]{1,0:T(8,128)(2,1)S(1)}, u32[]{:S(2)}, u32[]{:S(2)}) collective-permute-start(bf16[32,4096]{1,0:T(8,128)(2,1)S(1)} %get-tuple-element.60), channel_id=1, source_target_pairs={{0,8},{2,10},{4,12},{6,14},{8,16},{10,18},{12,20},{14,22},{16,24},... | collective-permute-start | bytes 786440 | tf_op jit(solution)/shard_map/ppermute | solution.py:448
  103.9 3.9 %collective-permute-start.20 = (f32[4,1792]{1,0:T(4,128)S(1)}, f32[4,1792]{1,0:T(4,128)S(1)}, u32[]{:S(2)}, u32[]{:S(2)}) collective-permute-start(f32[4,1792]{1,0:T(4,128)S(1)} %pad_maximum_fusion.2), channel_id=1, source_target_pairs={{0,1},{1,0},{2,3},{3,2},{4,5},{5,4},{6,7},{7,6},{8,9},{9,8},{10,11... | collective-permute-start | bytes 86024 | tf_op jit(solution)/shard_map/ppermute | solution.py:451
  105.5 3.9 %collective-permute-start.17 = (f32[16,512]{1,0:T(8,128)S(1)}, f32[16,512]{1,0:T(8,128)S(1)}, u32[]{:S(2)}, u32[]{:S(2)}) collective-permute-start(f32[16,512]{1,0:T(8,128)S(1)} %constant_dynamic-update-slice_fusion), channel_id=1, source_target_pairs={{0,1},{1,0},{2,3},{3,2},{4,5},{5,4},{6,7},{7,6},{8,9},{9,8},{10,11... | collective-permute-start | bytes 98312 | tf_op jit(solution)/shard_map/ppermute | solution.py:451
  107.9 2.0 %copy-start.12 = (bf16[256,1792]{1,0:T(8,128)(2,1)S(1)}, bf16[256,1792]{1,0:T(8,128)(2,1)}, u32[]{:S(2)}) copy-start(bf16[256,1792]{1,0:T(8,128)(2,1)} %copy-done.11) | copy-start | bytes 2752516
  110.0 1.7 %copy-start.7 = (f32[32,4096]{1,0:T(8,128)S(1)}, f32[32,4096]{1,0:T(8,128)}, u32[]{:S(2)}) copy-start(f32[32,4096]{1,0:T(8,128)} %copy-done.6) | copy-start | bytes 1572868
  110.0 2.5 %copy-start.20 = (f32[256,1792]{1,0:T(8,128)S(1)}, f32[256,1792]{1,0:T(8,128)}, u32[]{:S(2)}) copy-start(f32[256,1792]{1,0:T(8,128)} %get-tuple-element.51) | copy-start | bytes 5505028
